TPU v7x, 256 devices: a whole 4x4x8 slice. The times are simulated.
256 devices in a mesh: ctx: 64 (over x, z, core), tp: 4 (over y).
Axes of the slice: x: 4, y: 4, z: 8, core: 2. Of those that a mesh axis runs over, the one named last changes fastest.
Arguments:
- x_raw: bfloat16 [8192, 4096], P('ctx', 'tp'), may hold values from -6 to 6
- b_raw: bfloat16 [8192, 512], P('ctx'), may hold values from -0.59765625 to 0.59765625
- c_raw: bfloat16 [8192, 512], P('ctx'), may hold values from -0.59765625 to 0.59765625
- z_gate: bfloat16 [8192, 4096], P('ctx', 'tp'), may hold values from -6 to 6
- dt_raw: float32 [8192, 128], P('ctx', 'tp'), may hold values from -4 to 4
- conv_x: float32 [4, 4096], P(None, 'tp'), may hold values from -3 to 3
- conv_b: float32 [4, 512], replicated, may hold values from -3 to 3
- conv_c: float32 [4, 512], replicated, may hold values from -3 to 3
- dt_bias: float32 [128], P('tp'), may hold values from -1 to 1
- a_log: float32 [128], P('tp'), may hold values from -14 to -3
- d_skip: float32 [128], P('tp'), may hold values from 0.5 to 1.5
- gain: float32 [4096], P('tp'), may hold values from 0.5 to 1.5
- grad_out: bfloat16 [8192, 4096], P('ctx', 'tp'), may hold values from -6 to 6
Outputs:
- grad_x_raw: bfloat16 [8192, 4096], P('ctx', 'tp')
- grad_b_raw: bfloat16 [8192, 512], P('ctx')
- grad_c_raw: bfloat16 [8192, 512], P('ctx')
- grad_z_gate: bfloat16 [8192, 4096], P('ctx', 'tp')
- grad_dt_raw: float32 [8192, 128], P('ctx', 'tp')
- grad_conv_x: float32 [4, 4096], P(None, 'tp')
- grad_conv_b: float32 [4, 512], replicated
- grad_conv_c: float32 [4, 512], replicated
- grad_dt_bias: float32 [128], P('tp')
- grad_a_log: float32 [128], P('tp')
- grad_d_skip: float32 [128], P('tp')
- grad_gain: float32 [4096], P('tp')
All inputs are finite; a program needn't handle non-finite values.
Results may differ from a plain program's by a relative error of at most 0.00105.
Values may be sent and summed in bfloat16 or wider, within the bound.
No kernel may reach another device: no remote copies, remote signals or barrier semaphores. Data moves between devices by JAX's collectives and lax.ppermute only.
A program may use at most 192 MiB of HBM per device.

v0:
```python
import functools

import jax
import jax.numpy as jnp
from jax import lax
from jax.experimental import pallas as pl
from jax.experimental.pallas import tpu as pltpu
from jax.sharding import PartitionSpec as P

HEAD_DIM = 32
STATE = 128
GROUPS = 4
CONV = 4
SPAN = 128
TILE = 128
PER = 8
LOCAL = PER * GROUPS
ROWS = PER * HEAD_DIM
ALL = LOCAL * HEAD_DIM
HALF = ALL // 2
CHUNK = 2048
LEAD = 16
GROUP_WIDTH = 1024
EPSILON = 1e-05
F32 = jnp.float32
PARAMS = pltpu.CompilerParams(vmem_limit_bytes=48 << 20)


def dot(a, b, ca=1, cb=0):
    return lax.dot_general(
        a, b, (((ca,), (cb,)), ((), ())), precision=lax.Precision.HIGHEST, preferred_element_type=F32
    )


def group(g):
    return slice(g * ROWS, (g + 1) * ROWS)


def lanes(r):
    return slice(r * TILE, (r + 1) * TILE)


def spot(g, r):
    return slice(g * ROWS + r * HEAD_DIM, g * ROWS + (r + 1) * HEAD_DIM)


def put(dst, r, tile):
    turned = tile.T
    for g in range(GROUPS):
        dst[spot(g, r), :] = turned[g * HEAD_DIM : (g + 1) * HEAD_DIM]


def take(values, r):
    rows = slice(r * HEAD_DIM, (r + 1) * HEAD_DIM)
    return jnp.concatenate([v[rows] for v in values], axis=0).T


def heads_out(v, g):
    return jnp.concatenate(
        [jnp.broadcast_to(v[g * PER + r : g * PER + r + 1], (HEAD_DIM, v.shape[1])) for r in range(PER)], axis=0
    )


def heads_in(v):
    return jnp.concatenate(
        [jnp.sum(v[r * HEAD_DIM : (r + 1) * HEAD_DIM], axis=0, keepdims=True) for r in range(PER)], axis=0
    )


def sigmoid(v):
    return 1.0 / (1.0 + jnp.exp(-v))


def silu_slope(v):
    s = sigmoid(v)
    return s * (1.0 + v * (1.0 - s))


def extend(ext, raw, before):
    ext[0:LEAD, :] = before[...].astype(F32)
    ext[LEAD : LEAD + SPAN, :] = raw[...].astype(F32)


def conv_tile(ext, w, cols):
    total = w[0:1, cols] * ext[LEAD - 3 : LEAD - 3 + SPAN, cols]
    for k in range(1, CONV):
        total = total + w[k : k + 1, cols] * ext[LEAD - 3 + k : LEAD - 3 + k + SPAN, cols]
    return total


def conv_back_tile(ext, pad, w, cols, grad, own, head, wgrad):
    dpre = grad * silu_slope(conv_tile(ext, w, cols))
    pad[8 : 8 + SPAN, cols] = dpre
    for k in range(CONV):
        wgrad[k : k + 1, cols] = jnp.sum(
            dpre * ext[LEAD - 3 + k : LEAD - 3 + k + SPAN, cols], axis=0, keepdims=True
        )
    mine = w[0:1, cols] * pad[11 : 11 + SPAN, cols]
    ahead = w[0:1, cols] * pad[3:11, cols]
    for k in range(1, CONV):
        mine = mine + w[k : k + 1, cols] * pad[11 - k : 11 - k + SPAN, cols]
        ahead = ahead + w[k : k + 1, cols] * pad[3 - k : 11 - k, cols]
    own[:, cols] = mine
    head[:, cols] = ahead


def clear_pad(pad):
    pad[0:8, :] = jnp.zeros((8, pad.shape[1]), F32)
    pad[8 + SPAN : 16 + SPAN, :] = jnp.zeros((8, pad.shape[1]), F32)


def halves(core, full, keep, give):
    keep[...] = full[pl.ds(pl.multiple_of(core * HALF, HALF), HALF), :]
    give[0:HALF, :] = full[pl.ds(pl.multiple_of((1 - core) * HALF, HALF), HALF), :]


def unite(core, full, own, got):
    full[pl.ds(pl.multiple_of(core * HALF, HALF), HALF), :] = own[...]
    full[pl.ds(pl.multiple_of((1 - core) * HALF, HALF), HALF), :] = got[...]


def triangle(upper):
    rows = lax.broadcasted_iota(jnp.int32, (SPAN, SPAN), 0)
    cols = lax.broadcasted_iota(jnp.int32, (SPAN, SPAN), 1)
    return rows <= cols if upper else rows >= cols


def steps_kernel(dt, bias, alog, step, cum, ends):
    v = dt[...] + bias[...]
    step[...] = jnp.maximum(v, 0.0) + jnp.log1p(jnp.exp(-jnp.abs(v)))
    rates = -jnp.exp(alog[...]) * step[...]
    cum[...] = dot(rates, jnp.where(triangle(True), 1.0, 0.0))
    ends[...] = jnp.broadcast_to(jnp.exp(jnp.sum(rates, axis=1, keepdims=True)), ends.shape)


def turn_kernel(z, og, gain, zt, ogt, sgt):
    for r in range(PER):
        put(zt, r, z[:, lanes(r)].astype(F32))
        tile = og[:, lanes(r)].astype(F32)
        put(ogt, r, tile)
        put(sgt, r, tile * gain[:, lanes(r)])


def state_kernel(core, x, hx, b, hb, wx, wb, step, cum, ends, xt, zs, bc, keep, give, ext, extb, full):
    extend(ext, x, hx)
    extend(extb, b, hb)
    for g in range(GROUPS):
        pre = conv_tile(extb, wb, lanes(g))
        bc[:, lanes(g)] = pre * sigmoid(pre)
    for r in range(PER):
        pre = conv_tile(ext, wx, lanes(r))
        put(xt, r, pre * sigmoid(pre))
    scale = jnp.exp(-cum[...]) * step[...]
    for g in range(GROUPS):
        zg = xt[group(g), :] * heads_out(scale, g)
        zs[group(g), :] = zg
        full[group(g), :] = heads_out(ends[...], g) * dot(zg, bc[:, lanes(g)])
    halves(core[0], full, keep, give)
    give[HALF : HALF + LOCAL, :] = ends[...]


def local_kernel(c, hc, wc, bc, xt, zs, cum, skip, cc, mt, y, extc):
    extend(extc, c, hc)
    alpha = jnp.exp(cum[...])
    causal = triangle(True)
    for g in range(GROUPS):
        pre = conv_tile(extc, wc, lanes(g))
        cg = pre * sigmoid(pre)
        cc[:, lanes(g)] = cg
        m = jnp.where(causal, dot(bc[:, lanes(g)], cg, 1, 1), 0.0)
        mt[lanes(g), :] = m
        y[group(g), :] = heads_out(alpha, g) * dot(zs[group(g), :], m) + heads_out(skip[...], g) * xt[group(g), :]


def output_kernel(core, own, got, cc, y1, cum, zt, sgt, full, y, sums):
    unite(core[0], full, own, got)
    alpha = jnp.exp(cum[...])
    for g in range(GROUPS):
        yg = y1[group(g), :] + heads_out(alpha, g) * dot(full[group(g), :], cc[:, lanes(g)], 1, 1)
        y[group(g), :] = yg
        z = zt[group(g), :]
        gated = yg * z * sigmoid(z)
        sums[g : g + 1, :] = jnp.sum(gated * gated, axis=0, keepdims=True)
        sums[GROUPS + g : GROUPS + g + 1, :] = jnp.sum(sgt[group(g), :] * gated, axis=0, keepdims=True)


def gate_kernel(core, sums, y, zt, sgt, cum, cc, keep, give, dy, dg, full):
    alpha = jnp.exp(cum[...])
    for g in range(GROUPS):
        inv = lax.rsqrt(sums[g : g + 1, :] / GROUP_WIDTH + EPSILON)
        fix = inv * inv * inv * sums[GROUPS + g : GROUPS + g + 1, :] / GROUP_WIDTH
        z = zt[group(g), :]
        act = z * sigmoid(z)
        dgated = inv * sgt[group(g), :] - y[group(g), :] * act * fix
        dg[group(g), :] = dgated
        dyg = dgated * act
        dy[group(g), :] = dyg
        full[group(g), :] = dot(heads_out(alpha, g) * dyg, cc[:, lanes(g)])
    halves(core[0], full, keep, give)


def middle_kernel(
    sums, y, zt, ogt, dy, dg, full, mt, zs, xt, bc, cc, cum, skip, c, hc, wc,
    dz, db, dcum, dskip, gz, dgain, cown, chead, wcg, extc, padc, dc,
):
    alpha = jnp.exp(cum[...])
    causal = triangle(True)
    slope, shares = [], []
    for g in range(GROUPS):
        z, yg, dyg = zt[group(g), :], y[group(g), :], dy[group(g), :]
        inv = lax.rsqrt(sums[g : g + 1, :] / GROUP_WIDTH + EPSILON)
        slope.append(dg[group(g), :] * yg * silu_slope(z))
        shares.append(ogt[group(g), :] * yg * z * sigmoid(z) * inv)
        heads = slice(g * PER, (g + 1) * PER)
        x = xt[group(g), :]
        passed = heads_in(dyg * x)
        dskip[heads, :] = passed
        dcum[heads, :] = heads_in(dyg * (yg - heads_out(skip[...], g) * x))
        u = heads_out(alpha, g) * dyg
        dz[group(g), :] = dot(u, mt[lanes(g), :], 1, 1)
        dm = jnp.where(causal, dot(zs[group(g), :], u, 0, 0), 0.0)
        dc[:, lanes(g)] = dot(dm, bc[:, lanes(g)], 0, 0) + dot(u, full[group(g), :], 0, 0)
        db[:, lanes(g)] = dot(dm, cc[:, lanes(g)])
    for r in range(PER):
        gz[:, lanes(r)] = take(slope, r).astype(jnp.bfloat16)
        dgain[:, lanes(r)] = jnp.sum(take(shares, r), axis=0, keepdims=True)
    extend(extc, c, hc)
    clear_pad(padc)
    for g in range(GROUPS):
        conv_back_tile(extc, padc, wc, lanes(g), dc[:, lanes(g)], cown, chead, wcg)


def last_kernel(
    core, own, got, full, ends, dz1, db1, dcum1, dy, zs, xt, bc, cum, step, skip, dt, bias, alog, x, hx, wx, b, hb, wb,
    xown, xhead, wxg, bown, bhead, wbg, ddt, drate, later, ext, extb, pad, padb,
):
    unite(core[0], later, own, got)
    gamma = jnp.exp(-cum[...])
    scale = gamma * step[...]
    clear_pad(pad)
    clear_pad(padb)
    extend(ext, x, hx)
    extend(extb, b, hb)
    dxs, turned, straight = [], [], []
    at_end = lax.broadcasted_iota(jnp.int32, (PER, SPAN), 1) == SPAN - 1
    for g in range(GROUPS):
        heads = slice(g * PER, (g + 1) * PER)
        zg, xg = zs[group(g), :], xt[group(g), :]
        d = heads_out(ends[...], g) * later[group(g), :]
        second = dot(d, bc[:, lanes(g)], 1, 1)
        dzg = dz1[group(g), :] + second
        dxs.append(heads_out(scale, g) * dzg + heads_out(skip[...], g) * dy[group(g), :])
        edge = heads_in(zg * second + d * full[group(g), :])
        edge = jnp.sum(edge, axis=1, keepdims=True)
        turned.append(dcum1[heads, :] - heads_in(dzg * zg) + jnp.where(at_end, edge, 0.0))
        straight.append(heads_in(dzg * xg))
        dbg = db1[:, lanes(g)] + dot(zg, d, 0, 0)
        conv_back_tile(extb, padb, wb, lanes(g), dbg, bown, bhead, wbg)
    dlog = dot(jnp.concatenate(turned, axis=0), jnp.where(triangle(False), 1.0, 0.0))
    rate = -jnp.exp(alog[...])
    drate[...] = dlog * rate * step[...]
    dstep = jnp.concatenate(straight, axis=0) * gamma + dlog * rate
    ddt[...] = dstep * sigmoid(dt[...] + bias[...])
    for r in range(PER):
        conv_back_tile(ext, pad, wx, lanes(r), take(dxs, r), xown, xhead, wxg)


def scan_kernel(backward, s, d, o):
    count = s.shape[0]
    at = d.shape[2] - TILE
    carry = [jnp.zeros((1, TILE), F32)] * (CHUNK // TILE)
    for j in range(count):
        j = count - 1 - j if backward else j
        decay = d[j, :, at:]
        for k in range(CHUNK // TILE):
            o[j, :, lanes(k)] = carry[k]
            carry[k] = decay * carry[k] + s[j, :, lanes(k)]


def call(kernel, name, outs, args, scratch=(), scalars=0, flops=20_000_000):
    smem = pl.BlockSpec(memory_space=pltpu.SMEM)
    vmem = pl.BlockSpec(memory_space=pltpu.VMEM)
    return pl.pallas_call(
        kernel,
        out_shape=[jax.ShapeDtypeStruct(s, d) for s, d in outs],
        in_specs=[smem if i < scalars else vmem for i in range(len(args))],
        out_specs=[vmem] * len(outs),
        scratch_shapes=[pltpu.VMEM(s, F32) for s in scratch],
        compiler_params=PARAMS,
        cost_estimate=pl.CostEstimate(flops=flops, bytes_accessed=4 << 20, transcendentals=1 << 18),
        name=name,
    )(*args)


def swap_cores(v):
    return lax.ppermute(v, "ctx", [(i, i ^ 1) for i in range(lax.axis_size("ctx"))])


def alike(size, by):
    return [(i, i ^ by) for i in range(size)]


def over_chips(v):
    size = lax.axis_size("ctx")
    return lax.all_to_all(
        v, "ctx", 0, 0, axis_index_groups=[list(range(c, size, 2)) for c in range(2)]
    )


def wide(a):
    return jnp.repeat(a, HEAD_DIM, axis=0)


def pair_scan(keep, got, first, second, is_first, decays, backward):
    lead = jnp.where(is_first, keep, got)
    follow = jnp.where(is_first, got, keep)
    joint = (wide(second) * lead + follow).reshape(-1, 1, CHUNK)
    if decays is None:
        both = jnp.repeat(first * second, HALF // (LOCAL // 2) * STATE // CHUNK, axis=0)[:, None]
        joint = jnp.concatenate([joint, both], axis=2)
    pieces = over_chips(joint)
    decays = pieces if decays is None else decays
    (entering,) = call(
        functools.partial(scan_kernel, backward),
        "block_scan",
        [((pieces.shape[0], 1, CHUNK), F32)],
        (pieces, decays),
    )
    ahead = over_chips(entering).reshape(HALF, STATE)
    between = wide(first) * ahead + lead
    other = swap_cores(jnp.where(is_first, between, ahead))
    return jnp.where(is_first, ahead, between), other, decays


def butterfly(x, axis):
    by = 1
    while by < lax.axis_size(axis):
        x = x + lax.ppermute(x, axis, alike(lax.axis_size(axis), by))
        by *= 2
    return x


def by_group(v):
    return v.reshape((PER, GROUPS) + v.shape[1:]).swapaxes(0, 1).reshape(v.shape)


def by_head(v):
    return v.reshape((GROUPS, PER) + v.shape[1:]).swapaxes(0, 1).reshape(v.shape)


def body(
    x_raw, b_raw, c_raw, z_gate, dt_raw, conv_x, conv_b, conv_c, dt_bias, a_log, d_skip, gain, grad_out
):
    size = lax.axis_size("ctx")
    core = lax.axis_index("ctx") % 2
    cores = core.reshape(1)
    is_even = core == 0
    t_shape = ((ALL, SPAN), F32)
    bc_shape = ((SPAN, GROUPS * STATE), F32)
    h_shape = ((LOCAL, SPAN), F32)
    tails = jnp.concatenate([v[SPAN - LEAD :] for v in (x_raw, b_raw, c_raw)], axis=1)
    before = lax.ppermute(tails, "ctx", [(i, i + 1) for i in range(size - 1)])
    wx, wb = x_raw.shape[1], b_raw.shape[1]
    hx, hb, hc = before[:, :wx], before[:, wx : wx + wb], before[:, wx + wb :]

    dt = by_group(dt_raw.T)
    bias, alog, skip_col = (by_group(v)[:, None] for v in (dt_bias, a_log, d_skip))
    skip = jnp.broadcast_to(skip_col, h_shape[0])
    step, cum, ends = call(steps_kernel, "steps", [h_shape] * 3, (dt, bias, alog))
    zt, ogt, sgt = call(turn_kernel, "turn", [t_shape] * 3, (z_gate, grad_out, gain[None]))
    xt, zs, bc, keep, give = call(
        state_kernel,
        "state",
        [t_shape, t_shape, bc_shape, ((HALF, STATE), F32), ((HALF + LOCAL, STATE), F32)],
        (cores, x_raw, hx, b_raw, hb, conv_x, conv_b, step, cum, ends),
        [(LEAD + SPAN, wx), (LEAD + SPAN, wb), (ALL, STATE)],
        scalars=1,
    )
    got = swap_cores(give)
    mine = lax.dynamic_slice_in_dim(ends, core * (LOCAL // 2), LOCAL // 2)
    theirs = lax.dynamic_slice_in_dim(got[HALF:], core * (LOCAL // 2), LOCAL // 2)
    even, odd = jnp.where(is_even, mine, theirs), jnp.where(is_even, theirs, mine)
    enter_own, enter_got, decays = pair_scan(keep, got[:HALF], even, odd, is_even, None, False)

    cc, mt, y1 = call(
        local_kernel,
        "local",
        [bc_shape, ((GROUPS * SPAN, SPAN), F32), t_shape],
        (c_raw, hc, conv_c, bc, xt, zs, cum, skip),
        [(LEAD + SPAN, wb)],
    )
    enter, y, sums = call(
        output_kernel,
        "output",
        [t_shape, t_shape, ((2 * GROUPS, SPAN), F32)],
        (cores, enter_own, enter_got, cc, y1, cum, zt, sgt),
        scalars=1,
    )
    sums = butterfly(sums, "tp")
    keep, give, dy, dg = call(
        gate_kernel,
        "gate",
        [((HALF, STATE), F32)] * 2 + [t_shape, t_shape],
        (cores, sums, y, zt, sgt, cum, cc),
        [(ALL, STATE)],
        scalars=1,
    )
    got = swap_cores(give)
    later_own, later_got, _ = pair_scan(keep, got, odd, even, ~is_even, decays, True)
    own_shape, head_shape, w_shape = bc_shape, ((8, wb), F32), ((CONV, wb), F32)
    dz, db, dcum, dskip, grad_z, dgain, cown, chead, wcg = call(
        middle_kernel,
        "middle",
        [t_shape, bc_shape, h_shape, h_shape, ((SPAN, wx), jnp.bfloat16), ((1, wx), F32)]
        + [own_shape, head_shape, w_shape],
        (sums, y, zt, ogt, dy, dg, enter, mt, zs, xt, bc, cc, cum, skip, c_raw, hc, conv_c),
        [(LEAD + SPAN, wb), (LEAD + SPAN, wb), (SPAN, wb)],
    )
    xown, xhead, wxg, bown, bhead, wbg, ddt, drate = call(
        last_kernel,
        "last",
        [((SPAN, wx), F32), ((8, wx), F32), ((CONV, wx), F32), own_shape, head_shape, w_shape, h_shape, h_shape],
        (cores, later_own, later_got, enter, ends, dz, db, dcum, dy, zs, xt, bc, cum, step, skip, dt, bias, alog)
        + (x_raw, hx, conv_x, b_raw, hb, conv_b),
        [(ALL, STATE), (LEAD + SPAN, wx), (LEAD + SPAN, wb), (LEAD + SPAN, wx), (LEAD + SPAN, wb)],
        scalars=1,
    )
    heads = jnp.concatenate([xhead, bhead, chead], axis=1)
    heads = lax.ppermute(heads, "ctx", [(i + 1, i) for i in range(size - 1)])

    def settle(own, incoming):
        return jnp.concatenate([own[: SPAN - 8], own[SPAN - 8 :] + incoming], axis=0)

    grad_x_raw = settle(xown, heads[:, :wx]).astype(jnp.bfloat16)
    bc_part = jnp.concatenate(
        [settle(bown, heads[:, wx : wx + wb]), settle(cown, heads[:, wx + wb :])], axis=0
    )
    slices = jnp.stack(jnp.split(bc_part, GROUPS, axis=1))
    mine = jnp.sum(lax.all_to_all(slices, "tp", 0, 0), axis=0).astype(jnp.bfloat16)
    spread = lax.all_to_all(jnp.broadcast_to(mine, slices.shape), "tp", 0, 0)
    bc_grad = jnp.concatenate([spread[g] for g in range(GROUPS)], axis=1)
    grad_b_raw, grad_c_raw = bc_grad[:SPAN], bc_grad[SPAN:]
    small = by_head(jnp.stack([jnp.sum(v, axis=1) for v in (ddt, drate, dskip)], axis=1))
    parts = (wbg, wcg, wxg, dgain, small)
    packed = jnp.concatenate([part.reshape(-1) for part in parts])
    packed = butterfly(jnp.pad(packed, (0, -packed.size % 1024)).reshape(-1, TILE), "ctx")
    shared = (wbg.size + wcg.size) // TILE
    packed = jnp.concatenate([butterfly(packed[:shared], "tp").reshape(-1), packed[shared:].reshape(-1)])
    totals, start = [], 0
    for part in parts:
        totals.append(packed[start : start + part.size].reshape(part.shape))
        start += part.size
    conv_b_total, conv_c_total, conv_x_total, gain_total, small = totals
    return (
        grad_x_raw,
        grad_b_raw,
        grad_c_raw,
        grad_z,
        by_head(ddt).T,
        conv_x_total,
        conv_b_total,
        conv_c_total,
        small[:, 0],
        small[:, 1],
        small[:, 2],
        gain_total.reshape(-1),
    )


def solution(mesh):
    rows, cols, some = P("ctx", "tp"), P(None, "tp"), P("tp")
    return jax.shard_map(
        body,
        mesh=mesh,
        in_specs=(rows, P("ctx", None), P("ctx", None), rows, rows, cols, P(), P(), some, some, some, some, rows),
        out_specs=(rows, P("ctx", None), P("ctx", None), rows, rows, cols, P(), P(), some, some, some, some),
        check_vma=False,
    )
```

profile of v0, /device:TPU:32, one launch (start us, length us, event | category | flops | bytes accessed | tf_op | source)
XLA Modules:
  0.0 196.9 jit_solution(4585100008639124887)
XLA Ops:
  0.7 0.7 slice-done
  1.4 1.9 collective-permute-start
  6.2 0.8 collective-permute-done
  7.8 1.2 state.1
  9.0 1.5 collective-permute-start.1
  10.5 1.2 collective-permute-done.1
  12.6 24.1 %all_to_all.30.s.d = f32[32,1,2176]{2,1,0:T(1,128)S(1)} all-to-all(f32[32,1,2176]{2,1,0:T(1,128)S(1)} %pad_maximum_fusion.2), channel_id=1, replica_groups={{0,8,16,24,32,40,48,56,64,72,80,88,96,104,112,120,128,136,144,152,160,1..., dimensions={0} | all-to-all | bytes 557056 | tf_op jit(solution)/shard_map/all_to_all | solution.py:305
  36.8 16.4 %all_to_all.31 = f32[32,1,2048]{2,1,0:T(1,128)S(1)} all-to-all(f32[32,1,2048]{2,1,0:T(1,128)S(1)} %block_scan.2), channel_id=1, replica_groups={{0,8,16,24,32,40,48,56,64,72,80,88,96,104,112,120,128,136,144,152,160,1..., dimensions={0} | all-to-all | bytes 524288 | tf_op jit(solution)/shard_map/all_to_all | solution.py:305
  53.2 0.8 fusion.1
  55.4 0.9 copy-done.29
  56.7 0.8 copy-done.13
  58.2 2.2 %local.1 = (f32[128,512]{1,0:T(8,128)S(1)}, f32[512,128]{1,0:T(8,128)S(1)}, f32[1024,128]{1,0:T(8,128)S(1)}) custom-call(bf16[128,512]{1,0:T(8,128)(2,1)S(1)} %copy-done.7, bf16[16,512]{1,0:T(8,128)(2,1)S(1)} %get-tuple-element.110.hc, f32[4,512]{1,0:T(4,128)S(1)} %copy-done.51, f32[128,512]{1,0:T(8,128)S(1)} %get-tuple-element.55.bc, ...), custom_call_target="tpu_custom_call" | custom-call | flops 20000000 | bytes 4194304 | tf_op jit(solution)/shard_map/local/pallas_call | solution.py:283
  61.2 1.7 output.1
  62.9 1.7 collective-permute-start.3
  64.5 2.0 %collective-permute-done.3 = f32[8,128]{1,0:T(8,128)S(1)} collective-permute-done((f32[8,128]{1,0:T(8,128)S(1)}, f32[8,128]{1,0:T(8,128)S(1)}, u32[]{:S(2)}, u32[]{:S(2)}) %collective-permute-start.3) | collective-permute-done | bytes 4128 | tf_op jit(solution)/shard_map/ppermute | solution.py:338
  66.6 3.2 %collective-permute-start.4 = (f32[8,128]{1,0:T(8,128)S(1)}, f32[8,128]{1,0:T(8,128)S(1)}, u32[]{:S(2)}, u32[]{:S(2)}) collective-permute-start(f32[8,128]{1,0:T(8,128)S(1)} %add.65), channel_id=1, source_target_pairs={{0,2},{1,3},{2,0},{3,1},{4,6},{5,7},{6,4},{7,5},{8,10},{9,11},{10,... | collective-permute-start | bytes 12296 | tf_op jit(solution)/shard_map/ppermute | solution.py:338
  69.8 1.9 collective-permute-done.4
  71.7 1.6 gate.1
  73.9 0.8 copy-done.15
  74.8 1.9 collective-permute-done.5
  76.6 1.1 fusion.3
  77.7 16.9 %all_to_all.32.s = f32[32,1,2048]{2,1,0:T(1,128)S(1)} all-to-all(f32[32,1,2048]{2,1,0:T(1,128)S(1)} %bitcast.93), channel_id=1, replica_groups={{0,8,16,24,32,40,48,56,64,72,80,88,96,104,112,120,128,136,144,152,160,1..., dimensions={0} | all-to-all | bytes 524288 | tf_op jit(solution)/shard_map/all_to_all | solution.py:305
  94.9 16.3 %all_to_all.33 = f32[32,1,2048]{2,1,0:T(1,128)S(1)} all-to-all(f32[32,1,2048]{2,1,0:T(1,128)S(1)} %block_scan.3), channel_id=1, replica_groups={{0,8,16,24,32,40,48,56,64,72,80,88,96,104,112,120,128,136,144,152,160,1..., dimensions={0} | all-to-all | bytes 524288 | tf_op jit(solution)/shard_map/all_to_all | solution.py:305
  111.3 1.9 fusion.6
  113.8 4.4 %middle.1 = (f32[1024,128]{1,0:T(8,128)S(1)}, f32[128,512]{1,0:T(8,128)S(1)}, f32[32,128]{1,0:T(8,128)S(1)}, f32[32,128]{1,0:T(8,128)S(1)}, bf16[128,1024]{1,0:T...) custom-call(f32[8,128]{1,0:T(8,128)S(1)} %copy-done.50, ...), custom_call_target="tpu_custom_call" | custom-call | flops 20000000 | bytes 4194304 | tf_op jit(solution)/shard_map/middle/pallas_call | solution.py:283
  118.2 0.8 copy-done.17
  119.0 0.7 copy-done.26
  123.5 0.9 reduce_sum.39
  124.5 1.3 copy.50
  125.8 1.7 slice.122
  127.5 0.9 copy-done.4
  128.4 0.9 copy-done.9
  129.3 1.0 copy-done.18
  130.4 0.8 copy-done.20
  131.1 0.9 copy-done.27
  132.1 0.7 copy-done.36
  132.8 0.7 copy-done.38
  133.5 0.7 copy-done.40
  134.2 0.7 copy-done.42
  134.9 0.7 copy-done.44
  135.6 0.7 copy-done.46
  138.5 3.9 %last.1 = (f32[128,1024]{1,0:T(8,128)S(1)}, f32[8,1024]{1,0:T(8,128)S(1)}, f32[4,1024]{1,0:T(4,128)S(1)}, f32[128,512]{1,0:T(8,128)S(1)}, f32[8,512]{1,0:T(8,128...) custom-call(s32[1]{0:T(128)} %bitcast.core, f32[512,128]{1,0:T(8,128)S(1)} %copy-done.4, ...), custom_call_target="tpu_custom_call" | custom-call | flops 20000000 | bytes 4194304 | tf_op jit(solution)/shard_map/last/pallas_call | solution.py:283
  142.4 0.8 copy-done.31
  145.2 1.9 collective-permute-start.7
  147.9 1.1 collective-permute-done.7
  149.0 0.7 slice_add_fusion.2
  149.8 2.1 %collective-permute-done.9 = f32[80,128]{1,0:T(8,128)S(1)} collective-permute-done((f32[80,128]{1,0:T(8,128)S(1)}, f32[80,128]{1,0:T(8,128)S(1)}, u32[]{:S(2)}, u32[]{:S(2)}) %collective-permute-start.9) | collective-permute-done | bytes 40992 | tf_op jit(solution)/shard_map/ppermute | solution.py:338
  151.9 1.9 collective-permute-start.10
  153.9 3.0 %collective-permute-done.10 = f32[80,128]{1,0:T(8,128)S(1)} collective-permute-done((f32[80,128]{1,0:T(8,128)S(1)}, f32[80,128]{1,0:T(8,128)S(1)}, u32[]{:S(2)}, u32[]{:S(2)}) %collective-permute-start.10) | collective-permute-done | bytes 40992 | tf_op jit(solution)/shard_map/ppermute | solution.py:338
  156.9 2.6 %collective-permute-start.11 = (f32[80,128]{1,0:T(8,128)S(1)}, f32[80,128]{1,0:T(8,128)S(1)}, u32[]{:S(2)}, u32[]{:S(2)}) collective-permute-start(f32[80,128]{1,0:T(8,128)S(1)} %add.74), channel_id=1, source_target_pairs={{0,32},{4,36},{8,40},{12,44},{16,48},{20,52},{24,56},{28,60},{32,0... | collective-permute-start | bytes 122888 | tf_op jit(solution)/shard_map/ppermute | solution.py:338
  159.6 0.8 pad_maximum_fusion.1
  160.4 4.5 %all-to-all-start.4 = ((f32[4,256,128]{2,1,0:T(8,128)}), f32[4,256,128]{2,1,0:T(8,128)S(1)}, u32[]{:S(2)}, u32[]{:S(2)}) async-start(f32[4,256,128]{2,1,0:T(8,128)} %pad_maximum_fusion.1), calls=%async_computation.4 | async-start | bytes 1048576 | tf_op jit(solution)/shard_map/all_to_all | solution.py:439
  165.6 3.4 %collective-permute-done.12 = f32[80,128]{1,0:T(8,128)S(1)} collective-permute-done((f32[80,128]{1,0:T(8,128)S(1)}, f32[80,128]{1,0:T(8,128)S(1)}, u32[]{:S(2)}, u32[]{:S(2)}) %collective-permute-start.12) | collective-permute-done | bytes 40992 | tf_op jit(solution)/shard_map/ppermute | solution.py:338
  169.0 1.4 collective-permute-start.13
  170.4 0.7 pad_maximum_fusion.3
  171.1 3.4 %collective-permute-done.13 = f32[80,128]{1,0:T(8,128)S(1)} collective-permute-done((f32[80,128]{1,0:T(8,128)S(1)}, f32[80,128]{1,0:T(8,128)S(1)}, u32[]{:S(2)}, u32[]{:S(2)}) %collective-permute-start.13) | collective-permute-done | bytes 40992 | tf_op jit(solution)/shard_map/ppermute | solution.py:338
  174.5 2.1 %collective-permute-start.14 = (f32[32,128]{1,0:T(8,128)S(1)}, f32[32,128]{1,0:T(8,128)S(1)}, u32[]{:S(2)}, u32[]{:S(2)}) collective-permute-start(f32[32,128]{1,0:T(8,128)S(1)} %slice.158), channel_id=1, source_target_pairs={{0,1},{1,0},{2,3},{3,2},{4,5},{5,4},{6,7},{7,6},{8,9},{9,8},{10,11... | collective-permute-start | bytes 49160 | tf_op jit(solution)/shard_map/ppermute | solution.py:338
  177.3 1.0 collective-permute-done.14
  178.4 3.5 %collective-permute-start.15 = (f32[32,128]{1,0:T(8,128)S(1)}, f32[32,128]{1,0:T(8,128)S(1)}, u32[]{:S(2)}, u32[]{:S(2)}) collective-permute-start(f32[32,128]{1,0:T(8,128)S(1)} %get-tuple-element.112), channel_id=1, source_target_pairs={{0,2},{1,3},{2,0},{3,1},{4,6},{5,7},{6,4},{7,5},{8,10},{9,11},{10,... | collective-permute-start | bytes 49160 | tf_op jit(solution)/shard_map/ppermute | solution.py:338
  181.9 0.7 slice_reduce_fusion
  183.7 0.7 broadcast_in_dim.30
  184.4 5.0 %all-to-all-start.5 = ((bf16[4,256,128]{2,1,0:T(8,128)(2,1)}), bf16[4,256,128]{2,1,0:T(8,128)(2,1)S(1)}, u32[]{:S(2)}, u32[]{:S(2)}) async-start(bf16[4,256,128]{2,1,0:T(8,128)(2,1)} %broadcast_in_dim.30), calls=%async_computation.5 | async-start | bytes 524288 | tf_op jit(solution)/shard_map/all_to_all | solution.py:440
  190.6 5.5 %all-to-all-done.5 = bf16[4,256,128]{2,1,0:T(8,128)(2,1)S(1)} async-done(((bf16[4,256,128]{2,1,0:T(8,128)(2,1)}), bf16[4,256,128]{2,1,0:T(8,128)(2,1)S(1)}, u32[]{:S(2)}, u32[]{:S(2)}) %all-to-all-start.5) | async-done | bytes 262176 | tf_op jit(solution)/shard_map/all_to_all | solution.py:440
  196.2 0.7 fusion.11
  (211 shorter events, 21.8 us)
Async XLA Ops:
  0.6 0.8 slice-start
  0.7 0.8 slice-start.1
  0.7 0.7 slice-start.2
  1.4 5.6 %collective-permute-start = (bf16[16,2048]{1,0:T(8,128)(2,1)S(1)}, bf16[16,2048]{1,0:T(8,128)(2,1)S(1)}, u32[]{:S(2)}, u32[]{:S(2)}) collective-permute-start(bf16[16,2048]{1,0:T(8,128)(2,1)S(1)} %pad_maximum_fusion.5), channel_id=1, source_target_pairs={{0,4},{4,8},{8,12},{12,16},{16,20},{20,24},{24,28},{28,32},{32,36}... | collective-permute-start | bytes 196616 | tf_op jit(solution)/shard_map/ppermute | solution.py:362
  4.8 0.7 copy-start.43
  5.7 1.9 copy-start.2
  5.7 1.9 copy-start.39
  6.2 0.9 copy-start.41
  6.2 5.5 %copy-start.37 = (f32[32,128]{1,0:T(8,128)}, f32[32,128]{1,0:T(8,128)S(1)}, u32[]{:S(2)}) copy-start(f32[32,128]{1,0:T(8,128)S(1)} %get-tuple-element.50.ends) | copy-start | bytes 49156
  6.2 55.0 %copy-start.10 = (f32[32,128]{1,0:T(8,128)}, f32[32,128]{1,0:T(8,128)S(1)}, u32[]{:S(2)}) copy-start(f32[32,128]{1,0:T(8,128)S(1)} %get-tuple-element.52.cum) | copy-start | bytes 49156
  6.2 1.4 copy-start.8
  7.0 50.5 %copy-start.33 = (bf16[16,512]{1,0:T(8,128)(2,1)}, bf16[16,512]{1,0:T(8,128)(2,1)S(1)}, u32[]{:S(2)}) copy-start(bf16[16,512]{1,0:T(8,128)(2,1)S(1)} %get-tuple-element.110.hc) | copy-start | bytes 49156
  7.0 2.0 %copy-start.19 = (bf16[16,1024]{1,0:T(8,128)(2,1)}, bf16[16,1024]{1,0:T(8,128)(2,1)S(1)}, u32[]{:S(2)}) copy-start(bf16[16,1024]{1,0:T(8,128)(2,1)S(1)} %slice.142.hx) | copy-start | bytes 98308
  9.0 48.5 %copy-start = (f32[1024,128]{1,0:T(8,128)}, f32[1024,128]{1,0:T(8,128)S(1)}, u32[]{:S(2)}) copy-start(f32[1024,128]{1,0:T(8,128)S(1)} %get-tuple-element.56.xt) | copy-start | bytes 1572868
  9.0 2.7 %collective-permute-start.1 = (f32[544,128]{1,0:T(8,128)S(1)}, f32[544,128]{1,0:T(8,128)S(1)}, u32[]{:S(2)}, u32[]{:S(2)}) collective-permute-start(f32[544,128]{1,0:T(8,128)S(1)} %get-tuple-element.53), channel_id=1, source_target_pairs={{0,4},{4,0},{8,12},{12,8},{16,20},{20,16},{24,28},{28,24},{32,36},... | collective-permute-start | bytes 835592 | tf_op jit(solution)/shard_map/ppermute | solution.py:296
  11.7 41.5 %copy-start.67 = (f32[16,128]{1,0:T(8,128)}, f32[16,128]{1,0:T(8,128)S(1)}, u32[]{:S(2)}) copy-start(f32[16,128]{1,0:T(8,128)S(1)} %get-tuple-element.93) | copy-start | bytes 24580
  53.2 1.7 copy-start.28
  54.0 7.2 %collective-permute-start.2 = (f32[512,128]{1,0:T(8,128)}, f32[512,128]{1,0:T(8,128)}, u32[]{:S(2)}, u32[]{:S(2)}) collective-permute-start(f32[512,128]{1,0:T(8,128)} %get-tuple-element.94), channel_id=1, source_target_pairs={{0,4},{4,0},{8,12},{12,8},{16,20},{20,16},{24,28},{28,24},{32,36},... | collective-permute-start | bytes 786440 | tf_op jit(solution)/shard_map/ppermute | solution.py:296
  55.4 0.9 copy-start.29
  56.3 1.2 copy-start.7
  56.7 0.8 copy-start.13
  58.2 2.3 %copy-start.21 = (f32[32,128]{1,0:T(8,128)}, f32[32,128]{1,0:T(8,128)S(1)}, u32[]{:S(2)}) copy-start(f32[32,128]{1,0:T(8,128)S(1)} %broadcast_in_dim.28.skip) | copy-start | bytes 49156
  62.8 8.8 %copy-start.11 = (f32[32,128]{1,0:T(8,128)S(1)}, f32[32,128]{1,0:T(8,128)}, u32[]{:S(2)}) copy-start(f32[32,128]{1,0:T(8,128)} %copy-done.10) | copy-start | bytes 49156
  62.9 3.7 %collective-permute-start.3 = (f32[8,128]{1,0:T(8,128)S(1)}, f32[8,128]{1,0:T(8,128)S(1)}, u32[]{:S(2)}, u32[]{:S(2)}) collective-permute-start(f32[8,128]{1,0:T(8,128)S(1)} %get-tuple-element.62), channel_id=1, source_target_pairs={{0,1},{1,0},{2,3},{3,2},{4,5},{5,4},{6,7},{7,6},{8,9},{9,8},{10,11... | collective-permute-start | bytes 12296 | tf_op jit(solution)/shard_map/ppermute | solution.py:338
  66.6 5.1 %collective-permute-start.4 = (f32[8,128]{1,0:T(8,128)S(1)}, f32[8,128]{1,0:T(8,128)S(1)}, u32[]{:S(2)}, u32[]{:S(2)}) collective-permute-start(f32[8,128]{1,0:T(8,128)S(1)} %add.65), channel_id=1, source_target_pairs={{0,2},{1,3},{2,0},{3,1},{4,6},{5,7},{6,4},{7,5},{8,10},{9,11},{10,... | collective-permute-start | bytes 12296 | tf_op jit(solution)/shard_map/ppermute | solution.py:338
  71.7 1.6 copy-start.49
  73.9 0.8 copy-start.15
  74.8 1.9 collective-permute-start.5
  94.7 16.5 %copy-start.66 = (f32[16,128]{1,0:T(8,128)S(1)}, f32[16,128]{1,0:T(8,128)}, u32[]{:S(2)}) copy-start(f32[16,128]{1,0:T(8,128)} %copy-done.65) | copy-start | bytes 24580
  94.8 16.4 %copy-start.6 = (f32[512,128]{1,0:T(8,128)S(1)}, f32[512,128]{1,0:T(8,128)}, u32[]{:S(2)}) copy-start(f32[512,128]{1,0:T(8,128)} %copy-done.5) | copy-start | bytes 786436
  94.9 18.3 %copy-start.25 = (f32[512,128]{1,0:T(8,128)S(1)}, f32[512,128]{1,0:T(8,128)}, u32[]{:S(2)}) copy-start(f32[512,128]{1,0:T(8,128)} %copy-done.24) | copy-start | bytes 786436
  111.2 2.0 copy-start.12
  111.2 2.0 copy-start.14
  111.2 2.0 copy-start.16
  111.2 2.0 copy-start.22
  111.2 2.0 copy-start.34
  111.2 2.0 copy-start.52
  113.1 14.3 %collective-permute-start.6 = (f32[512,128]{1,0:T(8,128)}, f32[512,128]{1,0:T(8,128)}, u32[]{:S(2)}, u32[]{:S(2)}) collective-permute-start(f32[512,128]{1,0:T(8,128)} %get-tuple-element.96), channel_id=1, source_target_pairs={{0,4},{4,0},{8,12},{12,8},{16,20},{20,16},{24,28},{28,24},{32,36},... | collective-permute-start | bytes 786440 | tf_op jit(solution)/shard_map/ppermute | solution.py:296
  113.8 13.6 %copy-start.3 = (bf16[128,1024]{1,0:T(8,128)(2,1)S(1)}, bf16[128,1024]{1,0:T(8,128)(2,1)}, u32[]{:S(2)}) copy-start(bf16[128,1024]{1,0:T(8,128)(2,1)} %x.5) | copy-start | bytes 786436
  118.2 0.8 copy-start.17
  119.0 0.7 copy-start.26
  123.5 4.0 %copy-start.1 = (f32[1024,128]{1,0:T(8,128)S(1)}, f32[1024,128]{1,0:T(8,128)}, u32[]{:S(2)}) copy-start(f32[1024,128]{1,0:T(8,128)} %copy-done) | copy-start | bytes 1572868
  125.8 1.7 copy-start.23
  127.5 1.0 copy-start.4
  128.4 0.9 copy-start.9
  129.3 1.0 copy-start.18
  130.3 0.8 copy-start.20
  131.1 0.9 copy-start.27
  138.5 6.1 %copy-start.63 = (f32[1,1024]{1,0:T(1,128)S(1)}, f32[1,1024]{1,0:T(1,128)}, u32[]{:S(2)}) copy-start(f32[1,1024]{1,0:T(1,128)} %copy-done.62) | copy-start | bytes 12292
  138.5 6.7 %copy-start.59 = (f32[8,512]{1,0:T(8,128)S(1)}, f32[8,512]{1,0:T(8,128)}, u32[]{:S(2)}) copy-start(f32[8,512]{1,0:T(8,128)} %copy-done.58) | copy-start | bytes 49156
  142.4 0.8 copy-start.31
  143.2 3.9 %copy-start.32 = (f32[128,1024]{1,0:T(8,128)S(1)}, f32[128,1024]{1,0:T(8,128)}, u32[]{:S(2)}) copy-start(f32[128,1024]{1,0:T(8,128)} %copy-done.31) | copy-start | bytes 1572868
  144.6 3.2 %collective-permute-start.8 = (f32[80,128]{1,0:T(8,128)S(1)}, f32[80,128]{1,0:T(8,128)S(1)}, u32[]{:S(2)}, u32[]{:S(2)}) collective-permute-start(f32[80,128]{1,0:T(8,128)S(1)} %pad_bitcast_fusion), channel_id=1, source_target_pairs={{0,4},{4,0},{8,12},{12,8},{16,20},{20,16},{24,28},{28,24},{32,36},... | collective-permute-start | bytes 122888 | tf_op jit(solution)/shard_map/ppermute | solution.py:338
  145.2 3.8 %collective-permute-start.7 = (f32[8,2048]{1,0:T(8,128)S(1)}, f32[8,2048]{1,0:T(8,128)S(1)}, u32[]{:S(2)}, u32[]{:S(2)}) collective-permute-start(f32[8,2048]{1,0:T(8,128)S(1)} %pad_maximum_fusion.6), channel_id=1, source_target_pairs={{4,0},{8,4},{12,8},{16,12},{20,16},{24,20},{28,24},{32,28},{36,32}... | collective-permute-start | bytes 196616 | tf_op jit(solution)/shard_map/ppermute | solution.py:429
  147.2 2.5 %copy-start.64 = (f32[120,512]{1,0:T(8,128)S(1)}, f32[120,512]{1,0:T(8,128)}, u32[]{:S(2)}) copy-start(f32[120,512]{1,0:T(8,128)} %slice.122) | copy-start | bytes 737284
  147.8 4.1 %collective-permute-start.9 = (f32[80,128]{1,0:T(8,128)S(1)}, f32[80,128]{1,0:T(8,128)S(1)}, u32[]{:S(2)}, u32[]{:S(2)}) collective-permute-start(f32[80,128]{1,0:T(8,128)S(1)} %fusion.9), channel_id=1, source_target_pairs={{0,8},{4,12},{8,0},{12,4},{16,24},{20,28},{24,16},{28,20},{32,40},... | collective-permute-start | bytes 122888 | tf_op jit(solution)/shard_map/ppermute | solution.py:338
  151.9 5.0 %collective-permute-start.10 = (f32[80,128]{1,0:T(8,128)S(1)}, f32[80,128]{1,0:T(8,128)S(1)}, u32[]{:S(2)}, u32[]{:S(2)}) collective-permute-start(f32[80,128]{1,0:T(8,128)S(1)} %fusion.14), channel_id=1, source_target_pairs={{0,16},{4,20},{8,24},{12,28},{16,0},{20,4},{24,8},{28,12},{32,48},... | collective-permute-start | bytes 122888 | tf_op jit(solution)/shard_map/ppermute | solution.py:338
  156.9 8.0 %collective-permute-start.11 = (f32[80,128]{1,0:T(8,128)S(1)}, f32[80,128]{1,0:T(8,128)S(1)}, u32[]{:S(2)}, u32[]{:S(2)}) collective-permute-start(f32[80,128]{1,0:T(8,128)S(1)} %add.74), channel_id=1, source_target_pairs={{0,32},{4,36},{8,40},{12,44},{16,48},{20,52},{24,56},{28,60},{32,0... | collective-permute-start | bytes 122888 | tf_op jit(solution)/shard_map/ppermute | solution.py:338
  160.4 23.2 %all-to-all-start.4 = ((f32[4,256,128]{2,1,0:T(8,128)}), f32[4,256,128]{2,1,0:T(8,128)S(1)}, u32[]{:S(2)}, u32[]{:S(2)}) async-start(f32[4,256,128]{2,1,0:T(8,128)} %pad_maximum_fusion.1), calls=%async_computation.4 | async-start | bytes 1048576 | tf_op jit(solution)/shard_map/all_to_all | solution.py:439
  164.9 4.1 %collective-permute-start.12 = (f32[80,128]{1,0:T(8,128)S(1)}, f32[80,128]{1,0:T(8,128)S(1)}, u32[]{:S(2)}, u32[]{:S(2)}) collective-permute-start(f32[80,128]{1,0:T(8,128)S(1)} %add.75), channel_id=1, source_target_pairs={{0,64},{4,68},{8,72},{12,76},{16,80},{20,84},{24,88},{28,92},{32,9... | collective-permute-start | bytes 122888 | tf_op jit(solution)/shard_map/ppermute | solution.py:338
  169.0 5.5 %collective-permute-start.13 = (f32[80,128]{1,0:T(8,128)S(1)}, f32[80,128]{1,0:T(8,128)S(1)}, u32[]{:S(2)}, u32[]{:S(2)}) collective-permute-start(f32[80,128]{1,0:T(8,128)S(1)} %add.76), channel_id=1, source_target_pairs={{0,128},{4,132},{8,136},{12,140},{16,144},{20,148},{24,152},{28,15... | collective-permute-start | bytes 122888 | tf_op jit(solution)/shard_map/ppermute | solution.py:338
  174.5 3.8 %collective-permute-start.14 = (f32[32,128]{1,0:T(8,128)S(1)}, f32[32,128]{1,0:T(8,128)S(1)}, u32[]{:S(2)}, u32[]{:S(2)}) collective-permute-start(f32[32,128]{1,0:T(8,128)S(1)} %slice.158), channel_id=1, source_target_pairs={{0,1},{1,0},{2,3},{3,2},{4,5},{5,4},{6,7},{7,6},{8,9},{9,8},{10,11... | collective-permute-start | bytes 49160 | tf_op jit(solution)/shard_map/ppermute | solution.py:338
  178.4 5.2 %collective-permute-start.15 = (f32[32,128]{1,0:T(8,128)S(1)}, f32[32,128]{1,0:T(8,128)S(1)}, u32[]{:S(2)}, u32[]{:S(2)}) collective-permute-start(f32[32,128]{1,0:T(8,128)S(1)} %get-tuple-element.112), channel_id=1, source_target_pairs={{0,2},{1,3},{2,0},{3,1},{4,6},{5,7},{6,4},{7,5},{8,10},{9,11},{10,... | collective-permute-start | bytes 49160 | tf_op jit(solution)/shard_map/ppermute | solution.py:338
  184.4 11.7 %all-to-all-start.5 = ((bf16[4,256,128]{2,1,0:T(8,128)(2,1)}), bf16[4,256,128]{2,1,0:T(8,128)(2,1)S(1)}, u32[]{:S(2)}, u32[]{:S(2)}) async-start(bf16[4,256,128]{2,1,0:T(8,128)(2,1)} %broadcast_in_dim.30), calls=%async_computation.5 | async-start | bytes 524288 | tf_op jit(solution)/shard_map/all_to_all | solution.py:440
  (29 other events, 19.5 us)
where the time goes:
time: 200 us; the launch traced here: 197 us
  blocking collectives  73.7 us (37%)
  local copies, waits for them, and re-layouts  38 us (19%)
  starting transfers between devices  32.6 us (16%)
  waiting for transfers between devices  27.8 us (14%)
  Pallas kernels  16 us (8%)
  other arithmetic  7.57 us (4%)
    all_to_all x4, blocking collectives, over_chips(): lax.all_to_all(v, 'ctx', 0, 0, axis_index_groups=[list(range(c, size, 2))...  73.7 us
    unnamed x150, local copies, waits for them, and re-layouts  28.9 us
    ppermute x10, starting transfers between devices, butterfly(): x = x + lax.ppermute(x, axis, alike(lax.axis_size(axis), by))  17.8 us
    ppermute x10, waiting for transfers between devices, butterfly(): x = x + lax.ppermute(x, axis, alike(lax.axis_size(axis), by))  17.3 us
    pallas_call x10, Pallas kernels, call(): pl.pallas_call(kernel, out_shape=[jax.ShapeDtypeStruct(s, d) for s, d in...  16 us
    all_to_all x1, waiting for transfers between devices, body(): spread = lax.all_to_all(jnp.broadcast_to(mine, slices.shape), 'tp', 0, 0)  5.46 us
    all_to_all x1, starting transfers between devices, body(): spread = lax.all_to_all(jnp.broadcast_to(mine, slices.shape), 'tp', 0, 0)  5.03 us
    all_to_all x1, starting transfers between devices, body(): lax.all_to_all(slices, 'tp', 0, 0)  4.47 us
  transfers between devices with their start and end apart: 18, of which 13 were waited for; matrix products, arithmetic and copies ran while one was open for 6% of the time, Pallas kernels for 4%

commit v1 on v0

--- a/solution.py
+++ b/solution.py
@@ -5,7 +5,7 @@
 from jax import lax
 from jax.experimental import pallas as pl
 from jax.experimental.pallas import tpu as pltpu
-from jax.sharding import PartitionSpec as P
+from jax.sharding import Mesh, PartitionSpec as P
 
 HEAD_DIM = 32
 STATE = 128
@@ -23,7 +23,8 @@
 GROUP_WIDTH = 1024
 EPSILON = 1e-05
 F32 = jnp.float32
-PARAMS = pltpu.CompilerParams(vmem_limit_bytes=48 << 20)
+CTX = ("chip", "core")
+PARAMS = pltpu.CompilerParams(vmem_limit_bytes=16 << 20)
 
 
 def dot(a, b, ca=1, cb=0):
@@ -88,20 +89,18 @@
     return total
 
 
-def conv_back_tile(ext, pad, w, cols, grad, own, head, wgrad):
+def conv_back_tile(ext, pad, w, cols, grad):
     dpre = grad * silu_slope(conv_tile(ext, w, cols))
     pad[8 : 8 + SPAN, cols] = dpre
-    for k in range(CONV):
-        wgrad[k : k + 1, cols] = jnp.sum(
-            dpre * ext[LEAD - 3 + k : LEAD - 3 + k + SPAN, cols], axis=0, keepdims=True
-        )
+    taps = [
+        jnp.sum(dpre * ext[LEAD - 3 + k : LEAD - 3 + k + SPAN, cols], axis=0, keepdims=True) for k in range(CONV)
+    ]
     mine = w[0:1, cols] * pad[11 : 11 + SPAN, cols]
     ahead = w[0:1, cols] * pad[3:11, cols]
     for k in range(1, CONV):
         mine = mine + w[k : k + 1, cols] * pad[11 - k : 11 - k + SPAN, cols]
         ahead = ahead + w[k : k + 1, cols] * pad[3 - k : 11 - k, cols]
-    own[:, cols] = mine
-    head[:, cols] = ahead
+    return mine, ahead, taps
 
 
 def clear_pad(pad):
@@ -201,7 +200,7 @@
 
 def middle_kernel(
     sums, y, zt, ogt, dy, dg, full, mt, zs, xt, bc, cc, cum, skip, c, hc, wc,
-    dz, db, dcum, dskip, gz, dgain, cown, chead, wcg, extc, padc, dc,
+    dz, db, dcum, dskip, gz, early, cpart, extc, padc, dc,
 ):
     alpha = jnp.exp(cum[...])
     causal = triangle(True)
@@ -223,16 +222,21 @@
         db[:, lanes(g)] = dot(dm, cc[:, lanes(g)])
     for r in range(PER):
         gz[:, lanes(r)] = take(slope, r).astype(jnp.bfloat16)
-        dgain[:, lanes(r)] = jnp.sum(take(shares, r), axis=0, keepdims=True)
+        early[16 + r : 17 + r, :] = jnp.sum(take(shares, r), axis=0, keepdims=True)
     extend(extc, c, hc)
     clear_pad(padc)
     for g in range(GROUPS):
-        conv_back_tile(extc, padc, wc, lanes(g), dc[:, lanes(g)], cown, chead, wcg)
+        mine, ahead, taps = conv_back_tile(extc, padc, wc, lanes(g), dc[:, lanes(g)])
+        cpart[g, 0:SPAN, :] = mine
+        cpart[g, SPAN : SPAN + 8, :] = ahead
+        for k in range(CONV):
+            early[k * GROUPS + g : k * GROUPS + g + 1, :] = taps[k]
 
 
 def last_kernel(
-    core, own, got, full, ends, dz1, db1, dcum1, dy, zs, xt, bc, cum, step, skip, dt, bias, alog, x, hx, wx, b, hb, wb,
-    xown, xhead, wxg, bown, bhead, wbg, ddt, drate, later, ext, extb, pad, padb,
+    core, own, got, full, ends, dz1, db1, dcum1, dskip, early, cpart, dy, zs, xt, bc, cum, step, skip, dt, bias, alog,
+    x, hx, wx, b, hb, wb,
+    xown, heads, parts, packed, ddt, later, ext, extb, pad, padb,
 ):
     unite(core[0], later, own, got)
     gamma = jnp.exp(-cum[...])
@@ -244,7 +248,7 @@
     dxs, turned, straight = [], [], []
     at_end = lax.broadcasted_iota(jnp.int32, (PER, SPAN), 1) == SPAN - 1
     for g in range(GROUPS):
-        heads = slice(g * PER, (g + 1) * PER)
+        here = slice(g * PER, (g + 1) * PER)
         zg, xg = zs[group(g), :], xt[group(g), :]
         d = heads_out(ends[...], g) * later[group(g), :]
         second = dot(d, bc[:, lanes(g)], 1, 1)
@@ -252,17 +256,110 @@
         dxs.append(heads_out(scale, g) * dzg + heads_out(skip[...], g) * dy[group(g), :])
         edge = heads_in(zg * second + d * full[group(g), :])
         edge = jnp.sum(edge, axis=1, keepdims=True)
-        turned.append(dcum1[heads, :] - heads_in(dzg * zg) + jnp.where(at_end, edge, 0.0))
+        turned.append(dcum1[here, :] - heads_in(dzg * zg) + jnp.where(at_end, edge, 0.0))
         straight.append(heads_in(dzg * xg))
         dbg = db1[:, lanes(g)] + dot(zg, d, 0, 0)
-        conv_back_tile(extb, padb, wb, lanes(g), dbg, bown, bhead, wbg)
+        mine, ahead, taps = conv_back_tile(extb, padb, wb, lanes(g), dbg)
+        parts[g, 0:SPAN, :] = mine
+        parts[g, SPAN : 2 * SPAN, :] = cpart[g, 0:SPAN, :]
+        parts[g, 2 * SPAN : 2 * SPAN + 8, :] = ahead
+        parts[g, 2 * SPAN + 8 : 2 * SPAN + 16, :] = cpart[g, SPAN : SPAN + 8, :]
+        for k in range(CONV):
+            packed[k * GROUPS + g : k * GROUPS + g + 1, :] = taps[k]
     dlog = dot(jnp.concatenate(turned, axis=0), jnp.where(triangle(False), 1.0, 0.0))
     rate = -jnp.exp(alog[...])
-    drate[...] = dlog * rate * step[...]
     dstep = jnp.concatenate(straight, axis=0) * gamma + dlog * rate
-    ddt[...] = dstep * sigmoid(dt[...] + bias[...])
+    draw = dstep * sigmoid(dt[...] + bias[...])
+    ddt[...] = draw
+    each = jnp.concatenate([draw, dlog * rate * step[...], dskip[...], jnp.zeros((LOCAL, SPAN), F32)], axis=0)
+    packed[72:80, :] = dot(jnp.ones((8, SPAN), F32), each, 1, 1)
+    packed[16:32, :] = early[0:16, :]
+    packed[64:72, :] = early[16:24, :]
     for r in range(PER):
-        conv_back_tile(ext, pad, wx, lanes(r), take(dxs, r), xown, xhead, wxg)
+        mine, ahead, taps = conv_back_tile(ext, pad, wx, lanes(r), take(dxs, r))
+        xown[:, lanes(r)] = mine
+        heads[8 * r : 8 * r + 8, :] = ahead
+        for k in range(CONV):
+            packed[32 + k * PER + r : 33 + k * PER + r, :] = taps[k]
+
+
+def pair_decays(core, pair, lead):
+    mine, theirs = pair[0 : LOCAL // 2, :], pair[LOCAL // 2 : LOCAL, :]
+    leads = core == lead
+    return jnp.where(leads, mine, theirs), jnp.where(leads, theirs, mine), leads
+
+
+def join_first_kernel(core, keep, got, ends, joint, pair):
+    half = LOCAL // 2
+    pair[0:half, :] = ends[pl.ds(pl.multiple_of(core[0] * half, half), half), :]
+    pair[half:LOCAL, :] = got[pl.ds(pl.multiple_of(HALF + core[0] * half, half), half), :]
+    first, second, leads = pair_decays(core[0], pair, 0)
+    for h in range(half):
+        rows = slice(h * HEAD_DIM, (h + 1) * HEAD_DIM)
+        mine, theirs = keep[rows, :], got[rows, :]
+        both = second[h : h + 1] * jnp.where(leads, mine, theirs) + jnp.where(leads, theirs, mine)
+        for i in range(HEAD_DIM):
+            joint[2 * h + i // 16, :, lanes(i % 16)] = both[i : i + 1]
+        for i in range(2):
+            joint[2 * h + i, :, CHUNK:] = first[h : h + 1] * second[h : h + 1]
+
+
+def join_again_kernel(core, keep, got, pair, joint):
+    _, second, leads = pair_decays(core[0], pair, 1)
+    for h in range(LOCAL // 2):
+        rows = slice(h * HEAD_DIM, (h + 1) * HEAD_DIM)
+        mine, theirs = keep[rows, :], got[rows, :]
+        joint[rows, :] = second[h : h + 1] * jnp.where(leads, mine, theirs) + jnp.where(leads, theirs, mine)
+
+
+def split_kernel(lead, core, ahead, keep, got, pair, own, give):
+    first, _, leads = pair_decays(core[0], pair, lead)
+    for h in range(LOCAL // 2):
+        rows = slice(h * HEAD_DIM, (h + 1) * HEAD_DIM)
+        far = ahead[rows, :]
+        near = first[h : h + 1] * far + jnp.where(leads, keep[rows, :], got[rows, :])
+        own[rows, :] = jnp.where(leads, far, near)
+        give[rows, :] = jnp.where(leads, near, far)
+
+
+def add_kernel(slices, xheads, mine, heads):
+    total = slices[0]
+    for g in range(1, GROUPS):
+        total = total + slices[g]
+    mine[...] = total[0 : 2 * SPAN]
+    heads[0:64, :] = xheads[...]
+    heads[64:80, :] = total[2 * SPAN :]
+
+
+def settle_kernel(xown, mine, heads, gx, spread):
+    last = slice(SPAN - LEAD, SPAN)
+    none = jnp.zeros((LEAD - 8, TILE), F32)
+    for r in range(PER):
+        gx[0 : SPAN - LEAD, lanes(r)] = xown[0 : SPAN - LEAD, lanes(r)].astype(jnp.bfloat16)
+        more = jnp.concatenate([none, heads[8 * r : 8 * r + 8, :]], axis=0)
+        gx[last, lanes(r)] = (xown[last, lanes(r)] + more).astype(jnp.bfloat16)
+    for i in range(2):
+        more = jnp.concatenate([none, heads[64 + 8 * i : 72 + 8 * i, :]], axis=0)
+        body_rows = mine[i * SPAN : (i + 1) * SPAN - LEAD, :].astype(jnp.bfloat16)
+        last_rows = (mine[(i + 1) * SPAN - LEAD : (i + 1) * SPAN, :] + more).astype(jnp.bfloat16)
+        for g in range(GROUPS):
+            spread[g, i * SPAN : (i + 1) * SPAN - LEAD, :] = body_rows
+            spread[g, (i + 1) * SPAN - LEAD : (i + 1) * SPAN, :] = last_rows
+
+
+def finish_kernel(spread, bc_taps, packed, gb, gc, tx, tb, tc, tgain, small):
+    for g in range(GROUPS):
+        gb[:, lanes(g)] = spread[g, 0:SPAN, :]
+        gc[:, lanes(g)] = spread[g, SPAN : 2 * SPAN, :]
+    for k in range(CONV):
+        for g in range(GROUPS):
+            tb[k : k + 1, lanes(g)] = bc_taps[k * GROUPS + g : k * GROUPS + g + 1, :]
+            tc[k : k + 1, lanes(g)] = bc_taps[16 + k * GROUPS + g : 17 + k * GROUPS + g, :]
+        for r in range(PER):
+            tx[k : k + 1, lanes(r)] = packed[32 + k * PER + r : 33 + k * PER + r, :]
+    for r in range(PER):
+        tgain[:, lanes(r)] = packed[64 + r : 65 + r, :]
+    small[...] = packed[72:80, :]
 
 
 def scan_kernel(backward, s, d, o):
@@ -293,7 +390,7 @@
 
 
 def swap_cores(v):
-    return lax.ppermute(v, "ctx", [(i, i ^ 1) for i in range(lax.axis_size("ctx"))])
+    return lax.ppermute(v, "core", [(0, 1), (1, 0)])
 
 
 def alike(size, by):
@@ -301,35 +398,7 @@
 
 
 def over_chips(v):
-    size = lax.axis_size("ctx")
-    return lax.all_to_all(
-        v, "ctx", 0, 0, axis_index_groups=[list(range(c, size, 2)) for c in range(2)]
-    )
-
-
-def wide(a):
-    return jnp.repeat(a, HEAD_DIM, axis=0)
-
-
-def pair_scan(keep, got, first, second, is_first, decays, backward):
-    lead = jnp.where(is_first, keep, got)
-    follow = jnp.where(is_first, got, keep)
-    joint = (wide(second) * lead + follow).reshape(-1, 1, CHUNK)
-    if decays is None:
-        both = jnp.repeat(first * second, HALF // (LOCAL // 2) * STATE // CHUNK, axis=0)[:, None]
-        joint = jnp.concatenate([joint, both], axis=2)
-    pieces = over_chips(joint)
-    decays = pieces if decays is None else decays
-    (entering,) = call(
-        functools.partial(scan_kernel, backward),
-        "block_scan",
-        [((pieces.shape[0], 1, CHUNK), F32)],
-        (pieces, decays),
-    )
-    ahead = over_chips(entering).reshape(HALF, STATE)
-    between = wide(first) * ahead + lead
-    other = swap_cores(jnp.where(is_first, between, ahead))
-    return jnp.where(is_first, ahead, between), other, decays
+    return lax.all_to_all(v, "chip", 0, 0)
 
 
 def butterfly(x, axis):
@@ -351,15 +420,15 @@
 def body(
     x_raw, b_raw, c_raw, z_gate, dt_raw, conv_x, conv_b, conv_c, dt_bias, a_log, d_skip, gain, grad_out
 ):
-    size = lax.axis_size("ctx")
-    core = lax.axis_index("ctx") % 2
+    size = lax.axis_size(CTX)
+    core = lax.axis_index("core")
     cores = core.reshape(1)
     is_even = core == 0
     t_shape = ((ALL, SPAN), F32)
     bc_shape = ((SPAN, GROUPS * STATE), F32)
     h_shape = ((LOCAL, SPAN), F32)
     tails = jnp.concatenate([v[SPAN - LEAD :] for v in (x_raw, b_raw, c_raw)], axis=1)
-    before = lax.ppermute(tails, "ctx", [(i, i + 1) for i in range(size - 1)])
+    before = lax.ppermute(tails, CTX, [(i, i + 1) for i in range(size - 1)])
     wx, wb = x_raw.shape[1], b_raw.shape[1]
     hx, hb, hc = before[:, :wx], before[:, wx : wx + wb], before[:, wx + wb :]
 
@@ -377,10 +446,24 @@
         scalars=1,
     )
     got = swap_cores(give)
-    mine = lax.dynamic_slice_in_dim(ends, core * (LOCAL // 2), LOCAL // 2)
-    theirs = lax.dynamic_slice_in_dim(got[HALF:], core * (LOCAL // 2), LOCAL // 2)
-    even, odd = jnp.where(is_even, mine, theirs), jnp.where(is_even, theirs, mine)
-    enter_own, enter_got, decays = pair_scan(keep, got[:HALF], even, odd, is_even, None, False)
+    half_shape = ((HALF, STATE), F32)
+    chips = lax.axis_size("chip")
+    joint, pair = call(
+        join_first_kernel,
+        "join",
+        [((chips, 1, CHUNK + TILE), F32), h_shape],
+        (cores, keep, got, ends),
+        scalars=1,
+    )
+    firsts = over_chips(joint)
+    (entering,) = call(
+        functools.partial(scan_kernel, False), "block_scan", [((chips, 1, CHUNK), F32)], (firsts, firsts)
+    )
+    ahead = over_chips(entering).reshape(HALF, STATE)
+    enter_own, enter_give = call(
+        functools.partial(split_kernel, 0), "split", [half_shape] * 2, (cores, ahead, keep, got, pair), scalars=1
+    )
+    enter_got = swap_cores(enter_give)
 
     cc, mt, y1 = call(
         local_kernel,
@@ -396,7 +479,8 @@
         (cores, enter_own, enter_got, cc, y1, cum, zt, sgt),
         scalars=1,
     )
-    sums = butterfly(sums, "tp")
+    peers = lax.axis_size("tp")
+    sums = sums + sum(lax.ppermute(sums, "tp", [(i, (i + k) % peers) for i in range(peers)]) for k in range(1, peers))
     keep, give, dy, dg = call(
         gate_kernel,
         "gate",
@@ -406,51 +490,53 @@
         scalars=1,
     )
     got = swap_cores(give)
-    later_own, later_got, _ = pair_scan(keep, got, odd, even, ~is_even, decays, True)
-    own_shape, head_shape, w_shape = bc_shape, ((8, wb), F32), ((CONV, wb), F32)
-    dz, db, dcum, dskip, grad_z, dgain, cown, chead, wcg = call(
+    (joint,) = call(join_again_kernel, "join", [half_shape], (cores, keep, got, pair), scalars=1)
+    pieces = over_chips(joint.reshape(chips, 1, CHUNK))
+    (leaving,) = call(
+        functools.partial(scan_kernel, True), "block_scan", [((chips, 1, CHUNK), F32)], (pieces, firsts)
+    )
+    ahead = over_chips(leaving).reshape(HALF, STATE)
+    later_own, later_give = call(
+        functools.partial(split_kernel, 1), "split", [half_shape] * 2, (cores, ahead, keep, got, pair), scalars=1
+    )
+    later_got = swap_cores(later_give)
+    dz, db, dcum, dskip, grad_z, early, cpart = call(
         middle_kernel,
         "middle",
-        [t_shape, bc_shape, h_shape, h_shape, ((SPAN, wx), jnp.bfloat16), ((1, wx), F32)]
-        + [own_shape, head_shape, w_shape],
+        [t_shape, bc_shape, h_shape, h_shape, ((SPAN, wx), jnp.bfloat16), ((24, TILE), F32)]
+        + [((GROUPS, SPAN + 8, TILE), F32)],
         (sums, y, zt, ogt, dy, dg, enter, mt, zs, xt, bc, cc, cum, skip, c_raw, hc, conv_c),
         [(LEAD + SPAN, wb), (LEAD + SPAN, wb), (SPAN, wb)],
     )
-    xown, xhead, wxg, bown, bhead, wbg, ddt, drate = call(
+    xown, xheads, parts, packed, ddt = call(
         last_kernel,
         "last",
-        [((SPAN, wx), F32), ((8, wx), F32), ((CONV, wx), F32), own_shape, head_shape, w_shape, h_shape, h_shape],
-        (cores, later_own, later_got, enter, ends, dz, db, dcum, dy, zs, xt, bc, cum, step, skip, dt, bias, alog)
-        + (x_raw, hx, conv_x, b_raw, hb, conv_b),
+        [((SPAN, wx), F32), ((64, TILE), F32), ((GROUPS, 2 * SPAN + 16, TILE), F32), ((80, TILE), F32), h_shape],
+        (cores, later_own, later_got, enter, ends, dz, db, dcum, dskip, early, cpart)
+        + (dy, zs, xt, bc, cum, step, skip, dt, bias, alog, x_raw, hx, conv_x, b_raw, hb, conv_b),
         [(ALL, STATE), (LEAD + SPAN, wx), (LEAD + SPAN, wb), (LEAD + SPAN, wx), (LEAD + SPAN, wb)],
         scalars=1,
     )
-    heads = jnp.concatenate([xhead, bhead, chead], axis=1)
-    heads = lax.ppermute(heads, "ctx", [(i + 1, i) for i in range(size - 1)])
-
-    def settle(own, incoming):
-        return jnp.concatenate([own[: SPAN - 8], own[SPAN - 8 :] + incoming], axis=0)
-
-    grad_x_raw = settle(xown, heads[:, :wx]).astype(jnp.bfloat16)
-    bc_part = jnp.concatenate(
-        [settle(bown, heads[:, wx : wx + wb]), settle(cown, heads[:, wx + wb :])], axis=0
-    )
-    slices = jnp.stack(jnp.split(bc_part, GROUPS, axis=1))
-    mine = jnp.sum(lax.all_to_all(slices, "tp", 0, 0), axis=0).astype(jnp.bfloat16)
-    spread = lax.all_to_all(jnp.broadcast_to(mine, slices.shape), "tp", 0, 0)
-    bc_grad = jnp.concatenate([spread[g] for g in range(GROUPS)], axis=1)
-    grad_b_raw, grad_c_raw = bc_grad[:SPAN], bc_grad[SPAN:]
-    small = by_head(jnp.stack([jnp.sum(v, axis=1) for v in (ddt, drate, dskip)], axis=1))
-    parts = (wbg, wcg, wxg, dgain, small)
-    packed = jnp.concatenate([part.reshape(-1) for part in parts])
-    packed = butterfly(jnp.pad(packed, (0, -packed.size % 1024)).reshape(-1, TILE), "ctx")
-    shared = (wbg.size + wcg.size) // TILE
-    packed = jnp.concatenate([butterfly(packed[:shared], "tp").reshape(-1), packed[shared:].reshape(-1)])
-    totals, start = [], 0
-    for part in parts:
-        totals.append(packed[start : start + part.size].reshape(part.shape))
-        start += part.size
-    conv_b_total, conv_c_total, conv_x_total, gain_total, small = totals
+    slices = lax.all_to_all(parts, "tp", 0, 0)
+    packed = butterfly(packed, CTX)
+    bc_taps = butterfly(packed[:32], "tp")
+    mine, heads = call(add_kernel, "add", [((2 * SPAN, TILE), F32), ((80, TILE), F32)], (slices, xheads))
+    heads = lax.ppermute(heads, CTX, [(i + 1, i) for i in range(size - 1)])
+    grad_x_raw, spread = call(
+        settle_kernel,
+        "settle",
+        [((SPAN, wx), jnp.bfloat16), ((GROUPS, 2 * SPAN, TILE), jnp.bfloat16)],
+        (xown, mine, heads),
+    )
+    spread = lax.all_to_all(spread, "tp", 0, 0)
+    half_bc = ((SPAN, wb), jnp.bfloat16)
+    grad_b_raw, grad_c_raw, conv_x_total, conv_b_total, conv_c_total, gain_total, small = call(
+        finish_kernel,
+        "finish",
+        [half_bc, half_bc, ((CONV, wx), F32), ((CONV, wb), F32), ((CONV, wb), F32), ((1, wx), F32), ((8, TILE), F32)],
+        (spread, bc_taps, packed),
+    )
+    small = [by_head(small[0, i * LOCAL : (i + 1) * LOCAL]) for i in range(3)]
     return (
         grad_x_raw,
         grad_b_raw,
@@ -460,19 +546,19 @@
         conv_x_total,
         conv_b_total,
         conv_c_total,
-        small[:, 0],
-        small[:, 1],
-        small[:, 2],
+        *small,
         gain_total.reshape(-1),
     )
 
 
 def solution(mesh):
-    rows, cols, some = P("ctx", "tp"), P(None, "tp"), P("tp")
+    rows, cols, some = P(CTX, "tp"), P(None, "tp"), P("tp")
+    chips, tp = mesh.shape["ctx"] // 2, mesh.shape["tp"]
+    mesh = Mesh(mesh.devices.reshape(chips, 2, tp), (*CTX, "tp"))
     return jax.shard_map(
         body,
         mesh=mesh,
-        in_specs=(rows, P("ctx", None), P("ctx", None), rows, rows, cols, P(), P(), some, some, some, some, rows),
-        out_specs=(rows, P("ctx", None), P("ctx", None), rows, rows, cols, P(), P(), some, some, some, some),
+        in_specs=(rows, P(CTX, None), P(CTX, None), rows, rows, cols, P(), P(), some, some, some, some, rows),
+        out_specs=(rows, P(CTX, None), P(CTX, None), rows, rows, cols, P(), P(), some, some, some, some),
         check_vma=False,
     )

time: 200 us -> 161 us (0.81)
  local copies, waits for them, and re-layouts: 38 us -> 8.23 us
  other arithmetic: 7.57 us -> 0.06 us
  starting transfers between devices: 32.6 us -> 29.8 us
  waiting for transfers between devices: 27.8 us -> 30.1 us
    unnamed x150 -> x26, local copies, waits for them, and re-layouts: 28.9 us -> 3.69 us
    ppermute x10 -> x8, starting transfers between devices: 17.8 us -> 11.1 us  [butterfly(): x = x + lax.ppermute(x, axis, alike(lax.axis_size(axis), by))]
    ppermute x10 -> x8, waiting for transfers between devices: 17.3 us -> 22.8 us  [butterfly(): x = x + lax.ppermute(x, axis, alike(lax.axis_size(axis), by))]
    all_to_all x2, waiting for transfers between devices: 5.46 us -> 0.01 us  [the longest x1 0.01 us: body(): spread = lax.all_to_all(spread, 'tp', 0, 0)]
    ppermute x6 -> x9, starting transfers between devices: 5.34 us -> 10.3 us  [the longest x3 5.3 us: body(): lax.ppermute(sums, 'tp', [(i, (i + k) % peers) for i in range(peers)])]
    slice x10 -> x2, local copies, waits for them, and re-layouts: 3.76 us -> 0.09 us  [the longest x1 0.09 us: body(): small = [by_head(small[0, i * LOCAL:(i + 1) * LOCAL]) for i in range(3)]]
    select_n x2 -> x0, other arithmetic: 2.64 us -> none  [pair_scan(): other = swap_cores(jnp.where(is_first, between, ahead))]
    ppermute x6 -> x9, waiting for transfers between devices: 4.97 us -> 7.29 us  [the longest x3 2.91 us: body(): lax.ppermute(sums, 'tp', [(i, (i + k) % peers) for i in range(peers)])]
  transfers between devices with their start and end apart: 18 -> 19, of which waited for: 13 -> 12; matrix products, arithmetic and copies ran while one was open for 6% -> 1% of each run, Pallas kernels for 4% -> 4%
where the time goes in v1:
time: 161 us; the launch traced here: 159 us
  blocking collectives  74.4 us (46%)
  waiting for transfers between devices  30.1 us (19%)
  starting transfers between devices  29.8 us (19%)
  Pallas kernels  15.2 us (9%)
  local copies, waits for them, and re-layouts  8.23 us (5%)
    all_to_all x4, blocking collectives, over_chips(): return lax.all_to_all(v, 'chip', 0, 0)  74.4 us
    ppermute x8, waiting for transfers between devices, butterfly(): x = x + lax.ppermute(x, axis, alike(lax.axis_size(axis), by))  22.8 us
    pallas_call x17, Pallas kernels, call(): pl.pallas_call(kernel, out_shape=[jax.ShapeDtypeStruct(s, d) for s, d in...  15.2 us
    ppermute x8, starting transfers between devices, butterfly(): x = x + lax.ppermute(x, axis, alike(lax.axis_size(axis), by))  11.1 us
    ppermute x3, starting transfers between devices, body(): lax.ppermute(sums, 'tp', [(i, (i + k) % peers) for i in range(peers)])  5.3 us
    all_to_all x1, starting transfers between devices, body(): slices = lax.all_to_all(parts, 'tp', 0, 0)  4.5 us
    all_to_all x1, starting transfers between devices, body(): spread = lax.all_to_all(spread, 'tp', 0, 0)  3.94 us
    unnamed x26, local copies, waits for them, and re-layouts  3.69 us
  transfers between devices with their start and end apart: 19, of which 12 were waited for; matrix products, arithmetic and copies ran while one was open for 1% of the time, Pallas kernels for 4%

profile of v1, /device:TPU:32, one launch (start us, length us, event | category | flops | bytes accessed | tf_op | source)
XLA Modules:
  0.0 158.8 jit_solution(13089354562110624114)
XLA Ops:
  0.7 0.7 slice-done
  1.4 1.9 %collective-permute-start = (bf16[16,2048]{1,0:T(8,128)(2,1)S(1)}, bf16[16,2048]{1,0:T(8,128)(2,1)S(1)}, u32[]{:S(2)}, u32[]{:S(2)}) collective-permute-start(bf16[16,2048]{1,0:T(8,128)(2,1)S(1)} %pad_maximum_fusion), channel_id=1, source_target_pairs={{0,4},{4,8},{8,12},{12,16},{16,20},{20,24},{24,28},{28,32},{32,36}... | collective-permute-start | bytes 196616 | tf_op jit(solution)/shard_map/ppermute | solution.py:431
  3.4 0.6 copy-done.10
  4.1 0.1 copy.38
  4.3 0.6 copy-done.11
  4.9 0.1 copy.39
  5.1 0.2 steps.1
  5.3 1.7 %collective-permute-done = bf16[16,2048]{1,0:T(8,128)(2,1)S(1)} collective-permute-done((bf16[16,2048]{1,0:T(8,128)(2,1)S(1)}, bf16[16,2048]{1,0:T(8,128)(2,1)S(1)}, u32[]{:S(2)}, u32[]{:S(2)}) %collective-permute-start) | collective-permute-done | bytes 65568 | tf_op jit(solution)/shard_map/ppermute | solution.py:431
  7.1 0.7 copy-done.7
  7.7 1.2 state.1
  9.0 0.7 collective-permute-start.1
  9.6 1.2 collective-permute-done.1.got
  10.8 0.2 join.2
  11.0 24.9 %all_to_all.30.s.d = f32[32,1,2176]{2,1,0:T(1,128)S(1)} all-to-all(f32[32,1,2176]{2,1,0:T(1,128)S(1)} %get-tuple-element.67), channel_id=1, replica_groups=mesh['chip'=32,'core'=2,'tp'=4] {'chip'}, dimensions={0} | all-to-all | bytes 557056 | tf_op jit(solution)/shard_map/all_to_all | solution.py:401
  35.9 0.2 block_scan.2
  36.1 16.4 %all_to_all.31 = f32[32,1,2048]{2,1,0:T(1,128)S(1)} all-to-all(f32[32,1,2048]{2,1,0:T(1,128)S(1)} %block_scan.2), channel_id=1, replica_groups=mesh['chip'=32,'core'=2,'tp'=4] {'chip'}, dimensions={0} | all-to-all | bytes 524288 | tf_op jit(solution)/shard_map/all_to_all | solution.py:401
  52.6 0.1 collective-permute-start.2
  52.7 0.6 copy-done.12
  53.4 0.1 broadcast_in_dim.10
  53.5 0.5 copy-done.8
  54.1 0.3 turn.1
  54.5 0.5 copy-done.1
  55.0 0.2 copy-done.6
  55.1 2.3 %local.1 = (f32[128,512]{1,0:T(8,128)S(1)}, f32[512,128]{1,0:T(8,128)S(1)}, f32[1024,128]{1,0:T(8,128)S(1)}) custom-call(bf16[128,512]{1,0:T(8,128)(2,1)S(1)} %copy-done.1, bf16[16,512]{1,0:T(8,128)(2,1)S(1)} %get-tuple-element.115.hc, f32[4,512]{1,0:T(4,128)S(1)} %copy-done.6, f32[128,512]{1,0:T(8,128)S(1)} %get-tuple-element.71.bc, ...), custom_call_target="tpu_custom_call" | custom-call | flops 20000000 | bytes 4194304 | tf_op jit(solution)/shard_map/local/pallas_call | solution.py:380
  57.4 0.8 output.1
  58.2 3.1 %collective-permute-start.5 = (f32[8,128]{1,0:T(8,128)S(1)}, f32[8,128]{1,0:T(8,128)S(1)}, u32[]{:S(2)}, u32[]{:S(2)}) collective-permute-start(f32[8,128]{1,0:T(8,128)S(1)} %get-tuple-element.78), channel_id=1, source_target_pairs={{0,3},{1,0},{2,1},{3,2},{4,7},{5,4},{6,5},{7,6},{8,11},{9,8},{10,9... | collective-permute-start | bytes 12296 | tf_op jit(solution)/shard_map/ppermute | solution.py:483
  61.3 2.2 %collective-permute-start.4 = (f32[8,128]{1,0:T(8,128)S(1)}, f32[8,128]{1,0:T(8,128)S(1)}, u32[]{:S(2)}, u32[]{:S(2)}) collective-permute-start(f32[8,128]{1,0:T(8,128)S(1)} %get-tuple-element.78), channel_id=1, source_target_pairs={{0,2},{1,3},{2,0},{3,1},{4,6},{5,7},{6,4},{7,5},{8,10},{9,11},{10,... | collective-permute-start | bytes 12296 | tf_op jit(solution)/shard_map/ppermute | solution.py:483
  63.5 2.6 %collective-permute-done.3 = f32[8,128]{1,0:T(8,128)S(1)} collective-permute-done((f32[8,128]{1,0:T(8,128)S(1)}, f32[8,128]{1,0:T(8,128)S(1)}, u32[]{:S(2)}, u32[]{:S(2)}) %collective-permute-start.3) | collective-permute-done | bytes 4128 | tf_op jit(solution)/shard_map/ppermute | solution.py:483
  66.1 0.3 collective-permute-done.4
  66.4 0.9 gate.1
  67.2 0.1 collective-permute-start.6
  67.3 1.5 collective-permute-done.6.got
  68.9 16.9 %all_to_all.32.s = f32[32,1,2048]{2,1,0:T(1,128)S(1)} all-to-all(f32[32,1,2048]{2,1,0:T(1,128)S(1)} %bitcast.28), channel_id=1, replica_groups=mesh['chip'=32,'core'=2,'tp'=4] {'chip'}, dimensions={0} | all-to-all | bytes 524288 | tf_op jit(solution)/shard_map/all_to_all | solution.py:401
  85.9 0.2 block_scan.3
  86.1 16.2 %all_to_all.33 = f32[32,1,2048]{2,1,0:T(1,128)S(1)} all-to-all(f32[32,1,2048]{2,1,0:T(1,128)S(1)} %block_scan.3), channel_id=1, replica_groups=mesh['chip'=32,'core'=2,'tp'=4] {'chip'}, dimensions={0} | all-to-all | bytes 524288 | tf_op jit(solution)/shard_map/all_to_all | solution.py:401
  102.3 0.3 collective-permute-start.7
  102.6 3.4 %middle.1 = (f32[1024,128]{1,0:T(8,128)S(1)}, f32[128,512]{1,0:T(8,128)S(1)}, f32[32,128]{1,0:T(8,128)S(1)}, f32[32,128]{1,0:T(8,128)S(1)}, bf16[128,1024]{1,0:T...) custom-call(f32[8,128]{1,0:T(8,128)S(1)} %add_add_fusion.sums, f32[1024,128]{1,0:T(8,128)S(1)} %get-tuple-element.79.y, ...), custom_call_target="tpu_custom_call" | custom-call | flops 20000000 | bytes 4194304 | tf_op jit(solution)/shard_map/middle/pallas_call | solution.py:380
  106.0 3.8 %last.1 = (f32[128,1024]{1,0:T(8,128)S(1)}, f32[64,128]{1,0:T(8,128)S(1)}, f32[4,272,128]{2,1,0:T(8,128)}, f32[80,128]{1,0:T(8,128)S(1)}, f32[32,128]{1,0:T(8,128)S(1)}) custom-call(s32[1]{0:T(128)} %bitcast.core, f32[512,128]{1,0:T(8,128)S(1)} %get-tuple-element.82.own, f32[512,128]{1,0:T(8,128)S(1)} %collective-permute-done.7.got, ...), custom_call_target="tpu_custom_call" | custom-call | flops 20000000 | bytes 4194304 | tf_op jit(solution)/shard_map/last/pallas_call | solution.py:380
  109.8 4.5 %all-to-all-start.4 = ((f32[4,272,128]{2,1,0:T(8,128)}), f32[4,272,128]{2,1,0:T(8,128)S(1)}, u32[]{:S(2)}, u32[]{:S(2)}) async-start(f32[4,272,128]{2,1,0:T(8,128)} %get-tuple-element.96), calls=%async_computation.4 | async-start | bytes 1114112 | tf_op jit(solution)/shard_map/all_to_all | solution.py:520
  114.3 0.2 collective-permute-start.9
  114.5 1.0 collective-permute-done.9
  115.5 0.2 collective-permute-start.10
  115.7 3.8 %collective-permute-done.10 = f32[80,128]{1,0:T(8,128)S(1)} collective-permute-done((f32[80,128]{1,0:T(8,128)S(1)}, f32[80,128]{1,0:T(8,128)S(1)}, u32[]{:S(2)}, u32[]{:S(2)}) %collective-permute-start.10) | collective-permute-done | bytes 40992 | tf_op jit(solution)/shard_map/ppermute | solution.py:407
  119.5 0.9 collective-permute-start.11
  120.4 4.0 %collective-permute-done.11 = f32[80,128]{1,0:T(8,128)S(1)} collective-permute-done((f32[80,128]{1,0:T(8,128)S(1)}, f32[80,128]{1,0:T(8,128)S(1)}, u32[]{:S(2)}, u32[]{:S(2)}) %collective-permute-start.11) | collective-permute-done | bytes 40992 | tf_op jit(solution)/shard_map/ppermute | solution.py:407
  124.4 1.3 collective-permute-start.12
  125.7 6.7 %collective-permute-done.12 = f32[80,128]{1,0:T(8,128)S(1)} collective-permute-done((f32[80,128]{1,0:T(8,128)S(1)}, f32[80,128]{1,0:T(8,128)S(1)}, u32[]{:S(2)}, u32[]{:S(2)}) %collective-permute-start.12) | collective-permute-done | bytes 40992 | tf_op jit(solution)/shard_map/ppermute | solution.py:407
  132.3 1.0 collective-permute-start.13
  133.4 3.0 %collective-permute-done.13 = f32[80,128]{1,0:T(8,128)S(1)} collective-permute-done((f32[80,128]{1,0:T(8,128)S(1)}, f32[80,128]{1,0:T(8,128)S(1)}, u32[]{:S(2)}, u32[]{:S(2)}) %collective-permute-start.13) | collective-permute-done | bytes 40992 | tf_op jit(solution)/shard_map/ppermute | solution.py:407
  136.4 1.7 %collective-permute-start.14 = (f32[80,128]{1,0:T(8,128)S(1)}, f32[80,128]{1,0:T(8,128)S(1)}, u32[]{:S(2)}, u32[]{:S(2)}) collective-permute-start(f32[80,128]{1,0:T(8,128)S(1)} %add.41), channel_id=1, source_target_pairs={{0,128},{4,132},{8,136},{12,140},{16,144},{20,148},{24,152},{28,15... | collective-permute-start | bytes 122888 | tf_op jit(solution)/shard_map/ppermute | solution.py:407
  138.1 1.9 %collective-permute-start.8 = (f32[80,128]{1,0:T(8,128)S(1)}, f32[80,128]{1,0:T(8,128)S(1)}, u32[]{:S(2)}, u32[]{:S(2)}) collective-permute-start(f32[80,128]{1,0:T(8,128)S(1)} %get-tuple-element.99), channel_id=1, source_target_pairs={{4,0},{8,4},{12,8},{16,12},{20,16},{24,20},{28,24},{32,28},{36,32}... | collective-permute-start | bytes 122888 | tf_op jit(solution)/shard_map/ppermute | solution.py:524
  140.1 1.8 %collective-permute-done.14 = f32[80,128]{1,0:T(8,128)S(1)} collective-permute-done((f32[80,128]{1,0:T(8,128)S(1)}, f32[80,128]{1,0:T(8,128)S(1)}, u32[]{:S(2)}, u32[]{:S(2)}) %collective-permute-start.14) | collective-permute-done | bytes 40992 | tf_op jit(solution)/shard_map/ppermute | solution.py:407
  141.9 2.1 %collective-permute-start.15 = (f32[32,128]{1,0:T(8,128)S(1)}, f32[32,128]{1,0:T(8,128)S(1)}, u32[]{:S(2)}, u32[]{:S(2)}) collective-permute-start(f32[32,128]{1,0:T(8,128)S(1)} %slice.43), channel_id=1, source_target_pairs={{0,1},{1,0},{2,3},{3,2},{4,5},{5,4},{6,7},{7,6},{8,9},{9,8},{10,11... | collective-permute-start | bytes 49160 | tf_op jit(solution)/shard_map/ppermute | solution.py:407
  144.0 0.9 settle.1
  144.8 3.9 %all-to-all-start.5 = ((bf16[4,256,128]{2,1,0:T(8,128)(2,1)}), bf16[4,256,128]{2,1,0:T(8,128)(2,1)S(1)}, u32[]{:S(2)}, u32[]{:S(2)}) async-start(bf16[4,256,128]{2,1,0:T(8,128)(2,1)} %get-tuple-element.101), calls=%async_computation.5 | async-start | bytes 524288 | tf_op jit(solution)/shard_map/all_to_all | solution.py:531
  148.8 3.6 %collective-permute-start.16 = (f32[32,128]{1,0:T(8,128)S(1)}, f32[32,128]{1,0:T(8,128)S(1)}, u32[]{:S(2)}, u32[]{:S(2)}) collective-permute-start(f32[32,128]{1,0:T(8,128)S(1)} %slice_add_fusion), channel_id=1, source_target_pairs={{0,2},{1,3},{2,0},{3,1},{4,6},{5,7},{6,4},{7,5},{8,10},{9,11},{10,... | collective-permute-start | bytes 49160 | tf_op jit(solution)/shard_map/ppermute | solution.py:407
  152.4 0.6 copy.45
  153.0 2.6 %collective-permute-done.16 = f32[32,128]{1,0:T(8,128)S(1)} collective-permute-done((f32[32,128]{1,0:T(8,128)S(1)}, f32[32,128]{1,0:T(8,128)S(1)}, u32[]{:S(2)}, u32[]{:S(2)}) %collective-permute-start.16) | collective-permute-done | bytes 16416 | tf_op jit(solution)/shard_map/ppermute | solution.py:407
  155.7 0.8 finish.1
  156.4 0.1 slice_reduce_fusion
  156.6 0.1 copy.46
  156.7 0.6 reshape.81
  157.5 0.6 reshape.82
  158.2 0.6 reshape.83
  (62 shorter events, 1.3 us)
Async XLA Ops:
  0.6 0.8 slice-start
  0.7 0.8 slice-start.1
  0.7 0.7 slice-start.2
  1.4 1.9 %copy-start.9 = (f32[128,32]{0,1:T(8,128)S(1)}, f32[128,32]{0,1:T(8,128)}, u32[]{:S(2)}) copy-start(f32[128,32]{0,1:T(8,128)} %param.17) | copy-start | bytes 49156
  1.4 5.6 %collective-permute-start = (bf16[16,2048]{1,0:T(8,128)(2,1)S(1)}, bf16[16,2048]{1,0:T(8,128)(2,1)S(1)}, u32[]{:S(2)}, u32[]{:S(2)}) collective-permute-start(bf16[16,2048]{1,0:T(8,128)(2,1)S(1)} %pad_maximum_fusion), channel_id=1, source_target_pairs={{0,4},{4,8},{8,12},{12,16},{16,20},{20,24},{24,28},{28,32},{32,36}... | collective-permute-start | bytes 196616 | tf_op jit(solution)/shard_map/ppermute | solution.py:431
  3.4 0.7 copy-start.10
  4.2 0.7 copy-start.11
  5.1 1.9 %copy-start = (bf16[128,1024]{1,0:T(8,128)(2,1)S(1)}, bf16[128,1024]{1,0:T(8,128)(2,1)}, u32[]{:S(2)}) copy-start(bf16[128,1024]{1,0:T(8,128)(2,1)} %x.3) | copy-start | bytes 786436
  5.1 1.9 %copy-start.5 = (f32[4,1024]{1,0:T(4,128)S(1)}, f32[4,1024]{1,0:T(4,128)}, u32[]{:S(2)}) copy-start(f32[4,1024]{1,0:T(4,128)} %wx.3) | copy-start | bytes 49156
  5.3 1.7 %copy-start.2 = (bf16[128,512]{1,0:T(8,128)(2,1)S(1)}, bf16[128,512]{1,0:T(8,128)(2,1)}, u32[]{:S(2)}) copy-start(bf16[128,512]{1,0:T(8,128)(2,1)} %b.3) | copy-start | bytes 393220
  7.0 0.7 copy-start.7
  9.0 1.9 %collective-permute-start.1 = (f32[544,128]{1,0:T(8,128)S(1)}, f32[544,128]{1,0:T(8,128)S(1)}, u32[]{:S(2)}, u32[]{:S(2)}) collective-permute-start(f32[544,128]{1,0:T(8,128)S(1)} %get-tuple-element.66), channel_id=1, source_target_pairs={{0,4},{4,0},{1,5},{5,1},{2,6},{6,2},{3,7},{7,3},{8,12},{12,8},{9,1... | collective-permute-start | bytes 835592 | tf_op jit(solution)/shard_map/ppermute | solution.py:393
  52.5 1.0 copy-start.3
  52.5 1.0 copy-start.4
  52.5 0.7 copy-start.12
  52.6 4.8 %collective-permute-start.2 = (f32[512,128]{1,0:T(8,128)S(1)}, f32[512,128]{1,0:T(8,128)S(1)}, u32[]{:S(2)}, u32[]{:S(2)}) collective-permute-start(f32[512,128]{1,0:T(8,128)S(1)} %get-tuple-element.70), channel_id=1, source_target_pairs={{0,4},{4,0},{1,5},{5,1},{2,6},{6,2},{3,7},{7,3},{8,12},{12,8},{9,1... | collective-permute-start | bytes 786440 | tf_op jit(solution)/shard_map/ppermute | solution.py:393
  53.3 0.7 copy-start.8
  54.1 0.9 copy-start.1
  54.4 0.7 copy-start.6
  58.2 5.3 %collective-permute-start.5 = (f32[8,128]{1,0:T(8,128)S(1)}, f32[8,128]{1,0:T(8,128)S(1)}, u32[]{:S(2)}, u32[]{:S(2)}) collective-permute-start(f32[8,128]{1,0:T(8,128)S(1)} %get-tuple-element.78), channel_id=1, source_target_pairs={{0,3},{1,0},{2,1},{3,2},{4,7},{5,4},{6,5},{7,6},{8,11},{9,8},{10,9... | collective-permute-start | bytes 12296 | tf_op jit(solution)/shard_map/ppermute | solution.py:483
  61.3 4.8 %collective-permute-start.3 = (f32[8,128]{1,0:T(8,128)S(1)}, f32[8,128]{1,0:T(8,128)S(1)}, u32[]{:S(2)}, u32[]{:S(2)}) collective-permute-start(f32[8,128]{1,0:T(8,128)S(1)} %get-tuple-element.78), channel_id=1, source_target_pairs={{0,1},{1,2},{2,3},{3,0},{4,5},{5,6},{6,7},{7,4},{8,9},{9,10},{10,1... | collective-permute-start | bytes 12296 | tf_op jit(solution)/shard_map/ppermute | solution.py:483
  61.3 5.1 %collective-permute-start.4 = (f32[8,128]{1,0:T(8,128)S(1)}, f32[8,128]{1,0:T(8,128)S(1)}, u32[]{:S(2)}, u32[]{:S(2)}) collective-permute-start(f32[8,128]{1,0:T(8,128)S(1)} %get-tuple-element.78), channel_id=1, source_target_pairs={{0,2},{1,3},{2,0},{3,1},{4,6},{5,7},{6,4},{7,5},{8,10},{9,11},{10,... | collective-permute-start | bytes 12296 | tf_op jit(solution)/shard_map/ppermute | solution.py:483
  67.2 1.6 %collective-permute-start.6 = (f32[512,128]{1,0:T(8,128)S(1)}, f32[512,128]{1,0:T(8,128)S(1)}, u32[]{:S(2)}, u32[]{:S(2)}) collective-permute-start(f32[512,128]{1,0:T(8,128)S(1)} %get-tuple-element.81), channel_id=1, source_target_pairs={{0,4},{4,0},{1,5},{5,1},{2,6},{6,2},{3,7},{7,3},{8,12},{12,8},{9,1... | collective-permute-start | bytes 786440 | tf_op jit(solution)/shard_map/ppermute | solution.py:393
  102.3 3.7 %collective-permute-start.7 = (f32[512,128]{1,0:T(8,128)S(1)}, f32[512,128]{1,0:T(8,128)S(1)}, u32[]{:S(2)}, u32[]{:S(2)}) collective-permute-start(f32[512,128]{1,0:T(8,128)S(1)} %get-tuple-element.83), channel_id=1, source_target_pairs={{0,4},{4,0},{1,5},{5,1},{2,6},{6,2},{3,7},{7,3},{8,12},{12,8},{9,1... | collective-permute-start | bytes 786440 | tf_op jit(solution)/shard_map/ppermute | solution.py:393
  109.8 28.3 %all-to-all-start.4 = ((f32[4,272,128]{2,1,0:T(8,128)}), f32[4,272,128]{2,1,0:T(8,128)S(1)}, u32[]{:S(2)}, u32[]{:S(2)}) async-start(f32[4,272,128]{2,1,0:T(8,128)} %get-tuple-element.96), calls=%async_computation.4 | async-start | bytes 1114112 | tf_op jit(solution)/shard_map/all_to_all | solution.py:520
  114.3 1.2 collective-permute-start.9
  115.5 4.0 %collective-permute-start.10 = (f32[80,128]{1,0:T(8,128)S(1)}, f32[80,128]{1,0:T(8,128)S(1)}, u32[]{:S(2)}, u32[]{:S(2)}) collective-permute-start(f32[80,128]{1,0:T(8,128)S(1)} %add.37), channel_id=1, source_target_pairs={{0,8},{4,12},{8,0},{12,4},{16,24},{20,28},{24,16},{28,20},{32,40},... | collective-permute-start | bytes 122888 | tf_op jit(solution)/shard_map/ppermute | solution.py:407
  119.5 4.9 %collective-permute-start.11 = (f32[80,128]{1,0:T(8,128)S(1)}, f32[80,128]{1,0:T(8,128)S(1)}, u32[]{:S(2)}, u32[]{:S(2)}) collective-permute-start(f32[80,128]{1,0:T(8,128)S(1)} %add.38), channel_id=1, source_target_pairs={{0,16},{4,20},{8,24},{12,28},{16,0},{20,4},{24,8},{28,12},{32,48},... | collective-permute-start | bytes 122888 | tf_op jit(solution)/shard_map/ppermute | solution.py:407
  124.4 7.9 %collective-permute-start.12 = (f32[80,128]{1,0:T(8,128)S(1)}, f32[80,128]{1,0:T(8,128)S(1)}, u32[]{:S(2)}, u32[]{:S(2)}) collective-permute-start(f32[80,128]{1,0:T(8,128)S(1)} %add.39), channel_id=1, source_target_pairs={{0,32},{4,36},{8,40},{12,44},{16,48},{20,52},{24,56},{28,60},{32,0... | collective-permute-start | bytes 122888 | tf_op jit(solution)/shard_map/ppermute | solution.py:407
  132.3 4.0 %collective-permute-start.13 = (f32[80,128]{1,0:T(8,128)S(1)}, f32[80,128]{1,0:T(8,128)S(1)}, u32[]{:S(2)}, u32[]{:S(2)}) collective-permute-start(f32[80,128]{1,0:T(8,128)S(1)} %add.40), channel_id=1, source_target_pairs={{0,64},{4,68},{8,72},{12,76},{16,80},{20,84},{24,88},{28,92},{32,9... | collective-permute-start | bytes 122888 | tf_op jit(solution)/shard_map/ppermute | solution.py:407
  136.4 5.5 %collective-permute-start.14 = (f32[80,128]{1,0:T(8,128)S(1)}, f32[80,128]{1,0:T(8,128)S(1)}, u32[]{:S(2)}, u32[]{:S(2)}) collective-permute-start(f32[80,128]{1,0:T(8,128)S(1)} %add.41), channel_id=1, source_target_pairs={{0,128},{4,132},{8,136},{12,140},{16,144},{20,148},{24,152},{28,15... | collective-permute-start | bytes 122888 | tf_op jit(solution)/shard_map/ppermute | solution.py:407
  138.1 5.9 %collective-permute-start.8 = (f32[80,128]{1,0:T(8,128)S(1)}, f32[80,128]{1,0:T(8,128)S(1)}, u32[]{:S(2)}, u32[]{:S(2)}) collective-permute-start(f32[80,128]{1,0:T(8,128)S(1)} %get-tuple-element.99), channel_id=1, source_target_pairs={{4,0},{8,4},{12,8},{16,12},{20,16},{24,20},{28,24},{32,28},{36,32}... | collective-permute-start | bytes 122888 | tf_op jit(solution)/shard_map/ppermute | solution.py:524
  141.9 6.9 %collective-permute-start.15 = (f32[32,128]{1,0:T(8,128)S(1)}, f32[32,128]{1,0:T(8,128)S(1)}, u32[]{:S(2)}, u32[]{:S(2)}) collective-permute-start(f32[32,128]{1,0:T(8,128)S(1)} %slice.43), channel_id=1, source_target_pairs={{0,1},{1,0},{2,3},{3,2},{4,5},{5,4},{6,7},{7,6},{8,9},{9,8},{10,11... | collective-permute-start | bytes 49160 | tf_op jit(solution)/shard_map/ppermute | solution.py:407
  144.8 10.8 %all-to-all-start.5 = ((bf16[4,256,128]{2,1,0:T(8,128)(2,1)}), bf16[4,256,128]{2,1,0:T(8,128)(2,1)S(1)}, u32[]{:S(2)}, u32[]{:S(2)}) async-start(bf16[4,256,128]{2,1,0:T(8,128)(2,1)} %get-tuple-element.101), calls=%async_computation.5 | async-start | bytes 524288 | tf_op jit(solution)/shard_map/all_to_all | solution.py:531
  148.8 6.8 %collective-permute-start.16 = (f32[32,128]{1,0:T(8,128)S(1)}, f32[32,128]{1,0:T(8,128)S(1)}, u32[]{:S(2)}, u32[]{:S(2)}) collective-permute-start(f32[32,128]{1,0:T(8,128)S(1)} %slice_add_fusion), channel_id=1, source_target_pairs={{0,2},{1,3},{2,0},{3,1},{4,6},{5,7},{6,4},{7,5},{8,10},{9,11},{10,... | collective-permute-start | bytes 49160 | tf_op jit(solution)/shard_map/ppermute | solution.py:407

commit v2 on v1

--- a/solution.py
+++ b/solution.py
@@ -24,6 +24,7 @@
 EPSILON = 1e-05
 F32 = jnp.float32
 CTX = ("chip", "core")
+RING = 8
 PARAMS = pltpu.CompilerParams(vmem_limit_bytes=16 << 20)
 
 
@@ -236,7 +237,7 @@
 def last_kernel(
     core, own, got, full, ends, dz1, db1, dcum1, dskip, early, cpart, dy, zs, xt, bc, cum, step, skip, dt, bias, alog,
     x, hx, wx, b, hb, wb,
-    xown, heads, parts, packed, ddt, later, ext, extb, pad, padb,
+    xown, heads, keep, give, packed, ddt, parts, later, ext, extb, pad, padb,
 ):
     unite(core[0], later, own, got)
     gamma = jnp.exp(-cum[...])
@@ -272,9 +273,15 @@
     draw = dstep * sigmoid(dt[...] + bias[...])
     ddt[...] = draw
     each = jnp.concatenate([draw, dlog * rate * step[...], dskip[...], jnp.zeros((LOCAL, SPAN), F32)], axis=0)
-    packed[72:80, :] = dot(jnp.ones((8, SPAN), F32), each, 1, 1)
+    at = lax.broadcasted_iota(jnp.int32, (SPAN, SPAN), 0)
+    to = lax.broadcasted_iota(jnp.int32, (SPAN, SPAN), 1)
+    source = to // LOCAL * LOCAL + to % GROUPS * PER + to % LOCAL // GROUPS
+    packed[72:80, :] = dot(dot(jnp.ones((8, SPAN), F32), each, 1, 1), jnp.where(at == source, 1.0, 0.0))
     packed[16:32, :] = early[0:16, :]
     packed[64:72, :] = early[16:24, :]
+    side = core[1]
+    keep[...] = parts[pl.ds(side * 2, 2)]
+    give[...] = parts[pl.ds((1 - side) * 2, 2)]
     for r in range(PER):
         mine, ahead, taps = conv_back_tile(ext, pad, wx, lanes(r), take(dxs, r))
         xown[:, lanes(r)] = mine
@@ -322,35 +329,29 @@
         give[rows, :] = jnp.where(leads, near, far)
 
 
-def add_kernel(slices, xheads, mine, heads):
-    total = slices[0]
-    for g in range(1, GROUPS):
-        total = total + slices[g]
-    mine[...] = total[0 : 2 * SPAN]
-    heads[0:64, :] = xheads[...]
-    heads[64:80, :] = total[2 * SPAN :]
-
-
-def settle_kernel(xown, mine, heads, gx, spread):
+def settle_kernel(xown, mine, heads, gx, half):
     last = slice(SPAN - LEAD, SPAN)
     none = jnp.zeros((LEAD - 8, TILE), F32)
     for r in range(PER):
         gx[0 : SPAN - LEAD, lanes(r)] = xown[0 : SPAN - LEAD, lanes(r)].astype(jnp.bfloat16)
         more = jnp.concatenate([none, heads[8 * r : 8 * r + 8, :]], axis=0)
         gx[last, lanes(r)] = (xown[last, lanes(r)] + more).astype(jnp.bfloat16)
-    for i in range(2):
-        more = jnp.concatenate([none, heads[64 + 8 * i : 72 + 8 * i, :]], axis=0)
-        body_rows = mine[i * SPAN : (i + 1) * SPAN - LEAD, :].astype(jnp.bfloat16)
-        last_rows = (mine[(i + 1) * SPAN - LEAD : (i + 1) * SPAN, :] + more).astype(jnp.bfloat16)
-        for g in range(GROUPS):
-            spread[g, i * SPAN : (i + 1) * SPAN - LEAD, :] = body_rows
-            spread[g, (i + 1) * SPAN - LEAD : (i + 1) * SPAN, :] = last_rows
-
-
-def finish_kernel(spread, bc_taps, packed, gb, gc, tx, tb, tc, tgain, small):
-    for g in range(GROUPS):
-        gb[:, lanes(g)] = spread[g, 0:SPAN, :]
-        gc[:, lanes(g)] = spread[g, SPAN : 2 * SPAN, :]
+    for g in range(2):
+        for i in range(2):
+            at = 64 + 16 * g + 8 * i
+            more = jnp.concatenate([none, heads[at : at + 8, :]], axis=0)
+            start, stop = i * SPAN, (i + 1) * SPAN
+            half[g, start : stop - LEAD, :] = mine[g, start : stop - LEAD, :].astype(jnp.bfloat16)
+            half[g, stop - LEAD : stop, :] = (mine[g, stop - LEAD : stop, :] + more).astype(jnp.bfloat16)
+
+
+def finish_kernel(core, half, other, bc_taps, packed, gb, gc, tx, tb, tc, tgain, bias, rate, skip):
+    left = core[1] == 0
+    for g in range(GROUPS):
+        first, second = (half, other) if g < 2 else (other, half)
+        both = jnp.where(left, first[g % 2].astype(F32), second[g % 2].astype(F32)).astype(jnp.bfloat16)
+        gb[:, lanes(g)] = both[0:SPAN]
+        gc[:, lanes(g)] = both[SPAN : 2 * SPAN]
     for k in range(CONV):
         for g in range(GROUPS):
             tb[k : k + 1, lanes(g)] = bc_taps[k * GROUPS + g : k * GROUPS + g + 1, :]
@@ -359,7 +360,9 @@
             tx[k : k + 1, lanes(r)] = packed[32 + k * PER + r : 33 + k * PER + r, :]
     for r in range(PER):
         tgain[:, lanes(r)] = packed[64 + r : 65 + r, :]
-    small[...] = packed[72:80, :]
+    bias[...] = packed[72:73, 0:LOCAL]
+    rate[...] = packed[72:73, LOCAL : 2 * LOCAL]
+    skip[...] = packed[72:73, 2 * LOCAL : 3 * LOCAL]
 
 
 def scan_kernel(backward, s, d, o):
@@ -401,11 +404,32 @@
     return lax.all_to_all(v, "chip", 0, 0)
 
 
-def butterfly(x, axis):
-    by = 1
-    while by < lax.axis_size(axis):
-        x = x + lax.ppermute(x, axis, alike(lax.axis_size(axis), by))
-        by *= 2
+def fold(x, axis, partner):
+    return x + lax.ppermute(x, axis, [(i, partner(i)) for i in range(lax.axis_size(axis))])
+
+
+def mirror(within, block=1):
+    return lambda i: (i // block // within * within + within - 1 - i // block % within) * block + i % block
+
+
+def sum_steps(axis):
+    size = lax.axis_size(axis)
+    ring = min(RING, size)
+    steps, within = [], 2
+    while within <= ring:
+        half = within // 2
+        steps.append(mirror(within) if within in (2, ring) else (lambda i, half=half: i ^ half))
+        within *= 2
+    within = 2
+    while within * ring <= size:
+        steps.append(mirror(within, ring))
+        within *= 2
+    return steps
+
+
+def sum_over(x, axis):
+    for partner in sum_steps(axis):
+        x = fold(x, axis, partner)
     return x
 
 
@@ -422,7 +446,8 @@
 ):
     size = lax.axis_size(CTX)
     core = lax.axis_index("core")
-    cores = core.reshape(1)
+    side = lax.axis_index("tp") // (lax.axis_size("tp") // 2)
+    cores = jnp.stack([core, side])
     is_even = core == 0
     t_shape = ((ALL, SPAN), F32)
     bc_shape = ((SPAN, GROUPS * STATE), F32)
@@ -479,8 +504,7 @@
         (cores, enter_own, enter_got, cc, y1, cum, zt, sgt),
         scalars=1,
     )
-    peers = lax.axis_size("tp")
-    sums = sums + sum(lax.ppermute(sums, "tp", [(i, (i + k) % peers) for i in range(peers)]) for k in range(1, peers))
+    sums = sum_over(sums, "tp")
     keep, give, dy, dg = call(
         gate_kernel,
         "gate",
@@ -508,35 +532,53 @@
         (sums, y, zt, ogt, dy, dg, enter, mt, zs, xt, bc, cc, cum, skip, c_raw, hc, conv_c),
         [(LEAD + SPAN, wb), (LEAD + SPAN, wb), (SPAN, wb)],
     )
-    xown, xheads, parts, packed, ddt = call(
+    half_parts = ((2, 2 * SPAN + 16, TILE), F32)
+    xown, xheads, keep, give, packed, ddt = call(
         last_kernel,
         "last",
-        [((SPAN, wx), F32), ((64, TILE), F32), ((GROUPS, 2 * SPAN + 16, TILE), F32), ((80, TILE), F32), h_shape],
+        [((SPAN, wx), F32), ((64, TILE), F32), half_parts, half_parts, ((80, TILE), F32), h_shape],
         (cores, later_own, later_got, enter, ends, dz, db, dcum, dskip, early, cpart)
         + (dy, zs, xt, bc, cum, step, skip, dt, bias, alog, x_raw, hx, conv_x, b_raw, hb, conv_b),
-        [(ALL, STATE), (LEAD + SPAN, wx), (LEAD + SPAN, wb), (LEAD + SPAN, wx), (LEAD + SPAN, wb)],
+        [(GROUPS, 2 * SPAN + 16, TILE), (ALL, STATE)]
+        + [(LEAD + SPAN, wx), (LEAD + SPAN, wb), (LEAD + SPAN, wx), (LEAD + SPAN, wb)],
         scalars=1,
     )
-    slices = lax.all_to_all(parts, "tp", 0, 0)
-    packed = butterfly(packed, CTX)
-    bc_taps = butterfly(packed[:32], "tp")
-    mine, heads = call(add_kernel, "add", [((2 * SPAN, TILE), F32), ((80, TILE), F32)], (slices, xheads))
+    peers = lax.axis_size("tp")
+    across = [(i, peers - 1 - i) for i in range(peers)]
+    arrived = lax.ppermute(give, "tp", across)
+    packed = packed + swap_cores(packed)
+    steps = sum_steps("chip")
+    packed = fold(packed, "chip", steps[0])
+    arrived, packed = lax.optimization_barrier((arrived, packed))
+    mine = keep + arrived
+    arrived = lax.ppermute(mine, "tp", [(i, i ^ 1) for i in range(peers)])
+    for partner in steps[1:3]:
+        packed = fold(packed, "chip", partner)
+    arrived, packed = lax.optimization_barrier((arrived, packed))
+    mine = mine + arrived
+    heads = jnp.concatenate([xheads, mine[:, 2 * SPAN :].reshape(32, TILE)], axis=0)
     heads = lax.ppermute(heads, CTX, [(i + 1, i) for i in range(size - 1)])
-    grad_x_raw, spread = call(
+    for partner in steps[3:4]:
+        packed = fold(packed, "chip", partner)
+    heads, packed = lax.optimization_barrier((heads, packed))
+    grad_x_raw, half = call(
         settle_kernel,
         "settle",
-        [((SPAN, wx), jnp.bfloat16), ((GROUPS, 2 * SPAN, TILE), jnp.bfloat16)],
+        [((SPAN, wx), jnp.bfloat16), ((2, 2 * SPAN, TILE), jnp.bfloat16)],
         (xown, mine, heads),
     )
-    spread = lax.all_to_all(spread, "tp", 0, 0)
-    half_bc = ((SPAN, wb), jnp.bfloat16)
-    grad_b_raw, grad_c_raw, conv_x_total, conv_b_total, conv_c_total, gain_total, small = call(
+    other = lax.ppermute(half, "tp", across)
+    for partner in steps[4:]:
+        packed = fold(packed, "chip", partner)
+    bc_taps = sum_over(packed[:32], "tp")
+    half_bc, each = ((SPAN, wb), jnp.bfloat16), ((1, LOCAL), F32)
+    grad_b_raw, grad_c_raw, conv_x_total, conv_b_total, conv_c_total, gain_total, *small = call(
         finish_kernel,
         "finish",
-        [half_bc, half_bc, ((CONV, wx), F32), ((CONV, wb), F32), ((CONV, wb), F32), ((1, wx), F32), ((8, TILE), F32)],
-        (spread, bc_taps, packed),
-    )
-    small = [by_head(small[0, i * LOCAL : (i + 1) * LOCAL]) for i in range(3)]
+        [half_bc, half_bc, ((CONV, wx), F32), ((CONV, wb), F32), ((CONV, wb), F32), ((1, wx), F32)] + [each] * 3,
+        (cores, half, other, bc_taps, packed),
+        scalars=1,
+    )
     return (
         grad_x_raw,
         grad_b_raw,
@@ -546,7 +588,7 @@
         conv_x_total,
         conv_b_total,
         conv_c_total,
-        *small,
+        *(v.reshape(-1) for v in small),
         gain_total.reshape(-1),
     )
 

time: 161 us -> 160 us (level); the launches traced: 159 us -> 160 us
  starting transfers between devices: 29.8 us -> 24.6 us
  waiting for transfers between devices: 30.1 us -> 34.5 us
  Pallas kernels: 15.2 us -> 19.3 us
  local copies, waits for them, and re-layouts: 8.23 us -> 6.49 us
    all_to_all x2 -> x0, starting transfers between devices: 8.45 us -> none  [the longest x1 4.5 us: body(): slices = lax.all_to_all(parts, 'tp', 0, 0)]
    ppermute x11 -> x12, waiting for transfers between devices: 25.7 us -> 29.8 us  [the longest x9 27.8 us: fold(): lax.ppermute(x, axis, [(i, partner(i)) for i in range(lax.axis_size(axis))])]
    pallas_call x17 -> x16, Pallas kernels: 15.2 us -> 19.3 us  [call(): pl.pallas_call(kernel, out_shape=[jax.ShapeDtypeStruct(s, d) for s, d in...]
    ppermute x11 -> x12, starting transfers between devices: 16.4 us -> 18.7 us  [the longest x9 12.6 us: fold(): lax.ppermute(x, axis, [(i, partner(i)) for i in range(lax.axis_size(axis))])]
    reshape x3 -> x0, local copies, waits for them, and re-layouts: 1.79 us -> none  [by_head(): v.reshape((GROUPS, PER) + v.shape[1:]).swapaxes(0, 1).reshape(v.shape)]
    ppermute x4 -> x5, waiting for transfers between devices: 2.71 us -> 3.73 us  [swap_cores(): return lax.ppermute(v, 'core', [(0, 1), (1, 0)])]
  transfers between devices with their start and end apart: 19 -> 19, of which waited for: 12 -> 13; matrix products, arithmetic and copies ran while one was open for 1% -> 1% of each run, Pallas kernels for 4% -> 4%
where the time goes in v2:
time: 160 us
  blocking collectives  73.7 us (46%)
  waiting for transfers between devices  34.5 us (22%)
  starting transfers between devices  24.6 us (15%)
  Pallas kernels  19.3 us (12%)
  local copies, waits for them, and re-layouts  6.49 us (4%)
    all_to_all x4, blocking collectives, over_chips(): return lax.all_to_all(v, 'chip', 0, 0)  73.7 us
    ppermute x9, waiting for transfers between devices, fold(): lax.ppermute(x, axis, [(i, partner(i)) for i in range(lax.axis_size(axis))])  27.8 us
    pallas_call x16, Pallas kernels, call(): pl.pallas_call(kernel, out_shape=[jax.ShapeDtypeStruct(s, d) for s, d in...  19.3 us
    ppermute x9, starting transfers between devices, fold(): lax.ppermute(x, axis, [(i, partner(i)) for i in range(lax.axis_size(axis))])  12.6 us
    unnamed x26, local copies, waits for them, and re-layouts  4.32 us
    ppermute x5, waiting for transfers between devices, swap_cores(): return lax.ppermute(v, 'core', [(0, 1), (1, 0)])  3.73 us
  transfers between devices with their start and end apart: 19, of which 13 were waited for; matrix products, arithmetic and copies ran while one was open for 1% of the time, Pallas kernels for 4%

profile of v2, /device:TPU:32, one launch (start us, length us, event | category | flops | bytes accessed | tf_op | source)
XLA Modules:
  0.0 159.7 jit_solution(7073586296247161234)
XLA Ops:
  0.7 0.7 slice-done
  1.4 1.9 %collective-permute-start = (bf16[16,2048]{1,0:T(8,128)(2,1)S(1)}, bf16[16,2048]{1,0:T(8,128)(2,1)S(1)}, u32[]{:S(2)}, u32[]{:S(2)}) collective-permute-start(bf16[16,2048]{1,0:T(8,128)(2,1)S(1)} %pad_maximum_fusion), channel_id=1, source_target_pairs={{0,4},{4,8},{8,12},{12,16},{16,20},{20,24},{24,28},{28,32},{32,36}... | collective-permute-start | bytes 196616 | tf_op jit(solution)/shard_map/ppermute | solution.py:456
  3.4 0.7 copy-done.9
  4.1 0.7 copy-done.10
  4.8 0.1 copy.35
  5.0 0.6 copy-done.11
  5.8 0.2 steps.1
  6.1 0.9 collective-permute-done
  7.0 0.7 copy-done.7
  7.7 1.8 %state.1 = (f32[1024,128]{1,0:T(8,128)S(1)}, f32[1024,128]{1,0:T(8,128)S(1)}, f32[128,512]{1,0:T(8,128)S(1)}, f32[512,128]{1,0:T(8,128)S(1)}, f32[544,128]{1,0:T(8,128)S(1)}) custom-call(s32[2]{0:T(128)S(1)} %pad_add_fusion.core, bf16[128,1024]{1,0:T(8,128)(2,1)S(1)} %copy-done, bf16[16,1024]{1,0:T(8,128)(2,1)S(1)} %slice.32.hx, ...), custom_call_target="tpu_custom_call" | custom-call | flops 20000000 | bytes 4194304 | tf_op jit(solution)/shard_map/state/pallas_call | solution.py:383
  9.5 1.4 collective-permute-start.1
  10.9 1.2 collective-permute-done.1.got
  12.1 0.7 join.2
  12.8 24.2 %all_to_all.20.s.d = f32[32,1,2176]{2,1,0:T(1,128)S(1)} all-to-all(f32[32,1,2176]{2,1,0:T(1,128)S(1)} %get-tuple-element.74), channel_id=1, replica_groups=mesh['chip'=32,'core'=2,'tp'=4] {'chip'}, dimensions={0} | all-to-all | bytes 557056 | tf_op jit(solution)/shard_map/all_to_all | solution.py:404
  37.0 0.2 block_scan.2
  37.2 16.4 %all_to_all.21 = f32[32,1,2048]{2,1,0:T(1,128)S(1)} all-to-all(f32[32,1,2048]{2,1,0:T(1,128)S(1)} %block_scan.2), channel_id=1, replica_groups=mesh['chip'=32,'core'=2,'tp'=4] {'chip'}, dimensions={0} | all-to-all | bytes 524288 | tf_op jit(solution)/shard_map/all_to_all | solution.py:404
  53.6 0.6 split.2
  54.2 0.1 collective-permute-start.2
  54.3 0.5 copy-done.12
  55.0 0.1 broadcast_in_dim.10
  55.1 0.5 copy-done.8
  55.6 0.3 turn.1
  56.0 0.5 copy-done.1
  56.5 0.2 copy-done.6
  56.7 2.3 %local.1 = (f32[128,512]{1,0:T(8,128)S(1)}, f32[512,128]{1,0:T(8,128)S(1)}, f32[1024,128]{1,0:T(8,128)S(1)}) custom-call(bf16[128,512]{1,0:T(8,128)(2,1)S(1)} %copy-done.1, bf16[16,512]{1,0:T(8,128)(2,1)S(1)} %get-tuple-element.126.hc, f32[4,512]{1,0:T(4,128)S(1)} %copy-done.6, f32[128,512]{1,0:T(8,128)S(1)} %get-tuple-element.78.bc, ...), custom_call_target="tpu_custom_call" | custom-call | flops 20000000 | bytes 4194304 | tf_op jit(solution)/shard_map/local/pallas_call | solution.py:383
  58.9 1.3 output.1
  60.2 1.7 %collective-permute-start.3 = (f32[8,128]{1,0:T(8,128)S(1)}, f32[8,128]{1,0:T(8,128)S(1)}, u32[]{:S(2)}, u32[]{:S(2)}) collective-permute-start(f32[8,128]{1,0:T(8,128)S(1)} %get-tuple-element.85), channel_id=1, source_target_pairs={{0,1},{1,0},{2,3},{3,2},{4,5},{5,4},{6,7},{7,6},{8,9},{9,8},{10,11... | collective-permute-start | bytes 12296 | tf_op jit(solution)/shard_map/ppermute | solution.py:408
  61.9 2.0 %collective-permute-done.3 = f32[8,128]{1,0:T(8,128)S(1)} collective-permute-done((f32[8,128]{1,0:T(8,128)S(1)}, f32[8,128]{1,0:T(8,128)S(1)}, u32[]{:S(2)}, u32[]{:S(2)}) %collective-permute-start.3) | collective-permute-done | bytes 4128 | tf_op jit(solution)/shard_map/ppermute | solution.py:408
  63.9 3.0 %collective-permute-start.4 = (f32[8,128]{1,0:T(8,128)S(1)}, f32[8,128]{1,0:T(8,128)S(1)}, u32[]{:S(2)}, u32[]{:S(2)}) collective-permute-start(f32[8,128]{1,0:T(8,128)S(1)} %add.37), channel_id=1, source_target_pairs={{0,3},{1,2},{2,1},{3,0},{4,7},{5,6},{6,5},{7,4},{8,11},{9,10},{10,... | collective-permute-start | bytes 12296 | tf_op jit(solution)/shard_map/ppermute | solution.py:408
  67.0 1.8 %collective-permute-done.4 = f32[8,128]{1,0:T(8,128)S(1)} collective-permute-done((f32[8,128]{1,0:T(8,128)S(1)}, f32[8,128]{1,0:T(8,128)S(1)}, u32[]{:S(2)}, u32[]{:S(2)}) %collective-permute-start.4) | collective-permute-done | bytes 4128 | tf_op jit(solution)/shard_map/ppermute | solution.py:408
  68.8 1.4 gate.1
  70.2 0.1 collective-permute-start.5
  70.3 1.5 collective-permute-done.5.got
  71.8 0.6 join.3
  72.4 16.9 %all_to_all.22.s = f32[32,1,2048]{2,1,0:T(1,128)S(1)} all-to-all(f32[32,1,2048]{2,1,0:T(1,128)S(1)} %bitcast.30), channel_id=1, replica_groups=mesh['chip'=32,'core'=2,'tp'=4] {'chip'}, dimensions={0} | all-to-all | bytes 524288 | tf_op jit(solution)/shard_map/all_to_all | solution.py:404
  89.3 0.2 block_scan.3
  89.5 16.2 %all_to_all.23 = f32[32,1,2048]{2,1,0:T(1,128)S(1)} all-to-all(f32[32,1,2048]{2,1,0:T(1,128)S(1)} %block_scan.3), channel_id=1, replica_groups=mesh['chip'=32,'core'=2,'tp'=4] {'chip'}, dimensions={0} | all-to-all | bytes 524288 | tf_op jit(solution)/shard_map/all_to_all | solution.py:404
  105.7 0.6 split.3
  106.3 0.3 collective-permute-start.6
  106.6 3.4 %middle.1 = (f32[1024,128]{1,0:T(8,128)S(1)}, f32[128,512]{1,0:T(8,128)S(1)}, f32[32,128]{1,0:T(8,128)S(1)}, f32[32,128]{1,0:T(8,128)S(1)}, bf16[128,1024]{1,0:T...) custom-call(f32[8,128]{1,0:T(8,128)S(1)} %add.38.sums, f32[1024,128]{1,0:T(8,128)S(1)} %get-tuple-element.86.y, ...), custom_call_target="tpu_custom_call" | custom-call | flops 20000000 | bytes 4194304 | tf_op jit(solution)/shard_map/middle/pallas_call | solution.py:383
  110.0 3.7 %last.1 = (f32[128,1024]{1,0:T(8,128)S(1)}, f32[64,128]{1,0:T(8,128)S(1)}, f32[2,272,128]{2,1,0:T(8,128)S(1)}, f32[2,272,128]{2,1,0:T(8,128)S(1)}, f32[80,128]{1,0:T(8,128)S(1)}, /*index=5*/f32[32,128]{1,0:T(8,128)S(1)}) custom-call(s32[2]{0:T(128)S(1)} %pad_add_fusion.core, f32[512,128]{1,0:T(8,128)S(1)} %get-tuple-element.89.own, ...), custom_call_target="tpu_custom_call" | custom-call | flops 20000000 | bytes 4194304 | tf_op jit(solution)/shard_map/last/pallas_call | solution.py:383
  113.7 3.1 %collective-permute-start.7 = (f32[2,272,128]{2,1,0:T(8,128)S(1)}, f32[2,272,128]{2,1,0:T(8,128)S(1)}, u32[]{:S(2)}, u32[]{:S(2)}) collective-permute-start(f32[2,272,128]{2,1,0:T(8,128)S(1)} %get-tuple-element.104), channel_id=1, source_target_pairs={{0,3},{1,2},{2,1},{3,0},{4,7},{5,6},{6,5},{7,4},{8,11},{9,10},{10,... | collective-permute-start | bytes 835592 | tf_op jit(solution)/shard_map/ppermute | solution.py:548
  116.8 0.2 collective-permute-start.8
  117.0 1.0 collective-permute-done.8
  118.0 0.2 collective-permute-start.9
  118.2 3.8 %collective-permute-done.9 = f32[80,128]{1,0:T(8,128)S(1)} collective-permute-done((f32[80,128]{1,0:T(8,128)S(1)}, f32[80,128]{1,0:T(8,128)S(1)}, u32[]{:S(2)}, u32[]{:S(2)}) %collective-permute-start.9) | collective-permute-done | bytes 40992 | tf_op jit(solution)/shard_map/ppermute | solution.py:408
  122.0 2.1 %collective-permute-done.7 = f32[2,272,128]{2,1,0:T(8,128)S(1)} collective-permute-done((f32[2,272,128]{2,1,0:T(8,128)S(1)}, f32[2,272,128]{2,1,0:T(8,128)S(1)}, u32[]{:S(2)}, u32[]{:S(2)}) %collective-permute-start.7) | collective-permute-done | bytes 278560 | tf_op jit(solution)/shard_map/ppermute | solution.py:548
  124.1 0.1 collective-permute-start.10
  124.2 1.0 collective-permute-start.11
  125.2 4.0 %collective-permute-done.11 = f32[80,128]{1,0:T(8,128)S(1)} collective-permute-done((f32[80,128]{1,0:T(8,128)S(1)}, f32[80,128]{1,0:T(8,128)S(1)}, u32[]{:S(2)}, u32[]{:S(2)}) %collective-permute-start.11) | collective-permute-done | bytes 40992 | tf_op jit(solution)/shard_map/ppermute | solution.py:408
  129.2 1.6 %collective-permute-start.12 = (f32[80,128]{1,0:T(8,128)S(1)}, f32[80,128]{1,0:T(8,128)S(1)}, u32[]{:S(2)}, u32[]{:S(2)}) collective-permute-start(f32[80,128]{1,0:T(8,128)S(1)} %add.42), channel_id=1, source_target_pairs={{0,56},{8,48},{16,40},{24,32},{32,24},{40,16},{48,8},{56,0},{64,12... | collective-permute-start | bytes 122888 | tf_op jit(solution)/shard_map/ppermute | solution.py:408
  130.8 5.4 %collective-permute-done.12 = f32[80,128]{1,0:T(8,128)S(1)} collective-permute-done((f32[80,128]{1,0:T(8,128)S(1)}, f32[80,128]{1,0:T(8,128)S(1)}, u32[]{:S(2)}, u32[]{:S(2)}) %collective-permute-start.12) | collective-permute-done | bytes 40992 | tf_op jit(solution)/shard_map/ppermute | solution.py:408
  136.3 1.9 %collective-permute-start.13 = (f32[96,128]{1,0:T(8,128)S(1)}, f32[96,128]{1,0:T(8,128)S(1)}, u32[]{:S(2)}, u32[]{:S(2)}) collective-permute-start(f32[96,128]{1,0:T(8,128)S(1)} %pad_maximum_fusion.1), channel_id=1, source_target_pairs={{4,0},{8,4},{12,8},{16,12},{20,16},{24,20},{28,24},{32,28},{36,32}... | collective-permute-start | bytes 147464 | tf_op jit(solution)/shard_map/ppermute | solution.py:560
  138.2 0.7 collective-permute-start.14
  138.9 3.4 %collective-permute-done.14 = f32[80,128]{1,0:T(8,128)S(1)} collective-permute-done((f32[80,128]{1,0:T(8,128)S(1)}, f32[80,128]{1,0:T(8,128)S(1)}, u32[]{:S(2)}, u32[]{:S(2)}) %collective-permute-start.14) | collective-permute-done | bytes 40992 | tf_op jit(solution)/shard_map/ppermute | solution.py:408
  142.3 1.2 collective-permute-start.16
  143.6 4.0 %collective-permute-done.16 = f32[80,128]{1,0:T(8,128)S(1)} collective-permute-done((f32[80,128]{1,0:T(8,128)S(1)}, f32[80,128]{1,0:T(8,128)S(1)}, u32[]{:S(2)}, u32[]{:S(2)}) %collective-permute-start.16) | collective-permute-done | bytes 40992 | tf_op jit(solution)/shard_map/ppermute | solution.py:408
  147.6 2.0 %collective-permute-start.17 = (f32[32,128]{1,0:T(8,128)S(1)}, f32[32,128]{1,0:T(8,128)S(1)}, u32[]{:S(2)}, u32[]{:S(2)}) collective-permute-start(f32[32,128]{1,0:T(8,128)S(1)} %slice.36), channel_id=1, source_target_pairs={{0,1},{1,0},{2,3},{3,2},{4,5},{5,4},{6,7},{7,6},{8,9},{9,8},{10,11... | collective-permute-start | bytes 49160 | tf_op jit(solution)/shard_map/ppermute | solution.py:408
  149.7 0.8 settle.1
  150.4 3.0 %collective-permute-start.15 = (bf16[2,256,128]{2,1,0:T(8,128)(2,1)S(1)}, bf16[2,256,128]{2,1,0:T(8,128)(2,1)S(1)}, u32[]{:S(2)}, u32[]{:S(2)}) collective-permute-start(bf16[2,256,128]{2,1,0:T(8,128)(2,1)S(1)} %get-tuple-element.113.half), channel_id=1, source_target_pairs={{0,3},{1,2},{2,1},{3,0},{4,7},{5,6},{6,5},{7,4},{8,11},{9,10},{10,... | collective-permute-start | bytes 393224 | tf_op jit(solution)/shard_map/ppermute | solution.py:570
  153.4 1.1 collective-permute-start.18
  154.4 0.6 copy.42
  155.0 3.4 %collective-permute-done.18 = f32[32,128]{1,0:T(8,128)S(1)} collective-permute-done((f32[32,128]{1,0:T(8,128)S(1)}, f32[32,128]{1,0:T(8,128)S(1)}, u32[]{:S(2)}, u32[]{:S(2)}) %collective-permute-start.18) | collective-permute-done | bytes 16416 | tf_op jit(solution)/shard_map/ppermute | solution.py:408
  158.4 1.3 finish.1
  (57 shorter events, 0.9 us)
Async XLA Ops:
  0.6 0.8 slice-start
  0.7 0.8 slice-start.1
  0.7 0.7 slice-start.2
  1.4 5.6 %collective-permute-start = (bf16[16,2048]{1,0:T(8,128)(2,1)S(1)}, bf16[16,2048]{1,0:T(8,128)(2,1)S(1)}, u32[]{:S(2)}, u32[]{:S(2)}) collective-permute-start(bf16[16,2048]{1,0:T(8,128)(2,1)S(1)} %pad_maximum_fusion), channel_id=1, source_target_pairs={{0,4},{4,8},{8,12},{12,16},{16,20},{20,24},{24,28},{28,32},{32,36}... | collective-permute-start | bytes 196616 | tf_op jit(solution)/shard_map/ppermute | solution.py:456
  3.4 0.7 copy-start.9
  4.1 0.7 copy-start.10
  4.9 0.7 copy-start.11
  5.8 1.2 copy-start
  5.8 1.2 copy-start.5
  6.0 1.0 copy-start.2
  7.0 0.7 copy-start.7
  9.5 2.6 %collective-permute-start.1 = (f32[544,128]{1,0:T(8,128)S(1)}, f32[544,128]{1,0:T(8,128)S(1)}, u32[]{:S(2)}, u32[]{:S(2)}) collective-permute-start(f32[544,128]{1,0:T(8,128)S(1)} %get-tuple-element.73), channel_id=1, source_target_pairs={{0,4},{4,0},{1,5},{5,1},{2,6},{6,2},{3,7},{7,3},{8,12},{12,8},{9,1... | collective-permute-start | bytes 835592 | tf_op jit(solution)/shard_map/ppermute | solution.py:396
  53.6 1.5 copy-start.3
  53.6 1.5 copy-start.4
  54.2 0.7 copy-start.12
  54.2 4.7 %collective-permute-start.2 = (f32[512,128]{1,0:T(8,128)S(1)}, f32[512,128]{1,0:T(8,128)S(1)}, u32[]{:S(2)}, u32[]{:S(2)}) collective-permute-start(f32[512,128]{1,0:T(8,128)S(1)} %get-tuple-element.77), channel_id=1, source_target_pairs={{0,4},{4,0},{1,5},{5,1},{2,6},{6,2},{3,7},{7,3},{8,12},{12,8},{9,1... | collective-permute-start | bytes 786440 | tf_op jit(solution)/shard_map/ppermute | solution.py:396
  54.9 0.7 copy-start.8
  55.6 0.9 copy-start.1
  55.9 0.7 copy-start.6
  60.2 3.7 %collective-permute-start.3 = (f32[8,128]{1,0:T(8,128)S(1)}, f32[8,128]{1,0:T(8,128)S(1)}, u32[]{:S(2)}, u32[]{:S(2)}) collective-permute-start(f32[8,128]{1,0:T(8,128)S(1)} %get-tuple-element.85), channel_id=1, source_target_pairs={{0,1},{1,0},{2,3},{3,2},{4,5},{5,4},{6,7},{7,6},{8,9},{9,8},{10,11... | collective-permute-start | bytes 12296 | tf_op jit(solution)/shard_map/ppermute | solution.py:408
  63.9 4.8 %collective-permute-start.4 = (f32[8,128]{1,0:T(8,128)S(1)}, f32[8,128]{1,0:T(8,128)S(1)}, u32[]{:S(2)}, u32[]{:S(2)}) collective-permute-start(f32[8,128]{1,0:T(8,128)S(1)} %add.37), channel_id=1, source_target_pairs={{0,3},{1,2},{2,1},{3,0},{4,7},{5,6},{6,5},{7,4},{8,11},{9,10},{10,... | collective-permute-start | bytes 12296 | tf_op jit(solution)/shard_map/ppermute | solution.py:408
  70.2 1.6 %collective-permute-start.5 = (f32[512,128]{1,0:T(8,128)S(1)}, f32[512,128]{1,0:T(8,128)S(1)}, u32[]{:S(2)}, u32[]{:S(2)}) collective-permute-start(f32[512,128]{1,0:T(8,128)S(1)} %get-tuple-element.88), channel_id=1, source_target_pairs={{0,4},{4,0},{1,5},{5,1},{2,6},{6,2},{3,7},{7,3},{8,12},{12,8},{9,1... | collective-permute-start | bytes 786440 | tf_op jit(solution)/shard_map/ppermute | solution.py:396
  106.3 3.7 %collective-permute-start.6 = (f32[512,128]{1,0:T(8,128)S(1)}, f32[512,128]{1,0:T(8,128)S(1)}, u32[]{:S(2)}, u32[]{:S(2)}) collective-permute-start(f32[512,128]{1,0:T(8,128)S(1)} %get-tuple-element.90), channel_id=1, source_target_pairs={{0,4},{4,0},{1,5},{5,1},{2,6},{6,2},{3,7},{7,3},{8,12},{12,8},{9,1... | collective-permute-start | bytes 786440 | tf_op jit(solution)/shard_map/ppermute | solution.py:396
  113.7 10.4 %collective-permute-start.7 = (f32[2,272,128]{2,1,0:T(8,128)S(1)}, f32[2,272,128]{2,1,0:T(8,128)S(1)}, u32[]{:S(2)}, u32[]{:S(2)}) collective-permute-start(f32[2,272,128]{2,1,0:T(8,128)S(1)} %get-tuple-element.104), channel_id=1, source_target_pairs={{0,3},{1,2},{2,1},{3,0},{4,7},{5,6},{6,5},{7,4},{8,11},{9,10},{10,... | collective-permute-start | bytes 835592 | tf_op jit(solution)/shard_map/ppermute | solution.py:548
  116.8 1.2 collective-permute-start.8
  118.0 4.0 %collective-permute-start.9 = (f32[80,128]{1,0:T(8,128)S(1)}, f32[80,128]{1,0:T(8,128)S(1)}, u32[]{:S(2)}, u32[]{:S(2)}) collective-permute-start(f32[80,128]{1,0:T(8,128)S(1)} %add.39), channel_id=1, source_target_pairs={{0,8},{8,0},{16,24},{24,16},{32,40},{40,32},{48,56},{56,48},{64,72... | collective-permute-start | bytes 122888 | tf_op jit(solution)/shard_map/ppermute | solution.py:408
  124.1 12.1 %collective-permute-start.10 = (f32[2,272,128]{2,1,0:T(8,128)S(1)}, f32[2,272,128]{2,1,0:T(8,128)S(1)}, u32[]{:S(2)}, u32[]{:S(2)}) collective-permute-start(f32[2,272,128]{2,1,0:T(8,128)S(1)} %add.41), channel_id=1, source_target_pairs={{0,1},{1,0},{2,3},{3,2},{4,5},{5,4},{6,7},{7,6},{8,9},{9,8},{10,11... | collective-permute-start | bytes 835592 | tf_op jit(solution)/shard_map/ppermute | solution.py:554
  124.2 5.0 %collective-permute-start.11 = (f32[80,128]{1,0:T(8,128)S(1)}, f32[80,128]{1,0:T(8,128)S(1)}, u32[]{:S(2)}, u32[]{:S(2)}) collective-permute-start(f32[80,128]{1,0:T(8,128)S(1)} %add.40), channel_id=1, source_target_pairs={{0,16},{8,24},{16,0},{24,8},{32,48},{40,56},{48,32},{56,40},{64,80... | collective-permute-start | bytes 122888 | tf_op jit(solution)/shard_map/ppermute | solution.py:408
  129.2 7.0 %collective-permute-start.12 = (f32[80,128]{1,0:T(8,128)S(1)}, f32[80,128]{1,0:T(8,128)S(1)}, u32[]{:S(2)}, u32[]{:S(2)}) collective-permute-start(f32[80,128]{1,0:T(8,128)S(1)} %add.42), channel_id=1, source_target_pairs={{0,56},{8,48},{16,40},{24,32},{32,24},{40,16},{48,8},{56,0},{64,12... | collective-permute-start | bytes 122888 | tf_op jit(solution)/shard_map/ppermute | solution.py:408
  136.3 6.0 %collective-permute-start.13 = (f32[96,128]{1,0:T(8,128)S(1)}, f32[96,128]{1,0:T(8,128)S(1)}, u32[]{:S(2)}, u32[]{:S(2)}) collective-permute-start(f32[96,128]{1,0:T(8,128)S(1)} %pad_maximum_fusion.1), channel_id=1, source_target_pairs={{4,0},{8,4},{12,8},{16,12},{20,16},{24,20},{28,24},{32,28},{36,32}... | collective-permute-start | bytes 147464 | tf_op jit(solution)/shard_map/ppermute | solution.py:560
  138.2 4.1 %collective-permute-start.14 = (f32[80,128]{1,0:T(8,128)S(1)}, f32[80,128]{1,0:T(8,128)S(1)}, u32[]{:S(2)}, u32[]{:S(2)}) collective-permute-start(f32[80,128]{1,0:T(8,128)S(1)} %add.43), channel_id=1, source_target_pairs={{0,64},{8,72},{16,80},{24,88},{32,96},{40,104},{48,112},{56,120},{... | collective-permute-start | bytes 122888 | tf_op jit(solution)/shard_map/ppermute | solution.py:408
  142.3 5.3 %collective-permute-start.16 = (f32[80,128]{1,0:T(8,128)S(1)}, f32[80,128]{1,0:T(8,128)S(1)}, u32[]{:S(2)}, u32[]{:S(2)}) collective-permute-start(f32[80,128]{1,0:T(8,128)S(1)} %add.45), channel_id=1, source_target_pairs={{0,192},{8,200},{16,208},{24,216},{32,224},{40,232},{48,240},{56,2... | collective-permute-start | bytes 122888 | tf_op jit(solution)/shard_map/ppermute | solution.py:408
  147.6 5.7 %collective-permute-start.17 = (f32[32,128]{1,0:T(8,128)S(1)}, f32[32,128]{1,0:T(8,128)S(1)}, u32[]{:S(2)}, u32[]{:S(2)}) collective-permute-start(f32[32,128]{1,0:T(8,128)S(1)} %slice.36), channel_id=1, source_target_pairs={{0,1},{1,0},{2,3},{3,2},{4,5},{5,4},{6,7},{7,6},{8,9},{9,8},{10,11... | collective-permute-start | bytes 49160 | tf_op jit(solution)/shard_map/ppermute | solution.py:408
  150.4 8.0 %collective-permute-start.15 = (bf16[2,256,128]{2,1,0:T(8,128)(2,1)S(1)}, bf16[2,256,128]{2,1,0:T(8,128)(2,1)S(1)}, u32[]{:S(2)}, u32[]{:S(2)}) collective-permute-start(bf16[2,256,128]{2,1,0:T(8,128)(2,1)S(1)} %get-tuple-element.113.half), channel_id=1, source_target_pairs={{0,3},{1,2},{2,1},{3,0},{4,7},{5,6},{6,5},{7,4},{8,11},{9,10},{10,... | collective-permute-start | bytes 393224 | tf_op jit(solution)/shard_map/ppermute | solution.py:570
  153.4 5.0 %collective-permute-start.18 = (f32[32,128]{1,0:T(8,128)S(1)}, f32[32,128]{1,0:T(8,128)S(1)}, u32[]{:S(2)}, u32[]{:S(2)}) collective-permute-start(f32[32,128]{1,0:T(8,128)S(1)} %slice_add_fusion), channel_id=1, source_target_pairs={{0,3},{1,2},{2,1},{3,0},{4,7},{5,6},{6,5},{7,4},{8,11},{9,10},{10,... | collective-permute-start | bytes 49160 | tf_op jit(solution)/shard_map/ppermute | solution.py:408

commit v3 on v2

--- a/solution.py
+++ b/solution.py
@@ -125,10 +125,11 @@
     return rows <= cols if upper else rows >= cols
 
 
-def steps_kernel(dt, bias, alog, step, cum, ends):
-    v = dt[...] + bias[...]
+def steps_kernel(dt, heads, step, cum, ends, skip):
+    v = dt[...] + heads[:, 0:1]
+    skip[...] = jnp.broadcast_to(heads[:, 2:3], skip.shape)
     step[...] = jnp.maximum(v, 0.0) + jnp.log1p(jnp.exp(-jnp.abs(v)))
-    rates = -jnp.exp(alog[...]) * step[...]
+    rates = -jnp.exp(heads[:, 1:2]) * step[...]
     cum[...] = dot(rates, jnp.where(triangle(True), 1.0, 0.0))
     ends[...] = jnp.broadcast_to(jnp.exp(jnp.sum(rates, axis=1, keepdims=True)), ends.shape)
 
@@ -235,7 +236,7 @@
 
 
 def last_kernel(
-    core, own, got, full, ends, dz1, db1, dcum1, dskip, early, cpart, dy, zs, xt, bc, cum, step, skip, dt, bias, alog,
+    core, which, own, got, full, ends, dz1, db1, dcum1, dskip, early, cpart, dy, zs, xt, bc, cum, step, skip, dt, per_head,
     x, hx, wx, b, hb, wb,
     xown, heads, keep, give, packed, ddt, parts, later, ext, extb, pad, padb,
 ):
@@ -268,9 +269,9 @@
         for k in range(CONV):
             packed[k * GROUPS + g : k * GROUPS + g + 1, :] = taps[k]
     dlog = dot(jnp.concatenate(turned, axis=0), jnp.where(triangle(False), 1.0, 0.0))
-    rate = -jnp.exp(alog[...])
+    rate = -jnp.exp(per_head[:, 1:2])
     dstep = jnp.concatenate(straight, axis=0) * gamma + dlog * rate
-    draw = dstep * sigmoid(dt[...] + bias[...])
+    draw = dstep * sigmoid(dt[...] + per_head[:, 0:1])
     ddt[...] = draw
     each = jnp.concatenate([draw, dlog * rate * step[...], dskip[...], jnp.zeros((LOCAL, SPAN), F32)], axis=0)
     at = lax.broadcasted_iota(jnp.int32, (SPAN, SPAN), 0)
@@ -279,7 +280,7 @@
     packed[72:80, :] = dot(dot(jnp.ones((8, SPAN), F32), each, 1, 1), jnp.where(at == source, 1.0, 0.0))
     packed[16:32, :] = early[0:16, :]
     packed[64:72, :] = early[16:24, :]
-    side = core[1]
+    side = which[0]
     keep[...] = parts[pl.ds(side * 2, 2)]
     give[...] = parts[pl.ds((1 - side) * 2, 2)]
     for r in range(PER):
@@ -345,8 +346,8 @@
             half[g, stop - LEAD : stop, :] = (mine[g, stop - LEAD : stop, :] + more).astype(jnp.bfloat16)
 
 
-def finish_kernel(core, half, other, bc_taps, packed, gb, gc, tx, tb, tc, tgain, bias, rate, skip):
-    left = core[1] == 0
+def finish_kernel(which, half, other, bc_taps, packed, gb, gc, tx, tb, tc, tgain, bias, rate, skip):
+    left = which[0] == 0
     for g in range(GROUPS):
         first, second = (half, other) if g < 2 else (other, half)
         both = jnp.where(left, first[g % 2].astype(F32), second[g % 2].astype(F32)).astype(jnp.bfloat16)
@@ -408,29 +409,16 @@
     return x + lax.ppermute(x, axis, [(i, partner(i)) for i in range(lax.axis_size(axis))])
 
 
-def mirror(within, block=1):
-    return lambda i: (i // block // within * within + within - 1 - i // block % within) * block + i % block
-
-
-def sum_steps(axis):
-    size = lax.axis_size(axis)
-    ring = min(RING, size)
-    steps, within = [], 2
-    while within <= ring:
-        half = within // 2
-        steps.append(mirror(within) if within in (2, ring) else (lambda i, half=half: i ^ half))
-        within *= 2
-    within = 2
-    while within * ring <= size:
-        steps.append(mirror(within, ring))
-        within *= 2
-    return steps
-
-
-def sum_over(x, axis):
-    for partner in sum_steps(axis):
-        x = fold(x, axis, partner)
-    return x
+def sum_four(x, axis, block=1):
+    near, far, last = (
+        lax.ppermute(x, axis, [(i, (i // block ^ k) * block + i % block) for i in range(lax.axis_size(axis))])
+        for k in range(1, 4)
+    )
+    return (x + near) + (far + last)
+
+
+def mirror(within):
+    return lambda i: i // within * within + within - 1 - i % within
 
 
 def by_group(v):
@@ -447,7 +435,7 @@
     size = lax.axis_size(CTX)
     core = lax.axis_index("core")
     side = lax.axis_index("tp") // (lax.axis_size("tp") // 2)
-    cores = jnp.stack([core, side])
+    cores, sides = lax.optimization_barrier((core.reshape(1), side.reshape(1)))
     is_even = core == 0
     t_shape = ((ALL, SPAN), F32)
     bc_shape = ((SPAN, GROUPS * STATE), F32)
@@ -458,9 +446,8 @@
     hx, hb, hc = before[:, :wx], before[:, wx : wx + wb], before[:, wx + wb :]
 
     dt = by_group(dt_raw.T)
-    bias, alog, skip_col = (by_group(v)[:, None] for v in (dt_bias, a_log, d_skip))
-    skip = jnp.broadcast_to(skip_col, h_shape[0])
-    step, cum, ends = call(steps_kernel, "steps", [h_shape] * 3, (dt, bias, alog))
+    per_head = by_group(jnp.stack([dt_bias, a_log, d_skip], axis=1))
+    step, cum, ends, skip = call(steps_kernel, "steps", [h_shape] * 4, (dt, per_head))
     zt, ogt, sgt = call(turn_kernel, "turn", [t_shape] * 3, (z_gate, grad_out, gain[None]))
     xt, zs, bc, keep, give = call(
         state_kernel,
@@ -504,7 +491,7 @@
         (cores, enter_own, enter_got, cc, y1, cum, zt, sgt),
         scalars=1,
     )
-    sums = sum_over(sums, "tp")
+    sums = sum_four(sums, "tp")
     keep, give, dy, dg = call(
         gate_kernel,
         "gate",
@@ -537,30 +524,29 @@
         last_kernel,
         "last",
         [((SPAN, wx), F32), ((64, TILE), F32), half_parts, half_parts, ((80, TILE), F32), h_shape],
-        (cores, later_own, later_got, enter, ends, dz, db, dcum, dskip, early, cpart)
-        + (dy, zs, xt, bc, cum, step, skip, dt, bias, alog, x_raw, hx, conv_x, b_raw, hb, conv_b),
+        (cores, sides, later_own, later_got, enter, ends, dz, db, dcum, dskip, early, cpart)
+        + (dy, zs, xt, bc, cum, step, skip, dt, per_head, x_raw, hx, conv_x, b_raw, hb, conv_b),
         [(GROUPS, 2 * SPAN + 16, TILE), (ALL, STATE)]
         + [(LEAD + SPAN, wx), (LEAD + SPAN, wb), (LEAD + SPAN, wx), (LEAD + SPAN, wb)],
-        scalars=1,
+        scalars=2,
     )
     peers = lax.axis_size("tp")
     across = [(i, peers - 1 - i) for i in range(peers)]
     arrived = lax.ppermute(give, "tp", across)
     packed = packed + swap_cores(packed)
-    steps = sum_steps("chip")
+    steps = (mirror(2), lambda i: i ^ 2, mirror(RING))
     packed = fold(packed, "chip", steps[0])
     arrived, packed = lax.optimization_barrier((arrived, packed))
     mine = keep + arrived
     arrived = lax.ppermute(mine, "tp", [(i, i ^ 1) for i in range(peers)])
-    for partner in steps[1:3]:
-        packed = fold(packed, "chip", partner)
+    packed = fold(packed, "chip", steps[1])
     arrived, packed = lax.optimization_barrier((arrived, packed))
     mine = mine + arrived
     heads = jnp.concatenate([xheads, mine[:, 2 * SPAN :].reshape(32, TILE)], axis=0)
     heads = lax.ppermute(heads, CTX, [(i + 1, i) for i in range(size - 1)])
-    for partner in steps[3:4]:
-        packed = fold(packed, "chip", partner)
+    packed = fold(packed, "chip", steps[2])
     heads, packed = lax.optimization_barrier((heads, packed))
+    packed = sum_four(packed, "chip", RING)
     grad_x_raw, half = call(
         settle_kernel,
         "settle",
@@ -568,15 +554,13 @@
         (xown, mine, heads),
     )
     other = lax.ppermute(half, "tp", across)
-    for partner in steps[4:]:
-        packed = fold(packed, "chip", partner)
-    bc_taps = sum_over(packed[:32], "tp")
+    bc_taps = sum_four(packed[:32], "tp")
     half_bc, each = ((SPAN, wb), jnp.bfloat16), ((1, LOCAL), F32)
     grad_b_raw, grad_c_raw, conv_x_total, conv_b_total, conv_c_total, gain_total, *small = call(
         finish_kernel,
         "finish",
         [half_bc, half_bc, ((CONV, wx), F32), ((CONV, wb), F32), ((CONV, wb), F32), ((1, wx), F32)] + [each] * 3,
-        (cores, half, other, bc_taps, packed),
+        (sides, half, other, bc_taps, packed),
         scalars=1,
     )
     return (

time: 160 us -> 156 us (0.975)
  Pallas kernels: 19.3 us -> 14.6 us
    ppermute x9 -> x3, waiting for transfers between devices: 27.8 us -> 13.1 us  [fold(): lax.ppermute(x, axis, [(i, partner(i)) for i in range(lax.axis_size(axis))])]
    ppermute x0 -> x9, starting transfers between devices: none -> 11.5 us  [sum_four(): lax.ppermute(x, axis, [(i, (i // block ^ k) * block + i % block) for i in...]
    ppermute x9 -> x3, starting transfers between devices: 12.6 us -> 2.95 us  [fold(): lax.ppermute(x, axis, [(i, partner(i)) for i in range(lax.axis_size(axis))])]
    ppermute x0 -> x9, waiting for transfers between devices: none -> 7.57 us  [sum_four(): lax.ppermute(x, axis, [(i, (i // block ^ k) * block + i % block) for i in...]
    pallas_call x16, Pallas kernels: 19.3 us -> 14.6 us  [call(): pl.pallas_call(kernel, out_shape=[jax.ShapeDtypeStruct(s, d) for s, d in...]
    ppermute x1, waiting for transfers between devices: 0.01 us -> 4.13 us  [body(): other = lax.ppermute(half, 'tp', across)]
    ppermute x1, waiting for transfers between devices: 0.01 us -> 3.26 us  [body(): arrived = lax.ppermute(mine, 'tp', [(i, i ^ 1) for i in range(peers)])]
  transfers between devices with their start and end apart: 19 -> 22, of which waited for: 13 -> 15; matrix products, arithmetic and copies ran while one was open for 1% -> 1% of each run, Pallas kernels for 4% -> 5%
where the time goes in v3:
time: 156 us; the launch traced here: 155 us
  blocking collectives  72.9 us (47%)
  waiting for transfers between devices  35.3 us (23%)
  starting transfers between devices  25.3 us (16%)
  Pallas kernels  14.6 us (9%)
  local copies, waits for them, and re-layouts  6.25 us (4%)
    all_to_all x4, blocking collectives, over_chips(): return lax.all_to_all(v, 'chip', 0, 0)  72.9 us
    pallas_call x16, Pallas kernels, call(): pl.pallas_call(kernel, out_shape=[jax.ShapeDtypeStruct(s, d) for s, d in...  14.6 us
    ppermute x3, waiting for transfers between devices, fold(): lax.ppermute(x, axis, [(i, partner(i)) for i in range(lax.axis_size(axis))])  13.1 us
    ppermute x9, starting transfers between devices, sum_four(): lax.ppermute(x, axis, [(i, (i // block ^ k) * block + i % block) for i in...  11.5 us
    ppermute x9, waiting for transfers between devices, sum_four(): lax.ppermute(x, axis, [(i, (i // block ^ k) * block + i % block) for i in...  7.57 us
    unnamed x26, local copies, waits for them, and re-layouts  4.52 us
    ppermute x1, waiting for transfers between devices, body(): other = lax.ppermute(half, 'tp', across)  4.13 us
    ppermute x5, waiting for transfers between devices, swap_cores(): return lax.ppermute(v, 'core', [(0, 1), (1, 0)])  3.73 us
  transfers between devices with their start and end apart: 22, of which 15 were waited for; matrix products, arithmetic and copies ran while one was open for 1% of the time, Pallas kernels for 5%

profile of v3, /device:TPU:32, one launch (start us, length us, event | category | flops | bytes accessed | tf_op | source)
XLA Modules:
  0.0 155.3 jit_solution(9912876351750306277)
XLA Ops:
  0.7 0.7 slice-done
  1.4 1.9 %collective-permute-start = (bf16[16,2048]{1,0:T(8,128)(2,1)S(1)}, bf16[16,2048]{1,0:T(8,128)(2,1)S(1)}, u32[]{:S(2)}, u32[]{:S(2)}) collective-permute-start(bf16[16,2048]{1,0:T(8,128)(2,1)S(1)} %pad_maximum_fusion), channel_id=1, source_target_pairs={{0,4},{4,8},{8,12},{12,16},{16,20},{20,24},{24,28},{28,32},{32,36}... | collective-permute-start | bytes 196616 | tf_op jit(solution)/shard_map/ppermute | solution.py:444
  3.4 0.7 copy-done.9
  4.1 0.7 copy-done.10
  4.8 0.6 copy-done.11
  5.5 0.6 copy-done.12
  6.1 0.1 copy.35
  6.3 0.2 steps.1
  6.5 0.5 collective-permute-done
  7.0 0.2 copy-done
  7.2 0.2 copy-done.2
  7.5 1.2 state.1
  8.7 2.1 %collective-permute-start.1 = (f32[544,128]{1,0:T(8,128)S(1)}, f32[544,128]{1,0:T(8,128)S(1)}, u32[]{:S(2)}, u32[]{:S(2)}) collective-permute-start(f32[544,128]{1,0:T(8,128)S(1)} %get-tuple-element.78), channel_id=1, source_target_pairs={{0,4},{4,0},{1,5},{5,1},{2,6},{6,2},{3,7},{7,3},{8,12},{12,8},{9,1... | collective-permute-start | bytes 835592 | tf_op jit(solution)/shard_map/ppermute | solution.py:397
  10.8 1.2 collective-permute-done.1.got
  12.0 0.2 join.2
  12.2 23.2 %all_to_all.20.s.d = f32[32,1,2176]{2,1,0:T(1,128)S(1)} all-to-all(f32[32,1,2176]{2,1,0:T(1,128)S(1)} %get-tuple-element.79), channel_id=1, replica_groups=mesh['chip'=32,'core'=2,'tp'=4] {'chip'}, dimensions={0} | all-to-all | bytes 557056 | tf_op jit(solution)/shard_map/all_to_all | solution.py:405
  35.4 0.2 block_scan.2
  35.6 16.5 %all_to_all.21 = f32[32,1,2048]{2,1,0:T(1,128)S(1)} all-to-all(f32[32,1,2048]{2,1,0:T(1,128)S(1)} %block_scan.2), channel_id=1, replica_groups=mesh['chip'=32,'core'=2,'tp'=4] {'chip'}, dimensions={0} | all-to-all | bytes 524288 | tf_op jit(solution)/shard_map/all_to_all | solution.py:405
  52.2 0.1 collective-permute-start.2
  52.3 0.8 copy-done.3
  53.1 0.3 turn.1
  53.5 0.5 copy-done.1
  54.0 0.2 copy-done.6
  54.2 2.2 %local.1 = (f32[128,512]{1,0:T(8,128)S(1)}, f32[512,128]{1,0:T(8,128)S(1)}, f32[1024,128]{1,0:T(8,128)S(1)}) custom-call(bf16[128,512]{1,0:T(8,128)(2,1)S(1)} %copy-done.1, bf16[16,512]{1,0:T(8,128)(2,1)S(1)} %get-tuple-element.132.hc, f32[4,512]{1,0:T(4,128)S(1)} %copy-done.6, f32[128,512]{1,0:T(8,128)S(1)} %get-tuple-element.83.bc, ...), custom_call_target="tpu_custom_call" | custom-call | flops 20000000 | bytes 4194304 | tf_op jit(solution)/shard_map/local/pallas_call | solution.py:384
  56.5 0.8 output.1
  57.2 3.3 %collective-permute-start.4 = (f32[8,128]{1,0:T(8,128)S(1)}, f32[8,128]{1,0:T(8,128)S(1)}, u32[]{:S(2)}, u32[]{:S(2)}) collective-permute-start(f32[8,128]{1,0:T(8,128)S(1)} %get-tuple-element.91), channel_id=1, source_target_pairs={{0,2},{1,3},{2,0},{3,1},{4,6},{5,7},{6,4},{7,5},{8,10},{9,11},{10,... | collective-permute-start | bytes 12296 | tf_op jit(solution)/shard_map/ppermute | solution.py:414
  60.5 1.1 collective-permute-start.5
  61.6 0.9 collective-permute-done.4
  62.4 2.9 %collective-permute-done.5 = f32[8,128]{1,0:T(8,128)S(1)} collective-permute-done((f32[8,128]{1,0:T(8,128)S(1)}, f32[8,128]{1,0:T(8,128)S(1)}, u32[]{:S(2)}, u32[]{:S(2)}) %collective-permute-start.5) | collective-permute-done | bytes 4128 | tf_op jit(solution)/shard_map/ppermute | solution.py:414
  65.3 0.9 gate.1
  66.2 0.1 collective-permute-start.6
  66.3 1.5 collective-permute-done.6.got
  67.9 16.9 %all_to_all.22.s = f32[32,1,2048]{2,1,0:T(1,128)S(1)} all-to-all(f32[32,1,2048]{2,1,0:T(1,128)S(1)} %bitcast.30), channel_id=1, replica_groups=mesh['chip'=32,'core'=2,'tp'=4] {'chip'}, dimensions={0} | all-to-all | bytes 524288 | tf_op jit(solution)/shard_map/all_to_all | solution.py:405
  84.9 0.2 block_scan.3
  85.0 16.2 %all_to_all.23 = f32[32,1,2048]{2,1,0:T(1,128)S(1)} all-to-all(f32[32,1,2048]{2,1,0:T(1,128)S(1)} %block_scan.3), channel_id=1, replica_groups=mesh['chip'=32,'core'=2,'tp'=4] {'chip'}, dimensions={0} | all-to-all | bytes 524288 | tf_op jit(solution)/shard_map/all_to_all | solution.py:405
  101.3 0.3 collective-permute-start.7
  101.6 3.4 %middle.1 = (f32[1024,128]{1,0:T(8,128)S(1)}, f32[128,512]{1,0:T(8,128)S(1)}, f32[32,128]{1,0:T(8,128)S(1)}, f32[32,128]{1,0:T(8,128)S(1)}, bf16[128,1024]{1,0:T...) custom-call(f32[8,128]{1,0:T(8,128)S(1)} %add_add_fusion.2.sums, f32[1024,128]{1,0:T(8,128)S(1)} %get-tuple-element.92.y, ...), custom_call_target="tpu_custom_call" | custom-call | flops 20000000 | bytes 4194304 | tf_op jit(solution)/shard_map/middle/pallas_call | solution.py:384
  105.0 3.2 %last.1 = (f32[128,1024]{1,0:T(8,128)S(1)}, f32[64,128]{1,0:T(8,128)S(1)}, f32[2,272,128]{2,1,0:T(8,128)S(1)}, f32[2,272,128]{2,1,0:T(8,128)S(1)}, f32[80,128]{1,0:T(8,128)S(1)}, /*index=5*/f32[32,128]{1,0:T(8,128)S(1)}) custom-call(s32[1]{0:T(128)} %bitcast.core, s32[1]{0:T(128)} %bitcast.1.which, f32[512,128]{1,0:T(8,128)S(1)} %get-tuple-element.95.own, ...), custom_call_target="tpu_custom_call" | custom-call | flops 20000000 | bytes 4194304 | tf_op jit(solution)/shard_map/last/pallas_call | solution.py:384
  108.2 2.1 %collective-permute-start.8 = (f32[2,272,128]{2,1,0:T(8,128)S(1)}, f32[2,272,128]{2,1,0:T(8,128)S(1)}, u32[]{:S(2)}, u32[]{:S(2)}) collective-permute-start(f32[2,272,128]{2,1,0:T(8,128)S(1)} %get-tuple-element.110), channel_id=1, source_target_pairs={{0,3},{1,2},{2,1},{3,0},{4,7},{5,6},{6,5},{7,4},{8,11},{9,10},{10,... | collective-permute-start | bytes 835592 | tf_op jit(solution)/shard_map/ppermute | solution.py:535
  110.3 0.2 collective-permute-start.9
  110.5 1.0 collective-permute-done.9
  111.5 0.2 collective-permute-start.10
  111.8 3.8 %collective-permute-done.10 = f32[80,128]{1,0:T(8,128)S(1)} collective-permute-done((f32[80,128]{1,0:T(8,128)S(1)}, f32[80,128]{1,0:T(8,128)S(1)}, u32[]{:S(2)}, u32[]{:S(2)}) %collective-permute-start.10) | collective-permute-done | bytes 40992 | tf_op jit(solution)/shard_map/ppermute | solution.py:409
  115.5 3.0 %collective-permute-done.8 = f32[2,272,128]{2,1,0:T(8,128)S(1)} collective-permute-done((f32[2,272,128]{2,1,0:T(8,128)S(1)}, f32[2,272,128]{2,1,0:T(8,128)S(1)}, u32[]{:S(2)}, u32[]{:S(2)}) %collective-permute-start.8) | collective-permute-done | bytes 278560 | tf_op jit(solution)/shard_map/ppermute | solution.py:535
  118.7 1.0 collective-permute-start.12
  119.7 4.0 %collective-permute-done.12 = f32[80,128]{1,0:T(8,128)S(1)} collective-permute-done((f32[80,128]{1,0:T(8,128)S(1)}, f32[80,128]{1,0:T(8,128)S(1)}, u32[]{:S(2)}, u32[]{:S(2)}) %collective-permute-start.12) | collective-permute-done | bytes 40992 | tf_op jit(solution)/shard_map/ppermute | solution.py:409
  123.7 3.3 %collective-permute-done.11 = f32[2,272,128]{2,1,0:T(8,128)S(1)} collective-permute-done((f32[2,272,128]{2,1,0:T(8,128)S(1)}, f32[2,272,128]{2,1,0:T(8,128)S(1)}, u32[]{:S(2)}, u32[]{:S(2)}) %collective-permute-start.11) | collective-permute-done | bytes 278560 | tf_op jit(solution)/shard_map/ppermute | solution.py:541
  127.0 1.9 %collective-permute-start.13 = (f32[96,128]{1,0:T(8,128)S(1)}, f32[96,128]{1,0:T(8,128)S(1)}, u32[]{:S(2)}, u32[]{:S(2)}) collective-permute-start(f32[96,128]{1,0:T(8,128)S(1)} %pad_maximum_fusion.1), channel_id=1, source_target_pairs={{4,0},{8,4},{12,8},{16,12},{20,16},{24,20},{28,24},{32,28},{36,32}... | collective-permute-start | bytes 147464 | tf_op jit(solution)/shard_map/ppermute | solution.py:546
  128.9 1.7 %collective-permute-start.14 = (f32[80,128]{1,0:T(8,128)S(1)}, f32[80,128]{1,0:T(8,128)S(1)}, u32[]{:S(2)}, u32[]{:S(2)}) collective-permute-start(f32[80,128]{1,0:T(8,128)S(1)} %add.52), channel_id=1, source_target_pairs={{0,56},{8,48},{16,40},{24,32},{32,24},{40,16},{48,8},{56,0},{64,12... | collective-permute-start | bytes 122888 | tf_op jit(solution)/shard_map/ppermute | solution.py:409
  130.6 5.4 %collective-permute-done.14 = f32[80,128]{1,0:T(8,128)S(1)} collective-permute-done((f32[80,128]{1,0:T(8,128)S(1)}, f32[80,128]{1,0:T(8,128)S(1)}, u32[]{:S(2)}, u32[]{:S(2)}) %collective-permute-start.14) | collective-permute-done | bytes 40992 | tf_op jit(solution)/shard_map/ppermute | solution.py:409
  136.0 1.4 collective-permute-start.17
  137.4 2.0 %collective-permute-start.18 = (f32[80,128]{1,0:T(8,128)S(1)}, f32[80,128]{1,0:T(8,128)S(1)}, u32[]{:S(2)}, u32[]{:S(2)}) collective-permute-start(f32[80,128]{1,0:T(8,128)S(1)} %add.54), channel_id=1, source_target_pairs={{0,192},{8,200},{16,208},{24,216},{32,224},{40,232},{48,240},{56,2... | collective-permute-start | bytes 122888 | tf_op jit(solution)/shard_map/ppermute | solution.py:414
  139.4 0.2 collective-permute-start.16
  139.6 2.2 %collective-permute-done.17 = f32[80,128]{1,0:T(8,128)S(1)} collective-permute-done((f32[80,128]{1,0:T(8,128)S(1)}, f32[80,128]{1,0:T(8,128)S(1)}, u32[]{:S(2)}, u32[]{:S(2)}) %collective-permute-start.17) | collective-permute-done | bytes 40992 | tf_op jit(solution)/shard_map/ppermute | solution.py:414
  141.8 0.9 collective-permute-done.18
  142.6 0.8 collective-permute-done.16
  143.4 1.8 %collective-permute-start.20 = (f32[32,128]{1,0:T(8,128)S(1)}, f32[32,128]{1,0:T(8,128)S(1)}, u32[]{:S(2)}, u32[]{:S(2)}) collective-permute-start(f32[32,128]{1,0:T(8,128)S(1)} %slice.36), channel_id=1, source_target_pairs={{0,2},{1,3},{2,0},{3,1},{4,6},{5,7},{6,4},{7,5},{8,10},{9,11},{10,... | collective-permute-start | bytes 49160 | tf_op jit(solution)/shard_map/ppermute | solution.py:414
  145.3 1.2 collective-permute-start.21
  146.5 0.5 collective-permute-start.19
  147.0 0.6 copy.34
  147.6 0.8 settle.1
  148.4 2.0 %collective-permute-start.15 = (bf16[2,256,128]{2,1,0:T(8,128)(2,1)S(1)}, bf16[2,256,128]{2,1,0:T(8,128)(2,1)S(1)}, u32[]{:S(2)}, u32[]{:S(2)}) collective-permute-start(bf16[2,256,128]{2,1,0:T(8,128)(2,1)S(1)} %get-tuple-element.119.half), channel_id=1, source_target_pairs={{0,3},{1,2},{2,1},{3,0},{4,7},{5,6},{6,5},{7,4},{8,11},{9,10},{10,... | collective-permute-start | bytes 393224 | tf_op jit(solution)/shard_map/ppermute | solution.py:556
  150.4 4.1 %collective-permute-done.15.other = bf16[2,256,128]{2,1,0:T(8,128)(2,1)S(1)} collective-permute-done((bf16[2,256,128]{2,1,0:T(8,128)(2,1)S(1)}, bf16[2,256,128]{2,1,0:T(8,128)(2,1)S(1)}, u32[]{:S(2)}, u32[]{:S(2)}) %collective-permute-start.15) | collective-permute-done | bytes 131104 | tf_op jit(solution)/shard_map/ppermute | solution.py:556
  154.6 0.8 finish.1
  (54 shorter events, 0.8 us)
Async XLA Ops:
  0.6 0.8 slice-start
  0.7 0.8 slice-start.1
  0.7 0.7 slice-start.2
  1.4 5.6 %collective-permute-start = (bf16[16,2048]{1,0:T(8,128)(2,1)S(1)}, bf16[16,2048]{1,0:T(8,128)(2,1)S(1)}, u32[]{:S(2)}, u32[]{:S(2)}) collective-permute-start(bf16[16,2048]{1,0:T(8,128)(2,1)S(1)} %pad_maximum_fusion), channel_id=1, source_target_pairs={{0,4},{4,8},{8,12},{12,16},{16,20},{20,24},{24,28},{28,32},{32,36}... | collective-permute-start | bytes 196616 | tf_op jit(solution)/shard_map/ppermute | solution.py:444
  3.4 0.7 copy-start.9
  4.1 0.7 copy-start.10
  4.7 0.7 copy-start.11
  5.4 0.7 copy-start.12
  6.3 1.0 copy-start
  6.3 1.0 copy-start.5
  6.3 1.0 copy-start.7
  6.5 0.9 copy-start.2
  8.7 3.3 %collective-permute-start.1 = (f32[544,128]{1,0:T(8,128)S(1)}, f32[544,128]{1,0:T(8,128)S(1)}, u32[]{:S(2)}, u32[]{:S(2)}) collective-permute-start(f32[544,128]{1,0:T(8,128)S(1)} %get-tuple-element.78), channel_id=1, source_target_pairs={{0,4},{4,0},{1,5},{5,1},{2,6},{6,2},{3,7},{7,3},{8,12},{12,8},{9,1... | collective-permute-start | bytes 835592 | tf_op jit(solution)/shard_map/ppermute | solution.py:397
  52.1 1.0 copy-start.3
  52.1 1.0 copy-start.4
  52.1 1.0 copy-start.8
  52.2 4.3 %collective-permute-start.2 = (f32[512,128]{1,0:T(8,128)S(1)}, f32[512,128]{1,0:T(8,128)S(1)}, u32[]{:S(2)}, u32[]{:S(2)}) collective-permute-start(f32[512,128]{1,0:T(8,128)S(1)} %get-tuple-element.82), channel_id=1, source_target_pairs={{0,4},{4,0},{1,5},{5,1},{2,6},{6,2},{3,7},{7,3},{8,12},{12,8},{9,1... | collective-permute-start | bytes 786440 | tf_op jit(solution)/shard_map/ppermute | solution.py:397
  53.1 0.9 copy-start.1
  53.5 0.7 copy-start.6
  57.2 5.2 %collective-permute-start.4 = (f32[8,128]{1,0:T(8,128)S(1)}, f32[8,128]{1,0:T(8,128)S(1)}, u32[]{:S(2)}, u32[]{:S(2)}) collective-permute-start(f32[8,128]{1,0:T(8,128)S(1)} %get-tuple-element.91), channel_id=1, source_target_pairs={{0,2},{1,3},{2,0},{3,1},{4,6},{5,7},{6,4},{7,5},{8,10},{9,11},{10,... | collective-permute-start | bytes 12296 | tf_op jit(solution)/shard_map/ppermute | solution.py:414
  60.5 4.8 %collective-permute-start.5 = (f32[8,128]{1,0:T(8,128)S(1)}, f32[8,128]{1,0:T(8,128)S(1)}, u32[]{:S(2)}, u32[]{:S(2)}) collective-permute-start(f32[8,128]{1,0:T(8,128)S(1)} %get-tuple-element.91), channel_id=1, source_target_pairs={{0,3},{1,2},{2,1},{3,0},{4,7},{5,6},{6,5},{7,4},{8,11},{9,10},{10,... | collective-permute-start | bytes 12296 | tf_op jit(solution)/shard_map/ppermute | solution.py:414
  61.6 3.8 %collective-permute-start.3 = (f32[8,128]{1,0:T(8,128)S(1)}, f32[8,128]{1,0:T(8,128)S(1)}, u32[]{:S(2)}, u32[]{:S(2)}) collective-permute-start(f32[8,128]{1,0:T(8,128)S(1)} %get-tuple-element.91), channel_id=1, source_target_pairs={{0,1},{1,0},{2,3},{3,2},{4,5},{5,4},{6,7},{7,6},{8,9},{9,8},{10,11... | collective-permute-start | bytes 12296 | tf_op jit(solution)/shard_map/ppermute | solution.py:414
  66.2 1.6 %collective-permute-start.6 = (f32[512,128]{1,0:T(8,128)S(1)}, f32[512,128]{1,0:T(8,128)S(1)}, u32[]{:S(2)}, u32[]{:S(2)}) collective-permute-start(f32[512,128]{1,0:T(8,128)S(1)} %get-tuple-element.94), channel_id=1, source_target_pairs={{0,4},{4,0},{1,5},{5,1},{2,6},{6,2},{3,7},{7,3},{8,12},{12,8},{9,1... | collective-permute-start | bytes 786440 | tf_op jit(solution)/shard_map/ppermute | solution.py:397
  101.3 3.7 %collective-permute-start.7 = (f32[512,128]{1,0:T(8,128)S(1)}, f32[512,128]{1,0:T(8,128)S(1)}, u32[]{:S(2)}, u32[]{:S(2)}) collective-permute-start(f32[512,128]{1,0:T(8,128)S(1)} %get-tuple-element.96), channel_id=1, source_target_pairs={{0,4},{4,0},{1,5},{5,1},{2,6},{6,2},{3,7},{7,3},{8,12},{12,8},{9,1... | collective-permute-start | bytes 786440 | tf_op jit(solution)/shard_map/ppermute | solution.py:397
  108.2 10.3 %collective-permute-start.8 = (f32[2,272,128]{2,1,0:T(8,128)S(1)}, f32[2,272,128]{2,1,0:T(8,128)S(1)}, u32[]{:S(2)}, u32[]{:S(2)}) collective-permute-start(f32[2,272,128]{2,1,0:T(8,128)S(1)} %get-tuple-element.110), channel_id=1, source_target_pairs={{0,3},{1,2},{2,1},{3,0},{4,7},{5,6},{6,5},{7,4},{8,11},{9,10},{10,... | collective-permute-start | bytes 835592 | tf_op jit(solution)/shard_map/ppermute | solution.py:535
  110.3 1.2 collective-permute-start.9
  111.5 4.0 %collective-permute-start.10 = (f32[80,128]{1,0:T(8,128)S(1)}, f32[80,128]{1,0:T(8,128)S(1)}, u32[]{:S(2)}, u32[]{:S(2)}) collective-permute-start(f32[80,128]{1,0:T(8,128)S(1)} %add.49), channel_id=1, source_target_pairs={{0,8},{8,0},{16,24},{24,16},{32,40},{40,32},{48,56},{56,48},{64,72... | collective-permute-start | bytes 122888 | tf_op jit(solution)/shard_map/ppermute | solution.py:409
  118.6 8.4 %collective-permute-start.11 = (f32[2,272,128]{2,1,0:T(8,128)S(1)}, f32[2,272,128]{2,1,0:T(8,128)S(1)}, u32[]{:S(2)}, u32[]{:S(2)}) collective-permute-start(f32[2,272,128]{2,1,0:T(8,128)S(1)} %add.51), channel_id=1, source_target_pairs={{0,1},{1,0},{2,3},{3,2},{4,5},{5,4},{6,7},{7,6},{8,9},{9,8},{10,11... | collective-permute-start | bytes 835592 | tf_op jit(solution)/shard_map/ppermute | solution.py:541
  118.7 5.0 %collective-permute-start.12 = (f32[80,128]{1,0:T(8,128)S(1)}, f32[80,128]{1,0:T(8,128)S(1)}, u32[]{:S(2)}, u32[]{:S(2)}) collective-permute-start(f32[80,128]{1,0:T(8,128)S(1)} %add.50), channel_id=1, source_target_pairs={{0,16},{8,24},{16,0},{24,8},{32,48},{40,56},{48,32},{56,40},{64,80... | collective-permute-start | bytes 122888 | tf_op jit(solution)/shard_map/ppermute | solution.py:409
  127.0 9.0 %collective-permute-start.13 = (f32[96,128]{1,0:T(8,128)S(1)}, f32[96,128]{1,0:T(8,128)S(1)}, u32[]{:S(2)}, u32[]{:S(2)}) collective-permute-start(f32[96,128]{1,0:T(8,128)S(1)} %pad_maximum_fusion.1), channel_id=1, source_target_pairs={{4,0},{8,4},{12,8},{16,12},{20,16},{24,20},{28,24},{32,28},{36,32}... | collective-permute-start | bytes 147464 | tf_op jit(solution)/shard_map/ppermute | solution.py:546
  128.9 7.1 %collective-permute-start.14 = (f32[80,128]{1,0:T(8,128)S(1)}, f32[80,128]{1,0:T(8,128)S(1)}, u32[]{:S(2)}, u32[]{:S(2)}) collective-permute-start(f32[80,128]{1,0:T(8,128)S(1)} %add.52), channel_id=1, source_target_pairs={{0,56},{8,48},{16,40},{24,32},{32,24},{40,16},{48,8},{56,0},{64,12... | collective-permute-start | bytes 122888 | tf_op jit(solution)/shard_map/ppermute | solution.py:409
  136.0 5.7 %collective-permute-start.17 = (f32[80,128]{1,0:T(8,128)S(1)}, f32[80,128]{1,0:T(8,128)S(1)}, u32[]{:S(2)}, u32[]{:S(2)}) collective-permute-start(f32[80,128]{1,0:T(8,128)S(1)} %add.54), channel_id=1, source_target_pairs={{0,128},{8,136},{16,144},{24,152},{32,160},{40,168},{48,176},{56,1... | collective-permute-start | bytes 122888 | tf_op jit(solution)/shard_map/ppermute | solution.py:414
  137.4 5.2 %collective-permute-start.18 = (f32[80,128]{1,0:T(8,128)S(1)}, f32[80,128]{1,0:T(8,128)S(1)}, u32[]{:S(2)}, u32[]{:S(2)}) collective-permute-start(f32[80,128]{1,0:T(8,128)S(1)} %add.54), channel_id=1, source_target_pairs={{0,192},{8,200},{16,208},{24,216},{32,224},{40,232},{48,240},{56,2... | collective-permute-start | bytes 122888 | tf_op jit(solution)/shard_map/ppermute | solution.py:414
  139.4 4.0 %collective-permute-start.16 = (f32[80,128]{1,0:T(8,128)S(1)}, f32[80,128]{1,0:T(8,128)S(1)}, u32[]{:S(2)}, u32[]{:S(2)}) collective-permute-start(f32[80,128]{1,0:T(8,128)S(1)} %add.54), channel_id=1, source_target_pairs={{0,64},{8,72},{16,80},{24,88},{32,96},{40,104},{48,112},{56,120},{... | collective-permute-start | bytes 122888 | tf_op jit(solution)/shard_map/ppermute | solution.py:414
  143.4 7.0 %collective-permute-start.20 = (f32[32,128]{1,0:T(8,128)S(1)}, f32[32,128]{1,0:T(8,128)S(1)}, u32[]{:S(2)}, u32[]{:S(2)}) collective-permute-start(f32[32,128]{1,0:T(8,128)S(1)} %slice.36), channel_id=1, source_target_pairs={{0,2},{1,3},{2,0},{3,1},{4,6},{5,7},{6,4},{7,5},{8,10},{9,11},{10,... | collective-permute-start | bytes 49160 | tf_op jit(solution)/shard_map/ppermute | solution.py:414
  145.3 5.1 %collective-permute-start.21 = (f32[32,128]{1,0:T(8,128)S(1)}, f32[32,128]{1,0:T(8,128)S(1)}, u32[]{:S(2)}, u32[]{:S(2)}) collective-permute-start(f32[32,128]{1,0:T(8,128)S(1)} %slice.36), channel_id=1, source_target_pairs={{0,3},{1,2},{2,1},{3,0},{4,7},{5,6},{6,5},{7,4},{8,11},{9,10},{10,... | collective-permute-start | bytes 49160 | tf_op jit(solution)/shard_map/ppermute | solution.py:414
  146.5 3.9 %collective-permute-start.19 = (f32[32,128]{1,0:T(8,128)S(1)}, f32[32,128]{1,0:T(8,128)S(1)}, u32[]{:S(2)}, u32[]{:S(2)}) collective-permute-start(f32[32,128]{1,0:T(8,128)S(1)} %slice.36), channel_id=1, source_target_pairs={{0,1},{1,0},{2,3},{3,2},{4,5},{5,4},{6,7},{7,6},{8,9},{9,8},{10,11... | collective-permute-start | bytes 49160 | tf_op jit(solution)/shard_map/ppermute | solution.py:414
  148.4 6.2 %collective-permute-start.15 = (bf16[2,256,128]{2,1,0:T(8,128)(2,1)S(1)}, bf16[2,256,128]{2,1,0:T(8,128)(2,1)S(1)}, u32[]{:S(2)}, u32[]{:S(2)}) collective-permute-start(bf16[2,256,128]{2,1,0:T(8,128)(2,1)S(1)} %get-tuple-element.119.half), channel_id=1, source_target_pairs={{0,3},{1,2},{2,1},{3,0},{4,7},{5,6},{6,5},{7,4},{8,11},{9,10},{10,... | collective-permute-start | bytes 393224 | tf_op jit(solution)/shard_map/ppermute | solution.py:556

commit v4 on v3

--- a/solution.py
+++ b/solution.py
@@ -78,9 +78,15 @@
     return s * (1.0 + v * (1.0 - s))
 
 
-def extend(ext, raw, before):
-    ext[0:LEAD, :] = before[...].astype(F32)
+def extend(ext, raw, before, at):
+    ext[0:LEAD, :] = before[:, at : at + ext.shape[1]].astype(F32)
     ext[LEAD : LEAD + SPAN, :] = raw[...].astype(F32)
+
+
+def group_order():
+    to = lax.broadcasted_iota(jnp.int32, (LOCAL, LOCAL), 0)
+    at = lax.broadcasted_iota(jnp.int32, (LOCAL, LOCAL), 1)
+    return jnp.where(at == to % PER * GROUPS + to // PER, 1.0, 0.0)
 
 
 def conv_tile(ext, w, cols):
@@ -125,7 +131,11 @@
     return rows <= cols if upper else rows >= cols
 
 
-def steps_kernel(dt, heads, step, cum, ends, skip):
+def steps_kernel(raw, bias, alog, d_skip, dt, heads, step, cum, ends, skip):
+    order = group_order()
+    dt[...] = dot(order, raw[...])
+    rows = jnp.concatenate([bias[...], alog[...], d_skip[...], jnp.zeros((5, LOCAL), F32)], axis=0)
+    heads[...] = dot(order, rows, 1, 1)
     v = dt[...] + heads[:, 0:1]
     skip[...] = jnp.broadcast_to(heads[:, 2:3], skip.shape)
     step[...] = jnp.maximum(v, 0.0) + jnp.log1p(jnp.exp(-jnp.abs(v)))
@@ -142,9 +152,9 @@
         put(sgt, r, tile * gain[:, lanes(r)])
 
 
-def state_kernel(core, x, hx, b, hb, wx, wb, step, cum, ends, xt, zs, bc, keep, give, ext, extb, full):
-    extend(ext, x, hx)
-    extend(extb, b, hb)
+def state_kernel(core, x, b, before, wx, wb, step, cum, ends, xt, zs, bc, keep, give, ext, extb, full):
+    extend(ext, x, before, 0)
+    extend(extb, b, before, x.shape[1])
     for g in range(GROUPS):
         pre = conv_tile(extb, wb, lanes(g))
         bc[:, lanes(g)] = pre * sigmoid(pre)
@@ -160,8 +170,8 @@
     give[HALF : HALF + LOCAL, :] = ends[...]
 
 
-def local_kernel(c, hc, wc, bc, xt, zs, cum, skip, cc, mt, y, extc):
-    extend(extc, c, hc)
+def local_kernel(c, before, wc, bc, xt, zs, cum, skip, cc, mt, y, extc):
+    extend(extc, c, before, before.shape[1] - c.shape[1])
     alpha = jnp.exp(cum[...])
     causal = triangle(True)
     for g in range(GROUPS):
@@ -201,7 +211,7 @@
 
 
 def middle_kernel(
-    sums, y, zt, ogt, dy, dg, full, mt, zs, xt, bc, cc, cum, skip, c, hc, wc,
+    sums, y, zt, ogt, dy, dg, full, mt, zs, xt, bc, cc, cum, skip, c, before, wc,
     dz, db, dcum, dskip, gz, early, cpart, extc, padc, dc,
 ):
     alpha = jnp.exp(cum[...])
@@ -225,7 +235,7 @@
     for r in range(PER):
         gz[:, lanes(r)] = take(slope, r).astype(jnp.bfloat16)
         early[16 + r : 17 + r, :] = jnp.sum(take(shares, r), axis=0, keepdims=True)
-    extend(extc, c, hc)
+    extend(extc, c, before, before.shape[1] - c.shape[1])
     clear_pad(padc)
     for g in range(GROUPS):
         mine, ahead, taps = conv_back_tile(extc, padc, wc, lanes(g), dc[:, lanes(g)])
@@ -237,7 +247,7 @@
 
 def last_kernel(
     core, which, own, got, full, ends, dz1, db1, dcum1, dskip, early, cpart, dy, zs, xt, bc, cum, step, skip, dt, per_head,
-    x, hx, wx, b, hb, wb,
+    x, wx, b, wb, before,
     xown, heads, keep, give, packed, ddt, parts, later, ext, extb, pad, padb,
 ):
     unite(core[0], later, own, got)
@@ -245,8 +255,8 @@
     scale = gamma * step[...]
     clear_pad(pad)
     clear_pad(padb)
-    extend(ext, x, hx)
-    extend(extb, b, hb)
+    extend(ext, x, before, 0)
+    extend(extb, b, before, x.shape[1])
     dxs, turned, straight = [], [], []
     at_end = lax.broadcasted_iota(jnp.int32, (PER, SPAN), 1) == SPAN - 1
     for g in range(GROUPS):
@@ -272,7 +282,7 @@
     rate = -jnp.exp(per_head[:, 1:2])
     dstep = jnp.concatenate(straight, axis=0) * gamma + dlog * rate
     draw = dstep * sigmoid(dt[...] + per_head[:, 0:1])
-    ddt[...] = draw
+    ddt[...] = dot(group_order(), draw, 0, 0)
     each = jnp.concatenate([draw, dlog * rate * step[...], dskip[...], jnp.zeros((LOCAL, SPAN), F32)], axis=0)
     at = lax.broadcasted_iota(jnp.int32, (SPAN, SPAN), 0)
     to = lax.broadcasted_iota(jnp.int32, (SPAN, SPAN), 1)
@@ -421,14 +431,6 @@
     return lambda i: i // within * within + within - 1 - i % within
 
 
-def by_group(v):
-    return v.reshape((PER, GROUPS) + v.shape[1:]).swapaxes(0, 1).reshape(v.shape)
-
-
-def by_head(v):
-    return v.reshape((GROUPS, PER) + v.shape[1:]).swapaxes(0, 1).reshape(v.shape)
-
-
 def body(
     x_raw, b_raw, c_raw, z_gate, dt_raw, conv_x, conv_b, conv_c, dt_bias, a_log, d_skip, gain, grad_out
 ):
@@ -443,17 +445,19 @@
     tails = jnp.concatenate([v[SPAN - LEAD :] for v in (x_raw, b_raw, c_raw)], axis=1)
     before = lax.ppermute(tails, CTX, [(i, i + 1) for i in range(size - 1)])
     wx, wb = x_raw.shape[1], b_raw.shape[1]
-    hx, hb, hc = before[:, :wx], before[:, wx : wx + wb], before[:, wx + wb :]
-
-    dt = by_group(dt_raw.T)
-    per_head = by_group(jnp.stack([dt_bias, a_log, d_skip], axis=1))
-    step, cum, ends, skip = call(steps_kernel, "steps", [h_shape] * 4, (dt, per_head))
+
+    dt, per_head, step, cum, ends, skip = call(
+        steps_kernel,
+        "steps",
+        [h_shape, ((LOCAL, 8), F32)] + [h_shape] * 4,
+        (dt_raw.T, dt_bias[None], a_log[None], d_skip[None]),
+    )
     zt, ogt, sgt = call(turn_kernel, "turn", [t_shape] * 3, (z_gate, grad_out, gain[None]))
     xt, zs, bc, keep, give = call(
         state_kernel,
         "state",
         [t_shape, t_shape, bc_shape, ((HALF, STATE), F32), ((HALF + LOCAL, STATE), F32)],
-        (cores, x_raw, hx, b_raw, hb, conv_x, conv_b, step, cum, ends),
+        (cores, x_raw, b_raw, before, conv_x, conv_b, step, cum, ends),
         [(LEAD + SPAN, wx), (LEAD + SPAN, wb), (ALL, STATE)],
         scalars=1,
     )
@@ -481,7 +485,7 @@
         local_kernel,
         "local",
         [bc_shape, ((GROUPS * SPAN, SPAN), F32), t_shape],
-        (c_raw, hc, conv_c, bc, xt, zs, cum, skip),
+        (c_raw, before, conv_c, bc, xt, zs, cum, skip),
         [(LEAD + SPAN, wb)],
     )
     enter, y, sums = call(
@@ -516,7 +520,7 @@
         "middle",
         [t_shape, bc_shape, h_shape, h_shape, ((SPAN, wx), jnp.bfloat16), ((24, TILE), F32)]
         + [((GROUPS, SPAN + 8, TILE), F32)],
-        (sums, y, zt, ogt, dy, dg, enter, mt, zs, xt, bc, cc, cum, skip, c_raw, hc, conv_c),
+        (sums, y, zt, ogt, dy, dg, enter, mt, zs, xt, bc, cc, cum, skip, c_raw, before, conv_c),
         [(LEAD + SPAN, wb), (LEAD + SPAN, wb), (SPAN, wb)],
     )
     half_parts = ((2, 2 * SPAN + 16, TILE), F32)
@@ -525,7 +529,7 @@
         "last",
         [((SPAN, wx), F32), ((64, TILE), F32), half_parts, half_parts, ((80, TILE), F32), h_shape],
         (cores, sides, later_own, later_got, enter, ends, dz, db, dcum, dskip, early, cpart)
-        + (dy, zs, xt, bc, cum, step, skip, dt, per_head, x_raw, hx, conv_x, b_raw, hb, conv_b),
+        + (dy, zs, xt, bc, cum, step, skip, dt, per_head, x_raw, conv_x, b_raw, conv_b, before),
         [(GROUPS, 2 * SPAN + 16, TILE), (ALL, STATE)]
         + [(LEAD + SPAN, wx), (LEAD + SPAN, wb), (LEAD + SPAN, wx), (LEAD + SPAN, wb)],
         scalars=2,
@@ -534,25 +538,25 @@
     across = [(i, peers - 1 - i) for i in range(peers)]
     arrived = lax.ppermute(give, "tp", across)
     packed = packed + swap_cores(packed)
-    steps = (mirror(2), lambda i: i ^ 2, mirror(RING))
-    packed = fold(packed, "chip", steps[0])
+    packed = fold(packed, "chip", mirror(2))
+    packed = fold(packed, "chip", lambda i: i ^ 2)
     arrived, packed = lax.optimization_barrier((arrived, packed))
     mine = keep + arrived
     arrived = lax.ppermute(mine, "tp", [(i, i ^ 1) for i in range(peers)])
-    packed = fold(packed, "chip", steps[1])
+    packed = fold(packed, "chip", mirror(RING))
     arrived, packed = lax.optimization_barrier((arrived, packed))
     mine = mine + arrived
     heads = jnp.concatenate([xheads, mine[:, 2 * SPAN :].reshape(32, TILE)], axis=0)
     heads = lax.ppermute(heads, CTX, [(i + 1, i) for i in range(size - 1)])
-    packed = fold(packed, "chip", steps[2])
+    packed = sum_four(packed, "chip", RING)
     heads, packed = lax.optimization_barrier((heads, packed))
-    packed = sum_four(packed, "chip", RING)
     grad_x_raw, half = call(
         settle_kernel,
         "settle",
         [((SPAN, wx), jnp.bfloat16), ((2, 2 * SPAN, TILE), jnp.bfloat16)],
         (xown, mine, heads),
     )
+    half, packed = lax.optimization_barrier((half, packed))
     other = lax.ppermute(half, "tp", across)
     bc_taps = sum_four(packed[:32], "tp")
     half_bc, each = ((SPAN, wb), jnp.bfloat16), ((1, LOCAL), F32)
@@ -568,7 +572,7 @@
         grad_b_raw,
         grad_c_raw,
         grad_z,
-        by_head(ddt).T,
+        ddt.T,
         conv_x_total,
         conv_b_total,
         conv_c_total,

time: 156 us -> 149 us (0.955)
  waiting for transfers between devices: 35.3 us -> 30.9 us
  local copies, waits for them, and re-layouts: 6.25 us -> 2.86 us
  starting transfers between devices: 25.3 us -> 23.4 us
  blocking collectives: 72.9 us -> 74.7 us
    ppermute x1, waiting for transfers between devices: 3.26 us -> 0.01 us  [body(): arrived = lax.ppermute(mine, 'tp', [(i, i ^ 1) for i in range(peers)])]
    ppermute x1, waiting for transfers between devices: 3 us -> 0.01 us  [body(): arrived = lax.ppermute(give, 'tp', across)]
    unnamed x26, local copies, waits for them, and re-layouts: 4.52 us -> 2.11 us
    ppermute x5, starting transfers between devices: 2.77 us -> 0.76 us  [swap_cores(): return lax.ppermute(v, 'core', [(0, 1), (1, 0)])]
    ppermute x1, waiting for transfers between devices: 0.49 us -> 2.47 us  [body(): before = lax.ppermute(tails, CTX, [(i, i + 1) for i in range(size - 1)])]
    all_to_all x4, blocking collectives: 72.9 us -> 74.7 us  [over_chips(): return lax.all_to_all(v, 'chip', 0, 0)]
  transfers between devices with their start and end apart: 22 -> 22, of which waited for: 15 -> 14; matrix products, arithmetic and copies ran while one was open for 1% -> 0% of each run, Pallas kernels for 5% -> 4%
where the time goes in v4:
time: 149 us; the launch traced here: 148 us
  blocking collectives  74.7 us (50%)
  waiting for transfers between devices  30.9 us (21%)
  starting transfers between devices  23.4 us (16%)
  Pallas kernels  14.8 us (10%)
  local copies, waits for them, and re-layouts  2.86 us (2%)
    all_to_all x4, blocking collectives, over_chips(): return lax.all_to_all(v, 'chip', 0, 0)  74.7 us
    pallas_call x16, Pallas kernels, call(): pl.pallas_call(kernel, out_shape=[jax.ShapeDtypeStruct(s, d) for s, d in...  14.8 us
    ppermute x3, waiting for transfers between devices, fold(): lax.ppermute(x, axis, [(i, partner(i)) for i in range(lax.axis_size(axis))])  13.1 us
    ppermute x9, starting transfers between devices, sum_four(): lax.ppermute(x, axis, [(i, (i // block ^ k) * block + i % block) for i in...  12.5 us
    ppermute x9, waiting for transfers between devices, sum_four(): lax.ppermute(x, axis, [(i, (i // block ^ k) * block + i % block) for i in...  8.09 us
    ppermute x5, waiting for transfers between devices, swap_cores(): return lax.ppermute(v, 'core', [(0, 1), (1, 0)])  4.09 us
    ppermute x1, waiting for transfers between devices, body(): other = lax.ppermute(half, 'tp', across)  3.07 us
  transfers between devices with their start and end apart: 22, of which 14 were waited for; matrix products, arithmetic and copies ran while one was open for 0% of the time, Pallas kernels for 4%

profile of v4, /device:TPU:32, one launch (start us, length us, event | category | flops | bytes accessed | tf_op | source)
XLA Modules:
  0.0 147.7 jit_solution(5526289474446689717)
XLA Ops:
  0.6 0.0 slice-start
  0.7 0.0 slice-start.1
  0.7 0.0 slice-start.2
  0.7 0.7 slice-done
  1.4 1.9 %collective-permute-start = (bf16[16,2048]{1,0:T(8,128)(2,1)S(1)}, bf16[16,2048]{1,0:T(8,128)(2,1)S(1)}, u32[]{:S(2)}, u32[]{:S(2)}) collective-permute-start(bf16[16,2048]{1,0:T(8,128)(2,1)S(1)} %pad_maximum_fusion), channel_id=1, source_target_pairs={{0,4},{4,8},{8,12},{12,16},{16,20},{20,24},{24,28},{28,32},{32,36}... | collective-permute-start | bytes 196616 | tf_op jit(solution)/shard_map/ppermute | solution.py:446
  3.4 0.0 copy-start.11
  3.4 0.7 copy-done.9
  4.1 0.4 steps.1
  4.5 2.5 %collective-permute-done.before = bf16[16,2048]{1,0:T(8,128)(2,1)S(1)} collective-permute-done((bf16[16,2048]{1,0:T(8,128)(2,1)S(1)}, bf16[16,2048]{1,0:T(8,128)(2,1)S(1)}, u32[]{:S(2)}, u32[]{:S(2)}) %collective-permute-start) | collective-permute-done | bytes 65568 | tf_op jit(solution)/shard_map/ppermute | solution.py:446
  7.0 1.2 state.1
  8.3 0.1 collective-permute-start.1
  8.4 1.5 %collective-permute-done.1.got = f32[544,128]{1,0:T(8,128)S(1)} collective-permute-done((f32[544,128]{1,0:T(8,128)S(1)}, f32[544,128]{1,0:T(8,128)S(1)}, u32[]{:S(2)}, u32[]{:S(2)}) %collective-permute-start.1) | collective-permute-done | bytes 278560 | tf_op jit(solution)/shard_map/ppermute | solution.py:407
  9.9 0.2 join.2
  10.1 25.1 %all_to_all.20.s.d = f32[32,1,2176]{2,1,0:T(1,128)S(1)} all-to-all(f32[32,1,2176]{2,1,0:T(1,128)S(1)} %get-tuple-element.83), channel_id=1, replica_groups=mesh['chip'=32,'core'=2,'tp'=4] {'chip'}, dimensions={0} | all-to-all | bytes 557056 | tf_op jit(solution)/shard_map/all_to_all | solution.py:415
  35.2 0.2 block_scan.2
  35.4 16.4 %all_to_all.21 = f32[32,1,2048]{2,1,0:T(1,128)S(1)} all-to-all(f32[32,1,2048]{2,1,0:T(1,128)S(1)} %block_scan.2), channel_id=1, replica_groups=mesh['chip'=32,'core'=2,'tp'=4] {'chip'}, dimensions={0} | all-to-all | bytes 524288 | tf_op jit(solution)/shard_map/all_to_all | solution.py:415
  51.8 0.1 split.2
  51.9 0.1 collective-permute-start.2
  52.0 0.8 copy-done.3
  52.8 0.1 copy-done.4
  52.8 0.3 turn.1
  53.2 0.6 copy-done.1
  53.8 2.3 %local.1 = (f32[128,512]{1,0:T(8,128)S(1)}, f32[512,128]{1,0:T(8,128)S(1)}, f32[1024,128]{1,0:T(8,128)S(1)}) custom-call(bf16[128,512]{1,0:T(8,128)(2,1)S(1)} %copy-done.1, bf16[16,2048]{1,0:T(8,128)(2,1)S(1)} %collective-permute-done.before, f32[4,512]{1,0:T(4,128)S(1)} %copy-done.6, f32[128,512]{1,0:T(8,128)S(1)} %get-tuple-element.87.bc, ...), custom_call_target="tpu_custom_call" | custom-call | flops 20000000 | bytes 4194304 | tf_op jit(solution)/shard_map/local/pallas_call | solution.py:394
  56.0 0.8 output.1
  56.8 3.3 %collective-permute-start.4 = (f32[8,128]{1,0:T(8,128)S(1)}, f32[8,128]{1,0:T(8,128)S(1)}, u32[]{:S(2)}, u32[]{:S(2)}) collective-permute-start(f32[8,128]{1,0:T(8,128)S(1)} %get-tuple-element.95), channel_id=1, source_target_pairs={{0,2},{1,3},{2,0},{3,1},{4,6},{5,7},{6,4},{7,5},{8,10},{9,11},{10,... | collective-permute-start | bytes 12296 | tf_op jit(solution)/shard_map/ppermute | solution.py:424
  60.1 1.1 collective-permute-start.5
  61.1 0.9 collective-permute-done.4
  62.0 2.9 %collective-permute-done.5 = f32[8,128]{1,0:T(8,128)S(1)} collective-permute-done((f32[8,128]{1,0:T(8,128)S(1)}, f32[8,128]{1,0:T(8,128)S(1)}, u32[]{:S(2)}, u32[]{:S(2)}) %collective-permute-start.5) | collective-permute-done | bytes 4128 | tf_op jit(solution)/shard_map/ppermute | solution.py:424
  64.9 0.9 gate.1
  65.8 0.1 collective-permute-start.6
  65.9 1.5 %collective-permute-done.6.got = f32[512,128]{1,0:T(8,128)S(1)} collective-permute-done((f32[512,128]{1,0:T(8,128)S(1)}, f32[512,128]{1,0:T(8,128)S(1)}, u32[]{:S(2)}, u32[]{:S(2)}) %collective-permute-start.6) | collective-permute-done | bytes 262176 | tf_op jit(solution)/shard_map/ppermute | solution.py:407
  67.4 0.1 join.3
  67.5 17.0 %all_to_all.22.s = f32[32,1,2048]{2,1,0:T(1,128)S(1)} all-to-all(f32[32,1,2048]{2,1,0:T(1,128)S(1)} %bitcast.18), channel_id=1, replica_groups=mesh['chip'=32,'core'=2,'tp'=4] {'chip'}, dimensions={0} | all-to-all | bytes 524288 | tf_op jit(solution)/shard_map/all_to_all | solution.py:415
  84.4 0.2 block_scan.3
  84.6 16.2 %all_to_all.23 = f32[32,1,2048]{2,1,0:T(1,128)S(1)} all-to-all(f32[32,1,2048]{2,1,0:T(1,128)S(1)} %block_scan.3), channel_id=1, replica_groups=mesh['chip'=32,'core'=2,'tp'=4] {'chip'}, dimensions={0} | all-to-all | bytes 524288 | tf_op jit(solution)/shard_map/all_to_all | solution.py:415
  100.8 0.1 split.3
  100.9 0.3 collective-permute-start.7
  101.1 3.4 %middle.1 = (f32[1024,128]{1,0:T(8,128)S(1)}, f32[128,512]{1,0:T(8,128)S(1)}, f32[32,128]{1,0:T(8,128)S(1)}, f32[32,128]{1,0:T(8,128)S(1)}, bf16[128,1024]{1,0:T...) custom-call(f32[8,128]{1,0:T(8,128)S(1)} %add_add_fusion.2.sums, f32[1024,128]{1,0:T(8,128)S(1)} %get-tuple-element.96.y, ...), custom_call_target="tpu_custom_call" | custom-call | flops 20000000 | bytes 4194304 | tf_op jit(solution)/shard_map/middle/pallas_call | solution.py:394
  104.6 3.2 %last.1 = (f32[128,1024]{1,0:T(8,128)S(1)}, f32[64,128]{1,0:T(8,128)S(1)}, f32[2,272,128]{2,1,0:T(8,128)S(1)}, f32[2,272,128]{2,1,0:T(8,128)S(1)}, f32[80,128]{1,0:T(8,128)S(1)}, /*index=5*/f32[32,128]{1,0:T(8,128)}) custom-call(s32[1]{0:T(128)} %bitcast.core, s32[1]{0:T(128)} %bitcast.1.which, f32[512,128]{1,0:T(8,128)S(1)} %get-tuple-element.99.own, ...), custom_call_target="tpu_custom_call" | custom-call | flops 20000000 | bytes 4194304 | tf_op jit(solution)/shard_map/last/pallas_call | solution.py:394
  107.8 2.1 %collective-permute-start.8 = (f32[2,272,128]{2,1,0:T(8,128)S(1)}, f32[2,272,128]{2,1,0:T(8,128)S(1)}, u32[]{:S(2)}, u32[]{:S(2)}) collective-permute-start(f32[2,272,128]{2,1,0:T(8,128)S(1)} %get-tuple-element.116), channel_id=1, source_target_pairs={{0,3},{1,2},{2,1},{3,0},{4,7},{5,6},{6,5},{7,4},{8,11},{9,10},{10,... | collective-permute-start | bytes 835592 | tf_op jit(solution)/shard_map/ppermute | solution.py:539
  109.9 0.2 collective-permute-start.9
  110.1 1.0 collective-permute-done.9
  111.1 0.2 collective-permute-start.10
  111.4 3.8 %collective-permute-done.10 = f32[80,128]{1,0:T(8,128)S(1)} collective-permute-done((f32[80,128]{1,0:T(8,128)S(1)}, f32[80,128]{1,0:T(8,128)S(1)}, u32[]{:S(2)}, u32[]{:S(2)}) %collective-permute-start.10) | collective-permute-done | bytes 40992 | tf_op jit(solution)/shard_map/ppermute | solution.py:419
  115.1 0.9 collective-permute-start.11
  116.0 4.0 %collective-permute-done.11 = f32[80,128]{1,0:T(8,128)S(1)} collective-permute-done((f32[80,128]{1,0:T(8,128)S(1)}, f32[80,128]{1,0:T(8,128)S(1)}, u32[]{:S(2)}, u32[]{:S(2)}) %collective-permute-start.11) | collective-permute-done | bytes 40992 | tf_op jit(solution)/shard_map/ppermute | solution.py:419
  120.1 0.1 collective-permute-start.12
  120.2 1.7 %collective-permute-start.13 = (f32[80,128]{1,0:T(8,128)S(1)}, f32[80,128]{1,0:T(8,128)S(1)}, u32[]{:S(2)}, u32[]{:S(2)}) collective-permute-start(f32[80,128]{1,0:T(8,128)S(1)} %add.51), channel_id=1, source_target_pairs={{0,56},{8,48},{16,40},{24,32},{32,24},{40,16},{48,8},{56,0},{64,12... | collective-permute-start | bytes 122888 | tf_op jit(solution)/shard_map/ppermute | solution.py:419
  121.9 5.4 %collective-permute-done.13 = f32[80,128]{1,0:T(8,128)S(1)} collective-permute-done((f32[80,128]{1,0:T(8,128)S(1)}, f32[80,128]{1,0:T(8,128)S(1)}, u32[]{:S(2)}, u32[]{:S(2)}) %collective-permute-start.13) | collective-permute-done | bytes 40992 | tf_op jit(solution)/shard_map/ppermute | solution.py:419
  127.3 1.4 collective-permute-start.16
  128.7 2.0 %collective-permute-start.17 = (f32[80,128]{1,0:T(8,128)S(1)}, f32[80,128]{1,0:T(8,128)S(1)}, u32[]{:S(2)}, u32[]{:S(2)}) collective-permute-start(f32[80,128]{1,0:T(8,128)S(1)} %add.53), channel_id=1, source_target_pairs={{0,192},{8,200},{16,208},{24,216},{32,224},{40,232},{48,240},{56,2... | collective-permute-start | bytes 122888 | tf_op jit(solution)/shard_map/ppermute | solution.py:424
  130.7 0.2 collective-permute-start.15
  130.9 1.9 %collective-permute-start.14 = (f32[96,128]{1,0:T(8,128)S(1)}, f32[96,128]{1,0:T(8,128)S(1)}, u32[]{:S(2)}, u32[]{:S(2)}) collective-permute-start(f32[96,128]{1,0:T(8,128)S(1)} %pad_maximum_fusion.1), channel_id=1, source_target_pairs={{4,0},{8,4},{12,8},{16,12},{20,16},{24,20},{28,24},{32,28},{36,32}... | collective-permute-start | bytes 147464 | tf_op jit(solution)/shard_map/ppermute | solution.py:550
  132.9 0.0 collective-permute-done.16
  132.9 1.0 collective-permute-done.17
  133.9 0.8 collective-permute-done.15
  134.7 0.8 settle.1
  135.5 2.6 %collective-permute-start.20 = (f32[32,128]{1,0:T(8,128)S(1)}, f32[32,128]{1,0:T(8,128)S(1)}, u32[]{:S(2)}, u32[]{:S(2)}) collective-permute-start(f32[32,128]{1,0:T(8,128)S(1)} %slice.19), channel_id=1, source_target_pairs={{0,2},{1,3},{2,0},{3,1},{4,6},{5,7},{6,4},{7,5},{8,10},{9,11},{10,... | collective-permute-start | bytes 49160 | tf_op jit(solution)/shard_map/ppermute | solution.py:424
  138.0 2.0 %collective-permute-start.21 = (f32[32,128]{1,0:T(8,128)S(1)}, f32[32,128]{1,0:T(8,128)S(1)}, u32[]{:S(2)}, u32[]{:S(2)}) collective-permute-start(f32[32,128]{1,0:T(8,128)S(1)} %slice.19), channel_id=1, source_target_pairs={{0,3},{1,2},{2,1},{3,0},{4,7},{5,6},{6,5},{7,4},{8,11},{9,10},{10,... | collective-permute-start | bytes 49160 | tf_op jit(solution)/shard_map/ppermute | solution.py:424
  140.1 1.2 collective-permute-start.18
  141.3 1.7 %collective-permute-done.21 = f32[32,128]{1,0:T(8,128)S(1)} collective-permute-done((f32[32,128]{1,0:T(8,128)S(1)}, f32[32,128]{1,0:T(8,128)S(1)}, u32[]{:S(2)}, u32[]{:S(2)}) %collective-permute-start.21) | collective-permute-done | bytes 16416 | tf_op jit(solution)/shard_map/ppermute | solution.py:424
  143.0 0.8 collective-permute-done.19
  143.8 3.1 %collective-permute-done.18.other = bf16[2,256,128]{2,1,0:T(8,128)(2,1)S(1)} collective-permute-done((bf16[2,256,128]{2,1,0:T(8,128)(2,1)S(1)}, bf16[2,256,128]{2,1,0:T(8,128)(2,1)S(1)}, u32[]{:S(2)}, u32[]{:S(2)}) %collective-permute-start.18) | collective-permute-done | bytes 131104 | tf_op jit(solution)/shard_map/ppermute | solution.py:560
  146.9 0.8 finish.1
  (45 shorter events, 0.2 us)
Async XLA Ops:
  0.6 0.8 slice-start
  0.7 0.8 slice-start.1
  0.7 0.7 slice-start.2
  1.4 5.6 %collective-permute-start = (bf16[16,2048]{1,0:T(8,128)(2,1)S(1)}, bf16[16,2048]{1,0:T(8,128)(2,1)S(1)}, u32[]{:S(2)}, u32[]{:S(2)}) collective-permute-start(bf16[16,2048]{1,0:T(8,128)(2,1)S(1)} %pad_maximum_fusion), channel_id=1, source_target_pairs={{0,4},{4,8},{8,12},{12,16},{16,20},{20,24},{24,28},{28,32},{32,36}... | collective-permute-start | bytes 196616 | tf_op jit(solution)/shard_map/ppermute | solution.py:446
  3.4 0.7 copy-start.9
  3.4 0.7 copy-start.10
  3.4 0.7 copy-start.11
  3.4 0.7 copy-start.12
  3.4 3.6 %copy-start = (bf16[128,1024]{1,0:T(8,128)(2,1)S(1)}, bf16[128,1024]{1,0:T(8,128)(2,1)}, u32[]{:S(2)}) copy-start(bf16[128,1024]{1,0:T(8,128)(2,1)} %x.3) | copy-start | bytes 786436
  4.1 2.9 %copy-start.2 = (bf16[128,512]{1,0:T(8,128)(2,1)S(1)}, bf16[128,512]{1,0:T(8,128)(2,1)}, u32[]{:S(2)}) copy-start(bf16[128,512]{1,0:T(8,128)(2,1)} %b.3) | copy-start | bytes 393220
  4.1 2.9 %copy-start.5 = (f32[4,1024]{1,0:T(4,128)S(1)}, f32[4,1024]{1,0:T(4,128)}, u32[]{:S(2)}) copy-start(f32[4,1024]{1,0:T(4,128)} %wx.3) | copy-start | bytes 49156
  4.1 2.9 %copy-start.7 = (f32[4,512]{1,0:T(4,128)S(1)}, f32[4,512]{1,0:T(4,128)}, u32[]{:S(2)}) copy-start(f32[4,512]{1,0:T(4,128)} %wb.3) | copy-start | bytes 24580
  8.3 1.6 %collective-permute-start.1 = (f32[544,128]{1,0:T(8,128)S(1)}, f32[544,128]{1,0:T(8,128)S(1)}, u32[]{:S(2)}, u32[]{:S(2)}) collective-permute-start(f32[544,128]{1,0:T(8,128)S(1)} %get-tuple-element.82), channel_id=1, source_target_pairs={{0,4},{4,0},{1,5},{5,1},{2,6},{6,2},{3,7},{7,3},{8,12},{12,8},{9,1... | collective-permute-start | bytes 835592 | tf_op jit(solution)/shard_map/ppermute | solution.py:407
  51.8 1.0 copy-start.3
  51.8 1.0 copy-start.4
  51.8 1.0 copy-start.8
  51.9 4.1 %collective-permute-start.2 = (f32[512,128]{1,0:T(8,128)S(1)}, f32[512,128]{1,0:T(8,128)S(1)}, u32[]{:S(2)}, u32[]{:S(2)}) collective-permute-start(f32[512,128]{1,0:T(8,128)S(1)} %get-tuple-element.86), channel_id=1, source_target_pairs={{0,4},{4,0},{1,5},{5,1},{2,6},{6,2},{3,7},{7,3},{8,12},{12,8},{9,1... | collective-permute-start | bytes 786440 | tf_op jit(solution)/shard_map/ppermute | solution.py:407
  52.8 0.9 copy-start.1
  52.8 0.9 copy-start.6
  56.8 5.2 %collective-permute-start.4 = (f32[8,128]{1,0:T(8,128)S(1)}, f32[8,128]{1,0:T(8,128)S(1)}, u32[]{:S(2)}, u32[]{:S(2)}) collective-permute-start(f32[8,128]{1,0:T(8,128)S(1)} %get-tuple-element.95), channel_id=1, source_target_pairs={{0,2},{1,3},{2,0},{3,1},{4,6},{5,7},{6,4},{7,5},{8,10},{9,11},{10,... | collective-permute-start | bytes 12296 | tf_op jit(solution)/shard_map/ppermute | solution.py:424
  60.1 4.8 %collective-permute-start.5 = (f32[8,128]{1,0:T(8,128)S(1)}, f32[8,128]{1,0:T(8,128)S(1)}, u32[]{:S(2)}, u32[]{:S(2)}) collective-permute-start(f32[8,128]{1,0:T(8,128)S(1)} %get-tuple-element.95), channel_id=1, source_target_pairs={{0,3},{1,2},{2,1},{3,0},{4,7},{5,6},{6,5},{7,4},{8,11},{9,10},{10,... | collective-permute-start | bytes 12296 | tf_op jit(solution)/shard_map/ppermute | solution.py:424
  61.1 3.8 %collective-permute-start.3 = (f32[8,128]{1,0:T(8,128)S(1)}, f32[8,128]{1,0:T(8,128)S(1)}, u32[]{:S(2)}, u32[]{:S(2)}) collective-permute-start(f32[8,128]{1,0:T(8,128)S(1)} %get-tuple-element.95), channel_id=1, source_target_pairs={{0,1},{1,0},{2,3},{3,2},{4,5},{5,4},{6,7},{7,6},{8,9},{9,8},{10,11... | collective-permute-start | bytes 12296 | tf_op jit(solution)/shard_map/ppermute | solution.py:424
  65.8 1.6 %collective-permute-start.6 = (f32[512,128]{1,0:T(8,128)S(1)}, f32[512,128]{1,0:T(8,128)S(1)}, u32[]{:S(2)}, u32[]{:S(2)}) collective-permute-start(f32[512,128]{1,0:T(8,128)S(1)} %get-tuple-element.98), channel_id=1, source_target_pairs={{0,4},{4,0},{1,5},{5,1},{2,6},{6,2},{3,7},{7,3},{8,12},{12,8},{9,1... | collective-permute-start | bytes 786440 | tf_op jit(solution)/shard_map/ppermute | solution.py:407
  100.9 3.7 %collective-permute-start.7 = (f32[512,128]{1,0:T(8,128)S(1)}, f32[512,128]{1,0:T(8,128)S(1)}, u32[]{:S(2)}, u32[]{:S(2)}) collective-permute-start(f32[512,128]{1,0:T(8,128)S(1)} %get-tuple-element.100), channel_id=1, source_target_pairs={{0,4},{4,0},{1,5},{5,1},{2,6},{6,2},{3,7},{7,3},{8,12},{12,8},{9,1... | collective-permute-start | bytes 786440 | tf_op jit(solution)/shard_map/ppermute | solution.py:407
  107.8 12.3 %collective-permute-start.8 = (f32[2,272,128]{2,1,0:T(8,128)S(1)}, f32[2,272,128]{2,1,0:T(8,128)S(1)}, u32[]{:S(2)}, u32[]{:S(2)}) collective-permute-start(f32[2,272,128]{2,1,0:T(8,128)S(1)} %get-tuple-element.116), channel_id=1, source_target_pairs={{0,3},{1,2},{2,1},{3,0},{4,7},{5,6},{6,5},{7,4},{8,11},{9,10},{10,... | collective-permute-start | bytes 835592 | tf_op jit(solution)/shard_map/ppermute | solution.py:539
  109.9 1.2 collective-permute-start.9
  111.1 4.0 %collective-permute-start.10 = (f32[80,128]{1,0:T(8,128)S(1)}, f32[80,128]{1,0:T(8,128)S(1)}, u32[]{:S(2)}, u32[]{:S(2)}) collective-permute-start(f32[80,128]{1,0:T(8,128)S(1)} %add.49), channel_id=1, source_target_pairs={{0,8},{8,0},{16,24},{24,16},{32,40},{40,32},{48,56},{56,48},{64,72... | collective-permute-start | bytes 122888 | tf_op jit(solution)/shard_map/ppermute | solution.py:419
  115.1 4.9 %collective-permute-start.11 = (f32[80,128]{1,0:T(8,128)S(1)}, f32[80,128]{1,0:T(8,128)S(1)}, u32[]{:S(2)}, u32[]{:S(2)}) collective-permute-start(f32[80,128]{1,0:T(8,128)S(1)} %add.50), channel_id=1, source_target_pairs={{0,16},{8,24},{16,0},{24,8},{32,48},{40,56},{48,32},{56,40},{64,80... | collective-permute-start | bytes 122888 | tf_op jit(solution)/shard_map/ppermute | solution.py:419
  120.1 7.2 %collective-permute-start.12 = (f32[2,272,128]{2,1,0:T(8,128)S(1)}, f32[2,272,128]{2,1,0:T(8,128)S(1)}, u32[]{:S(2)}, u32[]{:S(2)}) collective-permute-start(f32[2,272,128]{2,1,0:T(8,128)S(1)} %add.52), channel_id=1, source_target_pairs={{0,1},{1,0},{2,3},{3,2},{4,5},{5,4},{6,7},{7,6},{8,9},{9,8},{10,11... | collective-permute-start | bytes 835592 | tf_op jit(solution)/shard_map/ppermute | solution.py:545
  120.2 7.1 %collective-permute-start.13 = (f32[80,128]{1,0:T(8,128)S(1)}, f32[80,128]{1,0:T(8,128)S(1)}, u32[]{:S(2)}, u32[]{:S(2)}) collective-permute-start(f32[80,128]{1,0:T(8,128)S(1)} %add.51), channel_id=1, source_target_pairs={{0,56},{8,48},{16,40},{24,32},{32,24},{40,16},{48,8},{56,0},{64,12... | collective-permute-start | bytes 122888 | tf_op jit(solution)/shard_map/ppermute | solution.py:419
  127.3 5.6 %collective-permute-start.16 = (f32[80,128]{1,0:T(8,128)S(1)}, f32[80,128]{1,0:T(8,128)S(1)}, u32[]{:S(2)}, u32[]{:S(2)}) collective-permute-start(f32[80,128]{1,0:T(8,128)S(1)} %add.53), channel_id=1, source_target_pairs={{0,128},{8,136},{16,144},{24,152},{32,160},{40,168},{48,176},{56,1... | collective-permute-start | bytes 122888 | tf_op jit(solution)/shard_map/ppermute | solution.py:424
  128.7 5.2 %collective-permute-start.17 = (f32[80,128]{1,0:T(8,128)S(1)}, f32[80,128]{1,0:T(8,128)S(1)}, u32[]{:S(2)}, u32[]{:S(2)}) collective-permute-start(f32[80,128]{1,0:T(8,128)S(1)} %add.53), channel_id=1, source_target_pairs={{0,192},{8,200},{16,208},{24,216},{32,224},{40,232},{48,240},{56,2... | collective-permute-start | bytes 122888 | tf_op jit(solution)/shard_map/ppermute | solution.py:424
  130.7 4.0 %collective-permute-start.15 = (f32[80,128]{1,0:T(8,128)S(1)}, f32[80,128]{1,0:T(8,128)S(1)}, u32[]{:S(2)}, u32[]{:S(2)}) collective-permute-start(f32[80,128]{1,0:T(8,128)S(1)} %add.53), channel_id=1, source_target_pairs={{0,64},{8,72},{16,80},{24,88},{32,96},{40,104},{48,112},{56,120},{... | collective-permute-start | bytes 122888 | tf_op jit(solution)/shard_map/ppermute | solution.py:424
  130.9 3.8 %collective-permute-start.14 = (f32[96,128]{1,0:T(8,128)S(1)}, f32[96,128]{1,0:T(8,128)S(1)}, u32[]{:S(2)}, u32[]{:S(2)}) collective-permute-start(f32[96,128]{1,0:T(8,128)S(1)} %pad_maximum_fusion.1), channel_id=1, source_target_pairs={{4,0},{8,4},{12,8},{16,12},{20,16},{24,20},{28,24},{32,28},{36,32}... | collective-permute-start | bytes 147464 | tf_op jit(solution)/shard_map/ppermute | solution.py:550
  135.5 5.8 %collective-permute-start.20 = (f32[32,128]{1,0:T(8,128)S(1)}, f32[32,128]{1,0:T(8,128)S(1)}, u32[]{:S(2)}, u32[]{:S(2)}) collective-permute-start(f32[32,128]{1,0:T(8,128)S(1)} %slice.19), channel_id=1, source_target_pairs={{0,2},{1,3},{2,0},{3,1},{4,6},{5,7},{6,4},{7,5},{8,10},{9,11},{10,... | collective-permute-start | bytes 49160 | tf_op jit(solution)/shard_map/ppermute | solution.py:424
  138.0 4.9 %collective-permute-start.21 = (f32[32,128]{1,0:T(8,128)S(1)}, f32[32,128]{1,0:T(8,128)S(1)}, u32[]{:S(2)}, u32[]{:S(2)}) collective-permute-start(f32[32,128]{1,0:T(8,128)S(1)} %slice.19), channel_id=1, source_target_pairs={{0,3},{1,2},{2,1},{3,0},{4,7},{5,6},{6,5},{7,4},{8,11},{9,10},{10,... | collective-permute-start | bytes 49160 | tf_op jit(solution)/shard_map/ppermute | solution.py:424
  140.1 3.7 %collective-permute-start.19 = (f32[32,128]{1,0:T(8,128)S(1)}, f32[32,128]{1,0:T(8,128)S(1)}, u32[]{:S(2)}, u32[]{:S(2)}) collective-permute-start(f32[32,128]{1,0:T(8,128)S(1)} %slice.19), channel_id=1, source_target_pairs={{0,1},{1,0},{2,3},{3,2},{4,5},{5,4},{6,7},{7,6},{8,9},{9,8},{10,11... | collective-permute-start | bytes 49160 | tf_op jit(solution)/shard_map/ppermute | solution.py:424
  140.1 6.8 %collective-permute-start.18 = (bf16[2,256,128]{2,1,0:T(8,128)(2,1)S(1)}, bf16[2,256,128]{2,1,0:T(8,128)(2,1)S(1)}, u32[]{:S(2)}, u32[]{:S(2)}) collective-permute-start(bf16[2,256,128]{2,1,0:T(8,128)(2,1)S(1)} %get-tuple-element.127.half), channel_id=1, source_target_pairs={{0,3},{1,2},{2,1},{3,0},{4,7},{5,6},{6,5},{7,4},{8,11},{9,10},{10,... | collective-permute-start | bytes 393224 | tf_op jit(solution)/shard_map/ppermute | solution.py:560

commit v5 on v4

--- a/solution.py
+++ b/solution.py
@@ -248,7 +248,7 @@
 def last_kernel(
     core, which, own, got, full, ends, dz1, db1, dcum1, dskip, early, cpart, dy, zs, xt, bc, cum, step, skip, dt, per_head,
     x, wx, b, wb, before,
-    xown, heads, keep, give, packed, ddt, parts, later, ext, extb, pad, padb,
+    xown, heads, keep, give_one, give_two, give_three, packed, ddt, parts, later, ext, extb, pad, padb,
 ):
     unite(core[0], later, own, got)
     gamma = jnp.exp(-cum[...])
@@ -290,9 +290,8 @@
     packed[72:80, :] = dot(dot(jnp.ones((8, SPAN), F32), each, 1, 1), jnp.where(at == source, 1.0, 0.0))
     packed[16:32, :] = early[0:16, :]
     packed[64:72, :] = early[16:24, :]
-    side = which[0]
-    keep[...] = parts[pl.ds(side * 2, 2)]
-    give[...] = parts[pl.ds((1 - side) * 2, 2)]
+    for k, quarter in enumerate((keep, give_one, give_two, give_three)):
+        quarter[...] = parts[lax.rem(which[0] + k, GROUPS)]
     for r in range(PER):
         mine, ahead, taps = conv_back_tile(ext, pad, wx, lanes(r), take(dxs, r))
         xown[:, lanes(r)] = mine
@@ -340,29 +339,26 @@
         give[rows, :] = jnp.where(leads, near, far)
 
 
-def settle_kernel(xown, mine, heads, gx, half):
+def settle_kernel(xown, mine, heads, gx, quarter):
     last = slice(SPAN - LEAD, SPAN)
     none = jnp.zeros((LEAD - 8, TILE), F32)
     for r in range(PER):
         gx[0 : SPAN - LEAD, lanes(r)] = xown[0 : SPAN - LEAD, lanes(r)].astype(jnp.bfloat16)
         more = jnp.concatenate([none, heads[8 * r : 8 * r + 8, :]], axis=0)
         gx[last, lanes(r)] = (xown[last, lanes(r)] + more).astype(jnp.bfloat16)
-    for g in range(2):
-        for i in range(2):
-            at = 64 + 16 * g + 8 * i
-            more = jnp.concatenate([none, heads[at : at + 8, :]], axis=0)
-            start, stop = i * SPAN, (i + 1) * SPAN
-            half[g, start : stop - LEAD, :] = mine[g, start : stop - LEAD, :].astype(jnp.bfloat16)
-            half[g, stop - LEAD : stop, :] = (mine[g, stop - LEAD : stop, :] + more).astype(jnp.bfloat16)
-
-
-def finish_kernel(which, half, other, bc_taps, packed, gb, gc, tx, tb, tc, tgain, bias, rate, skip):
-    left = which[0] == 0
-    for g in range(GROUPS):
-        first, second = (half, other) if g < 2 else (other, half)
-        both = jnp.where(left, first[g % 2].astype(F32), second[g % 2].astype(F32)).astype(jnp.bfloat16)
-        gb[:, lanes(g)] = both[0:SPAN]
-        gc[:, lanes(g)] = both[SPAN : 2 * SPAN]
+    for i in range(2):
+        more = jnp.concatenate([none, heads[64 + 8 * i : 72 + 8 * i, :]], axis=0)
+        start, stop = i * SPAN, (i + 1) * SPAN
+        quarter[start : stop - LEAD, :] = mine[start : stop - LEAD, :].astype(jnp.bfloat16)
+        quarter[stop - LEAD : stop, :] = (mine[stop - LEAD : stop, :] + more).astype(jnp.bfloat16)
+
+
+def finish_kernel(which, own, one, two, three, bc_taps, packed, gb, gc, tx, tb, tc, tgain, bias, rate, skip):
+    for k, quarter in enumerate((own, one, two, three)):
+        at = lax.rem(which[0] + GROUPS - k, GROUPS)
+        cols = pl.ds(pl.multiple_of(at * TILE, TILE), TILE)
+        gb[:, cols] = quarter[0:SPAN, :]
+        gc[:, cols] = quarter[SPAN : 2 * SPAN, :]
     for k in range(CONV):
         for g in range(GROUPS):
             tb[k : k + 1, lanes(g)] = bc_taps[k * GROUPS + g : k * GROUPS + g + 1, :]
@@ -419,12 +415,16 @@
     return x + lax.ppermute(x, axis, [(i, partner(i)) for i in range(lax.axis_size(axis))])
 
 
-def sum_four(x, axis, block=1):
+def sum_four(x, axis, one, two):
     near, far, last = (
-        lax.ppermute(x, axis, [(i, (i // block ^ k) * block + i % block) for i in range(lax.axis_size(axis))])
-        for k in range(1, 4)
+        lax.ppermute(x, axis, [(i, partner(i)) for i in range(lax.axis_size(axis))])
+        for partner in (one, two, lambda i: one(two(i)))
     )
     return (x + near) + (far + last)
+
+
+def flip(bits):
+    return lambda i: i ^ bits
 
 
 def mirror(within):
@@ -436,8 +436,8 @@
 ):
     size = lax.axis_size(CTX)
     core = lax.axis_index("core")
-    side = lax.axis_index("tp") // (lax.axis_size("tp") // 2)
-    cores, sides = lax.optimization_barrier((core.reshape(1), side.reshape(1)))
+    place = lax.axis_index("tp")
+    cores, places = lax.optimization_barrier((core.reshape(1), place.reshape(1)))
     is_even = core == 0
     t_shape = ((ALL, SPAN), F32)
     bc_shape = ((SPAN, GROUPS * STATE), F32)
@@ -495,7 +495,7 @@
         (cores, enter_own, enter_got, cc, y1, cum, zt, sgt),
         scalars=1,
     )
-    sums = sum_four(sums, "tp")
+    sums = sum_four(sums, "tp", flip(1), flip(2))
     keep, give, dy, dg = call(
         gate_kernel,
         "gate",
@@ -523,48 +523,48 @@
         (sums, y, zt, ogt, dy, dg, enter, mt, zs, xt, bc, cc, cum, skip, c_raw, before, conv_c),
         [(LEAD + SPAN, wb), (LEAD + SPAN, wb), (SPAN, wb)],
     )
-    half_parts = ((2, 2 * SPAN + 16, TILE), F32)
-    xown, xheads, keep, give, packed, ddt = call(
+    quarter = ((2 * SPAN + 16, TILE), F32)
+    xown, xheads, mine, *gives, packed, ddt = call(
         last_kernel,
         "last",
-        [((SPAN, wx), F32), ((64, TILE), F32), half_parts, half_parts, ((80, TILE), F32), h_shape],
-        (cores, sides, later_own, later_got, enter, ends, dz, db, dcum, dskip, early, cpart)
+        [((SPAN, wx), F32), ((64, TILE), F32)] + [quarter] * GROUPS + [((80, TILE), F32), h_shape],
+        (cores, places, later_own, later_got, enter, ends, dz, db, dcum, dskip, early, cpart)
         + (dy, zs, xt, bc, cum, step, skip, dt, per_head, x_raw, conv_x, b_raw, conv_b, before),
         [(GROUPS, 2 * SPAN + 16, TILE), (ALL, STATE)]
         + [(LEAD + SPAN, wx), (LEAD + SPAN, wb), (LEAD + SPAN, wx), (LEAD + SPAN, wb)],
         scalars=2,
     )
     peers = lax.axis_size("tp")
-    across = [(i, peers - 1 - i) for i in range(peers)]
-    arrived = lax.ppermute(give, "tp", across)
+
+    def ahead_by(v, k):
+        return lax.ppermute(v, "tp", [(i, (i + k) % peers) for i in range(peers)])
+
+    arrived = [ahead_by(v, k + 1) for k, v in enumerate(gives)]
     packed = packed + swap_cores(packed)
-    packed = fold(packed, "chip", mirror(2))
-    packed = fold(packed, "chip", lambda i: i ^ 2)
+    packed = fold(packed, "chip", flip(1))
     arrived, packed = lax.optimization_barrier((arrived, packed))
-    mine = keep + arrived
-    arrived = lax.ppermute(mine, "tp", [(i, i ^ 1) for i in range(peers)])
-    packed = fold(packed, "chip", mirror(RING))
-    arrived, packed = lax.optimization_barrier((arrived, packed))
-    mine = mine + arrived
-    heads = jnp.concatenate([xheads, mine[:, 2 * SPAN :].reshape(32, TILE)], axis=0)
+    mine = (mine + arrived[0]) + (arrived[1] + arrived[2])
+    heads = jnp.concatenate([xheads, mine[2 * SPAN :]], axis=0)
     heads = lax.ppermute(heads, CTX, [(i + 1, i) for i in range(size - 1)])
-    packed = sum_four(packed, "chip", RING)
+    packed = sum_four(packed, "chip", flip(2), mirror(RING))
     heads, packed = lax.optimization_barrier((heads, packed))
-    grad_x_raw, half = call(
+    grad_x_raw, quarter = call(
         settle_kernel,
         "settle",
-        [((SPAN, wx), jnp.bfloat16), ((2, 2 * SPAN, TILE), jnp.bfloat16)],
+        [((SPAN, wx), jnp.bfloat16), ((2 * SPAN, TILE), jnp.bfloat16)],
         (xown, mine, heads),
     )
-    half, packed = lax.optimization_barrier((half, packed))
-    other = lax.ppermute(half, "tp", across)
-    bc_taps = sum_four(packed[:32], "tp")
+    quarter, packed = lax.optimization_barrier((quarter, packed))
+    others = [ahead_by(quarter, k) for k in range(1, peers)]
+    packed = sum_four(packed, "chip", flip(RING), flip(2 * RING))
+    others, packed = lax.optimization_barrier((others, packed))
+    bc_taps = sum_four(packed[:32], "tp", flip(1), flip(2))
     half_bc, each = ((SPAN, wb), jnp.bfloat16), ((1, LOCAL), F32)
     grad_b_raw, grad_c_raw, conv_x_total, conv_b_total, conv_c_total, gain_total, *small = call(
         finish_kernel,
         "finish",
         [half_bc, half_bc, ((CONV, wx), F32), ((CONV, wb), F32), ((CONV, wb), F32), ((1, wx), F32)] + [each] * 3,
-        (sides, half, other, bc_taps, packed),
+        (places, quarter, *others, bc_taps, packed),
         scalars=1,
     )
     return (

time: 149 us -> 151 us (1.013)
  starting transfers between devices: 23.4 us -> 31.8 us
  waiting for transfers between devices: 30.9 us -> 24.3 us
    ppermute x12 -> x18, starting transfers between devices: 15.9 us -> 27 us  [the longest x12 17.8 us: sum_four(): lax.ppermute(x, axis, [(i, partner(i)) for i in range(lax.axis_size(axis))])]
    ppermute x3 -> x1, waiting for transfers between devices: 13.1 us -> 3.76 us  [fold(): lax.ppermute(x, axis, [(i, partner(i)) for i in range(lax.axis_size(axis))])]
    ppermute x3 -> x1, starting transfers between devices: 2.86 us -> 0.24 us  [fold(): lax.ppermute(x, axis, [(i, partner(i)) for i in range(lax.axis_size(axis))])]
    ppermute x12 -> x18, waiting for transfers between devices: 11.2 us -> 12 us  [the longest x12 7.16 us: sum_four(): lax.ppermute(x, axis, [(i, partner(i)) for i in range(lax.axis_size(axis))])]
  transfers between devices with their start and end apart: 22 -> 26, of which waited for: 14 -> 17; matrix products, arithmetic and copies ran while one was open for 0% -> 0% of each run, Pallas kernels for 4% -> 4%
where the time goes in v5:
time: 151 us; the launch traced here: 149 us
  blocking collectives  74.7 us (49%)
  starting transfers between devices  31.8 us (21%)
  waiting for transfers between devices  24.3 us (16%)
  Pallas kernels  15 us (10%)
  local copies, waits for them, and re-layouts  2.21 us (1%)
    all_to_all x4, blocking collectives, over_chips(): return lax.all_to_all(v, 'chip', 0, 0)  74.7 us
    ppermute x12, starting transfers between devices, sum_four(): lax.ppermute(x, axis, [(i, partner(i)) for i in range(lax.axis_size(axis))])  17.8 us
    pallas_call x16, Pallas kernels, call(): pl.pallas_call(kernel, out_shape=[jax.ShapeDtypeStruct(s, d) for s, d in...  15 us
    ppermute x6, starting transfers between devices, ahead_by(): return lax.ppermute(v, 'tp', [(i, (i + k) % peers) for i in range(peers)])  9.19 us
    ppermute x12, waiting for transfers between devices, sum_four(): lax.ppermute(x, axis, [(i, partner(i)) for i in range(lax.axis_size(axis))])  7.16 us
    ppermute x6, waiting for transfers between devices, ahead_by(): return lax.ppermute(v, 'tp', [(i, (i + k) % peers) for i in range(peers)])  4.79 us
    ppermute x5, waiting for transfers between devices, swap_cores(): return lax.ppermute(v, 'core', [(0, 1), (1, 0)])  4.29 us
    ppermute x1, waiting for transfers between devices, fold(): lax.ppermute(x, axis, [(i, partner(i)) for i in range(lax.axis_size(axis))])  3.76 us
  transfers between devices with their start and end apart: 26, of which 17 were waited for; matrix products, arithmetic and copies ran while one was open for 0% of the time, Pallas kernels for 4%

profile of v5, /device:TPU:32, one launch (start us, length us, event | category | flops | bytes accessed | tf_op | source)
XLA Modules:
  0.0 149.1 jit_solution(14398987898262443731)
XLA Ops:
  0.7 0.7 slice-done
  1.5 2.1 %collective-permute-start = (bf16[16,2048]{1,0:T(8,128)(2,1)S(1)}, bf16[16,2048]{1,0:T(8,128)(2,1)S(1)}, u32[]{:S(2)}, u32[]{:S(2)}) collective-permute-start(bf16[16,2048]{1,0:T(8,128)(2,1)S(1)} %pad_maximum_fusion), channel_id=1, source_target_pairs={{0,4},{4,8},{8,12},{12,16},{16,20},{20,24},{24,28},{28,32},{32,36}... | collective-permute-start | bytes 196616 | tf_op jit(solution)/shard_map/ppermute | solution.py:446
  3.6 0.4 steps.1
  4.0 3.1 %collective-permute-done.before = bf16[16,2048]{1,0:T(8,128)(2,1)S(1)} collective-permute-done((bf16[16,2048]{1,0:T(8,128)(2,1)S(1)}, bf16[16,2048]{1,0:T(8,128)(2,1)S(1)}, u32[]{:S(2)}, u32[]{:S(2)}) %collective-permute-start) | collective-permute-done | bytes 65568 | tf_op jit(solution)/shard_map/ppermute | solution.py:446
  7.2 1.2 state.1
  8.4 0.1 collective-permute-start.1
  8.5 1.5 %collective-permute-done.1.got = f32[544,128]{1,0:T(8,128)S(1)} collective-permute-done((f32[544,128]{1,0:T(8,128)S(1)}, f32[544,128]{1,0:T(8,128)S(1)}, u32[]{:S(2)}, u32[]{:S(2)}) %collective-permute-start.1) | collective-permute-done | bytes 278560 | tf_op jit(solution)/shard_map/ppermute | solution.py:403
  10.1 0.2 join.2
  10.3 25.1 %all_to_all.20.s.d = f32[32,1,2176]{2,1,0:T(1,128)S(1)} all-to-all(f32[32,1,2176]{2,1,0:T(1,128)S(1)} %get-tuple-element.89), channel_id=1, replica_groups=mesh['chip'=32,'core'=2,'tp'=4] {'chip'}, dimensions={0} | all-to-all | bytes 557056 | tf_op jit(solution)/shard_map/all_to_all | solution.py:411
  35.4 0.2 block_scan.2
  35.6 16.4 %all_to_all.21 = f32[32,1,2048]{2,1,0:T(1,128)S(1)} all-to-all(f32[32,1,2048]{2,1,0:T(1,128)S(1)} %block_scan.2), channel_id=1, replica_groups=mesh['chip'=32,'core'=2,'tp'=4] {'chip'}, dimensions={0} | all-to-all | bytes 524288 | tf_op jit(solution)/shard_map/all_to_all | solution.py:411
  52.0 0.1 split.2
  52.1 0.1 collective-permute-start.2
  52.2 0.8 copy-done.3
  52.9 0.1 copy-done.4
  53.0 0.3 turn.1
  53.4 0.6 copy-done.1
  53.9 2.3 %local.1 = (f32[128,512]{1,0:T(8,128)S(1)}, f32[512,128]{1,0:T(8,128)S(1)}, f32[1024,128]{1,0:T(8,128)S(1)}) custom-call(bf16[128,512]{1,0:T(8,128)(2,1)S(1)} %copy-done.1, bf16[16,2048]{1,0:T(8,128)(2,1)S(1)} %collective-permute-done.before, f32[4,512]{1,0:T(4,128)S(1)} %copy-done.6, f32[128,512]{1,0:T(8,128)S(1)} %get-tuple-element.93.bc, ...), custom_call_target="tpu_custom_call" | custom-call | flops 20000000 | bytes 4194304 | tf_op jit(solution)/shard_map/local/pallas_call | solution.py:390
  56.2 0.8 output.1
  57.0 3.3 %collective-permute-start.4 = (f32[8,128]{1,0:T(8,128)S(1)}, f32[8,128]{1,0:T(8,128)S(1)}, u32[]{:S(2)}, u32[]{:S(2)}) collective-permute-start(f32[8,128]{1,0:T(8,128)S(1)} %get-tuple-element.101), channel_id=1, source_target_pairs={{0,2},{1,3},{2,0},{3,1},{4,6},{5,7},{6,4},{7,5},{8,10},{9,11},{10,... | collective-permute-start | bytes 12296 | tf_op jit(solution)/shard_map/ppermute | solution.py:420
  60.2 1.1 collective-permute-start.5
  61.3 0.9 collective-permute-done.4
  62.2 2.9 %collective-permute-done.5 = f32[8,128]{1,0:T(8,128)S(1)} collective-permute-done((f32[8,128]{1,0:T(8,128)S(1)}, f32[8,128]{1,0:T(8,128)S(1)}, u32[]{:S(2)}, u32[]{:S(2)}) %collective-permute-start.5) | collective-permute-done | bytes 4128 | tf_op jit(solution)/shard_map/ppermute | solution.py:420
  65.1 0.9 gate.1
  65.9 0.1 collective-permute-start.6
  66.0 1.5 %collective-permute-done.6.got = f32[512,128]{1,0:T(8,128)S(1)} collective-permute-done((f32[512,128]{1,0:T(8,128)S(1)}, f32[512,128]{1,0:T(8,128)S(1)}, u32[]{:S(2)}, u32[]{:S(2)}) %collective-permute-start.6) | collective-permute-done | bytes 262176 | tf_op jit(solution)/shard_map/ppermute | solution.py:403
  67.6 0.1 join.3
  67.6 17.0 %all_to_all.22.s = f32[32,1,2048]{2,1,0:T(1,128)S(1)} all-to-all(f32[32,1,2048]{2,1,0:T(1,128)S(1)} %bitcast.17), channel_id=1, replica_groups=mesh['chip'=32,'core'=2,'tp'=4] {'chip'}, dimensions={0} | all-to-all | bytes 524288 | tf_op jit(solution)/shard_map/all_to_all | solution.py:411
  84.6 0.2 block_scan.3
  84.8 16.2 %all_to_all.23 = f32[32,1,2048]{2,1,0:T(1,128)S(1)} all-to-all(f32[32,1,2048]{2,1,0:T(1,128)S(1)} %block_scan.3), channel_id=1, replica_groups=mesh['chip'=32,'core'=2,'tp'=4] {'chip'}, dimensions={0} | all-to-all | bytes 524288 | tf_op jit(solution)/shard_map/all_to_all | solution.py:411
  101.0 0.1 split.3
  101.0 0.3 collective-permute-start.7
  101.3 3.4 %middle.1 = (f32[1024,128]{1,0:T(8,128)S(1)}, f32[128,512]{1,0:T(8,128)S(1)}, f32[32,128]{1,0:T(8,128)S(1)}, f32[32,128]{1,0:T(8,128)S(1)}, bf16[128,1024]{1,0:T...) custom-call(f32[8,128]{1,0:T(8,128)S(1)} %add_add_fusion.4.sums, f32[1024,128]{1,0:T(8,128)S(1)} %get-tuple-element.102.y, ...), custom_call_target="tpu_custom_call" | custom-call | flops 20000000 | bytes 4194304 | tf_op jit(solution)/shard_map/middle/pallas_call | solution.py:390
  104.7 3.5 %last.1 = (f32[128,1024]{1,0:T(8,128)S(1)}, f32[64,128]{1,0:T(8,128)S(1)}, f32[272,128]{1,0:T(8,128)S(1)}, f32[272,128]{1,0:T(8,128)S(1)}, f32[272,128]{1,0:T(8,...) custom-call(s32[1]{0:T(128)} %bitcast.core, s32[1]{0:T(128)} %bitcast.1.which, ...), custom_call_target="tpu_custom_call" | custom-call | flops 20000000 | bytes 4194304 | tf_op jit(solution)/shard_map/last/pallas_call | solution.py:390
  108.2 3.5 %collective-permute-start.9 = (f32[272,128]{1,0:T(8,128)S(1)}, f32[272,128]{1,0:T(8,128)S(1)}, u32[]{:S(2)}, u32[]{:S(2)}) collective-permute-start(f32[272,128]{1,0:T(8,128)S(1)} %get-tuple-element.123), channel_id=1, source_target_pairs={{0,2},{1,3},{2,0},{3,1},{4,6},{5,7},{6,4},{7,5},{8,10},{9,11},{10,... | collective-permute-start | bytes 417800 | tf_op jit(solution)/shard_map/ppermute | solution.py:540
  111.7 0.7 collective-permute-start.10
  112.4 1.2 collective-permute-done.11
  113.6 0.2 collective-permute-start.12
  113.8 3.8 %collective-permute-done.12 = f32[80,128]{1,0:T(8,128)S(1)} collective-permute-done((f32[80,128]{1,0:T(8,128)S(1)}, f32[80,128]{1,0:T(8,128)S(1)}, u32[]{:S(2)}, u32[]{:S(2)}) %collective-permute-start.12) | collective-permute-done | bytes 40992 | tf_op jit(solution)/shard_map/ppermute | solution.py:415
  117.6 1.1 collective-permute-done.9
  118.7 0.4 collective-permute-done.10
  119.1 1.6 %collective-permute-start.15 = (f32[80,128]{1,0:T(8,128)S(1)}, f32[80,128]{1,0:T(8,128)S(1)}, u32[]{:S(2)}, u32[]{:S(2)}) collective-permute-start(f32[80,128]{1,0:T(8,128)S(1)} %add.55), channel_id=1, source_target_pairs={{0,56},{8,48},{16,40},{24,32},{32,24},{40,16},{48,8},{56,0},{64,12... | collective-permute-start | bytes 122888 | tf_op jit(solution)/shard_map/ppermute | solution.py:420
  120.7 1.9 %collective-permute-start.16 = (f32[80,128]{1,0:T(8,128)S(1)}, f32[80,128]{1,0:T(8,128)S(1)}, u32[]{:S(2)}, u32[]{:S(2)}) collective-permute-start(f32[80,128]{1,0:T(8,128)S(1)} %add.55), channel_id=1, source_target_pairs={{0,40},{8,32},{16,56},{24,48},{32,8},{40,0},{48,24},{56,16},{64,10... | collective-permute-start | bytes 122888 | tf_op jit(solution)/shard_map/ppermute | solution.py:420
  122.7 2.9 %collective-permute-start.14 = (f32[80,128]{1,0:T(8,128)S(1)}, f32[80,128]{1,0:T(8,128)S(1)}, u32[]{:S(2)}, u32[]{:S(2)}) collective-permute-start(f32[80,128]{1,0:T(8,128)S(1)} %add.55), channel_id=1, source_target_pairs={{0,16},{8,24},{16,0},{24,8},{32,48},{40,56},{48,32},{56,40},{64,80... | collective-permute-start | bytes 122888 | tf_op jit(solution)/shard_map/ppermute | solution.py:420
  125.6 1.9 %collective-permute-start.13 = (f32[80,128]{1,0:T(8,128)S(1)}, f32[80,128]{1,0:T(8,128)S(1)}, u32[]{:S(2)}, u32[]{:S(2)}) collective-permute-start(f32[80,128]{1,0:T(8,128)S(1)} %pad_maximum_fusion.1), channel_id=1, source_target_pairs={{4,0},{8,4},{12,8},{16,12},{20,16},{24,20},{28,24},{32,28},{36,32}... | collective-permute-start | bytes 122888 | tf_op jit(solution)/shard_map/ppermute | solution.py:548
  127.6 0.3 collective-permute-done.16
  127.9 0.1 collective-permute-done.14
  128.0 1.2 collective-permute-done.13.heads
  129.2 0.8 settle.1
  130.0 1.3 collective-permute-start.21
  131.3 2.0 %collective-permute-start.22 = (f32[80,128]{1,0:T(8,128)S(1)}, f32[80,128]{1,0:T(8,128)S(1)}, u32[]{:S(2)}, u32[]{:S(2)}) collective-permute-start(f32[80,128]{1,0:T(8,128)S(1)} %add_add_fusion.2), channel_id=1, source_target_pairs={{0,192},{8,200},{16,208},{24,216},{32,224},{40,232},{48,240},{56,2... | collective-permute-start | bytes 122888 | tf_op jit(solution)/shard_map/ppermute | solution.py:420
  133.3 0.2 collective-permute-start.20
  133.5 0.9 collective-permute-start.17
  134.4 3.2 %collective-permute-start.18 = (bf16[256,128]{1,0:T(8,128)(2,1)S(1)}, bf16[256,128]{1,0:T(8,128)(2,1)S(1)}, u32[]{:S(2)}, u32[]{:S(2)}) collective-permute-start(bf16[256,128]{1,0:T(8,128)(2,1)S(1)} %get-tuple-element.135.own), channel_id=1, source_target_pairs={{0,2},{1,3},{2,0},{3,1},{4,6},{5,7},{6,4},{7,5},{8,10},{9,11},{10,... | collective-permute-start | bytes 196616 | tf_op jit(solution)/shard_map/ppermute | solution.py:540
  137.6 0.9 collective-permute-start.19
  138.5 0.4 collective-permute-done.17.one
  138.9 2.2 %collective-permute-done.18.two = bf16[256,128]{1,0:T(8,128)(2,1)S(1)} collective-permute-done((bf16[256,128]{1,0:T(8,128)(2,1)S(1)}, bf16[256,128]{1,0:T(8,128)(2,1)S(1)}, u32[]{:S(2)}, u32[]{:S(2)}) %collective-permute-start.18) | collective-permute-done | bytes 65568 | tf_op jit(solution)/shard_map/ppermute | solution.py:540
  141.1 0.7 collective-permute-done.19.three
  141.9 1.5 %collective-permute-start.24 = (f32[32,128]{1,0:T(8,128)S(1)}, f32[32,128]{1,0:T(8,128)S(1)}, u32[]{:S(2)}, u32[]{:S(2)}) collective-permute-start(f32[32,128]{1,0:T(8,128)S(1)} %slice.19), channel_id=1, source_target_pairs={{0,2},{1,3},{2,0},{3,1},{4,6},{5,7},{6,4},{7,5},{8,10},{9,11},{10,... | collective-permute-start | bytes 49160 | tf_op jit(solution)/shard_map/ppermute | solution.py:420
  143.4 1.2 collective-permute-start.25
  144.5 0.8 collective-permute-start.23
  145.3 1.8 %collective-permute-done.24 = f32[32,128]{1,0:T(8,128)S(1)} collective-permute-done((f32[32,128]{1,0:T(8,128)S(1)}, f32[32,128]{1,0:T(8,128)S(1)}, u32[]{:S(2)}, u32[]{:S(2)}) %collective-permute-start.24) | collective-permute-done | bytes 16416 | tf_op jit(solution)/shard_map/ppermute | solution.py:420
  147.1 1.2 collective-permute-done.25
  148.3 0.8 finish.1
  (51 shorter events, 0.2 us)
Async XLA Ops:
  0.6 0.8 slice-start
  0.7 0.8 slice-start.1
  0.7 0.7 slice-start.2
  1.4 2.1 %copy-start.10 = (f32[32]{0:T(128)S(1)}, f32[32]{0:T(128)}, u32[]{:S(2)}) copy-start(f32[32]{0:T(128)} %param.21) | copy-start | bytes 388
  1.4 2.1 %copy-start.11 = (f32[32]{0:T(128)S(1)}, f32[32]{0:T(128)}, u32[]{:S(2)}) copy-start(f32[32]{0:T(128)} %param.22) | copy-start | bytes 388
  1.4 2.1 %copy-start.12 = (f32[32]{0:T(128)S(1)}, f32[32]{0:T(128)}, u32[]{:S(2)}) copy-start(f32[32]{0:T(128)} %param.23) | copy-start | bytes 388
  1.4 2.1 %copy-start.9 = (f32[128,32]{0,1:T(8,128)S(1)}, f32[128,32]{0,1:T(8,128)}, u32[]{:S(2)}) copy-start(f32[128,32]{0,1:T(8,128)} %param.17) | copy-start | bytes 49156
  1.5 5.7 %collective-permute-start = (bf16[16,2048]{1,0:T(8,128)(2,1)S(1)}, bf16[16,2048]{1,0:T(8,128)(2,1)S(1)}, u32[]{:S(2)}, u32[]{:S(2)}) collective-permute-start(bf16[16,2048]{1,0:T(8,128)(2,1)S(1)} %pad_maximum_fusion), channel_id=1, source_target_pairs={{0,4},{4,8},{8,12},{12,16},{16,20},{20,24},{24,28},{28,32},{32,36}... | collective-permute-start | bytes 196616 | tf_op jit(solution)/shard_map/ppermute | solution.py:446
  3.5 3.7 %copy-start = (bf16[128,1024]{1,0:T(8,128)(2,1)S(1)}, bf16[128,1024]{1,0:T(8,128)(2,1)}, u32[]{:S(2)}) copy-start(bf16[128,1024]{1,0:T(8,128)(2,1)} %x.3) | copy-start | bytes 786436
  3.6 3.6 %copy-start.2 = (bf16[128,512]{1,0:T(8,128)(2,1)S(1)}, bf16[128,512]{1,0:T(8,128)(2,1)}, u32[]{:S(2)}) copy-start(bf16[128,512]{1,0:T(8,128)(2,1)} %b.3) | copy-start | bytes 393220
  3.6 3.6 %copy-start.5 = (f32[4,1024]{1,0:T(4,128)S(1)}, f32[4,1024]{1,0:T(4,128)}, u32[]{:S(2)}) copy-start(f32[4,1024]{1,0:T(4,128)} %wx.3) | copy-start | bytes 49156
  3.6 3.6 %copy-start.7 = (f32[4,512]{1,0:T(4,128)S(1)}, f32[4,512]{1,0:T(4,128)}, u32[]{:S(2)}) copy-start(f32[4,512]{1,0:T(4,128)} %wb.3) | copy-start | bytes 24580
  8.4 1.6 %collective-permute-start.1 = (f32[544,128]{1,0:T(8,128)S(1)}, f32[544,128]{1,0:T(8,128)S(1)}, u32[]{:S(2)}, u32[]{:S(2)}) collective-permute-start(f32[544,128]{1,0:T(8,128)S(1)} %get-tuple-element.88), channel_id=1, source_target_pairs={{0,4},{4,0},{1,5},{5,1},{2,6},{6,2},{3,7},{7,3},{8,12},{12,8},{9,1... | collective-permute-start | bytes 835592 | tf_op jit(solution)/shard_map/ppermute | solution.py:403
  52.0 1.0 copy-start.3
  52.0 1.0 copy-start.4
  52.0 1.0 copy-start.8
  52.1 4.1 %collective-permute-start.2 = (f32[512,128]{1,0:T(8,128)S(1)}, f32[512,128]{1,0:T(8,128)S(1)}, u32[]{:S(2)}, u32[]{:S(2)}) collective-permute-start(f32[512,128]{1,0:T(8,128)S(1)} %get-tuple-element.92), channel_id=1, source_target_pairs={{0,4},{4,0},{1,5},{5,1},{2,6},{6,2},{3,7},{7,3},{8,12},{12,8},{9,1... | collective-permute-start | bytes 786440 | tf_op jit(solution)/shard_map/ppermute | solution.py:403
  53.0 0.9 copy-start.1
  53.0 0.9 copy-start.6
  57.0 5.2 %collective-permute-start.4 = (f32[8,128]{1,0:T(8,128)S(1)}, f32[8,128]{1,0:T(8,128)S(1)}, u32[]{:S(2)}, u32[]{:S(2)}) collective-permute-start(f32[8,128]{1,0:T(8,128)S(1)} %get-tuple-element.101), channel_id=1, source_target_pairs={{0,2},{1,3},{2,0},{3,1},{4,6},{5,7},{6,4},{7,5},{8,10},{9,11},{10,... | collective-permute-start | bytes 12296 | tf_op jit(solution)/shard_map/ppermute | solution.py:420
  60.2 4.8 %collective-permute-start.5 = (f32[8,128]{1,0:T(8,128)S(1)}, f32[8,128]{1,0:T(8,128)S(1)}, u32[]{:S(2)}, u32[]{:S(2)}) collective-permute-start(f32[8,128]{1,0:T(8,128)S(1)} %get-tuple-element.101), channel_id=1, source_target_pairs={{0,3},{1,2},{2,1},{3,0},{4,7},{5,6},{6,5},{7,4},{8,11},{9,10},{10,... | collective-permute-start | bytes 12296 | tf_op jit(solution)/shard_map/ppermute | solution.py:420
  61.3 3.8 %collective-permute-start.3 = (f32[8,128]{1,0:T(8,128)S(1)}, f32[8,128]{1,0:T(8,128)S(1)}, u32[]{:S(2)}, u32[]{:S(2)}) collective-permute-start(f32[8,128]{1,0:T(8,128)S(1)} %get-tuple-element.101), channel_id=1, source_target_pairs={{0,1},{1,0},{2,3},{3,2},{4,5},{5,4},{6,7},{7,6},{8,9},{9,8},{10,11... | collective-permute-start | bytes 12296 | tf_op jit(solution)/shard_map/ppermute | solution.py:420
  65.9 1.6 %collective-permute-start.6 = (f32[512,128]{1,0:T(8,128)S(1)}, f32[512,128]{1,0:T(8,128)S(1)}, u32[]{:S(2)}, u32[]{:S(2)}) collective-permute-start(f32[512,128]{1,0:T(8,128)S(1)} %get-tuple-element.104), channel_id=1, source_target_pairs={{0,4},{4,0},{1,5},{5,1},{2,6},{6,2},{3,7},{7,3},{8,12},{12,8},{9,1... | collective-permute-start | bytes 786440 | tf_op jit(solution)/shard_map/ppermute | solution.py:403
  101.0 3.7 %collective-permute-start.7 = (f32[512,128]{1,0:T(8,128)S(1)}, f32[512,128]{1,0:T(8,128)S(1)}, u32[]{:S(2)}, u32[]{:S(2)}) collective-permute-start(f32[512,128]{1,0:T(8,128)S(1)} %get-tuple-element.106), channel_id=1, source_target_pairs={{0,4},{4,0},{1,5},{5,1},{2,6},{6,2},{3,7},{7,3},{8,12},{12,8},{9,1... | collective-permute-start | bytes 786440 | tf_op jit(solution)/shard_map/ppermute | solution.py:403
  108.2 9.4 %collective-permute-start.8 = (f32[272,128]{1,0:T(8,128)S(1)}, f32[272,128]{1,0:T(8,128)S(1)}, u32[]{:S(2)}, u32[]{:S(2)}) collective-permute-start(f32[272,128]{1,0:T(8,128)S(1)} %get-tuple-element.122), channel_id=1, source_target_pairs={{0,1},{1,2},{2,3},{3,0},{4,5},{5,6},{6,7},{7,4},{8,9},{9,10},{10,1... | collective-permute-start | bytes 417800 | tf_op jit(solution)/shard_map/ppermute | solution.py:540
  108.2 10.5 %collective-permute-start.9 = (f32[272,128]{1,0:T(8,128)S(1)}, f32[272,128]{1,0:T(8,128)S(1)}, u32[]{:S(2)}, u32[]{:S(2)}) collective-permute-start(f32[272,128]{1,0:T(8,128)S(1)} %get-tuple-element.123), channel_id=1, source_target_pairs={{0,2},{1,3},{2,0},{3,1},{4,6},{5,7},{6,4},{7,5},{8,10},{9,11},{10,... | collective-permute-start | bytes 417800 | tf_op jit(solution)/shard_map/ppermute | solution.py:540
  111.7 7.4 %collective-permute-start.10 = (f32[272,128]{1,0:T(8,128)S(1)}, f32[272,128]{1,0:T(8,128)S(1)}, u32[]{:S(2)}, u32[]{:S(2)}) collective-permute-start(f32[272,128]{1,0:T(8,128)S(1)} %get-tuple-element.124), channel_id=1, source_target_pairs={{0,3},{1,0},{2,1},{3,2},{4,7},{5,4},{6,5},{7,6},{8,11},{9,8},{10,9... | collective-permute-start | bytes 417800 | tf_op jit(solution)/shard_map/ppermute | solution.py:540
  112.4 1.2 collective-permute-start.11
  113.6 4.0 %collective-permute-start.12 = (f32[80,128]{1,0:T(8,128)S(1)}, f32[80,128]{1,0:T(8,128)S(1)}, u32[]{:S(2)}, u32[]{:S(2)}) collective-permute-start(f32[80,128]{1,0:T(8,128)S(1)} %add.54), channel_id=1, source_target_pairs={{0,8},{8,0},{16,24},{24,16},{32,40},{40,32},{48,56},{56,48},{64,72... | collective-permute-start | bytes 122888 | tf_op jit(solution)/shard_map/ppermute | solution.py:415
  119.1 8.5 %collective-permute-start.15 = (f32[80,128]{1,0:T(8,128)S(1)}, f32[80,128]{1,0:T(8,128)S(1)}, u32[]{:S(2)}, u32[]{:S(2)}) collective-permute-start(f32[80,128]{1,0:T(8,128)S(1)} %add.55), channel_id=1, source_target_pairs={{0,56},{8,48},{16,40},{24,32},{32,24},{40,16},{48,8},{56,0},{64,12... | collective-permute-start | bytes 122888 | tf_op jit(solution)/shard_map/ppermute | solution.py:420
  120.7 7.2 %collective-permute-start.16 = (f32[80,128]{1,0:T(8,128)S(1)}, f32[80,128]{1,0:T(8,128)S(1)}, u32[]{:S(2)}, u32[]{:S(2)}) collective-permute-start(f32[80,128]{1,0:T(8,128)S(1)} %add.55), channel_id=1, source_target_pairs={{0,40},{8,32},{16,56},{24,48},{32,8},{40,0},{48,24},{56,16},{64,10... | collective-permute-start | bytes 122888 | tf_op jit(solution)/shard_map/ppermute | solution.py:420
  122.7 5.4 %collective-permute-start.14 = (f32[80,128]{1,0:T(8,128)S(1)}, f32[80,128]{1,0:T(8,128)S(1)}, u32[]{:S(2)}, u32[]{:S(2)}) collective-permute-start(f32[80,128]{1,0:T(8,128)S(1)} %add.55), channel_id=1, source_target_pairs={{0,16},{8,24},{16,0},{24,8},{32,48},{40,56},{48,32},{56,40},{64,80... | collective-permute-start | bytes 122888 | tf_op jit(solution)/shard_map/ppermute | solution.py:420
  125.6 3.6 %collective-permute-start.13 = (f32[80,128]{1,0:T(8,128)S(1)}, f32[80,128]{1,0:T(8,128)S(1)}, u32[]{:S(2)}, u32[]{:S(2)}) collective-permute-start(f32[80,128]{1,0:T(8,128)S(1)} %pad_maximum_fusion.1), channel_id=1, source_target_pairs={{4,0},{8,4},{12,8},{16,12},{20,16},{24,20},{28,24},{32,28},{36,32}... | collective-permute-start | bytes 122888 | tf_op jit(solution)/shard_map/ppermute | solution.py:548
  130.0 7.6 %collective-permute-start.21 = (f32[80,128]{1,0:T(8,128)S(1)}, f32[80,128]{1,0:T(8,128)S(1)}, u32[]{:S(2)}, u32[]{:S(2)}) collective-permute-start(f32[80,128]{1,0:T(8,128)S(1)} %add_add_fusion.2), channel_id=1, source_target_pairs={{0,128},{8,136},{16,144},{24,152},{32,160},{40,168},{48,176},{56,1... | collective-permute-start | bytes 122888 | tf_op jit(solution)/shard_map/ppermute | solution.py:420
  131.3 7.2 %collective-permute-start.22 = (f32[80,128]{1,0:T(8,128)S(1)}, f32[80,128]{1,0:T(8,128)S(1)}, u32[]{:S(2)}, u32[]{:S(2)}) collective-permute-start(f32[80,128]{1,0:T(8,128)S(1)} %add_add_fusion.2), channel_id=1, source_target_pairs={{0,192},{8,200},{16,208},{24,216},{32,224},{40,232},{48,240},{56,2... | collective-permute-start | bytes 122888 | tf_op jit(solution)/shard_map/ppermute | solution.py:420
  133.3 5.2 %collective-permute-start.20 = (f32[80,128]{1,0:T(8,128)S(1)}, f32[80,128]{1,0:T(8,128)S(1)}, u32[]{:S(2)}, u32[]{:S(2)}) collective-permute-start(f32[80,128]{1,0:T(8,128)S(1)} %add_add_fusion.2), channel_id=1, source_target_pairs={{0,64},{8,72},{16,80},{24,88},{32,96},{40,104},{48,112},{56,120},{... | collective-permute-start | bytes 122888 | tf_op jit(solution)/shard_map/ppermute | solution.py:420
  133.5 5.5 %collective-permute-start.17 = (bf16[256,128]{1,0:T(8,128)(2,1)S(1)}, bf16[256,128]{1,0:T(8,128)(2,1)S(1)}, u32[]{:S(2)}, u32[]{:S(2)}) collective-permute-start(bf16[256,128]{1,0:T(8,128)(2,1)S(1)} %get-tuple-element.135.own), channel_id=1, source_target_pairs={{0,1},{1,2},{2,3},{3,0},{4,5},{5,6},{6,7},{7,4},{8,9},{9,10},{10,1... | collective-permute-start | bytes 196616 | tf_op jit(solution)/shard_map/ppermute | solution.py:540
  134.4 6.7 %collective-permute-start.18 = (bf16[256,128]{1,0:T(8,128)(2,1)S(1)}, bf16[256,128]{1,0:T(8,128)(2,1)S(1)}, u32[]{:S(2)}, u32[]{:S(2)}) collective-permute-start(bf16[256,128]{1,0:T(8,128)(2,1)S(1)} %get-tuple-element.135.own), channel_id=1, source_target_pairs={{0,2},{1,3},{2,0},{3,1},{4,6},{5,7},{6,4},{7,5},{8,10},{9,11},{10,... | collective-permute-start | bytes 196616 | tf_op jit(solution)/shard_map/ppermute | solution.py:540
  137.6 4.3 %collective-permute-start.19 = (bf16[256,128]{1,0:T(8,128)(2,1)S(1)}, bf16[256,128]{1,0:T(8,128)(2,1)S(1)}, u32[]{:S(2)}, u32[]{:S(2)}) collective-permute-start(bf16[256,128]{1,0:T(8,128)(2,1)S(1)} %get-tuple-element.135.own), channel_id=1, source_target_pairs={{0,3},{1,0},{2,1},{3,2},{4,7},{5,4},{6,5},{7,6},{8,11},{9,8},{10,9... | collective-permute-start | bytes 196616 | tf_op jit(solution)/shard_map/ppermute | solution.py:540
  141.9 5.2 %collective-permute-start.24 = (f32[32,128]{1,0:T(8,128)S(1)}, f32[32,128]{1,0:T(8,128)S(1)}, u32[]{:S(2)}, u32[]{:S(2)}) collective-permute-start(f32[32,128]{1,0:T(8,128)S(1)} %slice.19), channel_id=1, source_target_pairs={{0,2},{1,3},{2,0},{3,1},{4,6},{5,7},{6,4},{7,5},{8,10},{9,11},{10,... | collective-permute-start | bytes 49160 | tf_op jit(solution)/shard_map/ppermute | solution.py:420
  143.4 4.9 %collective-permute-start.25 = (f32[32,128]{1,0:T(8,128)S(1)}, f32[32,128]{1,0:T(8,128)S(1)}, u32[]{:S(2)}, u32[]{:S(2)}) collective-permute-start(f32[32,128]{1,0:T(8,128)S(1)} %slice.19), channel_id=1, source_target_pairs={{0,3},{1,2},{2,1},{3,0},{4,7},{5,6},{6,5},{7,4},{8,11},{9,10},{10,... | collective-permute-start | bytes 49160 | tf_op jit(solution)/shard_map/ppermute | solution.py:420
  144.5 3.8 %collective-permute-start.23 = (f32[32,128]{1,0:T(8,128)S(1)}, f32[32,128]{1,0:T(8,128)S(1)}, u32[]{:S(2)}, u32[]{:S(2)}) collective-permute-start(f32[32,128]{1,0:T(8,128)S(1)} %slice.19), channel_id=1, source_target_pairs={{0,1},{1,0},{2,3},{3,2},{4,5},{5,4},{6,7},{7,6},{8,9},{9,8},{10,11... | collective-permute-start | bytes 49160 | tf_op jit(solution)/shard_map/ppermute | solution.py:420

commit v6 on v4

--- a/solution.py
+++ b/solution.py
@@ -453,6 +453,7 @@
         (dt_raw.T, dt_bias[None], a_log[None], d_skip[None]),
     )
     zt, ogt, sgt = call(turn_kernel, "turn", [t_shape] * 3, (z_gate, grad_out, gain[None]))
+    before, zt, ogt, sgt = lax.optimization_barrier((before, zt, ogt, sgt))
     xt, zs, bc, keep, give = call(
         state_kernel,
         "state",
@@ -544,12 +545,10 @@
     mine = keep + arrived
     arrived = lax.ppermute(mine, "tp", [(i, i ^ 1) for i in range(peers)])
     packed = fold(packed, "chip", mirror(RING))
-    arrived, packed = lax.optimization_barrier((arrived, packed))
     mine = mine + arrived
     heads = jnp.concatenate([xheads, mine[:, 2 * SPAN :].reshape(32, TILE)], axis=0)
+    mine, heads, packed = lax.optimization_barrier((mine, heads, packed))
     heads = lax.ppermute(heads, CTX, [(i + 1, i) for i in range(size - 1)])
-    packed = sum_four(packed, "chip", RING)
-    heads, packed = lax.optimization_barrier((heads, packed))
     grad_x_raw, half = call(
         settle_kernel,
         "settle",
@@ -558,6 +557,8 @@
     )
     half, packed = lax.optimization_barrier((half, packed))
     other = lax.ppermute(half, "tp", across)
+    packed = sum_four(packed, "chip", RING)
+    other, packed = lax.optimization_barrier((other, packed))
     bc_taps = sum_four(packed[:32], "tp")
     half_bc, each = ((SPAN, wb), jnp.bfloat16), ((1, LOCAL), F32)
     grad_b_raw, grad_c_raw, conv_x_total, conv_b_total, conv_c_total, gain_total, *small = call(

time: 149 us -> 150 us (level)
  local copies, waits for them, and re-layouts: 2.86 us -> 5.15 us
  blocking collectives: 74.7 us -> 72.9 us
    ppermute x1, waiting for transfers between devices: 2.47 us -> 0.01 us  [body(): before = lax.ppermute(tails, CTX, [(i, i + 1) for i in range(size - 1)])]
    unnamed x26, local copies, waits for them, and re-layouts: 2.11 us -> 4.4 us
    ppermute x5, starting transfers between devices: 0.76 us -> 2.77 us  [swap_cores(): return lax.ppermute(v, 'core', [(0, 1), (1, 0)])]
    ppermute x9, waiting for transfers between devices: 8.09 us -> 9.95 us  [sum_four(): lax.ppermute(x, axis, [(i, (i // block ^ k) * block + i % block) for i in...]
    all_to_all x4, blocking collectives: 74.7 us -> 72.9 us  [over_chips(): return lax.all_to_all(v, 'chip', 0, 0)]
    ppermute x1, waiting for transfers between devices: 0.01 us -> 1.73 us  [body(): heads = lax.ppermute(heads, CTX, [(i + 1, i) for i in range(size - 1)])]
  transfers between devices with their start and end apart: 22 -> 22, of which waited for: 14 -> 16; matrix products, arithmetic and copies ran while one was open for 0% -> 0% of each run, Pallas kernels for 4% -> 4%
where the time goes in v6:
time: 150 us
  blocking collectives  72.9 us (49%)
  waiting for transfers between devices  31.5 us (21%)
  starting transfers between devices  24.2 us (16%)
  Pallas kernels  14.8 us (10%)
  local copies, waits for them, and re-layouts  5.15 us (3%)
    all_to_all x4, blocking collectives, over_chips(): return lax.all_to_all(v, 'chip', 0, 0)  72.9 us
    pallas_call x16, Pallas kernels, call(): pl.pallas_call(kernel, out_shape=[jax.ShapeDtypeStruct(s, d) for s, d in...  14.8 us
    ppermute x3, waiting for transfers between devices, fold(): lax.ppermute(x, axis, [(i, partner(i)) for i in range(lax.axis_size(axis))])  13.1 us
    ppermute x9, starting transfers between devices, sum_four(): lax.ppermute(x, axis, [(i, (i // block ^ k) * block + i % block) for i in...  11.3 us
    ppermute x9, waiting for transfers between devices, sum_four(): lax.ppermute(x, axis, [(i, (i // block ^ k) * block + i % block) for i in...  9.95 us
    unnamed x26, local copies, waits for them, and re-layouts  4.4 us
    ppermute x5, waiting for transfers between devices, swap_cores(): return lax.ppermute(v, 'core', [(0, 1), (1, 0)])  3.73 us
  transfers between devices with their start and end apart: 22, of which 16 were waited for; matrix products, arithmetic and copies ran while one was open for 0% of the time, Pallas kernels for 4%

profile of v6, /device:TPU:32, one launch (start us, length us, event | category | flops | bytes accessed | tf_op | source)
XLA Modules:
  0.0 149.6 jit_solution(15526083365622972721)
XLA Ops:
  0.7 0.7 slice-done
  1.4 1.9 %collective-permute-start = (bf16[16,2048]{1,0:T(8,128)(2,1)S(1)}, bf16[16,2048]{1,0:T(8,128)(2,1)S(1)}, u32[]{:S(2)}, u32[]{:S(2)}) collective-permute-start(bf16[16,2048]{1,0:T(8,128)(2,1)S(1)} %pad_maximum_fusion), channel_id=1, source_target_pairs={{0,4},{4,8},{8,12},{12,16},{16,20},{20,24},{24,28},{28,32},{32,36}... | collective-permute-start | bytes 196616 | tf_op jit(solution)/shard_map/ppermute | solution.py:446
  3.4 0.7 copy-done.8
  4.1 0.9 copy-done.3
  5.0 0.9 copy-done.4
  6.0 0.3 turn.1
  6.3 0.4 copy-done.9
  6.7 0.4 steps.1
  7.1 0.1 copy-done
  7.3 0.3 copy-done.2
  7.6 0.2 copy-done.7
  7.9 1.2 state.1
  9.1 2.1 %collective-permute-start.1 = (f32[544,128]{1,0:T(8,128)S(1)}, f32[544,128]{1,0:T(8,128)S(1)}, u32[]{:S(2)}, u32[]{:S(2)}) collective-permute-start(f32[544,128]{1,0:T(8,128)S(1)} %get-tuple-element.91), channel_id=1, source_target_pairs={{0,4},{4,0},{1,5},{5,1},{2,6},{6,2},{3,7},{7,3},{8,12},{12,8},{9,1... | collective-permute-start | bytes 835592 | tf_op jit(solution)/shard_map/ppermute | solution.py:407
  11.2 1.2 collective-permute-done.1.got
  12.4 0.2 join.2
  12.6 23.2 %all_to_all.20.s.d = f32[32,1,2176]{2,1,0:T(1,128)S(1)} all-to-all(f32[32,1,2176]{2,1,0:T(1,128)S(1)} %get-tuple-element.92), channel_id=1, replica_groups=mesh['chip'=32,'core'=2,'tp'=4] {'chip'}, dimensions={0} | all-to-all | bytes 557056 | tf_op jit(solution)/shard_map/all_to_all | solution.py:415
  35.8 0.2 block_scan.2
  36.0 16.5 %all_to_all.21 = f32[32,1,2048]{2,1,0:T(1,128)S(1)} all-to-all(f32[32,1,2048]{2,1,0:T(1,128)S(1)} %block_scan.2), channel_id=1, replica_groups=mesh['chip'=32,'core'=2,'tp'=4] {'chip'}, dimensions={0} | all-to-all | bytes 524288 | tf_op jit(solution)/shard_map/all_to_all | solution.py:415
  52.5 0.1 split.2
  52.6 0.1 collective-permute-start.2
  52.7 0.7 copy-done.1
  53.4 2.3 %local.1 = (f32[128,512]{1,0:T(8,128)S(1)}, f32[512,128]{1,0:T(8,128)S(1)}, f32[1024,128]{1,0:T(8,128)S(1)}) custom-call(bf16[128,512]{1,0:T(8,128)(2,1)S(1)} %copy-done.1, bf16[16,2048]{1,0:T(8,128)(2,1)S(1)} %collective-permute-done.before, f32[4,512]{1,0:T(4,128)S(1)} %copy-done.6, f32[128,512]{1,0:T(8,128)S(1)} %get-tuple-element.96.bc, ...), custom_call_target="tpu_custom_call" | custom-call | flops 20000000 | bytes 4194304 | tf_op jit(solution)/shard_map/local/pallas_call | solution.py:394
  55.7 0.8 output.1
  56.5 3.3 %collective-permute-start.4 = (f32[8,128]{1,0:T(8,128)S(1)}, f32[8,128]{1,0:T(8,128)S(1)}, u32[]{:S(2)}, u32[]{:S(2)}) collective-permute-start(f32[8,128]{1,0:T(8,128)S(1)} %get-tuple-element.104), channel_id=1, source_target_pairs={{0,2},{1,3},{2,0},{3,1},{4,6},{5,7},{6,4},{7,5},{8,10},{9,11},{10,... | collective-permute-start | bytes 12296 | tf_op jit(solution)/shard_map/ppermute | solution.py:424
  59.7 1.1 collective-permute-start.5
  60.8 0.9 collective-permute-done.4
  61.7 2.9 %collective-permute-done.5 = f32[8,128]{1,0:T(8,128)S(1)} collective-permute-done((f32[8,128]{1,0:T(8,128)S(1)}, f32[8,128]{1,0:T(8,128)S(1)}, u32[]{:S(2)}, u32[]{:S(2)}) %collective-permute-start.5) | collective-permute-done | bytes 4128 | tf_op jit(solution)/shard_map/ppermute | solution.py:424
  64.6 0.9 gate.1
  65.4 0.1 collective-permute-start.6
  65.5 1.5 %collective-permute-done.6.got = f32[512,128]{1,0:T(8,128)S(1)} collective-permute-done((f32[512,128]{1,0:T(8,128)S(1)}, f32[512,128]{1,0:T(8,128)S(1)}, u32[]{:S(2)}, u32[]{:S(2)}) %collective-permute-start.6) | collective-permute-done | bytes 262176 | tf_op jit(solution)/shard_map/ppermute | solution.py:407
  67.1 17.0 %all_to_all.22.s = f32[32,1,2048]{2,1,0:T(1,128)S(1)} all-to-all(f32[32,1,2048]{2,1,0:T(1,128)S(1)} %bitcast.18), channel_id=1, replica_groups=mesh['chip'=32,'core'=2,'tp'=4] {'chip'}, dimensions={0} | all-to-all | bytes 524288 | tf_op jit(solution)/shard_map/all_to_all | solution.py:415
  84.1 0.2 block_scan.3
  84.3 16.2 %all_to_all.23 = f32[32,1,2048]{2,1,0:T(1,128)S(1)} all-to-all(f32[32,1,2048]{2,1,0:T(1,128)S(1)} %block_scan.3), channel_id=1, replica_groups=mesh['chip'=32,'core'=2,'tp'=4] {'chip'}, dimensions={0} | all-to-all | bytes 524288 | tf_op jit(solution)/shard_map/all_to_all | solution.py:415
  100.5 0.3 collective-permute-start.7
  100.8 3.4 %middle.1 = (f32[1024,128]{1,0:T(8,128)S(1)}, f32[128,512]{1,0:T(8,128)S(1)}, f32[32,128]{1,0:T(8,128)S(1)}, f32[32,128]{1,0:T(8,128)S(1)}, bf16[128,1024]{1,0:T...) custom-call(f32[8,128]{1,0:T(8,128)S(1)} %add_add_fusion.2.sums, f32[1024,128]{1,0:T(8,128)S(1)} %get-tuple-element.105.y, ...), custom_call_target="tpu_custom_call" | custom-call | flops 20000000 | bytes 4194304 | tf_op jit(solution)/shard_map/middle/pallas_call | solution.py:394
  104.2 3.2 %last.1 = (f32[128,1024]{1,0:T(8,128)S(1)}, f32[64,128]{1,0:T(8,128)S(1)}, f32[2,272,128]{2,1,0:T(8,128)S(1)}, f32[2,272,128]{2,1,0:T(8,128)S(1)}, f32[80,128]{1,0:T(8,128)S(1)}, /*index=5*/f32[32,128]{1,0:T(8,128)}) custom-call(s32[1]{0:T(128)} %bitcast.core, s32[1]{0:T(128)} %bitcast.1.which, f32[512,128]{1,0:T(8,128)S(1)} %get-tuple-element.108.own, ...), custom_call_target="tpu_custom_call" | custom-call | flops 20000000 | bytes 4194304 | tf_op jit(solution)/shard_map/last/pallas_call | solution.py:394
  107.4 2.1 %collective-permute-start.8 = (f32[2,272,128]{2,1,0:T(8,128)S(1)}, f32[2,272,128]{2,1,0:T(8,128)S(1)}, u32[]{:S(2)}, u32[]{:S(2)}) collective-permute-start(f32[2,272,128]{2,1,0:T(8,128)S(1)} %get-tuple-element.125), channel_id=1, source_target_pairs={{0,3},{1,2},{2,1},{3,0},{4,7},{5,6},{6,5},{7,4},{8,11},{9,10},{10,... | collective-permute-start | bytes 835592 | tf_op jit(solution)/shard_map/ppermute | solution.py:540
  109.5 0.2 collective-permute-start.9
  109.8 1.0 collective-permute-done.9
  110.8 0.2 collective-permute-start.10
  111.0 3.8 %collective-permute-done.10 = f32[80,128]{1,0:T(8,128)S(1)} collective-permute-done((f32[80,128]{1,0:T(8,128)S(1)}, f32[80,128]{1,0:T(8,128)S(1)}, u32[]{:S(2)}, u32[]{:S(2)}) %collective-permute-start.10) | collective-permute-done | bytes 40992 | tf_op jit(solution)/shard_map/ppermute | solution.py:419
  114.8 0.9 collective-permute-start.11
  115.7 4.0 %collective-permute-done.11 = f32[80,128]{1,0:T(8,128)S(1)} collective-permute-done((f32[80,128]{1,0:T(8,128)S(1)}, f32[80,128]{1,0:T(8,128)S(1)}, u32[]{:S(2)}, u32[]{:S(2)}) %collective-permute-start.11) | collective-permute-done | bytes 40992 | tf_op jit(solution)/shard_map/ppermute | solution.py:419
  119.7 0.1 collective-permute-start.12
  119.8 1.7 %collective-permute-start.13 = (f32[80,128]{1,0:T(8,128)S(1)}, f32[80,128]{1,0:T(8,128)S(1)}, u32[]{:S(2)}, u32[]{:S(2)}) collective-permute-start(f32[80,128]{1,0:T(8,128)S(1)} %add.51), channel_id=1, source_target_pairs={{0,56},{8,48},{16,40},{24,32},{32,24},{40,16},{48,8},{56,0},{64,12... | collective-permute-start | bytes 122888 | tf_op jit(solution)/shard_map/ppermute | solution.py:419
  121.6 5.4 %collective-permute-done.13 = f32[80,128]{1,0:T(8,128)S(1)} collective-permute-done((f32[80,128]{1,0:T(8,128)S(1)}, f32[80,128]{1,0:T(8,128)S(1)}, u32[]{:S(2)}, u32[]{:S(2)}) %collective-permute-start.13) | collective-permute-done | bytes 40992 | tf_op jit(solution)/shard_map/ppermute | solution.py:419
  127.0 1.9 %collective-permute-start.14 = (f32[96,128]{1,0:T(8,128)S(1)}, f32[96,128]{1,0:T(8,128)S(1)}, u32[]{:S(2)}, u32[]{:S(2)}) collective-permute-start(f32[96,128]{1,0:T(8,128)S(1)} %pad_maximum_fusion.1), channel_id=1, source_target_pairs={{4,0},{8,4},{12,8},{16,12},{20,16},{24,20},{28,24},{32,28},{36,32}... | collective-permute-start | bytes 147464 | tf_op jit(solution)/shard_map/ppermute | solution.py:551
  128.9 1.7 %collective-permute-done.14.heads = f32[96,128]{1,0:T(8,128)S(1)} collective-permute-done((f32[96,128]{1,0:T(8,128)S(1)}, f32[96,128]{1,0:T(8,128)S(1)}, u32[]{:S(2)}, u32[]{:S(2)}) %collective-permute-start.14) | collective-permute-done | bytes 49184 | tf_op jit(solution)/shard_map/ppermute | solution.py:551
  130.7 0.8 settle.1
  131.4 1.3 collective-permute-start.17
  132.7 2.0 %collective-permute-start.18 = (f32[80,128]{1,0:T(8,128)S(1)}, f32[80,128]{1,0:T(8,128)S(1)}, u32[]{:S(2)}, u32[]{:S(2)}) collective-permute-start(f32[80,128]{1,0:T(8,128)S(1)} %add.54), channel_id=1, source_target_pairs={{0,192},{8,200},{16,208},{24,216},{32,224},{40,232},{48,240},{56,2... | collective-permute-start | bytes 122888 | tf_op jit(solution)/shard_map/ppermute | solution.py:424
  134.7 0.2 collective-permute-start.16
  134.9 1.2 collective-permute-start.15
  136.2 1.1 collective-permute-done.17
  137.3 0.9 collective-permute-done.18
  138.2 0.5 collective-permute-done.16
  138.7 2.9 %collective-permute-done.15.other = bf16[2,256,128]{2,1,0:T(8,128)(2,1)S(1)} collective-permute-done((bf16[2,256,128]{2,1,0:T(8,128)(2,1)S(1)}, bf16[2,256,128]{2,1,0:T(8,128)(2,1)S(1)}, u32[]{:S(2)}, u32[]{:S(2)}) %collective-permute-start.15) | collective-permute-done | bytes 131104 | tf_op jit(solution)/shard_map/ppermute | solution.py:559
  141.7 1.4 collective-permute-start.20
  143.0 2.0 %collective-permute-start.21 = (f32[32,128]{1,0:T(8,128)S(1)}, f32[32,128]{1,0:T(8,128)S(1)}, u32[]{:S(2)}, u32[]{:S(2)}) collective-permute-start(f32[32,128]{1,0:T(8,128)S(1)} %slice.19), channel_id=1, source_target_pairs={{0,3},{1,2},{2,1},{3,0},{4,7},{5,6},{6,5},{7,4},{8,11},{9,10},{10,... | collective-permute-start | bytes 49160 | tf_op jit(solution)/shard_map/ppermute | solution.py:424
  145.0 0.1 collective-permute-start.19
  145.2 1.8 %collective-permute-done.20 = f32[32,128]{1,0:T(8,128)S(1)} collective-permute-done((f32[32,128]{1,0:T(8,128)S(1)}, f32[32,128]{1,0:T(8,128)S(1)}, u32[]{:S(2)}, u32[]{:S(2)}) %collective-permute-start.20) | collective-permute-done | bytes 16416 | tf_op jit(solution)/shard_map/ppermute | solution.py:424
  146.9 1.1 collective-permute-done.21
  148.0 0.8 collective-permute-done.19
  148.8 0.8 finish.1
  (45 shorter events, 0.3 us)
Async XLA Ops:
  0.6 0.8 slice-start
  0.7 0.8 slice-start.1
  0.7 0.7 slice-start.2
  1.4 5.7 %collective-permute-start = (bf16[16,2048]{1,0:T(8,128)(2,1)S(1)}, bf16[16,2048]{1,0:T(8,128)(2,1)S(1)}, u32[]{:S(2)}, u32[]{:S(2)}) collective-permute-start(bf16[16,2048]{1,0:T(8,128)(2,1)S(1)} %pad_maximum_fusion), channel_id=1, source_target_pairs={{0,4},{4,8},{8,12},{12,16},{16,20},{20,24},{24,28},{28,32},{32,36}... | collective-permute-start | bytes 196616 | tf_op jit(solution)/shard_map/ppermute | solution.py:446
  3.4 0.7 copy-start.8
  4.1 0.9 copy-start.3
  5.0 0.9 copy-start.4
  6.0 0.7 copy-start.9
  6.0 0.7 copy-start.10
  6.0 0.7 copy-start.11
  6.0 0.7 copy-start.12
  6.3 1.0 copy-start
  6.7 0.9 copy-start.2
  6.7 0.9 copy-start.5
  7.1 0.7 copy-start.7
  9.1 3.3 %collective-permute-start.1 = (f32[544,128]{1,0:T(8,128)S(1)}, f32[544,128]{1,0:T(8,128)S(1)}, u32[]{:S(2)}, u32[]{:S(2)}) collective-permute-start(f32[544,128]{1,0:T(8,128)S(1)} %get-tuple-element.91), channel_id=1, source_target_pairs={{0,4},{4,0},{1,5},{5,1},{2,6},{6,2},{3,7},{7,3},{8,12},{12,8},{9,1... | collective-permute-start | bytes 835592 | tf_op jit(solution)/shard_map/ppermute | solution.py:407
  52.5 0.9 copy-start.1
  52.6 0.8 copy-start.6
  52.6 3.1 %collective-permute-start.2 = (f32[512,128]{1,0:T(8,128)S(1)}, f32[512,128]{1,0:T(8,128)S(1)}, u32[]{:S(2)}, u32[]{:S(2)}) collective-permute-start(f32[512,128]{1,0:T(8,128)S(1)} %get-tuple-element.95), channel_id=1, source_target_pairs={{0,4},{4,0},{1,5},{5,1},{2,6},{6,2},{3,7},{7,3},{8,12},{12,8},{9,1... | collective-permute-start | bytes 786440 | tf_op jit(solution)/shard_map/ppermute | solution.py:407
  56.5 5.2 %collective-permute-start.4 = (f32[8,128]{1,0:T(8,128)S(1)}, f32[8,128]{1,0:T(8,128)S(1)}, u32[]{:S(2)}, u32[]{:S(2)}) collective-permute-start(f32[8,128]{1,0:T(8,128)S(1)} %get-tuple-element.104), channel_id=1, source_target_pairs={{0,2},{1,3},{2,0},{3,1},{4,6},{5,7},{6,4},{7,5},{8,10},{9,11},{10,... | collective-permute-start | bytes 12296 | tf_op jit(solution)/shard_map/ppermute | solution.py:424
  59.7 4.8 %collective-permute-start.5 = (f32[8,128]{1,0:T(8,128)S(1)}, f32[8,128]{1,0:T(8,128)S(1)}, u32[]{:S(2)}, u32[]{:S(2)}) collective-permute-start(f32[8,128]{1,0:T(8,128)S(1)} %get-tuple-element.104), channel_id=1, source_target_pairs={{0,3},{1,2},{2,1},{3,0},{4,7},{5,6},{6,5},{7,4},{8,11},{9,10},{10,... | collective-permute-start | bytes 12296 | tf_op jit(solution)/shard_map/ppermute | solution.py:424
  60.8 3.8 %collective-permute-start.3 = (f32[8,128]{1,0:T(8,128)S(1)}, f32[8,128]{1,0:T(8,128)S(1)}, u32[]{:S(2)}, u32[]{:S(2)}) collective-permute-start(f32[8,128]{1,0:T(8,128)S(1)} %get-tuple-element.104), channel_id=1, source_target_pairs={{0,1},{1,0},{2,3},{3,2},{4,5},{5,4},{6,7},{7,6},{8,9},{9,8},{10,11... | collective-permute-start | bytes 12296 | tf_op jit(solution)/shard_map/ppermute | solution.py:424
  65.4 1.6 %collective-permute-start.6 = (f32[512,128]{1,0:T(8,128)S(1)}, f32[512,128]{1,0:T(8,128)S(1)}, u32[]{:S(2)}, u32[]{:S(2)}) collective-permute-start(f32[512,128]{1,0:T(8,128)S(1)} %get-tuple-element.107), channel_id=1, source_target_pairs={{0,4},{4,0},{1,5},{5,1},{2,6},{6,2},{3,7},{7,3},{8,12},{12,8},{9,1... | collective-permute-start | bytes 786440 | tf_op jit(solution)/shard_map/ppermute | solution.py:407
  100.5 3.7 %collective-permute-start.7 = (f32[512,128]{1,0:T(8,128)S(1)}, f32[512,128]{1,0:T(8,128)S(1)}, u32[]{:S(2)}, u32[]{:S(2)}) collective-permute-start(f32[512,128]{1,0:T(8,128)S(1)} %get-tuple-element.109), channel_id=1, source_target_pairs={{0,4},{4,0},{1,5},{5,1},{2,6},{6,2},{3,7},{7,3},{8,12},{12,8},{9,1... | collective-permute-start | bytes 786440 | tf_op jit(solution)/shard_map/ppermute | solution.py:407
  107.4 12.3 %collective-permute-start.8 = (f32[2,272,128]{2,1,0:T(8,128)S(1)}, f32[2,272,128]{2,1,0:T(8,128)S(1)}, u32[]{:S(2)}, u32[]{:S(2)}) collective-permute-start(f32[2,272,128]{2,1,0:T(8,128)S(1)} %get-tuple-element.125), channel_id=1, source_target_pairs={{0,3},{1,2},{2,1},{3,0},{4,7},{5,6},{6,5},{7,4},{8,11},{9,10},{10,... | collective-permute-start | bytes 835592 | tf_op jit(solution)/shard_map/ppermute | solution.py:540
  109.5 1.2 collective-permute-start.9
  110.8 4.0 %collective-permute-start.10 = (f32[80,128]{1,0:T(8,128)S(1)}, f32[80,128]{1,0:T(8,128)S(1)}, u32[]{:S(2)}, u32[]{:S(2)}) collective-permute-start(f32[80,128]{1,0:T(8,128)S(1)} %add.49), channel_id=1, source_target_pairs={{0,8},{8,0},{16,24},{24,16},{32,40},{40,32},{48,56},{56,48},{64,72... | collective-permute-start | bytes 122888 | tf_op jit(solution)/shard_map/ppermute | solution.py:419
  114.8 4.9 %collective-permute-start.11 = (f32[80,128]{1,0:T(8,128)S(1)}, f32[80,128]{1,0:T(8,128)S(1)}, u32[]{:S(2)}, u32[]{:S(2)}) collective-permute-start(f32[80,128]{1,0:T(8,128)S(1)} %add.50), channel_id=1, source_target_pairs={{0,16},{8,24},{16,0},{24,8},{32,48},{40,56},{48,32},{56,40},{64,80... | collective-permute-start | bytes 122888 | tf_op jit(solution)/shard_map/ppermute | solution.py:419
  119.7 7.2 %collective-permute-start.12 = (f32[2,272,128]{2,1,0:T(8,128)S(1)}, f32[2,272,128]{2,1,0:T(8,128)S(1)}, u32[]{:S(2)}, u32[]{:S(2)}) collective-permute-start(f32[2,272,128]{2,1,0:T(8,128)S(1)} %add.52), channel_id=1, source_target_pairs={{0,1},{1,0},{2,3},{3,2},{4,5},{5,4},{6,7},{7,6},{8,9},{9,8},{10,11... | collective-permute-start | bytes 835592 | tf_op jit(solution)/shard_map/ppermute | solution.py:546
  119.8 7.1 %collective-permute-start.13 = (f32[80,128]{1,0:T(8,128)S(1)}, f32[80,128]{1,0:T(8,128)S(1)}, u32[]{:S(2)}, u32[]{:S(2)}) collective-permute-start(f32[80,128]{1,0:T(8,128)S(1)} %add.51), channel_id=1, source_target_pairs={{0,56},{8,48},{16,40},{24,32},{32,24},{40,16},{48,8},{56,0},{64,12... | collective-permute-start | bytes 122888 | tf_op jit(solution)/shard_map/ppermute | solution.py:419
  127.0 3.7 %collective-permute-start.14 = (f32[96,128]{1,0:T(8,128)S(1)}, f32[96,128]{1,0:T(8,128)S(1)}, u32[]{:S(2)}, u32[]{:S(2)}) collective-permute-start(f32[96,128]{1,0:T(8,128)S(1)} %pad_maximum_fusion.1), channel_id=1, source_target_pairs={{4,0},{8,4},{12,8},{16,12},{20,16},{24,20},{28,24},{32,28},{36,32}... | collective-permute-start | bytes 147464 | tf_op jit(solution)/shard_map/ppermute | solution.py:551
  131.4 5.9 %collective-permute-start.17 = (f32[80,128]{1,0:T(8,128)S(1)}, f32[80,128]{1,0:T(8,128)S(1)}, u32[]{:S(2)}, u32[]{:S(2)}) collective-permute-start(f32[80,128]{1,0:T(8,128)S(1)} %add.54), channel_id=1, source_target_pairs={{0,128},{8,136},{16,144},{24,152},{32,160},{40,168},{48,176},{56,1... | collective-permute-start | bytes 122888 | tf_op jit(solution)/shard_map/ppermute | solution.py:424
  132.7 5.5 %collective-permute-start.18 = (f32[80,128]{1,0:T(8,128)S(1)}, f32[80,128]{1,0:T(8,128)S(1)}, u32[]{:S(2)}, u32[]{:S(2)}) collective-permute-start(f32[80,128]{1,0:T(8,128)S(1)} %add.54), channel_id=1, source_target_pairs={{0,192},{8,200},{16,208},{24,216},{32,224},{40,232},{48,240},{56,2... | collective-permute-start | bytes 122888 | tf_op jit(solution)/shard_map/ppermute | solution.py:424
  134.7 4.0 %collective-permute-start.16 = (f32[80,128]{1,0:T(8,128)S(1)}, f32[80,128]{1,0:T(8,128)S(1)}, u32[]{:S(2)}, u32[]{:S(2)}) collective-permute-start(f32[80,128]{1,0:T(8,128)S(1)} %add.54), channel_id=1, source_target_pairs={{0,64},{8,72},{16,80},{24,88},{32,96},{40,104},{48,112},{56,120},{... | collective-permute-start | bytes 122888 | tf_op jit(solution)/shard_map/ppermute | solution.py:424
  134.9 6.7 %collective-permute-start.15 = (bf16[2,256,128]{2,1,0:T(8,128)(2,1)S(1)}, bf16[2,256,128]{2,1,0:T(8,128)(2,1)S(1)}, u32[]{:S(2)}, u32[]{:S(2)}) collective-permute-start(bf16[2,256,128]{2,1,0:T(8,128)(2,1)S(1)} %get-tuple-element.135.half), channel_id=1, source_target_pairs={{0,3},{1,2},{2,1},{3,0},{4,7},{5,6},{6,5},{7,4},{8,11},{9,10},{10,... | collective-permute-start | bytes 393224 | tf_op jit(solution)/shard_map/ppermute | solution.py:559
  141.7 5.2 %collective-permute-start.20 = (f32[32,128]{1,0:T(8,128)S(1)}, f32[32,128]{1,0:T(8,128)S(1)}, u32[]{:S(2)}, u32[]{:S(2)}) collective-permute-start(f32[32,128]{1,0:T(8,128)S(1)} %slice.19), channel_id=1, source_target_pairs={{0,2},{1,3},{2,0},{3,1},{4,6},{5,7},{6,4},{7,5},{8,10},{9,11},{10,... | collective-permute-start | bytes 49160 | tf_op jit(solution)/shard_map/ppermute | solution.py:424
  143.0 4.9 %collective-permute-start.21 = (f32[32,128]{1,0:T(8,128)S(1)}, f32[32,128]{1,0:T(8,128)S(1)}, u32[]{:S(2)}, u32[]{:S(2)}) collective-permute-start(f32[32,128]{1,0:T(8,128)S(1)} %slice.19), channel_id=1, source_target_pairs={{0,3},{1,2},{2,1},{3,0},{4,7},{5,6},{6,5},{7,4},{8,11},{9,10},{10,... | collective-permute-start | bytes 49160 | tf_op jit(solution)/shard_map/ppermute | solution.py:424
  145.0 3.7 %collective-permute-start.19 = (f32[32,128]{1,0:T(8,128)S(1)}, f32[32,128]{1,0:T(8,128)S(1)}, u32[]{:S(2)}, u32[]{:S(2)}) collective-permute-start(f32[32,128]{1,0:T(8,128)S(1)} %slice.19), channel_id=1, source_target_pairs={{0,1},{1,0},{2,3},{3,2},{4,5},{5,4},{6,7},{7,6},{8,9},{9,8},{10,11... | collective-permute-start | bytes 49160 | tf_op jit(solution)/shard_map/ppermute | solution.py:424

commit v7 on v6

--- a/solution.py
+++ b/solution.py
@@ -28,10 +28,21 @@
 PARAMS = pltpu.CompilerParams(vmem_limit_bytes=16 << 20)
 
 
-def dot(a, b, ca=1, cb=0):
+def exact(a, b, ca=1, cb=0):
     return lax.dot_general(
         a, b, (((ca,), (cb,)), ((), ())), precision=lax.Precision.HIGHEST, preferred_element_type=F32
     )
+
+
+def dot(a, b, ca=1, cb=0):
+    high_a, high_b = a.astype(jnp.bfloat16), b.astype(jnp.bfloat16)
+    low_a = (a - high_a.astype(F32)).astype(jnp.bfloat16)
+    low_b = (b - high_b.astype(F32)).astype(jnp.bfloat16)
+
+    def part(x, y):
+        return lax.dot_general(x, y, (((ca,), (cb,)), ((), ())), preferred_element_type=F32)
+
+    return part(high_a, high_b) + (part(high_a, low_b) + part(low_a, high_b))
 
 
 def group(g):
@@ -133,14 +144,14 @@
 
 def steps_kernel(raw, bias, alog, d_skip, dt, heads, step, cum, ends, skip):
     order = group_order()
-    dt[...] = dot(order, raw[...])
+    dt[...] = exact(order, raw[...])
     rows = jnp.concatenate([bias[...], alog[...], d_skip[...], jnp.zeros((5, LOCAL), F32)], axis=0)
-    heads[...] = dot(order, rows, 1, 1)
+    heads[...] = exact(order, rows, 1, 1)
     v = dt[...] + heads[:, 0:1]
     skip[...] = jnp.broadcast_to(heads[:, 2:3], skip.shape)
     step[...] = jnp.maximum(v, 0.0) + jnp.log1p(jnp.exp(-jnp.abs(v)))
     rates = -jnp.exp(heads[:, 1:2]) * step[...]
-    cum[...] = dot(rates, jnp.where(triangle(True), 1.0, 0.0))
+    cum[...] = exact(rates, jnp.where(triangle(True), 1.0, 0.0))
     ends[...] = jnp.broadcast_to(jnp.exp(jnp.sum(rates, axis=1, keepdims=True)), ends.shape)
 
 
@@ -278,16 +289,16 @@
         parts[g, 2 * SPAN + 8 : 2 * SPAN + 16, :] = cpart[g, SPAN : SPAN + 8, :]
         for k in range(CONV):
             packed[k * GROUPS + g : k * GROUPS + g + 1, :] = taps[k]
-    dlog = dot(jnp.concatenate(turned, axis=0), jnp.where(triangle(False), 1.0, 0.0))
+    dlog = exact(jnp.concatenate(turned, axis=0), jnp.where(triangle(False), 1.0, 0.0))
     rate = -jnp.exp(per_head[:, 1:2])
     dstep = jnp.concatenate(straight, axis=0) * gamma + dlog * rate
     draw = dstep * sigmoid(dt[...] + per_head[:, 0:1])
-    ddt[...] = dot(group_order(), draw, 0, 0)
+    ddt[...] = exact(group_order(), draw, 0, 0)
     each = jnp.concatenate([draw, dlog * rate * step[...], dskip[...], jnp.zeros((LOCAL, SPAN), F32)], axis=0)
     at = lax.broadcasted_iota(jnp.int32, (SPAN, SPAN), 0)
     to = lax.broadcasted_iota(jnp.int32, (SPAN, SPAN), 1)
     source = to // LOCAL * LOCAL + to % GROUPS * PER + to % LOCAL // GROUPS
-    packed[72:80, :] = dot(dot(jnp.ones((8, SPAN), F32), each, 1, 1), jnp.where(at == source, 1.0, 0.0))
+    packed[72:80, :] = exact(exact(jnp.ones((8, SPAN), F32), each, 1, 1), jnp.where(at == source, 1.0, 0.0))
     packed[16:32, :] = early[0:16, :]
     packed[64:72, :] = early[16:24, :]
     side = which[0]
@@ -558,7 +569,6 @@
     half, packed = lax.optimization_barrier((half, packed))
     other = lax.ppermute(half, "tp", across)
     packed = sum_four(packed, "chip", RING)
-    other, packed = lax.optimization_barrier((other, packed))
     bc_taps = sum_four(packed[:32], "tp")
     half_bc, each = ((SPAN, wb), jnp.bfloat16), ((1, LOCAL), F32)
     grad_b_raw, grad_c_raw, conv_x_total, conv_b_total, conv_c_total, gain_total, *small = call(

time: 150 us -> 150 us (level); the launches traced: 150 us -> 148 us
  Pallas kernels: 14.8 us -> 12.5 us
    pallas_call x16, Pallas kernels: 14.8 us -> 12.5 us  [call(): pl.pallas_call(kernel, out_shape=[jax.ShapeDtypeStruct(s, d) for s, d in...]
  transfers between devices with their start and end apart: 22 -> 22, of which waited for: 16 -> 15; matrix products, arithmetic and copies ran while one was open for 0% -> 0% of each run, Pallas kernels for 4% -> 3%
where the time goes in v7:
time: 150 us; the launch traced here: 148 us
  blocking collectives  72.9 us (49%)
  waiting for transfers between devices  31.1 us (21%)
  starting transfers between devices  25.3 us (17%)
  Pallas kernels  12.5 us (8%)
  local copies, waits for them, and re-layouts  5.15 us (3%)
    all_to_all x4, blocking collectives, over_chips(): return lax.all_to_all(v, 'chip', 0, 0)  72.9 us
    ppermute x3, waiting for transfers between devices, fold(): lax.ppermute(x, axis, [(i, partner(i)) for i in range(lax.axis_size(axis))])  13.1 us
    pallas_call x16, Pallas kernels, call(): pl.pallas_call(kernel, out_shape=[jax.ShapeDtypeStruct(s, d) for s, d in...  12.5 us
    ppermute x9, starting transfers between devices, sum_four(): lax.ppermute(x, axis, [(i, (i // block ^ k) * block + i % block) for i in...  12.5 us
    ppermute x9, waiting for transfers between devices, sum_four(): lax.ppermute(x, axis, [(i, (i // block ^ k) * block + i % block) for i in...  10.1 us
    unnamed x26, local copies, waits for them, and re-layouts  4.4 us
    ppermute x5, waiting for transfers between devices, swap_cores(): return lax.ppermute(v, 'core', [(0, 1), (1, 0)])  3.73 us
  transfers between devices with their start and end apart: 22, of which 15 were waited for; matrix products, arithmetic and copies ran while one was open for 0% of the time, Pallas kernels for 3%

profile of v7, /device:TPU:32, one launch (start us, length us, event | category | flops | bytes accessed | tf_op | source)
XLA Modules:
  0.0 148.1 jit_solution(4587494632605431269)
XLA Ops:
  0.7 0.7 slice-done
  1.4 1.9 %collective-permute-start = (bf16[16,2048]{1,0:T(8,128)(2,1)S(1)}, bf16[16,2048]{1,0:T(8,128)(2,1)S(1)}, u32[]{:S(2)}, u32[]{:S(2)}) collective-permute-start(bf16[16,2048]{1,0:T(8,128)(2,1)S(1)} %pad_maximum_fusion), channel_id=1, source_target_pairs={{0,4},{4,8},{8,12},{12,16},{16,20},{20,24},{24,28},{28,32},{32,36}... | collective-permute-start | bytes 196616 | tf_op jit(solution)/shard_map/ppermute | solution.py:457
  3.4 0.7 copy-done.8
  4.1 0.9 copy-done.3
  5.0 0.9 copy-done.4
  6.0 0.3 turn.1
  6.3 0.4 copy-done.9
  6.7 0.4 steps.1
  7.1 0.0 collective-permute-done.before
  7.1 0.1 copy-done
  7.3 0.3 copy-done.2
  7.6 0.2 copy-done.7
  7.9 1.0 state.1
  8.9 2.1 %collective-permute-start.1 = (f32[544,128]{1,0:T(8,128)S(1)}, f32[544,128]{1,0:T(8,128)S(1)}, u32[]{:S(2)}, u32[]{:S(2)}) collective-permute-start(f32[544,128]{1,0:T(8,128)S(1)} %get-tuple-element.89), channel_id=1, source_target_pairs={{0,4},{4,0},{1,5},{5,1},{2,6},{6,2},{3,7},{7,3},{8,12},{12,8},{9,1... | collective-permute-start | bytes 835592 | tf_op jit(solution)/shard_map/ppermute | solution.py:418
  11.0 1.2 collective-permute-done.1.got
  12.2 0.2 join.2
  12.4 23.2 %all_to_all.20.s.d = f32[32,1,2176]{2,1,0:T(1,128)S(1)} all-to-all(f32[32,1,2176]{2,1,0:T(1,128)S(1)} %get-tuple-element.90), channel_id=1, replica_groups=mesh['chip'=32,'core'=2,'tp'=4] {'chip'}, dimensions={0} | all-to-all | bytes 557056 | tf_op jit(solution)/shard_map/all_to_all | solution.py:426
  35.6 0.2 block_scan.2
  35.8 16.5 %all_to_all.21 = f32[32,1,2048]{2,1,0:T(1,128)S(1)} all-to-all(f32[32,1,2048]{2,1,0:T(1,128)S(1)} %block_scan.2), channel_id=1, replica_groups=mesh['chip'=32,'core'=2,'tp'=4] {'chip'}, dimensions={0} | all-to-all | bytes 524288 | tf_op jit(solution)/shard_map/all_to_all | solution.py:426
  52.3 0.1 split.2
  52.4 0.1 collective-permute-start.2
  52.5 0.7 copy-done.1
  53.2 1.4 local.1
  54.6 0.5 output.1
  55.1 3.3 %collective-permute-start.4 = (f32[8,128]{1,0:T(8,128)S(1)}, f32[8,128]{1,0:T(8,128)S(1)}, u32[]{:S(2)}, u32[]{:S(2)}) collective-permute-start(f32[8,128]{1,0:T(8,128)S(1)} %get-tuple-element.102), channel_id=1, source_target_pairs={{0,2},{1,3},{2,0},{3,1},{4,6},{5,7},{6,4},{7,5},{8,10},{9,11},{10,... | collective-permute-start | bytes 12296 | tf_op jit(solution)/shard_map/ppermute | solution.py:435
  58.4 1.1 collective-permute-start.5
  59.5 0.9 collective-permute-done.4
  60.3 2.9 %collective-permute-done.5 = f32[8,128]{1,0:T(8,128)S(1)} collective-permute-done((f32[8,128]{1,0:T(8,128)S(1)}, f32[8,128]{1,0:T(8,128)S(1)}, u32[]{:S(2)}, u32[]{:S(2)}) %collective-permute-start.5) | collective-permute-done | bytes 4128 | tf_op jit(solution)/shard_map/ppermute | solution.py:435
  63.2 0.6 gate.1
  63.8 0.1 collective-permute-start.6
  63.9 1.5 %collective-permute-done.6.got = f32[512,128]{1,0:T(8,128)S(1)} collective-permute-done((f32[512,128]{1,0:T(8,128)S(1)}, f32[512,128]{1,0:T(8,128)S(1)}, u32[]{:S(2)}, u32[]{:S(2)}) %collective-permute-start.6) | collective-permute-done | bytes 262176 | tf_op jit(solution)/shard_map/ppermute | solution.py:418
  65.5 17.0 %all_to_all.22.s = f32[32,1,2048]{2,1,0:T(1,128)S(1)} all-to-all(f32[32,1,2048]{2,1,0:T(1,128)S(1)} %bitcast.18), channel_id=1, replica_groups=mesh['chip'=32,'core'=2,'tp'=4] {'chip'}, dimensions={0} | all-to-all | bytes 524288 | tf_op jit(solution)/shard_map/all_to_all | solution.py:426
  82.5 0.2 block_scan.3
  82.6 16.2 %all_to_all.23 = f32[32,1,2048]{2,1,0:T(1,128)S(1)} all-to-all(f32[32,1,2048]{2,1,0:T(1,128)S(1)} %block_scan.3), channel_id=1, replica_groups=mesh['chip'=32,'core'=2,'tp'=4] {'chip'}, dimensions={0} | all-to-all | bytes 524288 | tf_op jit(solution)/shard_map/all_to_all | solution.py:426
  98.8 0.1 split.3
  98.9 0.3 collective-permute-start.7
  99.2 2.9 %middle.1 = (f32[1024,128]{1,0:T(8,128)S(1)}, f32[128,512]{1,0:T(8,128)S(1)}, f32[32,128]{1,0:T(8,128)S(1)}, f32[32,128]{1,0:T(8,128)S(1)}, bf16[128,1024]{1,0:T...) custom-call(f32[8,128]{1,0:T(8,128)S(1)} %add_add_fusion.2.sums, f32[1024,128]{1,0:T(8,128)S(1)} %get-tuple-element.103.y, ...), custom_call_target="tpu_custom_call" | custom-call | flops 20000000 | bytes 4194304 | tf_op jit(solution)/shard_map/middle/pallas_call | solution.py:405
  102.1 3.1 %last.1 = (f32[128,1024]{1,0:T(8,128)S(1)}, f32[64,128]{1,0:T(8,128)S(1)}, f32[2,272,128]{2,1,0:T(8,128)S(1)}, f32[2,272,128]{2,1,0:T(8,128)S(1)}, f32[80,128]{1,0:T(8,128)S(1)}, /*index=5*/f32[32,128]{1,0:T(8,128)}) custom-call(s32[1]{0:T(128)} %bitcast.core, s32[1]{0:T(128)} %bitcast.1.which, f32[512,128]{1,0:T(8,128)S(1)} %get-tuple-element.106.own, ...), custom_call_target="tpu_custom_call" | custom-call | flops 20000000 | bytes 4194304 | tf_op jit(solution)/shard_map/last/pallas_call | solution.py:405
  105.2 2.0 %collective-permute-start.8 = (f32[2,272,128]{2,1,0:T(8,128)S(1)}, f32[2,272,128]{2,1,0:T(8,128)S(1)}, u32[]{:S(2)}, u32[]{:S(2)}) collective-permute-start(f32[2,272,128]{2,1,0:T(8,128)S(1)} %get-tuple-element.123), channel_id=1, source_target_pairs={{0,3},{1,2},{2,1},{3,0},{4,7},{5,6},{6,5},{7,4},{8,11},{9,10},{10,... | collective-permute-start | bytes 835592 | tf_op jit(solution)/shard_map/ppermute | solution.py:551
  107.2 0.2 collective-permute-start.9
  107.4 1.0 collective-permute-done.9
  108.4 0.2 collective-permute-start.10
  108.7 3.8 %collective-permute-done.10 = f32[80,128]{1,0:T(8,128)S(1)} collective-permute-done((f32[80,128]{1,0:T(8,128)S(1)}, f32[80,128]{1,0:T(8,128)S(1)}, u32[]{:S(2)}, u32[]{:S(2)}) %collective-permute-start.10) | collective-permute-done | bytes 40992 | tf_op jit(solution)/shard_map/ppermute | solution.py:430
  112.4 0.9 collective-permute-start.11
  113.4 4.0 %collective-permute-done.11 = f32[80,128]{1,0:T(8,128)S(1)} collective-permute-done((f32[80,128]{1,0:T(8,128)S(1)}, f32[80,128]{1,0:T(8,128)S(1)}, u32[]{:S(2)}, u32[]{:S(2)}) %collective-permute-start.11) | collective-permute-done | bytes 40992 | tf_op jit(solution)/shard_map/ppermute | solution.py:430
  117.4 0.1 collective-permute-start.12
  117.5 1.7 %collective-permute-start.13 = (f32[80,128]{1,0:T(8,128)S(1)}, f32[80,128]{1,0:T(8,128)S(1)}, u32[]{:S(2)}, u32[]{:S(2)}) collective-permute-start(f32[80,128]{1,0:T(8,128)S(1)} %add.51), channel_id=1, source_target_pairs={{0,56},{8,48},{16,40},{24,32},{32,24},{40,16},{48,8},{56,0},{64,12... | collective-permute-start | bytes 122888 | tf_op jit(solution)/shard_map/ppermute | solution.py:430
  119.2 5.4 %collective-permute-done.13 = f32[80,128]{1,0:T(8,128)S(1)} collective-permute-done((f32[80,128]{1,0:T(8,128)S(1)}, f32[80,128]{1,0:T(8,128)S(1)}, u32[]{:S(2)}, u32[]{:S(2)}) %collective-permute-start.13) | collective-permute-done | bytes 40992 | tf_op jit(solution)/shard_map/ppermute | solution.py:430
  124.7 1.9 %collective-permute-start.14 = (f32[96,128]{1,0:T(8,128)S(1)}, f32[96,128]{1,0:T(8,128)S(1)}, u32[]{:S(2)}, u32[]{:S(2)}) collective-permute-start(f32[96,128]{1,0:T(8,128)S(1)} %pad_maximum_fusion.1), channel_id=1, source_target_pairs={{4,0},{8,4},{12,8},{16,12},{20,16},{24,20},{28,24},{32,28},{36,32}... | collective-permute-start | bytes 147464 | tf_op jit(solution)/shard_map/ppermute | solution.py:562
  126.6 1.7 %collective-permute-done.14.heads = f32[96,128]{1,0:T(8,128)S(1)} collective-permute-done((f32[96,128]{1,0:T(8,128)S(1)}, f32[96,128]{1,0:T(8,128)S(1)}, u32[]{:S(2)}, u32[]{:S(2)}) %collective-permute-start.14) | collective-permute-done | bytes 49184 | tf_op jit(solution)/shard_map/ppermute | solution.py:562
  128.3 0.8 settle.1
  129.1 1.3 collective-permute-start.17
  130.4 2.0 %collective-permute-start.18 = (f32[80,128]{1,0:T(8,128)S(1)}, f32[80,128]{1,0:T(8,128)S(1)}, u32[]{:S(2)}, u32[]{:S(2)}) collective-permute-start(f32[80,128]{1,0:T(8,128)S(1)} %add.54), channel_id=1, source_target_pairs={{0,192},{8,200},{16,208},{24,216},{32,224},{40,232},{48,240},{56,2... | collective-permute-start | bytes 122888 | tf_op jit(solution)/shard_map/ppermute | solution.py:435
  132.4 0.2 collective-permute-start.16
  132.6 2.4 %collective-permute-done.17 = f32[80,128]{1,0:T(8,128)S(1)} collective-permute-done((f32[80,128]{1,0:T(8,128)S(1)}, f32[80,128]{1,0:T(8,128)S(1)}, u32[]{:S(2)}, u32[]{:S(2)}) %collective-permute-start.17) | collective-permute-done | bytes 40992 | tf_op jit(solution)/shard_map/ppermute | solution.py:435
  135.0 0.9 collective-permute-done.18
  135.9 0.5 collective-permute-done.16
  136.4 2.7 %collective-permute-start.20 = (f32[32,128]{1,0:T(8,128)S(1)}, f32[32,128]{1,0:T(8,128)S(1)}, u32[]{:S(2)}, u32[]{:S(2)}) collective-permute-start(f32[32,128]{1,0:T(8,128)S(1)} %slice.21), channel_id=1, source_target_pairs={{0,2},{1,3},{2,0},{3,1},{4,6},{5,7},{6,4},{7,5},{8,10},{9,11},{10,... | collective-permute-start | bytes 49160 | tf_op jit(solution)/shard_map/ppermute | solution.py:435
  139.1 2.0 %collective-permute-start.21 = (f32[32,128]{1,0:T(8,128)S(1)}, f32[32,128]{1,0:T(8,128)S(1)}, u32[]{:S(2)}, u32[]{:S(2)}) collective-permute-start(f32[32,128]{1,0:T(8,128)S(1)} %slice.21), channel_id=1, source_target_pairs={{0,3},{1,2},{2,1},{3,0},{4,7},{5,6},{6,5},{7,4},{8,11},{9,10},{10,... | collective-permute-start | bytes 49160 | tf_op jit(solution)/shard_map/ppermute | solution.py:435
  141.1 1.2 collective-permute-start.15
  142.3 1.9 %collective-permute-done.21 = f32[32,128]{1,0:T(8,128)S(1)} collective-permute-done((f32[32,128]{1,0:T(8,128)S(1)}, f32[32,128]{1,0:T(8,128)S(1)}, u32[]{:S(2)}, u32[]{:S(2)}) %collective-permute-start.21) | collective-permute-done | bytes 16416 | tf_op jit(solution)/shard_map/ppermute | solution.py:435
  144.2 0.6 collective-permute-done.19
  144.9 2.4 %collective-permute-done.15.other = bf16[2,256,128]{2,1,0:T(8,128)(2,1)S(1)} collective-permute-done((bf16[2,256,128]{2,1,0:T(8,128)(2,1)S(1)}, bf16[2,256,128]{2,1,0:T(8,128)(2,1)S(1)}, u32[]{:S(2)}, u32[]{:S(2)}) %collective-permute-start.15) | collective-permute-done | bytes 131104 | tf_op jit(solution)/shard_map/ppermute | solution.py:570
  147.3 0.8 finish.1
  (45 shorter events, 0.3 us)
Async XLA Ops:
  0.6 0.8 slice-start
  0.7 0.8 slice-start.1
  0.7 0.7 slice-start.2
  1.4 5.7 %collective-permute-start = (bf16[16,2048]{1,0:T(8,128)(2,1)S(1)}, bf16[16,2048]{1,0:T(8,128)(2,1)S(1)}, u32[]{:S(2)}, u32[]{:S(2)}) collective-permute-start(bf16[16,2048]{1,0:T(8,128)(2,1)S(1)} %pad_maximum_fusion), channel_id=1, source_target_pairs={{0,4},{4,8},{8,12},{12,16},{16,20},{20,24},{24,28},{28,32},{32,36}... | collective-permute-start | bytes 196616 | tf_op jit(solution)/shard_map/ppermute | solution.py:457
  3.4 0.7 copy-start.8
  4.1 0.9 copy-start.3
  5.0 0.9 copy-start.4
  6.0 0.7 copy-start.9
  6.0 0.7 copy-start.10
  6.0 0.7 copy-start.11
  6.0 0.7 copy-start.12
  6.3 1.0 copy-start
  6.7 0.9 copy-start.2
  6.7 0.9 copy-start.5
  7.1 0.7 copy-start.7
  8.9 3.3 %collective-permute-start.1 = (f32[544,128]{1,0:T(8,128)S(1)}, f32[544,128]{1,0:T(8,128)S(1)}, u32[]{:S(2)}, u32[]{:S(2)}) collective-permute-start(f32[544,128]{1,0:T(8,128)S(1)} %get-tuple-element.89), channel_id=1, source_target_pairs={{0,4},{4,0},{1,5},{5,1},{2,6},{6,2},{3,7},{7,3},{8,12},{12,8},{9,1... | collective-permute-start | bytes 835592 | tf_op jit(solution)/shard_map/ppermute | solution.py:418
  52.3 0.9 copy-start.1
  52.3 0.8 copy-start.6
  52.4 2.3 %collective-permute-start.2 = (f32[512,128]{1,0:T(8,128)S(1)}, f32[512,128]{1,0:T(8,128)S(1)}, u32[]{:S(2)}, u32[]{:S(2)}) collective-permute-start(f32[512,128]{1,0:T(8,128)S(1)} %get-tuple-element.93), channel_id=1, source_target_pairs={{0,4},{4,0},{1,5},{5,1},{2,6},{6,2},{3,7},{7,3},{8,12},{12,8},{9,1... | collective-permute-start | bytes 786440 | tf_op jit(solution)/shard_map/ppermute | solution.py:418
  55.1 5.2 %collective-permute-start.4 = (f32[8,128]{1,0:T(8,128)S(1)}, f32[8,128]{1,0:T(8,128)S(1)}, u32[]{:S(2)}, u32[]{:S(2)}) collective-permute-start(f32[8,128]{1,0:T(8,128)S(1)} %get-tuple-element.102), channel_id=1, source_target_pairs={{0,2},{1,3},{2,0},{3,1},{4,6},{5,7},{6,4},{7,5},{8,10},{9,11},{10,... | collective-permute-start | bytes 12296 | tf_op jit(solution)/shard_map/ppermute | solution.py:435
  58.4 4.8 %collective-permute-start.5 = (f32[8,128]{1,0:T(8,128)S(1)}, f32[8,128]{1,0:T(8,128)S(1)}, u32[]{:S(2)}, u32[]{:S(2)}) collective-permute-start(f32[8,128]{1,0:T(8,128)S(1)} %get-tuple-element.102), channel_id=1, source_target_pairs={{0,3},{1,2},{2,1},{3,0},{4,7},{5,6},{6,5},{7,4},{8,11},{9,10},{10,... | collective-permute-start | bytes 12296 | tf_op jit(solution)/shard_map/ppermute | solution.py:435
  59.5 3.8 %collective-permute-start.3 = (f32[8,128]{1,0:T(8,128)S(1)}, f32[8,128]{1,0:T(8,128)S(1)}, u32[]{:S(2)}, u32[]{:S(2)}) collective-permute-start(f32[8,128]{1,0:T(8,128)S(1)} %get-tuple-element.102), channel_id=1, source_target_pairs={{0,1},{1,0},{2,3},{3,2},{4,5},{5,4},{6,7},{7,6},{8,9},{9,8},{10,11... | collective-permute-start | bytes 12296 | tf_op jit(solution)/shard_map/ppermute | solution.py:435
  63.8 1.6 %collective-permute-start.6 = (f32[512,128]{1,0:T(8,128)S(1)}, f32[512,128]{1,0:T(8,128)S(1)}, u32[]{:S(2)}, u32[]{:S(2)}) collective-permute-start(f32[512,128]{1,0:T(8,128)S(1)} %get-tuple-element.105), channel_id=1, source_target_pairs={{0,4},{4,0},{1,5},{5,1},{2,6},{6,2},{3,7},{7,3},{8,12},{12,8},{9,1... | collective-permute-start | bytes 786440 | tf_op jit(solution)/shard_map/ppermute | solution.py:418
  98.9 3.2 %collective-permute-start.7 = (f32[512,128]{1,0:T(8,128)S(1)}, f32[512,128]{1,0:T(8,128)S(1)}, u32[]{:S(2)}, u32[]{:S(2)}) collective-permute-start(f32[512,128]{1,0:T(8,128)S(1)} %get-tuple-element.107), channel_id=1, source_target_pairs={{0,4},{4,0},{1,5},{5,1},{2,6},{6,2},{3,7},{7,3},{8,12},{12,8},{9,1... | collective-permute-start | bytes 786440 | tf_op jit(solution)/shard_map/ppermute | solution.py:418
  105.2 12.2 %collective-permute-start.8 = (f32[2,272,128]{2,1,0:T(8,128)S(1)}, f32[2,272,128]{2,1,0:T(8,128)S(1)}, u32[]{:S(2)}, u32[]{:S(2)}) collective-permute-start(f32[2,272,128]{2,1,0:T(8,128)S(1)} %get-tuple-element.123), channel_id=1, source_target_pairs={{0,3},{1,2},{2,1},{3,0},{4,7},{5,6},{6,5},{7,4},{8,11},{9,10},{10,... | collective-permute-start | bytes 835592 | tf_op jit(solution)/shard_map/ppermute | solution.py:551
  107.2 1.2 collective-permute-start.9
  108.4 4.0 %collective-permute-start.10 = (f32[80,128]{1,0:T(8,128)S(1)}, f32[80,128]{1,0:T(8,128)S(1)}, u32[]{:S(2)}, u32[]{:S(2)}) collective-permute-start(f32[80,128]{1,0:T(8,128)S(1)} %add.49), channel_id=1, source_target_pairs={{0,8},{8,0},{16,24},{24,16},{32,40},{40,32},{48,56},{56,48},{64,72... | collective-permute-start | bytes 122888 | tf_op jit(solution)/shard_map/ppermute | solution.py:430
  112.4 4.9 %collective-permute-start.11 = (f32[80,128]{1,0:T(8,128)S(1)}, f32[80,128]{1,0:T(8,128)S(1)}, u32[]{:S(2)}, u32[]{:S(2)}) collective-permute-start(f32[80,128]{1,0:T(8,128)S(1)} %add.50), channel_id=1, source_target_pairs={{0,16},{8,24},{16,0},{24,8},{32,48},{40,56},{48,32},{56,40},{64,80... | collective-permute-start | bytes 122888 | tf_op jit(solution)/shard_map/ppermute | solution.py:430
  117.4 7.2 %collective-permute-start.12 = (f32[2,272,128]{2,1,0:T(8,128)S(1)}, f32[2,272,128]{2,1,0:T(8,128)S(1)}, u32[]{:S(2)}, u32[]{:S(2)}) collective-permute-start(f32[2,272,128]{2,1,0:T(8,128)S(1)} %add.52), channel_id=1, source_target_pairs={{0,1},{1,0},{2,3},{3,2},{4,5},{5,4},{6,7},{7,6},{8,9},{9,8},{10,11... | collective-permute-start | bytes 835592 | tf_op jit(solution)/shard_map/ppermute | solution.py:557
  117.5 7.1 %collective-permute-start.13 = (f32[80,128]{1,0:T(8,128)S(1)}, f32[80,128]{1,0:T(8,128)S(1)}, u32[]{:S(2)}, u32[]{:S(2)}) collective-permute-start(f32[80,128]{1,0:T(8,128)S(1)} %add.51), channel_id=1, source_target_pairs={{0,56},{8,48},{16,40},{24,32},{32,24},{40,16},{48,8},{56,0},{64,12... | collective-permute-start | bytes 122888 | tf_op jit(solution)/shard_map/ppermute | solution.py:430
  124.7 3.7 %collective-permute-start.14 = (f32[96,128]{1,0:T(8,128)S(1)}, f32[96,128]{1,0:T(8,128)S(1)}, u32[]{:S(2)}, u32[]{:S(2)}) collective-permute-start(f32[96,128]{1,0:T(8,128)S(1)} %pad_maximum_fusion.1), channel_id=1, source_target_pairs={{4,0},{8,4},{12,8},{16,12},{20,16},{24,20},{28,24},{32,28},{36,32}... | collective-permute-start | bytes 147464 | tf_op jit(solution)/shard_map/ppermute | solution.py:562
  129.1 5.9 %collective-permute-start.17 = (f32[80,128]{1,0:T(8,128)S(1)}, f32[80,128]{1,0:T(8,128)S(1)}, u32[]{:S(2)}, u32[]{:S(2)}) collective-permute-start(f32[80,128]{1,0:T(8,128)S(1)} %add.54), channel_id=1, source_target_pairs={{0,128},{8,136},{16,144},{24,152},{32,160},{40,168},{48,176},{56,1... | collective-permute-start | bytes 122888 | tf_op jit(solution)/shard_map/ppermute | solution.py:435
  130.4 5.5 %collective-permute-start.18 = (f32[80,128]{1,0:T(8,128)S(1)}, f32[80,128]{1,0:T(8,128)S(1)}, u32[]{:S(2)}, u32[]{:S(2)}) collective-permute-start(f32[80,128]{1,0:T(8,128)S(1)} %add.54), channel_id=1, source_target_pairs={{0,192},{8,200},{16,208},{24,216},{32,224},{40,232},{48,240},{56,2... | collective-permute-start | bytes 122888 | tf_op jit(solution)/shard_map/ppermute | solution.py:435
  132.4 4.0 %collective-permute-start.16 = (f32[80,128]{1,0:T(8,128)S(1)}, f32[80,128]{1,0:T(8,128)S(1)}, u32[]{:S(2)}, u32[]{:S(2)}) collective-permute-start(f32[80,128]{1,0:T(8,128)S(1)} %add.54), channel_id=1, source_target_pairs={{0,64},{8,72},{16,80},{24,88},{32,96},{40,104},{48,112},{56,120},{... | collective-permute-start | bytes 122888 | tf_op jit(solution)/shard_map/ppermute | solution.py:435
  136.4 5.9 %collective-permute-start.20 = (f32[32,128]{1,0:T(8,128)S(1)}, f32[32,128]{1,0:T(8,128)S(1)}, u32[]{:S(2)}, u32[]{:S(2)}) collective-permute-start(f32[32,128]{1,0:T(8,128)S(1)} %slice.21), channel_id=1, source_target_pairs={{0,2},{1,3},{2,0},{3,1},{4,6},{5,7},{6,4},{7,5},{8,10},{9,11},{10,... | collective-permute-start | bytes 49160 | tf_op jit(solution)/shard_map/ppermute | solution.py:435
  139.1 5.1 %collective-permute-start.21 = (f32[32,128]{1,0:T(8,128)S(1)}, f32[32,128]{1,0:T(8,128)S(1)}, u32[]{:S(2)}, u32[]{:S(2)}) collective-permute-start(f32[32,128]{1,0:T(8,128)S(1)} %slice.21), channel_id=1, source_target_pairs={{0,3},{1,2},{2,1},{3,0},{4,7},{5,6},{6,5},{7,4},{8,11},{9,10},{10,... | collective-permute-start | bytes 49160 | tf_op jit(solution)/shard_map/ppermute | solution.py:435
  141.1 3.7 %collective-permute-start.19 = (f32[32,128]{1,0:T(8,128)S(1)}, f32[32,128]{1,0:T(8,128)S(1)}, u32[]{:S(2)}, u32[]{:S(2)}) collective-permute-start(f32[32,128]{1,0:T(8,128)S(1)} %slice.21), channel_id=1, source_target_pairs={{0,1},{1,0},{2,3},{3,2},{4,5},{5,4},{6,7},{7,6},{8,9},{9,8},{10,11... | collective-permute-start | bytes 49160 | tf_op jit(solution)/shard_map/ppermute | solution.py:435
  141.1 6.2 %collective-permute-start.15 = (bf16[2,256,128]{2,1,0:T(8,128)(2,1)S(1)}, bf16[2,256,128]{2,1,0:T(8,128)(2,1)S(1)}, u32[]{:S(2)}, u32[]{:S(2)}) collective-permute-start(bf16[2,256,128]{2,1,0:T(8,128)(2,1)S(1)} %get-tuple-element.133.half), channel_id=1, source_target_pairs={{0,3},{1,2},{2,1},{3,0},{4,7},{5,6},{6,5},{7,4},{8,11},{9,10},{10,... | collective-permute-start | bytes 393224 | tf_op jit(solution)/shard_map/ppermute | solution.py:570

commit v8 on v7

--- a/solution.py
+++ b/solution.py
@@ -367,13 +367,16 @@
             half[g, stop - LEAD : stop, :] = (mine[g, stop - LEAD : stop, :] + more).astype(jnp.bfloat16)
 
 
-def finish_kernel(which, half, other, bc_taps, packed, gb, gc, tx, tb, tc, tgain, bias, rate, skip):
+def place_kernel(which, half, other, gb, gc):
     left = which[0] == 0
     for g in range(GROUPS):
         first, second = (half, other) if g < 2 else (other, half)
         both = jnp.where(left, first[g % 2].astype(F32), second[g % 2].astype(F32)).astype(jnp.bfloat16)
         gb[:, lanes(g)] = both[0:SPAN]
         gc[:, lanes(g)] = both[SPAN : 2 * SPAN]
+
+
+def finish_kernel(bc_taps, packed, tx, tb, tc, tgain, bias, rate, skip):
     for k in range(CONV):
         for g in range(GROUPS):
             tb[k : k + 1, lanes(g)] = bc_taps[k * GROUPS + g : k * GROUPS + g + 1, :]
@@ -430,12 +433,16 @@
     return x + lax.ppermute(x, axis, [(i, partner(i)) for i in range(lax.axis_size(axis))])
 
 
-def sum_four(x, axis, block=1):
-    near, far, last = (
+def sum_four(x, axis, block=1, behind=None):
+    sent = [
         lax.ppermute(x, axis, [(i, (i // block ^ k) * block + i % block) for i in range(lax.axis_size(axis))])
         for k in range(1, 4)
-    )
-    return (x + near) + (far + last)
+    ]
+    if behind is not None:
+        *sent, behind = lax.optimization_barrier((*sent, behind))
+    near, far, last = sent
+    total = (x + near) + (far + last)
+    return total if behind is None else (total, behind)
 
 
 def mirror(within):
@@ -568,15 +575,17 @@
     )
     half, packed = lax.optimization_barrier((half, packed))
     other = lax.ppermute(half, "tp", across)
-    packed = sum_four(packed, "chip", RING)
+    half_bc, each = ((SPAN, wb), jnp.bfloat16), ((1, LOCAL), F32)
+    grad_b_raw, grad_c_raw = call(
+        place_kernel, "place", [half_bc, half_bc], (sides, half, other), scalars=1, flops=20_000_000_000
+    )
+    packed, grad_b_raw = sum_four(packed, "chip", RING, grad_b_raw)
     bc_taps = sum_four(packed[:32], "tp")
-    half_bc, each = ((SPAN, wb), jnp.bfloat16), ((1, LOCAL), F32)
-    grad_b_raw, grad_c_raw, conv_x_total, conv_b_total, conv_c_total, gain_total, *small = call(
+    conv_x_total, conv_b_total, conv_c_total, gain_total, *small = call(
         finish_kernel,
         "finish",
-        [half_bc, half_bc, ((CONV, wx), F32), ((CONV, wb), F32), ((CONV, wb), F32), ((1, wx), F32)] + [each] * 3,
-        (sides, half, other, bc_taps, packed),
-        scalars=1,
+        [((CONV, wx), F32), ((CONV, wb), F32), ((CONV, wb), F32), ((1, wx), F32)] + [each] * 3,
+        (bc_taps, packed),
     )
     return (
         grad_x_raw,

time: 150 us -> 147 us (0.980); the launches traced: 148 us -> 147 us
  waiting for transfers between devices: 31.1 us -> 28.5 us
    ppermute x9, waiting for transfers between devices: 10.1 us -> 8.32 us  [sum_four(): lax.ppermute(x, axis, [(i, (i // block ^ k) * block + i % block) for i in...]
    pallas_call x16 -> x17, Pallas kernels: 12.5 us -> 13.2 us  [call(): pl.pallas_call(kernel, out_shape=[jax.ShapeDtypeStruct(s, d) for s, d in...]
  transfers between devices with their start and end apart: 22 -> 22, of which waited for: 15 -> 13; matrix products, arithmetic and copies ran while one was open for 0% -> 0% of each run, Pallas kernels for 3% -> 4%
where the time goes in v8:
time: 147 us
  blocking collectives  72.9 us (50%)
  waiting for transfers between devices  28.5 us (19%)
  starting transfers between devices  25.9 us (18%)
  Pallas kernels  13.2 us (9%)
  local copies, waits for them, and re-layouts  5.15 us (4%)
    all_to_all x4, blocking collectives, over_chips(): return lax.all_to_all(v, 'chip', 0, 0)  72.9 us
    pallas_call x17, Pallas kernels, call(): pl.pallas_call(kernel, out_shape=[jax.ShapeDtypeStruct(s, d) for s, d in...  13.2 us
    ppermute x3, waiting for transfers between devices, fold(): lax.ppermute(x, axis, [(i, partner(i)) for i in range(lax.axis_size(axis))])  13.1 us
    ppermute x9, starting transfers between devices, sum_four(): lax.ppermute(x, axis, [(i, (i // block ^ k) * block + i % block) for i in...  13.1 us
    ppermute x9, waiting for transfers between devices, sum_four(): lax.ppermute(x, axis, [(i, (i // block ^ k) * block + i % block) for i in...  8.32 us
    unnamed x26, local copies, waits for them, and re-layouts  4.4 us
    ppermute x5, waiting for transfers between devices, swap_cores(): return lax.ppermute(v, 'core', [(0, 1), (1, 0)])  3.73 us
  transfers between devices with their start and end apart: 22, of which 13 were waited for; matrix products, arithmetic and copies ran while one was open for 0% of the time, Pallas kernels for 4%

profile of v8, /device:TPU:32, one launch (start us, length us, event | category | flops | bytes accessed | tf_op | source)
XLA Modules:
  0.0 146.6 jit_solution(2194536736180213570)
XLA Ops:
  0.7 0.7 slice-done
  1.4 1.9 %collective-permute-start = (bf16[16,2048]{1,0:T(8,128)(2,1)S(1)}, bf16[16,2048]{1,0:T(8,128)(2,1)S(1)}, u32[]{:S(2)}, u32[]{:S(2)}) collective-permute-start(bf16[16,2048]{1,0:T(8,128)(2,1)S(1)} %pad_maximum_fusion), channel_id=1, source_target_pairs={{0,4},{4,8},{8,12},{12,16},{16,20},{20,24},{24,28},{28,32},{32,36}... | collective-permute-start | bytes 196616 | tf_op jit(solution)/shard_map/ppermute | solution.py:464
  3.4 0.7 copy-done.8
  4.1 0.9 copy-done.3
  5.0 0.9 copy-done.4
  6.0 0.3 turn.1
  6.3 0.4 copy-done.9
  6.7 0.4 steps.1
  7.1 0.0 collective-permute-done.before
  7.1 0.1 copy-done
  7.3 0.3 copy-done.2
  7.6 0.2 copy-done.7
  7.9 1.0 state.1
  8.9 2.1 %collective-permute-start.1 = (f32[544,128]{1,0:T(8,128)S(1)}, f32[544,128]{1,0:T(8,128)S(1)}, u32[]{:S(2)}, u32[]{:S(2)}) collective-permute-start(f32[544,128]{1,0:T(8,128)S(1)} %get-tuple-element.93), channel_id=1, source_target_pairs={{0,4},{4,0},{1,5},{5,1},{2,6},{6,2},{3,7},{7,3},{8,12},{12,8},{9,1... | collective-permute-start | bytes 835592 | tf_op jit(solution)/shard_map/ppermute | solution.py:421
  11.0 1.2 collective-permute-done.1.got
  12.2 0.2 join.2
  12.4 23.2 %all_to_all.20.s.d = f32[32,1,2176]{2,1,0:T(1,128)S(1)} all-to-all(f32[32,1,2176]{2,1,0:T(1,128)S(1)} %get-tuple-element.94), channel_id=1, replica_groups=mesh['chip'=32,'core'=2,'tp'=4] {'chip'}, dimensions={0} | all-to-all | bytes 557056 | tf_op jit(solution)/shard_map/all_to_all | solution.py:429
  35.6 0.2 block_scan.2
  35.8 16.5 %all_to_all.21 = f32[32,1,2048]{2,1,0:T(1,128)S(1)} all-to-all(f32[32,1,2048]{2,1,0:T(1,128)S(1)} %block_scan.2), channel_id=1, replica_groups=mesh['chip'=32,'core'=2,'tp'=4] {'chip'}, dimensions={0} | all-to-all | bytes 524288 | tf_op jit(solution)/shard_map/all_to_all | solution.py:429
  52.3 0.1 split.2
  52.4 0.1 collective-permute-start.2
  52.5 0.7 copy-done.1
  53.2 1.4 local.1
  54.6 0.5 output.1
  55.1 3.3 %collective-permute-start.4 = (f32[8,128]{1,0:T(8,128)S(1)}, f32[8,128]{1,0:T(8,128)S(1)}, u32[]{:S(2)}, u32[]{:S(2)}) collective-permute-start(f32[8,128]{1,0:T(8,128)S(1)} %get-tuple-element.106), channel_id=1, source_target_pairs={{0,2},{1,3},{2,0},{3,1},{4,6},{5,7},{6,4},{7,5},{8,10},{9,11},{10,... | collective-permute-start | bytes 12296 | tf_op jit(solution)/shard_map/ppermute | solution.py:438
  58.4 1.1 collective-permute-start.5
  59.5 0.9 collective-permute-done.4
  60.3 2.9 %collective-permute-done.5 = f32[8,128]{1,0:T(8,128)S(1)} collective-permute-done((f32[8,128]{1,0:T(8,128)S(1)}, f32[8,128]{1,0:T(8,128)S(1)}, u32[]{:S(2)}, u32[]{:S(2)}) %collective-permute-start.5) | collective-permute-done | bytes 4128 | tf_op jit(solution)/shard_map/ppermute | solution.py:438
  63.2 0.6 gate.1
  63.8 0.1 collective-permute-start.6
  63.9 1.5 %collective-permute-done.6.got = f32[512,128]{1,0:T(8,128)S(1)} collective-permute-done((f32[512,128]{1,0:T(8,128)S(1)}, f32[512,128]{1,0:T(8,128)S(1)}, u32[]{:S(2)}, u32[]{:S(2)}) %collective-permute-start.6) | collective-permute-done | bytes 262176 | tf_op jit(solution)/shard_map/ppermute | solution.py:421
  65.5 16.9 %all_to_all.22.s = f32[32,1,2048]{2,1,0:T(1,128)S(1)} all-to-all(f32[32,1,2048]{2,1,0:T(1,128)S(1)} %bitcast.18), channel_id=1, replica_groups=mesh['chip'=32,'core'=2,'tp'=4] {'chip'}, dimensions={0} | all-to-all | bytes 524288 | tf_op jit(solution)/shard_map/all_to_all | solution.py:429
  82.5 0.2 block_scan.3
  82.6 16.2 %all_to_all.23 = f32[32,1,2048]{2,1,0:T(1,128)S(1)} all-to-all(f32[32,1,2048]{2,1,0:T(1,128)S(1)} %block_scan.3), channel_id=1, replica_groups=mesh['chip'=32,'core'=2,'tp'=4] {'chip'}, dimensions={0} | all-to-all | bytes 524288 | tf_op jit(solution)/shard_map/all_to_all | solution.py:429
  98.8 0.1 split.3
  98.9 0.3 collective-permute-start.7
  99.2 2.9 %middle.1 = (f32[1024,128]{1,0:T(8,128)S(1)}, f32[128,512]{1,0:T(8,128)S(1)}, f32[32,128]{1,0:T(8,128)S(1)}, f32[32,128]{1,0:T(8,128)S(1)}, bf16[128,1024]{1,0:T...) custom-call(f32[8,128]{1,0:T(8,128)S(1)} %add_add_fusion.2.sums, f32[1024,128]{1,0:T(8,128)S(1)} %get-tuple-element.107.y, ...), custom_call_target="tpu_custom_call" | custom-call | flops 20000000 | bytes 4194304 | tf_op jit(solution)/shard_map/middle/pallas_call | solution.py:408
  102.1 3.1 %last.1 = (f32[128,1024]{1,0:T(8,128)S(1)}, f32[64,128]{1,0:T(8,128)S(1)}, f32[2,272,128]{2,1,0:T(8,128)S(1)}, f32[2,272,128]{2,1,0:T(8,128)S(1)}, f32[80,128]{1,0:T(8,128)S(1)}, /*index=5*/f32[32,128]{1,0:T(8,128)}) custom-call(s32[1]{0:T(128)} %bitcast.core, s32[1]{0:T(128)} %bitcast.1.which, f32[512,128]{1,0:T(8,128)S(1)} %get-tuple-element.110.own, ...), custom_call_target="tpu_custom_call" | custom-call | flops 20000000 | bytes 4194304 | tf_op jit(solution)/shard_map/last/pallas_call | solution.py:408
  105.2 2.0 %collective-permute-start.8 = (f32[2,272,128]{2,1,0:T(8,128)S(1)}, f32[2,272,128]{2,1,0:T(8,128)S(1)}, u32[]{:S(2)}, u32[]{:S(2)}) collective-permute-start(f32[2,272,128]{2,1,0:T(8,128)S(1)} %get-tuple-element.127), channel_id=1, source_target_pairs={{0,3},{1,2},{2,1},{3,0},{4,7},{5,6},{6,5},{7,4},{8,11},{9,10},{10,... | collective-permute-start | bytes 835592 | tf_op jit(solution)/shard_map/ppermute | solution.py:558
  107.2 0.2 collective-permute-start.9
  107.4 1.0 collective-permute-done.9
  108.4 0.2 collective-permute-start.10
  108.7 3.8 %collective-permute-done.10 = f32[80,128]{1,0:T(8,128)S(1)} collective-permute-done((f32[80,128]{1,0:T(8,128)S(1)}, f32[80,128]{1,0:T(8,128)S(1)}, u32[]{:S(2)}, u32[]{:S(2)}) %collective-permute-start.10) | collective-permute-done | bytes 40992 | tf_op jit(solution)/shard_map/ppermute | solution.py:433
  112.4 0.9 collective-permute-start.11
  113.4 4.0 %collective-permute-done.11 = f32[80,128]{1,0:T(8,128)S(1)} collective-permute-done((f32[80,128]{1,0:T(8,128)S(1)}, f32[80,128]{1,0:T(8,128)S(1)}, u32[]{:S(2)}, u32[]{:S(2)}) %collective-permute-start.11) | collective-permute-done | bytes 40992 | tf_op jit(solution)/shard_map/ppermute | solution.py:433
  117.4 0.1 collective-permute-start.12
  117.5 1.7 %collective-permute-start.13 = (f32[80,128]{1,0:T(8,128)S(1)}, f32[80,128]{1,0:T(8,128)S(1)}, u32[]{:S(2)}, u32[]{:S(2)}) collective-permute-start(f32[80,128]{1,0:T(8,128)S(1)} %add.51), channel_id=1, source_target_pairs={{0,56},{8,48},{16,40},{24,32},{32,24},{40,16},{48,8},{56,0},{64,12... | collective-permute-start | bytes 122888 | tf_op jit(solution)/shard_map/ppermute | solution.py:433
  119.2 5.4 %collective-permute-done.13 = f32[80,128]{1,0:T(8,128)S(1)} collective-permute-done((f32[80,128]{1,0:T(8,128)S(1)}, f32[80,128]{1,0:T(8,128)S(1)}, u32[]{:S(2)}, u32[]{:S(2)}) %collective-permute-start.13) | collective-permute-done | bytes 40992 | tf_op jit(solution)/shard_map/ppermute | solution.py:433
  124.7 1.9 %collective-permute-start.14 = (f32[96,128]{1,0:T(8,128)S(1)}, f32[96,128]{1,0:T(8,128)S(1)}, u32[]{:S(2)}, u32[]{:S(2)}) collective-permute-start(f32[96,128]{1,0:T(8,128)S(1)} %pad_maximum_fusion.1), channel_id=1, source_target_pairs={{4,0},{8,4},{12,8},{16,12},{20,16},{24,20},{28,24},{32,28},{36,32}... | collective-permute-start | bytes 147464 | tf_op jit(solution)/shard_map/ppermute | solution.py:569
  126.6 1.7 %collective-permute-done.14.heads = f32[96,128]{1,0:T(8,128)S(1)} collective-permute-done((f32[96,128]{1,0:T(8,128)S(1)}, f32[96,128]{1,0:T(8,128)S(1)}, u32[]{:S(2)}, u32[]{:S(2)}) %collective-permute-start.14) | collective-permute-done | bytes 49184 | tf_op jit(solution)/shard_map/ppermute | solution.py:569
  128.3 0.8 settle.1
  129.1 1.2 collective-permute-start.18
  130.3 0.6 collective-permute-start.15
  131.0 2.0 %collective-permute-start.16 = (f32[80,128]{1,0:T(8,128)S(1)}, f32[80,128]{1,0:T(8,128)S(1)}, u32[]{:S(2)}, u32[]{:S(2)}) collective-permute-start(f32[80,128]{1,0:T(8,128)S(1)} %add.54), channel_id=1, source_target_pairs={{0,128},{8,136},{16,144},{24,152},{32,160},{40,168},{48,176},{56,1... | collective-permute-start | bytes 122888 | tf_op jit(solution)/shard_map/ppermute | solution.py:438
  133.0 2.1 %collective-permute-start.17 = (f32[80,128]{1,0:T(8,128)S(1)}, f32[80,128]{1,0:T(8,128)S(1)}, u32[]{:S(2)}, u32[]{:S(2)}) collective-permute-start(f32[80,128]{1,0:T(8,128)S(1)} %add.54), channel_id=1, source_target_pairs={{0,192},{8,200},{16,208},{24,216},{32,224},{40,232},{48,240},{56,2... | collective-permute-start | bytes 122888 | tf_op jit(solution)/shard_map/ppermute | solution.py:438
  135.0 1.6 %collective-permute-done.18.other = bf16[2,256,128]{2,1,0:T(8,128)(2,1)S(1)} collective-permute-done((bf16[2,256,128]{2,1,0:T(8,128)(2,1)S(1)}, bf16[2,256,128]{2,1,0:T(8,128)(2,1)S(1)}, u32[]{:S(2)}, u32[]{:S(2)}) %collective-permute-start.18) | collective-permute-done | bytes 131104 | tf_op jit(solution)/shard_map/ppermute | solution.py:577
  136.6 0.8 place.1
  137.4 0.8 collective-permute-done.17
  138.2 2.8 %collective-permute-start.20 = (f32[32,128]{1,0:T(8,128)S(1)}, f32[32,128]{1,0:T(8,128)S(1)}, u32[]{:S(2)}, u32[]{:S(2)}) collective-permute-start(f32[32,128]{1,0:T(8,128)S(1)} %slice.21), channel_id=1, source_target_pairs={{0,2},{1,3},{2,0},{3,1},{4,6},{5,7},{6,4},{7,5},{8,10},{9,11},{10,... | collective-permute-start | bytes 49160 | tf_op jit(solution)/shard_map/ppermute | solution.py:438
  141.0 1.2 collective-permute-start.21
  142.3 1.3 collective-permute-done.20
  143.5 2.5 %collective-permute-done.21 = f32[32,128]{1,0:T(8,128)S(1)} collective-permute-done((f32[32,128]{1,0:T(8,128)S(1)}, f32[32,128]{1,0:T(8,128)S(1)}, u32[]{:S(2)}, u32[]{:S(2)}) %collective-permute-start.21) | collective-permute-done | bytes 16416 | tf_op jit(solution)/shard_map/ppermute | solution.py:438
  146.0 0.0 collective-permute-done.19
  146.0 0.6 finish.1
  (46 shorter events, 0.3 us)
Async XLA Ops:
  0.6 0.8 slice-start
  0.7 0.8 slice-start.1
  0.7 0.7 slice-start.2
  1.4 5.7 %collective-permute-start = (bf16[16,2048]{1,0:T(8,128)(2,1)S(1)}, bf16[16,2048]{1,0:T(8,128)(2,1)S(1)}, u32[]{:S(2)}, u32[]{:S(2)}) collective-permute-start(bf16[16,2048]{1,0:T(8,128)(2,1)S(1)} %pad_maximum_fusion), channel_id=1, source_target_pairs={{0,4},{4,8},{8,12},{12,16},{16,20},{20,24},{24,28},{28,32},{32,36}... | collective-permute-start | bytes 196616 | tf_op jit(solution)/shard_map/ppermute | solution.py:464
  3.4 0.7 copy-start.8
  4.1 0.9 copy-start.3
  5.0 0.9 copy-start.4
  6.0 0.7 copy-start.9
  6.0 0.7 copy-start.10
  6.0 0.7 copy-start.11
  6.0 0.7 copy-start.12
  6.3 1.0 copy-start
  6.7 0.9 copy-start.2
  6.7 0.9 copy-start.5
  7.1 0.7 copy-start.7
  8.9 3.3 %collective-permute-start.1 = (f32[544,128]{1,0:T(8,128)S(1)}, f32[544,128]{1,0:T(8,128)S(1)}, u32[]{:S(2)}, u32[]{:S(2)}) collective-permute-start(f32[544,128]{1,0:T(8,128)S(1)} %get-tuple-element.93), channel_id=1, source_target_pairs={{0,4},{4,0},{1,5},{5,1},{2,6},{6,2},{3,7},{7,3},{8,12},{12,8},{9,1... | collective-permute-start | bytes 835592 | tf_op jit(solution)/shard_map/ppermute | solution.py:421
  52.3 0.9 copy-start.1
  52.3 0.8 copy-start.6
  52.4 2.3 %collective-permute-start.2 = (f32[512,128]{1,0:T(8,128)S(1)}, f32[512,128]{1,0:T(8,128)S(1)}, u32[]{:S(2)}, u32[]{:S(2)}) collective-permute-start(f32[512,128]{1,0:T(8,128)S(1)} %get-tuple-element.97), channel_id=1, source_target_pairs={{0,4},{4,0},{1,5},{5,1},{2,6},{6,2},{3,7},{7,3},{8,12},{12,8},{9,1... | collective-permute-start | bytes 786440 | tf_op jit(solution)/shard_map/ppermute | solution.py:421
  55.1 5.2 %collective-permute-start.4 = (f32[8,128]{1,0:T(8,128)S(1)}, f32[8,128]{1,0:T(8,128)S(1)}, u32[]{:S(2)}, u32[]{:S(2)}) collective-permute-start(f32[8,128]{1,0:T(8,128)S(1)} %get-tuple-element.106), channel_id=1, source_target_pairs={{0,2},{1,3},{2,0},{3,1},{4,6},{5,7},{6,4},{7,5},{8,10},{9,11},{10,... | collective-permute-start | bytes 12296 | tf_op jit(solution)/shard_map/ppermute | solution.py:438
  58.4 4.8 %collective-permute-start.5 = (f32[8,128]{1,0:T(8,128)S(1)}, f32[8,128]{1,0:T(8,128)S(1)}, u32[]{:S(2)}, u32[]{:S(2)}) collective-permute-start(f32[8,128]{1,0:T(8,128)S(1)} %get-tuple-element.106), channel_id=1, source_target_pairs={{0,3},{1,2},{2,1},{3,0},{4,7},{5,6},{6,5},{7,4},{8,11},{9,10},{10,... | collective-permute-start | bytes 12296 | tf_op jit(solution)/shard_map/ppermute | solution.py:438
  59.5 3.8 %collective-permute-start.3 = (f32[8,128]{1,0:T(8,128)S(1)}, f32[8,128]{1,0:T(8,128)S(1)}, u32[]{:S(2)}, u32[]{:S(2)}) collective-permute-start(f32[8,128]{1,0:T(8,128)S(1)} %get-tuple-element.106), channel_id=1, source_target_pairs={{0,1},{1,0},{2,3},{3,2},{4,5},{5,4},{6,7},{7,6},{8,9},{9,8},{10,11... | collective-permute-start | bytes 12296 | tf_op jit(solution)/shard_map/ppermute | solution.py:438
  63.8 1.6 %collective-permute-start.6 = (f32[512,128]{1,0:T(8,128)S(1)}, f32[512,128]{1,0:T(8,128)S(1)}, u32[]{:S(2)}, u32[]{:S(2)}) collective-permute-start(f32[512,128]{1,0:T(8,128)S(1)} %get-tuple-element.109), channel_id=1, source_target_pairs={{0,4},{4,0},{1,5},{5,1},{2,6},{6,2},{3,7},{7,3},{8,12},{12,8},{9,1... | collective-permute-start | bytes 786440 | tf_op jit(solution)/shard_map/ppermute | solution.py:421
  98.9 3.2 %collective-permute-start.7 = (f32[512,128]{1,0:T(8,128)S(1)}, f32[512,128]{1,0:T(8,128)S(1)}, u32[]{:S(2)}, u32[]{:S(2)}) collective-permute-start(f32[512,128]{1,0:T(8,128)S(1)} %get-tuple-element.111), channel_id=1, source_target_pairs={{0,4},{4,0},{1,5},{5,1},{2,6},{6,2},{3,7},{7,3},{8,12},{12,8},{9,1... | collective-permute-start | bytes 786440 | tf_op jit(solution)/shard_map/ppermute | solution.py:421
  105.2 12.2 %collective-permute-start.8 = (f32[2,272,128]{2,1,0:T(8,128)S(1)}, f32[2,272,128]{2,1,0:T(8,128)S(1)}, u32[]{:S(2)}, u32[]{:S(2)}) collective-permute-start(f32[2,272,128]{2,1,0:T(8,128)S(1)} %get-tuple-element.127), channel_id=1, source_target_pairs={{0,3},{1,2},{2,1},{3,0},{4,7},{5,6},{6,5},{7,4},{8,11},{9,10},{10,... | collective-permute-start | bytes 835592 | tf_op jit(solution)/shard_map/ppermute | solution.py:558
  107.2 1.2 collective-permute-start.9
  108.4 4.0 %collective-permute-start.10 = (f32[80,128]{1,0:T(8,128)S(1)}, f32[80,128]{1,0:T(8,128)S(1)}, u32[]{:S(2)}, u32[]{:S(2)}) collective-permute-start(f32[80,128]{1,0:T(8,128)S(1)} %add.49), channel_id=1, source_target_pairs={{0,8},{8,0},{16,24},{24,16},{32,40},{40,32},{48,56},{56,48},{64,72... | collective-permute-start | bytes 122888 | tf_op jit(solution)/shard_map/ppermute | solution.py:433
  112.4 4.9 %collective-permute-start.11 = (f32[80,128]{1,0:T(8,128)S(1)}, f32[80,128]{1,0:T(8,128)S(1)}, u32[]{:S(2)}, u32[]{:S(2)}) collective-permute-start(f32[80,128]{1,0:T(8,128)S(1)} %add.50), channel_id=1, source_target_pairs={{0,16},{8,24},{16,0},{24,8},{32,48},{40,56},{48,32},{56,40},{64,80... | collective-permute-start | bytes 122888 | tf_op jit(solution)/shard_map/ppermute | solution.py:433
  117.4 7.2 %collective-permute-start.12 = (f32[2,272,128]{2,1,0:T(8,128)S(1)}, f32[2,272,128]{2,1,0:T(8,128)S(1)}, u32[]{:S(2)}, u32[]{:S(2)}) collective-permute-start(f32[2,272,128]{2,1,0:T(8,128)S(1)} %add.52), channel_id=1, source_target_pairs={{0,1},{1,0},{2,3},{3,2},{4,5},{5,4},{6,7},{7,6},{8,9},{9,8},{10,11... | collective-permute-start | bytes 835592 | tf_op jit(solution)/shard_map/ppermute | solution.py:564
  117.5 7.1 %collective-permute-start.13 = (f32[80,128]{1,0:T(8,128)S(1)}, f32[80,128]{1,0:T(8,128)S(1)}, u32[]{:S(2)}, u32[]{:S(2)}) collective-permute-start(f32[80,128]{1,0:T(8,128)S(1)} %add.51), channel_id=1, source_target_pairs={{0,56},{8,48},{16,40},{24,32},{32,24},{40,16},{48,8},{56,0},{64,12... | collective-permute-start | bytes 122888 | tf_op jit(solution)/shard_map/ppermute | solution.py:433
  124.7 3.7 %collective-permute-start.14 = (f32[96,128]{1,0:T(8,128)S(1)}, f32[96,128]{1,0:T(8,128)S(1)}, u32[]{:S(2)}, u32[]{:S(2)}) collective-permute-start(f32[96,128]{1,0:T(8,128)S(1)} %pad_maximum_fusion.1), channel_id=1, source_target_pairs={{4,0},{8,4},{12,8},{16,12},{20,16},{24,20},{28,24},{32,28},{36,32}... | collective-permute-start | bytes 147464 | tf_op jit(solution)/shard_map/ppermute | solution.py:569
  129.1 7.5 %collective-permute-start.18 = (bf16[2,256,128]{2,1,0:T(8,128)(2,1)S(1)}, bf16[2,256,128]{2,1,0:T(8,128)(2,1)S(1)}, u32[]{:S(2)}, u32[]{:S(2)}) collective-permute-start(bf16[2,256,128]{2,1,0:T(8,128)(2,1)S(1)} %get-tuple-element.138.half), channel_id=1, source_target_pairs={{0,3},{1,2},{2,1},{3,0},{4,7},{5,6},{6,5},{7,4},{8,11},{9,10},{10,... | collective-permute-start | bytes 393224 | tf_op jit(solution)/shard_map/ppermute | solution.py:577
  130.3 7.0 %collective-permute-start.15 = (f32[80,128]{1,0:T(8,128)S(1)}, f32[80,128]{1,0:T(8,128)S(1)}, u32[]{:S(2)}, u32[]{:S(2)}) collective-permute-start(f32[80,128]{1,0:T(8,128)S(1)} %add.54), channel_id=1, source_target_pairs={{0,64},{8,72},{16,80},{24,88},{32,96},{40,104},{48,112},{56,120},{... | collective-permute-start | bytes 122888 | tf_op jit(solution)/shard_map/ppermute | solution.py:438
  131.0 6.4 %collective-permute-start.16 = (f32[80,128]{1,0:T(8,128)S(1)}, f32[80,128]{1,0:T(8,128)S(1)}, u32[]{:S(2)}, u32[]{:S(2)}) collective-permute-start(f32[80,128]{1,0:T(8,128)S(1)} %add.54), channel_id=1, source_target_pairs={{0,128},{8,136},{16,144},{24,152},{32,160},{40,168},{48,176},{56,1... | collective-permute-start | bytes 122888 | tf_op jit(solution)/shard_map/ppermute | solution.py:438
  133.0 5.2 %collective-permute-start.17 = (f32[80,128]{1,0:T(8,128)S(1)}, f32[80,128]{1,0:T(8,128)S(1)}, u32[]{:S(2)}, u32[]{:S(2)}) collective-permute-start(f32[80,128]{1,0:T(8,128)S(1)} %add.54), channel_id=1, source_target_pairs={{0,192},{8,200},{16,208},{24,216},{32,224},{40,232},{48,240},{56,2... | collective-permute-start | bytes 122888 | tf_op jit(solution)/shard_map/ppermute | solution.py:438
  138.2 5.3 %collective-permute-start.20 = (f32[32,128]{1,0:T(8,128)S(1)}, f32[32,128]{1,0:T(8,128)S(1)}, u32[]{:S(2)}, u32[]{:S(2)}) collective-permute-start(f32[32,128]{1,0:T(8,128)S(1)} %slice.21), channel_id=1, source_target_pairs={{0,2},{1,3},{2,0},{3,1},{4,6},{5,7},{6,4},{7,5},{8,10},{9,11},{10,... | collective-permute-start | bytes 49160 | tf_op jit(solution)/shard_map/ppermute | solution.py:438
  141.0 4.9 %collective-permute-start.21 = (f32[32,128]{1,0:T(8,128)S(1)}, f32[32,128]{1,0:T(8,128)S(1)}, u32[]{:S(2)}, u32[]{:S(2)}) collective-permute-start(f32[32,128]{1,0:T(8,128)S(1)} %slice.21), channel_id=1, source_target_pairs={{0,3},{1,2},{2,1},{3,0},{4,7},{5,6},{6,5},{7,4},{8,11},{9,10},{10,... | collective-permute-start | bytes 49160 | tf_op jit(solution)/shard_map/ppermute | solution.py:438
  142.3 3.7 %collective-permute-start.19 = (f32[32,128]{1,0:T(8,128)S(1)}, f32[32,128]{1,0:T(8,128)S(1)}, u32[]{:S(2)}, u32[]{:S(2)}) collective-permute-start(f32[32,128]{1,0:T(8,128)S(1)} %slice.21), channel_id=1, source_target_pairs={{0,1},{1,0},{2,3},{3,2},{4,5},{5,4},{6,7},{7,6},{8,9},{9,8},{10,11... | collective-permute-start | bytes 49160 | tf_op jit(solution)/shard_map/ppermute | solution.py:438

commit v9 on v8

--- a/solution.py
+++ b/solution.py
@@ -556,8 +556,7 @@
     peers = lax.axis_size("tp")
     across = [(i, peers - 1 - i) for i in range(peers)]
     arrived = lax.ppermute(give, "tp", across)
-    packed = packed + swap_cores(packed)
-    packed = fold(packed, "chip", mirror(2))
+    packed = sum_four(packed, CTX)
     packed = fold(packed, "chip", lambda i: i ^ 2)
     arrived, packed = lax.optimization_barrier((arrived, packed))
     mine = keep + arrived

time: 147 us -> 148 us (level)
  starting transfers between devices: 25.9 us -> 28.4 us
  waiting for transfers between devices: 28.5 us -> 26.7 us
    ppermute x3 -> x2, waiting for transfers between devices: 13.1 us -> 8.94 us  [fold(): lax.ppermute(x, axis, [(i, partner(i)) for i in range(lax.axis_size(axis))])]
    ppermute x1, waiting for transfers between devices: 0.01 us -> 2.68 us  [body(): arrived = lax.ppermute(give, 'tp', across)]
    ppermute x9 -> x12, starting transfers between devices: 13.1 us -> 14.8 us  [sum_four(): lax.ppermute(x, axis, [(i, (i // block ^ k) * block + i % block) for i in...]
    ppermute x5 -> x4, waiting for transfers between devices: 3.73 us -> 2.71 us  [swap_cores(): return lax.ppermute(v, 'core', [(0, 1), (1, 0)])]
    ppermute x9 -> x12, waiting for transfers between devices: 8.32 us -> 9.06 us  [sum_four(): lax.ppermute(x, axis, [(i, (i // block ^ k) * block + i % block) for i in...]
    ppermute x3 -> x2, starting transfers between devices: 2.87 us -> 3.15 us  [fold(): lax.ppermute(x, axis, [(i, partner(i)) for i in range(lax.axis_size(axis))])]
  transfers between devices with their start and end apart: 22 -> 23, of which waited for: 13 -> 16; matrix products, arithmetic and copies ran while one was open for 0% -> 0% of each run, Pallas kernels for 4% -> 4%
where the time goes in v9:
time: 148 us; the launch traced here: 147 us
  blocking collectives  72.9 us (49%)
  starting transfers between devices  28.4 us (19%)
  waiting for transfers between devices  26.7 us (18%)
  Pallas kernels  13.2 us (9%)
  local copies, waits for them, and re-layouts  5.15 us (3%)
    all_to_all x4, blocking collectives, over_chips(): return lax.all_to_all(v, 'chip', 0, 0)  72.9 us
    ppermute x12, starting transfers between devices, sum_four(): lax.ppermute(x, axis, [(i, (i // block ^ k) * block + i % block) for i in...  14.8 us
    pallas_call x17, Pallas kernels, call(): pl.pallas_call(kernel, out_shape=[jax.ShapeDtypeStruct(s, d) for s, d in...  13.2 us
    ppermute x12, waiting for transfers between devices, sum_four(): lax.ppermute(x, axis, [(i, (i // block ^ k) * block + i % block) for i in...  9.06 us
    ppermute x2, waiting for transfers between devices, fold(): lax.ppermute(x, axis, [(i, partner(i)) for i in range(lax.axis_size(axis))])  8.94 us
    unnamed x26, local copies, waits for them, and re-layouts  4.4 us
    ppermute x2, starting transfers between devices, fold(): lax.ppermute(x, axis, [(i, partner(i)) for i in range(lax.axis_size(axis))])  3.15 us
  transfers between devices with their start and end apart: 23, of which 16 were waited for; matrix products, arithmetic and copies ran while one was open for 0% of the time, Pallas kernels for 4%

profile of v9, /device:TPU:32, one launch (start us, length us, event | category | flops | bytes accessed | tf_op | source)
XLA Modules:
  0.0 147.4 jit_solution(13175980175104424186)
XLA Ops:
  0.7 0.7 slice-done
  1.4 1.9 %collective-permute-start = (bf16[16,2048]{1,0:T(8,128)(2,1)S(1)}, bf16[16,2048]{1,0:T(8,128)(2,1)S(1)}, u32[]{:S(2)}, u32[]{:S(2)}) collective-permute-start(bf16[16,2048]{1,0:T(8,128)(2,1)S(1)} %pad_maximum_fusion), channel_id=1, source_target_pairs={{0,4},{4,8},{8,12},{12,16},{16,20},{20,24},{24,28},{28,32},{32,36}... | collective-permute-start | bytes 196616 | tf_op jit(solution)/shard_map/ppermute | solution.py:464
  3.4 0.7 copy-done.8
  4.1 0.9 copy-done.3
  5.0 0.9 copy-done.4
  6.0 0.3 turn.1
  6.3 0.4 copy-done.9
  6.7 0.4 steps.1
  7.1 0.1 copy-done
  7.3 0.3 copy-done.2
  7.6 0.2 copy-done.7
  7.9 1.0 state.1
  8.9 2.1 %collective-permute-start.1 = (f32[544,128]{1,0:T(8,128)S(1)}, f32[544,128]{1,0:T(8,128)S(1)}, u32[]{:S(2)}, u32[]{:S(2)}) collective-permute-start(f32[544,128]{1,0:T(8,128)S(1)} %get-tuple-element.93), channel_id=1, source_target_pairs={{0,4},{4,0},{1,5},{5,1},{2,6},{6,2},{3,7},{7,3},{8,12},{12,8},{9,1... | collective-permute-start | bytes 835592 | tf_op jit(solution)/shard_map/ppermute | solution.py:421
  11.0 1.2 collective-permute-done.1.got
  12.2 0.2 join.2
  12.4 23.2 %all_to_all.20.s.d = f32[32,1,2176]{2,1,0:T(1,128)S(1)} all-to-all(f32[32,1,2176]{2,1,0:T(1,128)S(1)} %get-tuple-element.94), channel_id=1, replica_groups=mesh['chip'=32,'core'=2,'tp'=4] {'chip'}, dimensions={0} | all-to-all | bytes 557056 | tf_op jit(solution)/shard_map/all_to_all | solution.py:429
  35.6 0.2 block_scan.2
  35.8 16.5 %all_to_all.21 = f32[32,1,2048]{2,1,0:T(1,128)S(1)} all-to-all(f32[32,1,2048]{2,1,0:T(1,128)S(1)} %block_scan.2), channel_id=1, replica_groups=mesh['chip'=32,'core'=2,'tp'=4] {'chip'}, dimensions={0} | all-to-all | bytes 524288 | tf_op jit(solution)/shard_map/all_to_all | solution.py:429
  52.4 0.1 collective-permute-start.2
  52.5 0.7 copy-done.1
  53.2 1.4 local.1
  54.6 0.5 output.1
  55.1 3.3 %collective-permute-start.4 = (f32[8,128]{1,0:T(8,128)S(1)}, f32[8,128]{1,0:T(8,128)S(1)}, u32[]{:S(2)}, u32[]{:S(2)}) collective-permute-start(f32[8,128]{1,0:T(8,128)S(1)} %get-tuple-element.106), channel_id=1, source_target_pairs={{0,2},{1,3},{2,0},{3,1},{4,6},{5,7},{6,4},{7,5},{8,10},{9,11},{10,... | collective-permute-start | bytes 12296 | tf_op jit(solution)/shard_map/ppermute | solution.py:438
  58.4 1.1 collective-permute-start.5
  59.5 0.9 collective-permute-done.4
  60.3 2.9 %collective-permute-done.5 = f32[8,128]{1,0:T(8,128)S(1)} collective-permute-done((f32[8,128]{1,0:T(8,128)S(1)}, f32[8,128]{1,0:T(8,128)S(1)}, u32[]{:S(2)}, u32[]{:S(2)}) %collective-permute-start.5) | collective-permute-done | bytes 4128 | tf_op jit(solution)/shard_map/ppermute | solution.py:438
  63.2 0.6 gate.1
  63.8 0.1 collective-permute-start.6
  63.9 1.5 %collective-permute-done.6.got = f32[512,128]{1,0:T(8,128)S(1)} collective-permute-done((f32[512,128]{1,0:T(8,128)S(1)}, f32[512,128]{1,0:T(8,128)S(1)}, u32[]{:S(2)}, u32[]{:S(2)}) %collective-permute-start.6) | collective-permute-done | bytes 262176 | tf_op jit(solution)/shard_map/ppermute | solution.py:421
  65.5 16.9 %all_to_all.22.s = f32[32,1,2048]{2,1,0:T(1,128)S(1)} all-to-all(f32[32,1,2048]{2,1,0:T(1,128)S(1)} %bitcast.18), channel_id=1, replica_groups=mesh['chip'=32,'core'=2,'tp'=4] {'chip'}, dimensions={0} | all-to-all | bytes 524288 | tf_op jit(solution)/shard_map/all_to_all | solution.py:429
  82.5 0.2 block_scan.3
  82.6 16.2 %all_to_all.23 = f32[32,1,2048]{2,1,0:T(1,128)S(1)} all-to-all(f32[32,1,2048]{2,1,0:T(1,128)S(1)} %block_scan.3), channel_id=1, replica_groups=mesh['chip'=32,'core'=2,'tp'=4] {'chip'}, dimensions={0} | all-to-all | bytes 524288 | tf_op jit(solution)/shard_map/all_to_all | solution.py:429
  98.9 0.3 collective-permute-start.7
  99.2 2.9 %middle.1 = (f32[1024,128]{1,0:T(8,128)S(1)}, f32[128,512]{1,0:T(8,128)S(1)}, f32[32,128]{1,0:T(8,128)S(1)}, f32[32,128]{1,0:T(8,128)S(1)}, bf16[128,1024]{1,0:T...) custom-call(f32[8,128]{1,0:T(8,128)S(1)} %add_add_fusion.3.sums, f32[1024,128]{1,0:T(8,128)S(1)} %get-tuple-element.107.y, ...), custom_call_target="tpu_custom_call" | custom-call | flops 20000000 | bytes 4194304 | tf_op jit(solution)/shard_map/middle/pallas_call | solution.py:408
  102.1 3.1 %last.1 = (f32[128,1024]{1,0:T(8,128)S(1)}, f32[64,128]{1,0:T(8,128)S(1)}, f32[2,272,128]{2,1,0:T(8,128)S(1)}, f32[2,272,128]{2,1,0:T(8,128)S(1)}, f32[80,128]{1,0:T(8,128)S(1)}, /*index=5*/f32[32,128]{1,0:T(8,128)}) custom-call(s32[1]{0:T(128)} %bitcast.core, s32[1]{0:T(128)} %bitcast.1.which, f32[512,128]{1,0:T(8,128)S(1)} %get-tuple-element.110.own, ...), custom_call_target="tpu_custom_call" | custom-call | flops 20000000 | bytes 4194304 | tf_op jit(solution)/shard_map/last/pallas_call | solution.py:408
  105.2 0.2 collective-permute-start.10
  105.4 1.6 %collective-permute-start.11 = (f32[80,128]{1,0:T(8,128)S(1)}, f32[80,128]{1,0:T(8,128)S(1)}, u32[]{:S(2)}, u32[]{:S(2)}) collective-permute-start(f32[80,128]{1,0:T(8,128)S(1)} %get-tuple-element.128), channel_id=1, source_target_pairs={{0,12},{4,8},{8,4},{12,0},{16,28},{20,24},{24,20},{28,16},{32,44},... | collective-permute-start | bytes 122888 | tf_op jit(solution)/shard_map/ppermute | solution.py:438
  107.0 0.3 collective-permute-start.9
  107.3 2.0 %collective-permute-start.8 = (f32[2,272,128]{2,1,0:T(8,128)S(1)}, f32[2,272,128]{2,1,0:T(8,128)S(1)}, u32[]{:S(2)}, u32[]{:S(2)}) collective-permute-start(f32[2,272,128]{2,1,0:T(8,128)S(1)} %get-tuple-element.127), channel_id=1, source_target_pairs={{0,3},{1,2},{2,1},{3,0},{4,7},{5,6},{6,5},{7,4},{8,11},{9,10},{10,... | collective-permute-start | bytes 835592 | tf_op jit(solution)/shard_map/ppermute | solution.py:558
  109.4 0.2 collective-permute-done.10
  109.6 1.4 collective-permute-start.12
  111.1 3.6 %collective-permute-done.12 = f32[80,128]{1,0:T(8,128)S(1)} collective-permute-done((f32[80,128]{1,0:T(8,128)S(1)}, f32[80,128]{1,0:T(8,128)S(1)}, u32[]{:S(2)}, u32[]{:S(2)}) %collective-permute-start.12) | collective-permute-done | bytes 40992 | tf_op jit(solution)/shard_map/ppermute | solution.py:433
  114.6 2.7 %collective-permute-done.8 = f32[2,272,128]{2,1,0:T(8,128)S(1)} collective-permute-done((f32[2,272,128]{2,1,0:T(8,128)S(1)}, f32[2,272,128]{2,1,0:T(8,128)S(1)}, u32[]{:S(2)}, u32[]{:S(2)}) %collective-permute-start.8) | collective-permute-done | bytes 278560 | tf_op jit(solution)/shard_map/ppermute | solution.py:558
  117.4 0.1 collective-permute-start.13
  117.5 1.7 %collective-permute-start.14 = (f32[80,128]{1,0:T(8,128)S(1)}, f32[80,128]{1,0:T(8,128)S(1)}, u32[]{:S(2)}, u32[]{:S(2)}) collective-permute-start(f32[80,128]{1,0:T(8,128)S(1)} %add.55), channel_id=1, source_target_pairs={{0,56},{8,48},{16,40},{24,32},{32,24},{40,16},{48,8},{56,0},{64,12... | collective-permute-start | bytes 122888 | tf_op jit(solution)/shard_map/ppermute | solution.py:433
  119.2 5.4 %collective-permute-done.14 = f32[80,128]{1,0:T(8,128)S(1)} collective-permute-done((f32[80,128]{1,0:T(8,128)S(1)}, f32[80,128]{1,0:T(8,128)S(1)}, u32[]{:S(2)}, u32[]{:S(2)}) %collective-permute-start.14) | collective-permute-done | bytes 40992 | tf_op jit(solution)/shard_map/ppermute | solution.py:433
  124.6 0.8 collective-permute-done.13
  125.4 1.9 %collective-permute-start.15 = (f32[96,128]{1,0:T(8,128)S(1)}, f32[96,128]{1,0:T(8,128)S(1)}, u32[]{:S(2)}, u32[]{:S(2)}) collective-permute-start(f32[96,128]{1,0:T(8,128)S(1)} %pad_maximum_fusion.1), channel_id=1, source_target_pairs={{4,0},{8,4},{12,8},{16,12},{20,16},{24,20},{28,24},{32,28},{36,32}... | collective-permute-start | bytes 147464 | tf_op jit(solution)/shard_map/ppermute | solution.py:568
  127.4 1.7 %collective-permute-done.15.heads = f32[96,128]{1,0:T(8,128)S(1)} collective-permute-done((f32[96,128]{1,0:T(8,128)S(1)}, f32[96,128]{1,0:T(8,128)S(1)}, u32[]{:S(2)}, u32[]{:S(2)}) %collective-permute-start.15) | collective-permute-done | bytes 49184 | tf_op jit(solution)/shard_map/ppermute | solution.py:568
  129.1 0.8 settle.1
  129.9 2.0 %collective-permute-start.19 = (bf16[2,256,128]{2,1,0:T(8,128)(2,1)S(1)}, bf16[2,256,128]{2,1,0:T(8,128)(2,1)S(1)}, u32[]{:S(2)}, u32[]{:S(2)}) collective-permute-start(bf16[2,256,128]{2,1,0:T(8,128)(2,1)S(1)} %get-tuple-element.138.half), channel_id=1, source_target_pairs={{0,3},{1,2},{2,1},{3,0},{4,7},{5,6},{6,5},{7,4},{8,11},{9,10},{10,... | collective-permute-start | bytes 393224 | tf_op jit(solution)/shard_map/ppermute | solution.py:576
  131.9 0.6 collective-permute-start.16
  132.5 2.0 %collective-permute-start.17 = (f32[80,128]{1,0:T(8,128)S(1)}, f32[80,128]{1,0:T(8,128)S(1)}, u32[]{:S(2)}, u32[]{:S(2)}) collective-permute-start(f32[80,128]{1,0:T(8,128)S(1)} %add.58), channel_id=1, source_target_pairs={{0,128},{8,136},{16,144},{24,152},{32,160},{40,168},{48,176},{56,1... | collective-permute-start | bytes 122888 | tf_op jit(solution)/shard_map/ppermute | solution.py:438
  134.5 2.1 %collective-permute-start.18 = (f32[80,128]{1,0:T(8,128)S(1)}, f32[80,128]{1,0:T(8,128)S(1)}, u32[]{:S(2)}, u32[]{:S(2)}) collective-permute-start(f32[80,128]{1,0:T(8,128)S(1)} %add.58), channel_id=1, source_target_pairs={{0,192},{8,200},{16,208},{24,216},{32,224},{40,232},{48,240},{56,2... | collective-permute-start | bytes 122888 | tf_op jit(solution)/shard_map/ppermute | solution.py:438
  136.6 0.8 collective-permute-done.19.other
  137.3 0.8 place.1
  138.1 1.6 %collective-permute-done.18 = f32[80,128]{1,0:T(8,128)S(1)} collective-permute-done((f32[80,128]{1,0:T(8,128)S(1)}, f32[80,128]{1,0:T(8,128)S(1)}, u32[]{:S(2)}, u32[]{:S(2)}) %collective-permute-start.18) | collective-permute-done | bytes 40992 | tf_op jit(solution)/shard_map/ppermute | solution.py:438
  139.7 1.2 collective-permute-start.21
  141.0 2.0 %collective-permute-start.22 = (f32[32,128]{1,0:T(8,128)S(1)}, f32[32,128]{1,0:T(8,128)S(1)}, u32[]{:S(2)}, u32[]{:S(2)}) collective-permute-start(f32[32,128]{1,0:T(8,128)S(1)} %slice.21), channel_id=1, source_target_pairs={{0,3},{1,2},{2,1},{3,0},{4,7},{5,6},{6,5},{7,4},{8,11},{9,10},{10,... | collective-permute-start | bytes 49160 | tf_op jit(solution)/shard_map/ppermute | solution.py:438
  143.0 0.3 collective-permute-start.20
  143.3 1.8 %collective-permute-done.21 = f32[32,128]{1,0:T(8,128)S(1)} collective-permute-done((f32[32,128]{1,0:T(8,128)S(1)}, f32[32,128]{1,0:T(8,128)S(1)}, u32[]{:S(2)}, u32[]{:S(2)}) %collective-permute-start.21) | collective-permute-done | bytes 16416 | tf_op jit(solution)/shard_map/ppermute | solution.py:438
  145.1 0.9 collective-permute-done.22
  145.9 0.8 collective-permute-done.20
  146.8 0.6 finish.1
  (47 shorter events, 0.5 us)
Async XLA Ops:
  0.6 0.8 slice-start
  0.7 0.8 slice-start.1
  0.7 0.7 slice-start.2
  1.4 5.7 %collective-permute-start = (bf16[16,2048]{1,0:T(8,128)(2,1)S(1)}, bf16[16,2048]{1,0:T(8,128)(2,1)S(1)}, u32[]{:S(2)}, u32[]{:S(2)}) collective-permute-start(bf16[16,2048]{1,0:T(8,128)(2,1)S(1)} %pad_maximum_fusion), channel_id=1, source_target_pairs={{0,4},{4,8},{8,12},{12,16},{16,20},{20,24},{24,28},{28,32},{32,36}... | collective-permute-start | bytes 196616 | tf_op jit(solution)/shard_map/ppermute | solution.py:464
  3.4 0.7 copy-start.8
  4.1 0.9 copy-start.3
  5.0 0.9 copy-start.4
  6.0 0.7 copy-start.9
  6.0 0.7 copy-start.10
  6.0 0.7 copy-start.11
  6.0 0.7 copy-start.12
  6.3 1.0 copy-start
  6.7 0.9 copy-start.2
  6.7 0.9 copy-start.5
  7.1 0.7 copy-start.7
  8.9 3.3 %collective-permute-start.1 = (f32[544,128]{1,0:T(8,128)S(1)}, f32[544,128]{1,0:T(8,128)S(1)}, u32[]{:S(2)}, u32[]{:S(2)}) collective-permute-start(f32[544,128]{1,0:T(8,128)S(1)} %get-tuple-element.93), channel_id=1, source_target_pairs={{0,4},{4,0},{1,5},{5,1},{2,6},{6,2},{3,7},{7,3},{8,12},{12,8},{9,1... | collective-permute-start | bytes 835592 | tf_op jit(solution)/shard_map/ppermute | solution.py:421
  52.3 0.9 copy-start.1
  52.3 0.8 copy-start.6
  52.4 2.3 %collective-permute-start.2 = (f32[512,128]{1,0:T(8,128)S(1)}, f32[512,128]{1,0:T(8,128)S(1)}, u32[]{:S(2)}, u32[]{:S(2)}) collective-permute-start(f32[512,128]{1,0:T(8,128)S(1)} %get-tuple-element.97), channel_id=1, source_target_pairs={{0,4},{4,0},{1,5},{5,1},{2,6},{6,2},{3,7},{7,3},{8,12},{12,8},{9,1... | collective-permute-start | bytes 786440 | tf_op jit(solution)/shard_map/ppermute | solution.py:421
  55.1 5.2 %collective-permute-start.4 = (f32[8,128]{1,0:T(8,128)S(1)}, f32[8,128]{1,0:T(8,128)S(1)}, u32[]{:S(2)}, u32[]{:S(2)}) collective-permute-start(f32[8,128]{1,0:T(8,128)S(1)} %get-tuple-element.106), channel_id=1, source_target_pairs={{0,2},{1,3},{2,0},{3,1},{4,6},{5,7},{6,4},{7,5},{8,10},{9,11},{10,... | collective-permute-start | bytes 12296 | tf_op jit(solution)/shard_map/ppermute | solution.py:438
  58.4 4.8 %collective-permute-start.5 = (f32[8,128]{1,0:T(8,128)S(1)}, f32[8,128]{1,0:T(8,128)S(1)}, u32[]{:S(2)}, u32[]{:S(2)}) collective-permute-start(f32[8,128]{1,0:T(8,128)S(1)} %get-tuple-element.106), channel_id=1, source_target_pairs={{0,3},{1,2},{2,1},{3,0},{4,7},{5,6},{6,5},{7,4},{8,11},{9,10},{10,... | collective-permute-start | bytes 12296 | tf_op jit(solution)/shard_map/ppermute | solution.py:438
  59.5 3.8 %collective-permute-start.3 = (f32[8,128]{1,0:T(8,128)S(1)}, f32[8,128]{1,0:T(8,128)S(1)}, u32[]{:S(2)}, u32[]{:S(2)}) collective-permute-start(f32[8,128]{1,0:T(8,128)S(1)} %get-tuple-element.106), channel_id=1, source_target_pairs={{0,1},{1,0},{2,3},{3,2},{4,5},{5,4},{6,7},{7,6},{8,9},{9,8},{10,11... | collective-permute-start | bytes 12296 | tf_op jit(solution)/shard_map/ppermute | solution.py:438
  63.8 1.6 %collective-permute-start.6 = (f32[512,128]{1,0:T(8,128)S(1)}, f32[512,128]{1,0:T(8,128)S(1)}, u32[]{:S(2)}, u32[]{:S(2)}) collective-permute-start(f32[512,128]{1,0:T(8,128)S(1)} %get-tuple-element.109), channel_id=1, source_target_pairs={{0,4},{4,0},{1,5},{5,1},{2,6},{6,2},{3,7},{7,3},{8,12},{12,8},{9,1... | collective-permute-start | bytes 786440 | tf_op jit(solution)/shard_map/ppermute | solution.py:421
  98.9 3.2 %collective-permute-start.7 = (f32[512,128]{1,0:T(8,128)S(1)}, f32[512,128]{1,0:T(8,128)S(1)}, u32[]{:S(2)}, u32[]{:S(2)}) collective-permute-start(f32[512,128]{1,0:T(8,128)S(1)} %get-tuple-element.111), channel_id=1, source_target_pairs={{0,4},{4,0},{1,5},{5,1},{2,6},{6,2},{3,7},{7,3},{8,12},{12,8},{9,1... | collective-permute-start | bytes 786440 | tf_op jit(solution)/shard_map/ppermute | solution.py:421
  105.2 4.4 %collective-permute-start.10 = (f32[80,128]{1,0:T(8,128)S(1)}, f32[80,128]{1,0:T(8,128)S(1)}, u32[]{:S(2)}, u32[]{:S(2)}) collective-permute-start(f32[80,128]{1,0:T(8,128)S(1)} %get-tuple-element.128), channel_id=1, source_target_pairs={{0,8},{4,12},{8,0},{12,4},{16,24},{20,28},{24,16},{28,20},{32,40},... | collective-permute-start | bytes 122888 | tf_op jit(solution)/shard_map/ppermute | solution.py:438
  105.4 4.2 %collective-permute-start.11 = (f32[80,128]{1,0:T(8,128)S(1)}, f32[80,128]{1,0:T(8,128)S(1)}, u32[]{:S(2)}, u32[]{:S(2)}) collective-permute-start(f32[80,128]{1,0:T(8,128)S(1)} %get-tuple-element.128), channel_id=1, source_target_pairs={{0,12},{4,8},{8,4},{12,0},{16,28},{20,24},{24,20},{28,16},{32,44},... | collective-permute-start | bytes 122888 | tf_op jit(solution)/shard_map/ppermute | solution.py:438
  107.0 2.6 %collective-permute-start.9 = (f32[80,128]{1,0:T(8,128)S(1)}, f32[80,128]{1,0:T(8,128)S(1)}, u32[]{:S(2)}, u32[]{:S(2)}) collective-permute-start(f32[80,128]{1,0:T(8,128)S(1)} %get-tuple-element.128), channel_id=1, source_target_pairs={{0,4},{4,0},{8,12},{12,8},{16,20},{20,16},{24,28},{28,24},{32,36},... | collective-permute-start | bytes 122888 | tf_op jit(solution)/shard_map/ppermute | solution.py:438
  107.3 10.0 %collective-permute-start.8 = (f32[2,272,128]{2,1,0:T(8,128)S(1)}, f32[2,272,128]{2,1,0:T(8,128)S(1)}, u32[]{:S(2)}, u32[]{:S(2)}) collective-permute-start(f32[2,272,128]{2,1,0:T(8,128)S(1)} %get-tuple-element.127), channel_id=1, source_target_pairs={{0,3},{1,2},{2,1},{3,0},{4,7},{5,6},{6,5},{7,4},{8,11},{9,10},{10,... | collective-permute-start | bytes 835592 | tf_op jit(solution)/shard_map/ppermute | solution.py:558
  109.6 5.0 %collective-permute-start.12 = (f32[80,128]{1,0:T(8,128)S(1)}, f32[80,128]{1,0:T(8,128)S(1)}, u32[]{:S(2)}, u32[]{:S(2)}) collective-permute-start(f32[80,128]{1,0:T(8,128)S(1)} %add_add_fusion.1), channel_id=1, source_target_pairs={{0,16},{8,24},{16,0},{24,8},{32,48},{40,56},{48,32},{56,40},{64,80... | collective-permute-start | bytes 122888 | tf_op jit(solution)/shard_map/ppermute | solution.py:433
  117.4 8.0 %collective-permute-start.13 = (f32[2,272,128]{2,1,0:T(8,128)S(1)}, f32[2,272,128]{2,1,0:T(8,128)S(1)}, u32[]{:S(2)}, u32[]{:S(2)}) collective-permute-start(f32[2,272,128]{2,1,0:T(8,128)S(1)} %add.56), channel_id=1, source_target_pairs={{0,1},{1,0},{2,3},{3,2},{4,5},{5,4},{6,7},{7,6},{8,9},{9,8},{10,11... | collective-permute-start | bytes 835592 | tf_op jit(solution)/shard_map/ppermute | solution.py:563
  117.5 7.1 %collective-permute-start.14 = (f32[80,128]{1,0:T(8,128)S(1)}, f32[80,128]{1,0:T(8,128)S(1)}, u32[]{:S(2)}, u32[]{:S(2)}) collective-permute-start(f32[80,128]{1,0:T(8,128)S(1)} %add.55), channel_id=1, source_target_pairs={{0,56},{8,48},{16,40},{24,32},{32,24},{40,16},{48,8},{56,0},{64,12... | collective-permute-start | bytes 122888 | tf_op jit(solution)/shard_map/ppermute | solution.py:433
  125.4 3.7 %collective-permute-start.15 = (f32[96,128]{1,0:T(8,128)S(1)}, f32[96,128]{1,0:T(8,128)S(1)}, u32[]{:S(2)}, u32[]{:S(2)}) collective-permute-start(f32[96,128]{1,0:T(8,128)S(1)} %pad_maximum_fusion.1), channel_id=1, source_target_pairs={{4,0},{8,4},{12,8},{16,12},{20,16},{24,20},{28,24},{32,28},{36,32}... | collective-permute-start | bytes 147464 | tf_op jit(solution)/shard_map/ppermute | solution.py:568
  129.9 7.5 %collective-permute-start.19 = (bf16[2,256,128]{2,1,0:T(8,128)(2,1)S(1)}, bf16[2,256,128]{2,1,0:T(8,128)(2,1)S(1)}, u32[]{:S(2)}, u32[]{:S(2)}) collective-permute-start(bf16[2,256,128]{2,1,0:T(8,128)(2,1)S(1)} %get-tuple-element.138.half), channel_id=1, source_target_pairs={{0,3},{1,2},{2,1},{3,0},{4,7},{5,6},{6,5},{7,4},{8,11},{9,10},{10,... | collective-permute-start | bytes 393224 | tf_op jit(solution)/shard_map/ppermute | solution.py:576
  131.9 6.2 %collective-permute-start.16 = (f32[80,128]{1,0:T(8,128)S(1)}, f32[80,128]{1,0:T(8,128)S(1)}, u32[]{:S(2)}, u32[]{:S(2)}) collective-permute-start(f32[80,128]{1,0:T(8,128)S(1)} %add.58), channel_id=1, source_target_pairs={{0,64},{8,72},{16,80},{24,88},{32,96},{40,104},{48,112},{56,120},{... | collective-permute-start | bytes 122888 | tf_op jit(solution)/shard_map/ppermute | solution.py:438
  132.5 5.6 %collective-permute-start.17 = (f32[80,128]{1,0:T(8,128)S(1)}, f32[80,128]{1,0:T(8,128)S(1)}, u32[]{:S(2)}, u32[]{:S(2)}) collective-permute-start(f32[80,128]{1,0:T(8,128)S(1)} %add.58), channel_id=1, source_target_pairs={{0,128},{8,136},{16,144},{24,152},{32,160},{40,168},{48,176},{56,1... | collective-permute-start | bytes 122888 | tf_op jit(solution)/shard_map/ppermute | solution.py:438
  134.5 5.2 %collective-permute-start.18 = (f32[80,128]{1,0:T(8,128)S(1)}, f32[80,128]{1,0:T(8,128)S(1)}, u32[]{:S(2)}, u32[]{:S(2)}) collective-permute-start(f32[80,128]{1,0:T(8,128)S(1)} %add.58), channel_id=1, source_target_pairs={{0,192},{8,200},{16,208},{24,216},{32,224},{40,232},{48,240},{56,2... | collective-permute-start | bytes 122888 | tf_op jit(solution)/shard_map/ppermute | solution.py:438
  139.7 5.3 %collective-permute-start.21 = (f32[32,128]{1,0:T(8,128)S(1)}, f32[32,128]{1,0:T(8,128)S(1)}, u32[]{:S(2)}, u32[]{:S(2)}) collective-permute-start(f32[32,128]{1,0:T(8,128)S(1)} %slice.21), channel_id=1, source_target_pairs={{0,2},{1,3},{2,0},{3,1},{4,6},{5,7},{6,4},{7,5},{8,10},{9,11},{10,... | collective-permute-start | bytes 49160 | tf_op jit(solution)/shard_map/ppermute | solution.py:438
  141.0 4.9 %collective-permute-start.22 = (f32[32,128]{1,0:T(8,128)S(1)}, f32[32,128]{1,0:T(8,128)S(1)}, u32[]{:S(2)}, u32[]{:S(2)}) collective-permute-start(f32[32,128]{1,0:T(8,128)S(1)} %slice.21), channel_id=1, source_target_pairs={{0,3},{1,2},{2,1},{3,0},{4,7},{5,6},{6,5},{7,4},{8,11},{9,10},{10,... | collective-permute-start | bytes 49160 | tf_op jit(solution)/shard_map/ppermute | solution.py:438
  143.0 3.7 %collective-permute-start.20 = (f32[32,128]{1,0:T(8,128)S(1)}, f32[32,128]{1,0:T(8,128)S(1)}, u32[]{:S(2)}, u32[]{:S(2)}) collective-permute-start(f32[32,128]{1,0:T(8,128)S(1)} %slice.21), channel_id=1, source_target_pairs={{0,1},{1,0},{2,3},{3,2},{4,5},{5,4},{6,7},{7,6},{8,9},{9,8},{10,11... | collective-permute-start | bytes 49160 | tf_op jit(solution)/shard_map/ppermute | solution.py:438

commit v10 on v8

--- a/solution.py
+++ b/solution.py
@@ -351,13 +351,17 @@
         give[rows, :] = jnp.where(leads, near, far)
 
 
-def settle_kernel(xown, mine, heads, gx, half):
+def settle_x_kernel(xown, heads, gx):
     last = slice(SPAN - LEAD, SPAN)
     none = jnp.zeros((LEAD - 8, TILE), F32)
     for r in range(PER):
         gx[0 : SPAN - LEAD, lanes(r)] = xown[0 : SPAN - LEAD, lanes(r)].astype(jnp.bfloat16)
         more = jnp.concatenate([none, heads[8 * r : 8 * r + 8, :]], axis=0)
         gx[last, lanes(r)] = (xown[last, lanes(r)] + more).astype(jnp.bfloat16)
+
+
+def settle_kernel(mine, heads, half):
+    none = jnp.zeros((LEAD - 8, TILE), F32)
     for g in range(2):
         for i in range(2):
             at = 64 + 16 * g + 8 * i
@@ -567,12 +571,8 @@
     heads = jnp.concatenate([xheads, mine[:, 2 * SPAN :].reshape(32, TILE)], axis=0)
     mine, heads, packed = lax.optimization_barrier((mine, heads, packed))
     heads = lax.ppermute(heads, CTX, [(i + 1, i) for i in range(size - 1)])
-    grad_x_raw, half = call(
-        settle_kernel,
-        "settle",
-        [((SPAN, wx), jnp.bfloat16), ((2, 2 * SPAN, TILE), jnp.bfloat16)],
-        (xown, mine, heads),
-    )
+    (half,) = call(settle_kernel, "settle", [((2, 2 * SPAN, TILE), jnp.bfloat16)], (mine, heads))
+    (grad_x_raw,) = call(settle_x_kernel, "settle_x", [((SPAN, wx), jnp.bfloat16)], (xown, heads))
     half, packed = lax.optimization_barrier((half, packed))
     other = lax.ppermute(half, "tp", across)
     half_bc, each = ((SPAN, wb), jnp.bfloat16), ((1, LOCAL), F32)

time: 147 us -> 147 us (level)
    pallas_call x17 -> x18, Pallas kernels: 13.2 us -> 13.2 us  [call(): pl.pallas_call(kernel, out_shape=[jax.ShapeDtypeStruct(s, d) for s, d in...]
  transfers between devices with their start and end apart: 22 -> 22, of which waited for: 13 -> 13; matrix products, arithmetic and copies ran while one was open for 0% -> 0% of each run, Pallas kernels for 4% -> 5%
where the time goes in v10:
time: 147 us; the launch traced here: 146 us
  blocking collectives  72.9 us (50%)
  waiting for transfers between devices  27.7 us (19%)
  starting transfers between devices  26 us (18%)
  Pallas kernels  13.2 us (9%)
  local copies, waits for them, and re-layouts  5.15 us (4%)
    all_to_all x4, blocking collectives, over_chips(): return lax.all_to_all(v, 'chip', 0, 0)  72.9 us
    pallas_call x18, Pallas kernels, call(): pl.pallas_call(kernel, out_shape=[jax.ShapeDtypeStruct(s, d) for s, d in...  13.2 us
    ppermute x3, waiting for transfers between devices, fold(): lax.ppermute(x, axis, [(i, partner(i)) for i in range(lax.axis_size(axis))])  13.1 us
    ppermute x9, starting transfers between devices, sum_four(): lax.ppermute(x, axis, [(i, (i // block ^ k) * block + i % block) for i in...  13.1 us
    ppermute x9, waiting for transfers between devices, sum_four(): lax.ppermute(x, axis, [(i, (i // block ^ k) * block + i % block) for i in...  7.57 us
    unnamed x26, local copies, waits for them, and re-layouts  4.4 us
    ppermute x5, waiting for transfers between devices, swap_cores(): return lax.ppermute(v, 'core', [(0, 1), (1, 0)])  3.73 us
  transfers between devices with their start and end apart: 22, of which 13 were waited for; matrix products, arithmetic and copies ran while one was open for 0% of the time, Pallas kernels for 5%

profile of v10, /device:TPU:32, one launch (start us, length us, event | category | flops | bytes accessed | tf_op | source)
XLA Modules:
  0.0 146.0 jit_solution(12335547874388110702)
XLA Ops:
  0.7 0.7 slice-done
  1.4 1.9 %collective-permute-start = (bf16[16,2048]{1,0:T(8,128)(2,1)S(1)}, bf16[16,2048]{1,0:T(8,128)(2,1)S(1)}, u32[]{:S(2)}, u32[]{:S(2)}) collective-permute-start(bf16[16,2048]{1,0:T(8,128)(2,1)S(1)} %pad_maximum_fusion), channel_id=1, source_target_pairs={{0,4},{4,8},{8,12},{12,16},{16,20},{20,24},{24,28},{28,32},{32,36}... | collective-permute-start | bytes 196616 | tf_op jit(solution)/shard_map/ppermute | solution.py:468
  3.4 0.7 copy-done.8
  4.1 0.9 copy-done.3
  5.0 0.9 copy-done.4
  6.0 0.3 turn.1
  6.3 0.4 copy-done.9
  6.7 0.4 steps.1
  7.1 0.0 collective-permute-done.before
  7.1 0.1 copy-done
  7.3 0.3 copy-done.2
  7.6 0.2 copy-done.7
  7.9 1.0 state.1
  8.9 2.1 %collective-permute-start.1 = (f32[544,128]{1,0:T(8,128)S(1)}, f32[544,128]{1,0:T(8,128)S(1)}, u32[]{:S(2)}, u32[]{:S(2)}) collective-permute-start(f32[544,128]{1,0:T(8,128)S(1)} %get-tuple-element.91), channel_id=1, source_target_pairs={{0,4},{4,0},{1,5},{5,1},{2,6},{6,2},{3,7},{7,3},{8,12},{12,8},{9,1... | collective-permute-start | bytes 835592 | tf_op jit(solution)/shard_map/ppermute | solution.py:425
  11.0 1.2 collective-permute-done.1.got
  12.2 0.2 join.2
  12.4 23.2 %all_to_all.20.s.d = f32[32,1,2176]{2,1,0:T(1,128)S(1)} all-to-all(f32[32,1,2176]{2,1,0:T(1,128)S(1)} %get-tuple-element.92), channel_id=1, replica_groups=mesh['chip'=32,'core'=2,'tp'=4] {'chip'}, dimensions={0} | all-to-all | bytes 557056 | tf_op jit(solution)/shard_map/all_to_all | solution.py:433
  35.6 0.2 block_scan.2
  35.8 16.5 %all_to_all.21 = f32[32,1,2048]{2,1,0:T(1,128)S(1)} all-to-all(f32[32,1,2048]{2,1,0:T(1,128)S(1)} %block_scan.2), channel_id=1, replica_groups=mesh['chip'=32,'core'=2,'tp'=4] {'chip'}, dimensions={0} | all-to-all | bytes 524288 | tf_op jit(solution)/shard_map/all_to_all | solution.py:433
  52.3 0.1 split.2
  52.4 0.1 collective-permute-start.2
  52.5 0.7 copy-done.1
  53.2 1.4 local.1
  54.6 0.5 output.1
  55.1 3.3 %collective-permute-start.4 = (f32[8,128]{1,0:T(8,128)S(1)}, f32[8,128]{1,0:T(8,128)S(1)}, u32[]{:S(2)}, u32[]{:S(2)}) collective-permute-start(f32[8,128]{1,0:T(8,128)S(1)} %get-tuple-element.104), channel_id=1, source_target_pairs={{0,2},{1,3},{2,0},{3,1},{4,6},{5,7},{6,4},{7,5},{8,10},{9,11},{10,... | collective-permute-start | bytes 12296 | tf_op jit(solution)/shard_map/ppermute | solution.py:442
  58.4 1.1 collective-permute-start.5
  59.5 0.9 collective-permute-done.4
  60.3 2.9 %collective-permute-done.5 = f32[8,128]{1,0:T(8,128)S(1)} collective-permute-done((f32[8,128]{1,0:T(8,128)S(1)}, f32[8,128]{1,0:T(8,128)S(1)}, u32[]{:S(2)}, u32[]{:S(2)}) %collective-permute-start.5) | collective-permute-done | bytes 4128 | tf_op jit(solution)/shard_map/ppermute | solution.py:442
  63.2 0.6 gate.1
  63.8 0.1 collective-permute-start.6
  63.9 1.5 %collective-permute-done.6.got = f32[512,128]{1,0:T(8,128)S(1)} collective-permute-done((f32[512,128]{1,0:T(8,128)S(1)}, f32[512,128]{1,0:T(8,128)S(1)}, u32[]{:S(2)}, u32[]{:S(2)}) %collective-permute-start.6) | collective-permute-done | bytes 262176 | tf_op jit(solution)/shard_map/ppermute | solution.py:425
  65.5 16.9 %all_to_all.22.s = f32[32,1,2048]{2,1,0:T(1,128)S(1)} all-to-all(f32[32,1,2048]{2,1,0:T(1,128)S(1)} %bitcast.18), channel_id=1, replica_groups=mesh['chip'=32,'core'=2,'tp'=4] {'chip'}, dimensions={0} | all-to-all | bytes 524288 | tf_op jit(solution)/shard_map/all_to_all | solution.py:433
  82.5 0.2 block_scan.3
  82.6 16.2 %all_to_all.23 = f32[32,1,2048]{2,1,0:T(1,128)S(1)} all-to-all(f32[32,1,2048]{2,1,0:T(1,128)S(1)} %block_scan.3), channel_id=1, replica_groups=mesh['chip'=32,'core'=2,'tp'=4] {'chip'}, dimensions={0} | all-to-all | bytes 524288 | tf_op jit(solution)/shard_map/all_to_all | solution.py:433
  98.8 0.1 split.3
  98.9 0.3 collective-permute-start.7
  99.2 2.9 %middle.1 = (f32[1024,128]{1,0:T(8,128)S(1)}, f32[128,512]{1,0:T(8,128)S(1)}, f32[32,128]{1,0:T(8,128)S(1)}, f32[32,128]{1,0:T(8,128)S(1)}, bf16[128,1024]{1,0:T...) custom-call(f32[8,128]{1,0:T(8,128)S(1)} %add_add_fusion.2.sums, f32[1024,128]{1,0:T(8,128)S(1)} %get-tuple-element.105.y, ...), custom_call_target="tpu_custom_call" | custom-call | flops 20000000 | bytes 4194304 | tf_op jit(solution)/shard_map/middle/pallas_call | solution.py:412
  102.1 3.1 %last.1 = (f32[128,1024]{1,0:T(8,128)S(1)}, f32[64,128]{1,0:T(8,128)S(1)}, f32[2,272,128]{2,1,0:T(8,128)S(1)}, f32[2,272,128]{2,1,0:T(8,128)S(1)}, f32[80,128]{1,0:T(8,128)S(1)}, /*index=5*/f32[32,128]{1,0:T(8,128)}) custom-call(s32[1]{0:T(128)} %bitcast.core, s32[1]{0:T(128)} %bitcast.1.which, f32[512,128]{1,0:T(8,128)S(1)} %get-tuple-element.108.own, ...), custom_call_target="tpu_custom_call" | custom-call | flops 20000000 | bytes 4194304 | tf_op jit(solution)/shard_map/last/pallas_call | solution.py:412
  105.2 2.0 %collective-permute-start.8 = (f32[2,272,128]{2,1,0:T(8,128)S(1)}, f32[2,272,128]{2,1,0:T(8,128)S(1)}, u32[]{:S(2)}, u32[]{:S(2)}) collective-permute-start(f32[2,272,128]{2,1,0:T(8,128)S(1)} %get-tuple-element.125), channel_id=1, source_target_pairs={{0,3},{1,2},{2,1},{3,0},{4,7},{5,6},{6,5},{7,4},{8,11},{9,10},{10,... | collective-permute-start | bytes 835592 | tf_op jit(solution)/shard_map/ppermute | solution.py:562
  107.2 0.2 collective-permute-start.9
  107.4 1.0 collective-permute-done.9
  108.4 0.2 collective-permute-start.10
  108.7 3.8 %collective-permute-done.10 = f32[80,128]{1,0:T(8,128)S(1)} collective-permute-done((f32[80,128]{1,0:T(8,128)S(1)}, f32[80,128]{1,0:T(8,128)S(1)}, u32[]{:S(2)}, u32[]{:S(2)}) %collective-permute-start.10) | collective-permute-done | bytes 40992 | tf_op jit(solution)/shard_map/ppermute | solution.py:437
  112.4 0.9 collective-permute-start.11
  113.4 4.0 %collective-permute-done.11 = f32[80,128]{1,0:T(8,128)S(1)} collective-permute-done((f32[80,128]{1,0:T(8,128)S(1)}, f32[80,128]{1,0:T(8,128)S(1)}, u32[]{:S(2)}, u32[]{:S(2)}) %collective-permute-start.11) | collective-permute-done | bytes 40992 | tf_op jit(solution)/shard_map/ppermute | solution.py:437
  117.4 0.1 collective-permute-start.12
  117.5 1.7 %collective-permute-start.13 = (f32[80,128]{1,0:T(8,128)S(1)}, f32[80,128]{1,0:T(8,128)S(1)}, u32[]{:S(2)}, u32[]{:S(2)}) collective-permute-start(f32[80,128]{1,0:T(8,128)S(1)} %add.51), channel_id=1, source_target_pairs={{0,56},{8,48},{16,40},{24,32},{32,24},{40,16},{48,8},{56,0},{64,12... | collective-permute-start | bytes 122888 | tf_op jit(solution)/shard_map/ppermute | solution.py:437
  119.2 5.4 %collective-permute-done.13 = f32[80,128]{1,0:T(8,128)S(1)} collective-permute-done((f32[80,128]{1,0:T(8,128)S(1)}, f32[80,128]{1,0:T(8,128)S(1)}, u32[]{:S(2)}, u32[]{:S(2)}) %collective-permute-start.13) | collective-permute-done | bytes 40992 | tf_op jit(solution)/shard_map/ppermute | solution.py:437
  124.7 1.9 %collective-permute-start.14 = (f32[96,128]{1,0:T(8,128)S(1)}, f32[96,128]{1,0:T(8,128)S(1)}, u32[]{:S(2)}, u32[]{:S(2)}) collective-permute-start(f32[96,128]{1,0:T(8,128)S(1)} %pad_maximum_fusion.1), channel_id=1, source_target_pairs={{4,0},{8,4},{12,8},{16,12},{20,16},{24,20},{28,24},{32,28},{36,32}... | collective-permute-start | bytes 147464 | tf_op jit(solution)/shard_map/ppermute | solution.py:573
  126.6 1.7 %collective-permute-done.14.heads = f32[96,128]{1,0:T(8,128)S(1)} collective-permute-done((f32[96,128]{1,0:T(8,128)S(1)}, f32[96,128]{1,0:T(8,128)S(1)}, u32[]{:S(2)}, u32[]{:S(2)}) %collective-permute-start.14) | collective-permute-done | bytes 49184 | tf_op jit(solution)/shard_map/ppermute | solution.py:573
  128.4 1.3 collective-permute-start.18
  129.7 0.6 collective-permute-start.15
  130.3 2.0 %collective-permute-start.16 = (f32[80,128]{1,0:T(8,128)S(1)}, f32[80,128]{1,0:T(8,128)S(1)}, u32[]{:S(2)}, u32[]{:S(2)}) collective-permute-start(f32[80,128]{1,0:T(8,128)S(1)} %add.54), channel_id=1, source_target_pairs={{0,128},{8,136},{16,144},{24,152},{32,160},{40,168},{48,176},{56,1... | collective-permute-start | bytes 122888 | tf_op jit(solution)/shard_map/ppermute | solution.py:442
  132.3 2.1 %collective-permute-start.17 = (f32[80,128]{1,0:T(8,128)S(1)}, f32[80,128]{1,0:T(8,128)S(1)}, u32[]{:S(2)}, u32[]{:S(2)}) collective-permute-start(f32[80,128]{1,0:T(8,128)S(1)} %add.54), channel_id=1, source_target_pairs={{0,192},{8,200},{16,208},{24,216},{32,224},{40,232},{48,240},{56,2... | collective-permute-start | bytes 122888 | tf_op jit(solution)/shard_map/ppermute | solution.py:442
  134.4 1.6 %collective-permute-done.18.other = bf16[2,256,128]{2,1,0:T(8,128)(2,1)S(1)} collective-permute-done((bf16[2,256,128]{2,1,0:T(8,128)(2,1)S(1)}, bf16[2,256,128]{2,1,0:T(8,128)(2,1)S(1)}, u32[]{:S(2)}, u32[]{:S(2)}) %collective-permute-start.18) | collective-permute-done | bytes 131104 | tf_op jit(solution)/shard_map/ppermute | solution.py:577
  135.9 0.8 place.1
  136.7 0.8 collective-permute-done.17
  137.6 2.8 %collective-permute-start.20 = (f32[32,128]{1,0:T(8,128)S(1)}, f32[32,128]{1,0:T(8,128)S(1)}, u32[]{:S(2)}, u32[]{:S(2)}) collective-permute-start(f32[32,128]{1,0:T(8,128)S(1)} %slice.21), channel_id=1, source_target_pairs={{0,2},{1,3},{2,0},{3,1},{4,6},{5,7},{6,4},{7,5},{8,10},{9,11},{10,... | collective-permute-start | bytes 49160 | tf_op jit(solution)/shard_map/ppermute | solution.py:442
  140.4 1.2 collective-permute-start.21
  141.6 0.7 settle_x.1
  142.4 0.5 collective-permute-done.20
  142.9 2.5 %collective-permute-done.21 = f32[32,128]{1,0:T(8,128)S(1)} collective-permute-done((f32[32,128]{1,0:T(8,128)S(1)}, f32[32,128]{1,0:T(8,128)S(1)}, u32[]{:S(2)}, u32[]{:S(2)}) %collective-permute-start.21) | collective-permute-done | bytes 16416 | tf_op jit(solution)/shard_map/ppermute | solution.py:442
  145.3 0.0 collective-permute-done.19
  145.4 0.6 finish.1
  (47 shorter events, 0.3 us)
Async XLA Ops:
  0.6 0.8 slice-start
  0.7 0.8 slice-start.1
  0.7 0.7 slice-start.2
  1.4 5.7 %collective-permute-start = (bf16[16,2048]{1,0:T(8,128)(2,1)S(1)}, bf16[16,2048]{1,0:T(8,128)(2,1)S(1)}, u32[]{:S(2)}, u32[]{:S(2)}) collective-permute-start(bf16[16,2048]{1,0:T(8,128)(2,1)S(1)} %pad_maximum_fusion), channel_id=1, source_target_pairs={{0,4},{4,8},{8,12},{12,16},{16,20},{20,24},{24,28},{28,32},{32,36}... | collective-permute-start | bytes 196616 | tf_op jit(solution)/shard_map/ppermute | solution.py:468
  3.4 0.7 copy-start.8
  4.1 0.9 copy-start.3
  5.0 0.9 copy-start.4
  6.0 0.7 copy-start.9
  6.0 0.7 copy-start.10
  6.0 0.7 copy-start.11
  6.0 0.7 copy-start.12
  6.3 1.0 copy-start
  6.7 0.9 copy-start.2
  6.7 0.9 copy-start.5
  7.1 0.7 copy-start.7
  8.9 3.3 %collective-permute-start.1 = (f32[544,128]{1,0:T(8,128)S(1)}, f32[544,128]{1,0:T(8,128)S(1)}, u32[]{:S(2)}, u32[]{:S(2)}) collective-permute-start(f32[544,128]{1,0:T(8,128)S(1)} %get-tuple-element.91), channel_id=1, source_target_pairs={{0,4},{4,0},{1,5},{5,1},{2,6},{6,2},{3,7},{7,3},{8,12},{12,8},{9,1... | collective-permute-start | bytes 835592 | tf_op jit(solution)/shard_map/ppermute | solution.py:425
  52.3 0.9 copy-start.1
  52.3 0.8 copy-start.6
  52.4 2.3 %collective-permute-start.2 = (f32[512,128]{1,0:T(8,128)S(1)}, f32[512,128]{1,0:T(8,128)S(1)}, u32[]{:S(2)}, u32[]{:S(2)}) collective-permute-start(f32[512,128]{1,0:T(8,128)S(1)} %get-tuple-element.95), channel_id=1, source_target_pairs={{0,4},{4,0},{1,5},{5,1},{2,6},{6,2},{3,7},{7,3},{8,12},{12,8},{9,1... | collective-permute-start | bytes 786440 | tf_op jit(solution)/shard_map/ppermute | solution.py:425
  55.1 5.2 %collective-permute-start.4 = (f32[8,128]{1,0:T(8,128)S(1)}, f32[8,128]{1,0:T(8,128)S(1)}, u32[]{:S(2)}, u32[]{:S(2)}) collective-permute-start(f32[8,128]{1,0:T(8,128)S(1)} %get-tuple-element.104), channel_id=1, source_target_pairs={{0,2},{1,3},{2,0},{3,1},{4,6},{5,7},{6,4},{7,5},{8,10},{9,11},{10,... | collective-permute-start | bytes 12296 | tf_op jit(solution)/shard_map/ppermute | solution.py:442
  58.4 4.8 %collective-permute-start.5 = (f32[8,128]{1,0:T(8,128)S(1)}, f32[8,128]{1,0:T(8,128)S(1)}, u32[]{:S(2)}, u32[]{:S(2)}) collective-permute-start(f32[8,128]{1,0:T(8,128)S(1)} %get-tuple-element.104), channel_id=1, source_target_pairs={{0,3},{1,2},{2,1},{3,0},{4,7},{5,6},{6,5},{7,4},{8,11},{9,10},{10,... | collective-permute-start | bytes 12296 | tf_op jit(solution)/shard_map/ppermute | solution.py:442
  59.5 3.8 %collective-permute-start.3 = (f32[8,128]{1,0:T(8,128)S(1)}, f32[8,128]{1,0:T(8,128)S(1)}, u32[]{:S(2)}, u32[]{:S(2)}) collective-permute-start(f32[8,128]{1,0:T(8,128)S(1)} %get-tuple-element.104), channel_id=1, source_target_pairs={{0,1},{1,0},{2,3},{3,2},{4,5},{5,4},{6,7},{7,6},{8,9},{9,8},{10,11... | collective-permute-start | bytes 12296 | tf_op jit(solution)/shard_map/ppermute | solution.py:442
  63.8 1.6 %collective-permute-start.6 = (f32[512,128]{1,0:T(8,128)S(1)}, f32[512,128]{1,0:T(8,128)S(1)}, u32[]{:S(2)}, u32[]{:S(2)}) collective-permute-start(f32[512,128]{1,0:T(8,128)S(1)} %get-tuple-element.107), channel_id=1, source_target_pairs={{0,4},{4,0},{1,5},{5,1},{2,6},{6,2},{3,7},{7,3},{8,12},{12,8},{9,1... | collective-permute-start | bytes 786440 | tf_op jit(solution)/shard_map/ppermute | solution.py:425
  98.9 3.2 %collective-permute-start.7 = (f32[512,128]{1,0:T(8,128)S(1)}, f32[512,128]{1,0:T(8,128)S(1)}, u32[]{:S(2)}, u32[]{:S(2)}) collective-permute-start(f32[512,128]{1,0:T(8,128)S(1)} %get-tuple-element.109), channel_id=1, source_target_pairs={{0,4},{4,0},{1,5},{5,1},{2,6},{6,2},{3,7},{7,3},{8,12},{12,8},{9,1... | collective-permute-start | bytes 786440 | tf_op jit(solution)/shard_map/ppermute | solution.py:425
  105.2 12.2 %collective-permute-start.8 = (f32[2,272,128]{2,1,0:T(8,128)S(1)}, f32[2,272,128]{2,1,0:T(8,128)S(1)}, u32[]{:S(2)}, u32[]{:S(2)}) collective-permute-start(f32[2,272,128]{2,1,0:T(8,128)S(1)} %get-tuple-element.125), channel_id=1, source_target_pairs={{0,3},{1,2},{2,1},{3,0},{4,7},{5,6},{6,5},{7,4},{8,11},{9,10},{10,... | collective-permute-start | bytes 835592 | tf_op jit(solution)/shard_map/ppermute | solution.py:562
  107.2 1.2 collective-permute-start.9
  108.4 4.0 %collective-permute-start.10 = (f32[80,128]{1,0:T(8,128)S(1)}, f32[80,128]{1,0:T(8,128)S(1)}, u32[]{:S(2)}, u32[]{:S(2)}) collective-permute-start(f32[80,128]{1,0:T(8,128)S(1)} %add.49), channel_id=1, source_target_pairs={{0,8},{8,0},{16,24},{24,16},{32,40},{40,32},{48,56},{56,48},{64,72... | collective-permute-start | bytes 122888 | tf_op jit(solution)/shard_map/ppermute | solution.py:437
  112.4 4.9 %collective-permute-start.11 = (f32[80,128]{1,0:T(8,128)S(1)}, f32[80,128]{1,0:T(8,128)S(1)}, u32[]{:S(2)}, u32[]{:S(2)}) collective-permute-start(f32[80,128]{1,0:T(8,128)S(1)} %add.50), channel_id=1, source_target_pairs={{0,16},{8,24},{16,0},{24,8},{32,48},{40,56},{48,32},{56,40},{64,80... | collective-permute-start | bytes 122888 | tf_op jit(solution)/shard_map/ppermute | solution.py:437
  117.4 7.2 %collective-permute-start.12 = (f32[2,272,128]{2,1,0:T(8,128)S(1)}, f32[2,272,128]{2,1,0:T(8,128)S(1)}, u32[]{:S(2)}, u32[]{:S(2)}) collective-permute-start(f32[2,272,128]{2,1,0:T(8,128)S(1)} %add.52), channel_id=1, source_target_pairs={{0,1},{1,0},{2,3},{3,2},{4,5},{5,4},{6,7},{7,6},{8,9},{9,8},{10,11... | collective-permute-start | bytes 835592 | tf_op jit(solution)/shard_map/ppermute | solution.py:568
  117.5 7.1 %collective-permute-start.13 = (f32[80,128]{1,0:T(8,128)S(1)}, f32[80,128]{1,0:T(8,128)S(1)}, u32[]{:S(2)}, u32[]{:S(2)}) collective-permute-start(f32[80,128]{1,0:T(8,128)S(1)} %add.51), channel_id=1, source_target_pairs={{0,56},{8,48},{16,40},{24,32},{32,24},{40,16},{48,8},{56,0},{64,12... | collective-permute-start | bytes 122888 | tf_op jit(solution)/shard_map/ppermute | solution.py:437
  124.7 3.7 %collective-permute-start.14 = (f32[96,128]{1,0:T(8,128)S(1)}, f32[96,128]{1,0:T(8,128)S(1)}, u32[]{:S(2)}, u32[]{:S(2)}) collective-permute-start(f32[96,128]{1,0:T(8,128)S(1)} %pad_maximum_fusion.1), channel_id=1, source_target_pairs={{4,0},{8,4},{12,8},{16,12},{20,16},{24,20},{28,24},{32,28},{36,32}... | collective-permute-start | bytes 147464 | tf_op jit(solution)/shard_map/ppermute | solution.py:573
  128.4 7.6 %collective-permute-start.18 = (bf16[2,256,128]{2,1,0:T(8,128)(2,1)S(1)}, bf16[2,256,128]{2,1,0:T(8,128)(2,1)S(1)}, u32[]{:S(2)}, u32[]{:S(2)}) collective-permute-start(bf16[2,256,128]{2,1,0:T(8,128)(2,1)S(1)} %settle.1.half), channel_id=1, source_target_pairs={{0,3},{1,2},{2,1},{3,0},{4,7},{5,6},{6,5},{7,4},{8,11},{9,10},{10,... | collective-permute-start | bytes 393224 | tf_op jit(solution)/shard_map/ppermute | solution.py:577
  129.7 7.0 %collective-permute-start.15 = (f32[80,128]{1,0:T(8,128)S(1)}, f32[80,128]{1,0:T(8,128)S(1)}, u32[]{:S(2)}, u32[]{:S(2)}) collective-permute-start(f32[80,128]{1,0:T(8,128)S(1)} %add.54), channel_id=1, source_target_pairs={{0,64},{8,72},{16,80},{24,88},{32,96},{40,104},{48,112},{56,120},{... | collective-permute-start | bytes 122888 | tf_op jit(solution)/shard_map/ppermute | solution.py:442
  130.3 6.4 %collective-permute-start.16 = (f32[80,128]{1,0:T(8,128)S(1)}, f32[80,128]{1,0:T(8,128)S(1)}, u32[]{:S(2)}, u32[]{:S(2)}) collective-permute-start(f32[80,128]{1,0:T(8,128)S(1)} %add.54), channel_id=1, source_target_pairs={{0,128},{8,136},{16,144},{24,152},{32,160},{40,168},{48,176},{56,1... | collective-permute-start | bytes 122888 | tf_op jit(solution)/shard_map/ppermute | solution.py:442
  132.3 5.2 %collective-permute-start.17 = (f32[80,128]{1,0:T(8,128)S(1)}, f32[80,128]{1,0:T(8,128)S(1)}, u32[]{:S(2)}, u32[]{:S(2)}) collective-permute-start(f32[80,128]{1,0:T(8,128)S(1)} %add.54), channel_id=1, source_target_pairs={{0,192},{8,200},{16,208},{24,216},{32,224},{40,232},{48,240},{56,2... | collective-permute-start | bytes 122888 | tf_op jit(solution)/shard_map/ppermute | solution.py:442
  137.6 5.3 %collective-permute-start.20 = (f32[32,128]{1,0:T(8,128)S(1)}, f32[32,128]{1,0:T(8,128)S(1)}, u32[]{:S(2)}, u32[]{:S(2)}) collective-permute-start(f32[32,128]{1,0:T(8,128)S(1)} %slice.21), channel_id=1, source_target_pairs={{0,2},{1,3},{2,0},{3,1},{4,6},{5,7},{6,4},{7,5},{8,10},{9,11},{10,... | collective-permute-start | bytes 49160 | tf_op jit(solution)/shard_map/ppermute | solution.py:442
  140.4 4.9 %collective-permute-start.21 = (f32[32,128]{1,0:T(8,128)S(1)}, f32[32,128]{1,0:T(8,128)S(1)}, u32[]{:S(2)}, u32[]{:S(2)}) collective-permute-start(f32[32,128]{1,0:T(8,128)S(1)} %slice.21), channel_id=1, source_target_pairs={{0,3},{1,2},{2,1},{3,0},{4,7},{5,6},{6,5},{7,4},{8,11},{9,10},{10,... | collective-permute-start | bytes 49160 | tf_op jit(solution)/shard_map/ppermute | solution.py:442
  141.6 3.7 %collective-permute-start.19 = (f32[32,128]{1,0:T(8,128)S(1)}, f32[32,128]{1,0:T(8,128)S(1)}, u32[]{:S(2)}, u32[]{:S(2)}) collective-permute-start(f32[32,128]{1,0:T(8,128)S(1)} %slice.21), channel_id=1, source_target_pairs={{0,1},{1,0},{2,3},{3,2},{4,5},{5,4},{6,7},{7,6},{8,9},{9,8},{10,11... | collective-permute-start | bytes 49160 | tf_op jit(solution)/shard_map/ppermute | solution.py:442
